TPU v7x, 256 devices: a whole 4x4x8 slice. The times are simulated.
256 devices in a mesh: seq: 64 (over z, y, core), head: 4 (over x).
Axes of the slice: x: 4, y: 4, z: 8, core: 2. Of those that a mesh axis runs over, the one named last changes fastest.
Arguments:
- query_rows: bfloat16 [65536, 3072], P('seq', 'head'), may hold values from -6 to 6
- key_rows: bfloat16 [65536, 3072], P('seq', 'head'), may hold values from -6 to 6
- value_rows: bfloat16 [65536, 3072], P('seq', 'head'), may hold values from -6 to 6
- query_gain: float32 [128], replicated, may hold values from 1 to 2.5
- key_gain: float32 [128], replicated, may hold values from 1 to 2.5
- head_class: int32 [24], P('head'), may hold values from 0 to 1, as said below
- out_weight: bfloat16 [3072, 3072], P('head'), may hold values from -0.109375 to 0.109375
Outputs:
- attn_out: bfloat16 [65536, 3072], P('seq', 'head')
Inputs may be any that keep to these rules, and one draw needn't show every extreme that they name: `head_class`: in every group of 6 consecutive heads, 1 to 4 heads are temporal, and some group has exactly 4.
All inputs are finite; a program needn't handle non-finite values.
Results may differ from a plain program's by a relative error of at most 0.013.
Values may be sent and summed in bfloat16 or wider, within the bound.
No kernel may reach another device: no remote copies, remote signals or barrier semaphores. Data moves between devices by JAX's collectives and lax.ppermute only.
A program may use at most 128 MiB of HBM per device.

v0:
```python
import math

import jax
import jax.numpy as jnp
from jax import lax
from jax.sharding import PartitionSpec as P

FRAMES = 32


epsilon = 1e-06


def from_partner(block, axis, stride):
    count = lax.axis_size(axis)
    route = []
    for low in range(count):
        high = low | 1 << stride
        if high != low and high < count:
            route += [(low, high), (high, low)]
    return lax.ppermute(block, axis, route)


def normed(row_block, gain_row, head_count):
    widened = row_block.astype(jnp.float32).reshape(row_block.shape[0], head_count, -1)
    scaled = (
        widened
        * lax.rsqrt(jnp.mean(widened * widened, axis=-1, keepdims=True) + epsilon)
        * gain_row
    )
    return scaled.astype(jnp.bfloat16)


def softmax_weights(scores):
    exponent = jnp.exp(scores)
    return (exponent / jnp.sum(exponent, axis=-1, keepdims=True)).astype(jnp.bfloat16)


def attend_head(pieces):
    query_part, key_part, value_part = pieces
    head_size = query_part.shape[-1]
    spatial_scores = jnp.einsum(
        "nqd,nkd->nqk", query_part, key_part, preferred_element_type=jnp.float32
    ) * (1.0 / math.sqrt(head_size))
    spatial_weights = softmax_weights(spatial_scores)
    spatial_out = jnp.einsum(
        "nqk,nkd->nqd", spatial_weights, value_part, preferred_element_type=jnp.float32
    )
    return spatial_out.astype(jnp.bfloat16)


def spatial(queries, keys_in, values_in):
    token_count, head_count, head_size = queries.shape
    other_keys, other_values = from_partner((keys_in, values_in), "seq", 0)
    keys_in = jnp.concatenate([keys_in, other_keys], axis=0)
    values_in = jnp.concatenate([values_in, other_values], axis=0)
    key_len = 2 * token_count
    block_count = token_count // token_count

    def by_head(array_in, length):
        return jnp.moveaxis(array_in, 1, 0).reshape(head_count, block_count, length, head_size)

    results = lax.map(
        attend_head,
        (by_head(queries, token_count), by_head(keys_in, key_len), by_head(values_in, key_len)),
    )
    return jnp.moveaxis(results.reshape(head_count, token_count, head_size), 0, 1)


def attend_frames(pieces):
    query_part, key_part, value_part = pieces
    token_count = query_part.shape[0]
    head_count = query_part.shape[2]
    head_size = query_part.shape[3]
    shaped = (FRAMES, token_count // FRAMES, head_count, head_size)
    temporal_scores = jnp.einsum(
        "fphd,gphd->phfg",
        query_part.reshape(shaped),
        key_part.reshape(shaped),
        preferred_element_type=jnp.float32,
    ) * (1.0 / math.sqrt(head_size))
    temporal_weights = softmax_weights(temporal_scores)
    temporal_out = jnp.einsum(
        "phfg,gphd->fphd",
        temporal_weights,
        value_part.reshape(shaped),
        preferred_element_type=jnp.float32,
    ).astype(jnp.bfloat16)
    return lax.all_to_all(
        temporal_out.reshape(query_part.shape), "seq", split_axis=0, concat_axis=1, tiled=True
    )


def temporal(query_heads, key_heads, value_heads, seq_count):
    token_count = query_heads.shape[0]

    def regroup(array_in):
        return array_in.reshape(
            token_count // seq_count, seq_count, array_in.shape[1], array_in.shape[2]
        )

    returned = attend_frames(
        (
            lax.all_to_all(regroup(query_heads), "seq", split_axis=1, concat_axis=0, tiled=True),
            lax.all_to_all(regroup(key_heads), "seq", split_axis=1, concat_axis=0, tiled=True),
            lax.all_to_all(regroup(value_heads), "seq", split_axis=1, concat_axis=0, tiled=True),
        )
    )
    return returned.reshape(query_heads.shape)


def body(query_rows, key_rows, value_rows, query_gain, key_gain, head_class, out_weight):
    head_count = head_class.shape[0]
    token_count = query_rows.shape[0]
    head_size = query_rows.shape[1] // head_count
    seq_count = lax.axis_size("seq")
    query_normed = normed(query_rows, query_gain, head_count)
    key_normed = normed(key_rows, key_gain, head_count)
    value_heads = value_rows.reshape(token_count, head_count, head_size)
    local_out = spatial(query_normed, key_normed, value_heads)
    flags = head_class == 1
    far_out = temporal(query_normed, key_normed, value_heads, seq_count)
    chosen = jnp.where(flags[None, :, None], far_out, local_out)
    flattened = chosen.reshape(token_count, head_count * head_size)
    partial_value = jnp.dot(flattened, out_weight, preferred_element_type=jnp.float32)
    summed = lax.psum_scatter(
        partial_value.astype(jnp.bfloat16), "head", scatter_dimension=1, tiled=True
    )
    return summed


def solution(mesh):
    return jax.shard_map(
        body,
        mesh=mesh,
        in_specs=(
            P("seq", "head"),
            P("seq", "head"),
            P("seq", "head"),
            P(),
            P(),
            P("head"),
            P("head", None),
        ),
        out_specs=P("seq", "head"),
        check_vma=False,
    )
```

profile of v0, /device:TPU:8, one launch (start us, length us, event | category | flops | bytes accessed | tf_op | source)
XLA Modules:
  0.0 315.1 jit_solution(1044183878601048914)
XLA Ops:
  13.3 4.6 %reshape.117 = f32[16,64,6,128]{3,2,1,0:T(8,128)} reshape(f32[1024,768]{1,0:T(8,128)} %copy.56) | data formatting | bytes 6291456 | tf_op jit(solution)/shard_map/reshape | solution.py:25
  25.2 12.3 %all-to-all-start.1 = ((bf16[16,64,6,128]{3,0,2,1:T(8,128)(2,1)}), bf16[16,64,6,128]{3,0,2,1:T(8,128)(2,1)}, u32[]{:S(2)}, u32[]{:S(2)}) async-start(bf16[16,64,6,128]{3,0,2,1:T(8,128)(2,1)} %copy.58), calls=%async_computation.1 | async-start | bytes 3145728 | tf_op jit(solution)/shard_map/all_to_all | solution.py:105
  43.2 3.5 %convert_element_type.38 = f32[1024,768]{0,1:T(8,128)} convert(bf16[1024,768]{0,1:T(8,128)(2,1)} %copy.50) | non-fusion elementwise | flops 786432 | bytes 4718592 | tf_op jit(solution)/shard_map/convert_element_type | solution.py:25
  46.7 4.7 %reshape.114 = f32[16,64,6,128]{3,2,1,0:T(8,128)} reshape(f32[1024,768]{1,0:T(8,128)} %copy.51) | data formatting | bytes 6291456 | tf_op jit(solution)/shard_map/reshape | solution.py:25
  60.7 16.8 %all-to-all-done.1 = bf16[16,64,6,128]{3,0,2,1:T(8,128)(2,1)} async-done(((bf16[16,64,6,128]{3,0,2,1:T(8,128)(2,1)}), bf16[16,64,6,128]{3,0,2,1:T(8,128)(2,1)}, u32[]{:S(2)}, u32[]{:S(2)}) %all-to-all-start.1) | async-done | bytes 1572896 | tf_op jit(solution)/shard_map/all_to_all | solution.py:105
  77.4 5.6 %all-to-all-start = ((bf16[16,64,6,128]{3,0,2,1:T(8,128)(2,1)}), bf16[16,64,6,128]{3,0,2,1:T(8,128)(2,1)}, u32[]{:S(2)}, u32[]{:S(2)}) async-start(bf16[16,64,6,128]{3,0,2,1:T(8,128)(2,1)} %copy.53), calls=%async_computation | async-start | bytes 3145728 | tf_op jit(solution)/shard_map/all_to_all | solution.py:104
  83.1 4.3 %reshape_reshape.3 = bf16[16,64,6,128]{3,2,1,0:T(8,128)(2,1)} reshape(bf16[1024,768]{1,0:T(8,128)(2,1)} %param.11) | data formatting | bytes 3145728 | tf_op jit(solution)/shard_map/reshape;reshape | solution.py:98
  87.4 4.6 %copy.62 = bf16[16,64,6,128]{3,0,2,1:T(8,128)(2,1)} copy(bf16[16,64,6,128]{3,2,1,0:T(8,128)(2,1)} %reshape_reshape.3) | data formatting | bytes 3145728 | tf_op jit(solution)/shard_map/reshape;reshape | solution.py:98
  91.9 31.1 %all-to-all-done = bf16[16,64,6,128]{3,0,2,1:T(8,128)(2,1)} async-done(((bf16[16,64,6,128]{3,0,2,1:T(8,128)(2,1)}), bf16[16,64,6,128]{3,0,2,1:T(8,128)(2,1)}, u32[]{:S(2)}, u32[]{:S(2)}) %all-to-all-start) | async-done | bytes 1572896 | tf_op jit(solution)/shard_map/all_to_all | solution.py:104
  123.0 5.6 %all-to-all-start.2 = ((bf16[16,64,6,128]{3,0,2,1:T(8,128)(2,1)}), bf16[16,64,6,128]{3,0,2,1:T(8,128)(2,1)}, u32[]{:S(2)}, u32[]{:S(2)}) async-start(bf16[16,64,6,128]{3,0,2,1:T(8,128)(2,1)} %copy.62), calls=%async_computation.2 | async-start | bytes 3145728 | tf_op jit(solution)/shard_map/all_to_all | solution.py:106
  137.9 3.4 %maximum_bitcast_fusion.1 = bf16[6,1,2048,128]{2,3,0,1:T(8,128)(2,1)} fusion(bf16[1024,6,128]{0,2,1:T(8,128)(2,1)} %collective-permute-done.1, bf16[1024,6,128]{0,2,1:T(8,128)(2,1)S(1)} %bitcast.82), kind=kLoop, calls=%fused_computation.21 | loop fusion | flops 6291456 | bytes 6291456 | tf_op jit(solution)/shard_map/reshape | solution.py:61
  144.7 5.0 %fusion.15 = (f32[32,6,32]{2,1,0:T(8,128)S(1)}, f32[32,6,32,32]{2,3,1,0:T(8,128)}) fusion(bf16[32,32,6,128]{3,1,0,2:T(8,128)(2,1)S(1)} %bitcast.83, bf16[32,32,6,128]{3,1,0,2:T(8,128)(2,1)S(1)} %bitcast.84), kind=kOutput, calls=%fused_computation.28 | convolution fusion | flops 50718720 | bytes 3956736 | tf_op jit(solution)/shard_map/fphd,gphd->phfg/dot_general | solution.py:76
  149.7 18.9 %all-to-all-done.2 = bf16[16,64,6,128]{3,0,2,1:T(8,128)(2,1)} async-done(((bf16[16,64,6,128]{3,0,2,1:T(8,128)(2,1)}), bf16[16,64,6,128]{3,0,2,1:T(8,128)(2,1)}, u32[]{:S(2)}, u32[]{:S(2)}) %all-to-all-start.2) | async-done | bytes 1572896 | tf_op jit(solution)/shard_map/all_to_all | solution.py:106
  176.0 5.6 %all-to-all-start.3 = ((bf16[1024,1,6,128]{3,2,1,0:T(8,128)(2,1)}), bf16[1024,1,6,128]{3,2,1,0:T(8,128)(2,1)}, u32[]{:S(2)}, u32[]{:S(2)}) async-start(bf16[1024,1,6,128]{3,2,1,0:T(8,128)(2,1)} %copy.67), calls=%async_computation.3 | async-start | bytes 4194304 | tf_op jit(solution)/shard_map/all_to_all | solution.py:89
  181.9 37.0 %while.10 = (s32[]{:T(128)}, bf16[6,1,1024,128]{3,2,1,0:T(8,128)(2,1)}, bf16[6,1,1024,128]{2,3,0,1:T(8,128)(2,1)}, bf16[6,1,2048,128]{2,3,0,1:T(8,128)(2,1)S(1)}, bf16[6,1,2048,128]{2,3,0,1:T(8,128)(2,1)}, /*index=5*/s32[]{:T(128)}) while((s32[]{:T(128)}, bf16[6,1,1024,128]{3,2,1,0:T(8,128)(2,1)}, bf16[6,1,1024,128]{2,3,0,1:T(8,128)(2,1)}, ...), condition=%wide.region_5.6_spmd, body=%wide.region_3.0_spmd.sunk | while | flops 1084357632 | bytes 18360396 | solution.py:63
  184.5 3.6 %fusion.33 = bf16[6,1,1024,128]{3,2,1,0:T(8,128)(2,1)} fusion(bf16[6,1,1024,128]{3,2,1,0:T(8,128)(2,1)} %get-tuple-element.104, s32[]{:T(128)S(6)} %copy.95, f32[1024,2048]{1,0:T(8,128)S(1)} %get-tuple-element.95, f32[1024]{0:T(1024)S(1)} %get-tuple-element.96, bf16[6,1,2048,128]{2,3,0,1:T(8,128)(2,1)} %get-tuple-element.113), kind=kOutput, calls=%fused_computation.6.clone.1 | convolution fusion | flops 543293440 | bytes 9180160 | tf_op jit(solution)/shard_map/while/body/eval_jaxpr/nqk,nkd->nqd/dot_general | solution.py:46
  190.7 3.6 %fusion.33 = bf16[6,1,1024,128]{3,2,1,0:T(8,128)(2,1)} fusion(bf16[6,1,1024,128]{3,2,1,0:T(8,128)(2,1)} %get-tuple-element.104, s32[]{:T(128)S(6)} %copy.95, f32[1024,2048]{1,0:T(8,128)S(1)} %get-tuple-element.95, f32[1024]{0:T(1024)S(1)} %get-tuple-element.96, bf16[6,1,2048,128]{2,3,0,1:T(8,128)(2,1)} %get-tuple-element.113), kind=kOutput, calls=%fused_computation.6.clone.1 | convolution fusion | flops 543293440 | bytes 9180160 | tf_op jit(solution)/shard_map/while/body/eval_jaxpr/nqk,nkd->nqd/dot_general | solution.py:46
  196.8 3.6 %fusion.33 = bf16[6,1,1024,128]{3,2,1,0:T(8,128)(2,1)} fusion(bf16[6,1,1024,128]{3,2,1,0:T(8,128)(2,1)} %get-tuple-element.104, s32[]{:T(128)S(6)} %copy.95, f32[1024,2048]{1,0:T(8,128)S(1)} %get-tuple-element.95, f32[1024]{0:T(1024)S(1)} %get-tuple-element.96, bf16[6,1,2048,128]{2,3,0,1:T(8,128)(2,1)} %get-tuple-element.113), kind=kOutput, calls=%fused_computation.6.clone.1 | convolution fusion | flops 543293440 | bytes 9180160 | tf_op jit(solution)/shard_map/while/body/eval_jaxpr/nqk,nkd->nqd/dot_general | solution.py:46
  203.0 3.6 %fusion.33 = bf16[6,1,1024,128]{3,2,1,0:T(8,128)(2,1)} fusion(bf16[6,1,1024,128]{3,2,1,0:T(8,128)(2,1)} %get-tuple-element.104, s32[]{:T(128)S(6)} %copy.95, f32[1024,2048]{1,0:T(8,128)S(1)} %get-tuple-element.95, f32[1024]{0:T(1024)S(1)} %get-tuple-element.96, bf16[6,1,2048,128]{2,3,0,1:T(8,128)(2,1)} %get-tuple-element.113), kind=kOutput, calls=%fused_computation.6.clone.1 | convolution fusion | flops 543293440 | bytes 9180160 | tf_op jit(solution)/shard_map/while/body/eval_jaxpr/nqk,nkd->nqd/dot_general | solution.py:46
  209.2 3.6 %fusion.33 = bf16[6,1,1024,128]{3,2,1,0:T(8,128)(2,1)} fusion(bf16[6,1,1024,128]{3,2,1,0:T(8,128)(2,1)} %get-tuple-element.104, s32[]{:T(128)S(6)} %copy.95, f32[1024,2048]{1,0:T(8,128)S(1)} %get-tuple-element.95, f32[1024]{0:T(1024)S(1)} %get-tuple-element.96, bf16[6,1,2048,128]{2,3,0,1:T(8,128)(2,1)} %get-tuple-element.113), kind=kOutput, calls=%fused_computation.6.clone.1 | convolution fusion | flops 543293440 | bytes 9180160 | tf_op jit(solution)/shard_map/while/body/eval_jaxpr/nqk,nkd->nqd/dot_general | solution.py:46
  215.3 3.6 %fusion.33 = bf16[6,1,1024,128]{3,2,1,0:T(8,128)(2,1)} fusion(bf16[6,1,1024,128]{3,2,1,0:T(8,128)(2,1)} %get-tuple-element.104, s32[]{:T(128)S(6)} %copy.95, f32[1024,2048]{1,0:T(8,128)S(1)} %get-tuple-element.95, f32[1024]{0:T(1024)S(1)} %get-tuple-element.96, bf16[6,1,2048,128]{2,3,0,1:T(8,128)(2,1)} %get-tuple-element.113), kind=kOutput, calls=%fused_computation.6.clone.1 | convolution fusion | flops 543293440 | bytes 9180160 | tf_op jit(solution)/shard_map/while/body/eval_jaxpr/nqk,nkd->nqd/dot_general | solution.py:46
  218.9 13.9 %all-to-all-done.3 = bf16[1024,1,6,128]{3,2,1,0:T(8,128)(2,1)} async-done(((bf16[1024,1,6,128]{3,2,1,0:T(8,128)(2,1)}), bf16[1024,1,6,128]{3,2,1,0:T(8,128)(2,1)}, u32[]{:S(2)}, u32[]{:S(2)}) %all-to-all-start.3) | async-done | bytes 1572896 | tf_op jit(solution)/shard_map/all_to_all | solution.py:89
  236.0 9.4 %convolution_convert_fusion = bf16[1024,3072]{1,0:T(8,128)(2,1)} fusion(bf16[1024,768]{0,1:T(8,128)(2,1)S(1)} %bitcast.88, bf16[768,3072]{1,0:T(8,128)(2,1)} %param.15), kind=kOutput, calls=%fused_computation.17 | convolution fusion | flops 4834983936 | bytes 12582912 | tf_op jit(solution)/shard_map/dot_general | solution.py:125
  245.4 62.9 %reduce-scatter.2.cloned.1.call-done = bf16[1024,768]{1,0:T(8,128)(2,1)} async-done(((bf16[1024,3072]{1,0:T(8,128)(2,1)}), bf16[1024,768]{1,0:T(8,128)(2,1)}) %reduce-scatter.2.cloned.1.call-update) | async-done | bytes 1572880 | tf_op jit(solution)/shard_map/reduce_scatter | solution.py:126
  (59 shorter events, 68.0 us)
Async XLA Ops:
  8.3 1.1 copy-start.1
  17.8 1.4 copy-start.5
  25.2 52.2 %all-to-all-start.1 = ((bf16[16,64,6,128]{3,0,2,1:T(8,128)(2,1)}), bf16[16,64,6,128]{3,0,2,1:T(8,128)(2,1)}, u32[]{:S(2)}, u32[]{:S(2)}) async-start(bf16[16,64,6,128]{3,0,2,1:T(8,128)(2,1)} %copy.58), calls=%async_computation.1 | async-start | bytes 3145728 | tf_op jit(solution)/shard_map/all_to_all | solution.py:105
  51.4 3.4 %copy-start.6 = (f32[128]{0:T(128)S(1)}, f32[128]{0:T(128)}, u32[]{:S(2)}) copy-start(f32[128]{0:T(128)} %param.12) | copy-start | bytes 1540
  77.4 45.6 %all-to-all-start = ((bf16[16,64,6,128]{3,0,2,1:T(8,128)(2,1)}), bf16[16,64,6,128]{3,0,2,1:T(8,128)(2,1)}, u32[]{:S(2)}, u32[]{:S(2)}) async-start(bf16[16,64,6,128]{3,0,2,1:T(8,128)(2,1)} %copy.53), calls=%async_computation | async-start | bytes 3145728 | tf_op jit(solution)/shard_map/all_to_all | solution.py:104
  123.0 45.6 %all-to-all-start.2 = ((bf16[16,64,6,128]{3,0,2,1:T(8,128)(2,1)}), bf16[16,64,6,128]{3,0,2,1:T(8,128)(2,1)}, u32[]{:S(2)}, u32[]{:S(2)}) async-start(bf16[16,64,6,128]{3,0,2,1:T(8,128)(2,1)} %copy.62), calls=%async_computation.2 | async-start | bytes 3145728 | tf_op jit(solution)/shard_map/all_to_all | solution.py:106
  128.6 5.1 %copy-start.7 = (s32[6]{0:T(128)S(1)}, s32[6]{0:T(128)}, u32[]{:S(2)}) copy-start(s32[6]{0:T(128)} %param.14) | copy-start | bytes 76
  130.4 3.3 %copy-start = (f32[1024,768]{0,1:T(8,128)S(1)}, f32[1024,768]{0,1:T(8,128)}, u32[]{:S(2)}) copy-start(f32[1024,768]{0,1:T(8,128)} %convert_element_type.38) | copy-start | bytes 9437188
  130.4 5.1 %collective-permute-start = (bf16[1024,6,128]{0,2,1:T(8,128)(2,1)}, bf16[1024,6,128]{0,2,1:T(8,128)(2,1)}, u32[]{:S(2)}, u32[]{:S(2)}) collective-permute-start(bf16[1024,6,128]{0,2,1:T(8,128)(2,1)} %multiply_convert_fusion.2), channel_id=1, source_target_pairs={{0,4},{4,0},{8,12},{12,8},{16,20},{20,16},{24,28},{28,24},{32,36},... | collective-permute-start | bytes 4718600 | tf_op jit(solution)/shard_map/ppermute | solution.py:21
  133.3 4.5 %collective-permute-start.1 = (bf16[1024,6,128]{0,2,1:T(8,128)(2,1)}, bf16[1024,6,128]{0,2,1:T(8,128)(2,1)}, u32[]{:S(2)}, u32[]{:S(2)}) collective-permute-start(bf16[1024,6,128]{0,2,1:T(8,128)(2,1)} %bitcast.81), channel_id=1, source_target_pairs={{0,4},{4,0},{8,12},{12,8},{16,20},{20,16},{24,28},{28,24},{32,36},... | collective-permute-start | bytes 4718600 | tf_op jit(solution)/shard_map/ppermute | solution.py:21
  135.5 2.4 copy-start.2
  168.6 2.4 copy-start.3
  176.0 56.8 %all-to-all-start.3 = ((bf16[1024,1,6,128]{3,2,1,0:T(8,128)(2,1)}), bf16[1024,1,6,128]{3,2,1,0:T(8,128)(2,1)}, u32[]{:S(2)}, u32[]{:S(2)}) async-start(bf16[1024,1,6,128]{3,2,1,0:T(8,128)(2,1)} %copy.67), calls=%async_computation.3 | async-start | bytes 4194304 | tf_op jit(solution)/shard_map/all_to_all | solution.py:89
  181.6 126.6 %reduce-scatter.2.cloned.1.call-start = ((), (), s32[]{:S(2)}) async-start(), calls=%async_computation.5 | async-start | bytes 7864320 | tf_op jit(solution)/shard_map/reduce_scatter | solution.py:126
  218.9 16.1 %copy-start.4 = (bf16[6,1,1024,128]{3,2,1,0:T(8,128)(2,1)S(1)}, bf16[6,1,1024,128]{3,2,1,0:T(8,128)(2,1)}, u32[]{:S(2)}) copy-start(bf16[6,1,1024,128]{3,2,1,0:T(8,128)(2,1)} %get-tuple-element.32) | copy-start | bytes 4718596
Sparse Core Ops, SparseCore 0:
  245.6 62.6 reduce-scatter.1
where the time goes:
time: 318 us; the launch traced here: 315 us
  waiting for transfers between devices  144 us (45%)
  matrix products  53 us (17%)
  local copies, waits for them, and re-layouts  51.6 us (16%)
  starting transfers between devices  29.9 us (9%)
  other arithmetic  23.4 us (7%)
  between operations  13.6 us (4%)
    reduce_scatter x1, waiting for transfers between devices, body(): lax.psum_scatter(partial_value.astype(jnp.bfloat16), 'head', scatter_dime...  62.9 us
    all_to_all x1, waiting for transfers between devices, temporal(): lax.all_to_all(regroup(query_heads), 'seq', split_axis=1, concat_axis=0,...  31.1 us
    dot_general x6, matrix products, attend_head(): jnp.einsum('nqk,nkd->nqd', spatial_weights, value_part, preferred_element...  21.4 us
    all_to_all x1, waiting for transfers between devices, temporal(): lax.all_to_all(regroup(value_heads), 'seq', split_axis=1, concat_axis=0,...  18.9 us
    all_to_all x1, waiting for transfers between devices, temporal(): lax.all_to_all(regroup(key_heads), 'seq', split_axis=1, concat_axis=0, ti...  16.8 us
    dot_general x6, matrix products, attend_head(): jnp.einsum('nqd,nkd->nqk', query_part, key_part, preferred_element_type=j...  15.6 us
    all_to_all x1, waiting for transfers between devices, attend_frames(): lax.all_to_all(temporal_out.reshape(query_part.shape), 'seq', split_axis=...  13.9 us
    all_to_all x1, starting transfers between devices, temporal(): lax.all_to_all(regroup(key_heads), 'seq', split_axis=1, concat_axis=0, ti...  12.3 us
  transfers between devices with their start and end apart: 7, of which 5 were waited for; matrix products, arithmetic and copies ran while one was open for 28% of the time, Pallas kernels for 0%

commit v1 on v0

v1 whole, which is shorter than its diff:
```python
import functools
import math

import jax
import jax.numpy as jnp
from jax import lax
from jax.experimental import pallas as pl
from jax.experimental.pallas import tpu as pltpu
from jax.sharding import PartitionSpec as P

FRAMES = 32
TMAX = 4
CORES = 2
HD = 128
EPSILON = 1e-06
LOG2_SCALE = math.log2(math.e) / math.sqrt(HD)
VMEM_LIMIT = 40 * 1024 * 1024


def temporal_count(classes, head_count):
    total = classes[0]
    for head in range(1, head_count):
        total = total + classes[head]
    return total


def head_of(classes, slot, head_count):
    temporal_seen = jnp.int32(0)
    spatial_seen = temporal_count(classes, head_count)
    found = jnp.int32(0)
    for head in range(head_count):
        kind = classes[head]
        rank = jnp.where(kind == 1, temporal_seen, spatial_seen)
        found = jnp.where(rank == slot, jnp.int32(head), found)
        temporal_seen = temporal_seen + kind
        spatial_seen = spatial_seen + 1 - kind
    return found


def normed(rows, gain):
    widened = rows.astype(jnp.float32)
    mean = jnp.mean(widened * widened, axis=-1, keepdims=True)
    return (widened * lax.rsqrt(mean + EPSILON) * gain).astype(jnp.bfloat16)


def scores_of(queries, keys):
    return lax.dot_general(queries, keys, (((1,), (1,)), ((), ())), preferred_element_type=jnp.float32)


def pack_kernel(classes, query, key, value, query_gain, key_gain, out):
    out[:, :HD] = normed(query[...], query_gain[...])
    out[:, HD : 2 * HD] = normed(key[...], key_gain[...])
    out[:, 2 * HD :] = value[...]


def pack(head_class, query_rows, key_rows, value_rows, query_gain, key_gain):
    tokens, width = query_rows.shape
    head_count = width // HD
    block = tokens // 2

    def rows(slot, row, classes):
        return row, head_of(classes, slot, head_count)

    row_spec = pl.BlockSpec((block, HD), rows)
    gain_spec = pl.BlockSpec((1, HD), lambda slot, row, classes: (0, 0))
    return pl.pallas_call(
        pack_kernel,
        grid_spec=pltpu.PrefetchScalarGridSpec(
            num_scalar_prefetch=1,
            grid=(TMAX, tokens // block),
            in_specs=[row_spec, row_spec, row_spec, gain_spec, gain_spec],
            out_specs=pl.BlockSpec((block, 3 * HD), lambda slot, row, classes: (row, slot)),
        ),
        out_shape=jax.ShapeDtypeStruct((tokens, TMAX * 3 * HD), jnp.bfloat16),
        cost_estimate=pl.CostEstimate(flops=8 * tokens * TMAX * HD, bytes_accessed=12 * tokens * TMAX * HD, transcendentals=0),
        name="pack",
    )(head_class, query_rows, key_rows, value_rows, query_gain, key_gain)


def spatial_kernel(head_count, classes, query, key, other_key, value, other_value, query_gain, key_gain, front, back, keys, values):
    slot = pl.program_id(0)
    tokens = query.shape[0]
    chunk = tokens // 4
    is_front = slot < TMAX

    @pl.when(slot >= temporal_count(classes, head_count))
    def _():
        keys[:tokens] = normed(key[...], key_gain[...])
        keys[tokens:] = normed(other_key[...], key_gain[...])
        values[:tokens, :HD] = value[...]
        values[tokens:, :HD] = other_value[...]
        values[:, HD:] = jnp.ones((2 * tokens, HD), jnp.bfloat16)

        def step(index, carry):
            rows = pl.ds(pl.multiple_of(index * chunk, chunk), chunk)
            queries = normed(query[rows, :], query_gain[...])
            weights = jnp.exp2(scores_of(queries, keys[...]) * LOG2_SCALE).astype(jnp.bfloat16)
            summed = jnp.dot(weights, values[...], preferred_element_type=jnp.float32)
            result = (summed[:, :HD] / summed[:, HD:]).astype(jnp.bfloat16)

            @pl.when(is_front)
            def _():
                front[rows, :] = result

            @pl.when(jnp.logical_not(is_front))
            def _():
                back[rows, :] = result

            return carry

        lax.fori_loop(0, tokens // chunk, step, 0)

    @pl.when(slot < temporal_count(classes, head_count))
    def _():
        front[...] = jnp.zeros_like(front)


def spatial(head_class, query_rows, key_rows, other_keys, value_rows, other_values, query_gain, key_gain):
    tokens, width = query_rows.shape
    head_count = width // HD

    def rows(slot, classes):
        return 0, head_of(classes, slot, head_count)

    row_spec = pl.BlockSpec((tokens, HD), rows)
    gain_spec = pl.BlockSpec((1, HD), lambda slot, classes: (0, 0))
    return pl.pallas_call(
        functools.partial(spatial_kernel, head_count),
        grid_spec=pltpu.PrefetchScalarGridSpec(
            num_scalar_prefetch=1,
            grid=(head_count,),
            in_specs=[row_spec] * 5 + [gain_spec] * 2,
            out_specs=[
                pl.BlockSpec((tokens, HD), lambda slot, classes: (0, jnp.minimum(slot, TMAX - 1))),
                pl.BlockSpec((tokens, HD), lambda slot, classes: (0, jnp.maximum(slot - TMAX, 0))),
            ],
            scratch_shapes=[
                pltpu.VMEM((2 * tokens, HD), jnp.bfloat16),
                pltpu.VMEM((2 * tokens, 2 * HD), jnp.bfloat16),
            ],
        ),
        out_shape=[
            jax.ShapeDtypeStruct((tokens, TMAX * HD), jnp.bfloat16),
            jax.ShapeDtypeStruct((tokens, width - TMAX * HD), jnp.bfloat16),
        ],
        compiler_params=pltpu.CompilerParams(vmem_limit_bytes=VMEM_LIMIT),
        cost_estimate=pl.CostEstimate(
            flops=16 * tokens * tokens * width, bytes_accessed=12 * tokens * width, transcendentals=2 * tokens * tokens * head_count
        ),
        name="spatial",
    )(head_class, query_rows, key_rows, other_keys, value_rows, other_values, query_gain, key_gain)


def temporal_kernel(head_count, first, classes, packed, out):
    slot = first + pl.program_id(0)
    frames, places = packed.shape[0], packed.shape[1]
    count = frames * places

    @pl.when(slot < temporal_count(classes, head_count))
    def _():
        block = packed[...]
        queries = block[:, :, :HD].reshape(count, HD)
        keys = block[:, :, HD : 2 * HD].reshape(count, HD)
        values = block[:, :, 2 * HD :].reshape(count, HD)
        row = lax.broadcasted_iota(jnp.int32, (count, count), 0)
        column = lax.broadcasted_iota(jnp.int32, (count, count), 1)
        same = (row & (places - 1)) == (column & (places - 1))
        scaled = jnp.where(same, scores_of(queries, keys) * LOG2_SCALE, -1e30)
        weights = jnp.exp2(scaled).astype(jnp.bfloat16)
        both = jnp.concatenate([values, jnp.ones_like(values)], axis=1)
        summed = jnp.dot(weights, both, preferred_element_type=jnp.float32)
        out[...] = (summed[:, :HD] / summed[:, HD:]).astype(jnp.bfloat16).reshape(out.shape)

    @pl.when(slot >= temporal_count(classes, head_count))
    def _():
        out[...] = jnp.zeros_like(out)


def temporal(head_class, packed, first, slots):
    frames, positions, _ = packed.shape
    places = 16
    return pl.pallas_call(
        functools.partial(temporal_kernel, head_class.shape[0], first),
        grid_spec=pltpu.PrefetchScalarGridSpec(
            num_scalar_prefetch=1,
            grid=(slots, positions // places),
            in_specs=[pl.BlockSpec((frames, places, 3 * HD), lambda slot, part, classes: (0, part, slot + first))],
            out_specs=pl.BlockSpec((frames, places, HD), lambda slot, part, classes: (0, part, slot)),
        ),
        out_shape=jax.ShapeDtypeStruct((frames, positions, slots * HD), jnp.bfloat16),
        compiler_params=pltpu.CompilerParams(vmem_limit_bytes=VMEM_LIMIT),
        cost_estimate=pl.CostEstimate(
            flops=6 * frames * frames * places * positions * slots * HD,
            bytes_accessed=8 * frames * positions * slots * HD,
            transcendentals=frames * frames * places * positions * slots,
        ),
        name="temporal",
    )(head_class, packed)


def weight_kernel(classes, place, weight, out):
    out[...] = weight[...][None]


def weight_blocks(head_class, place, weight, group_count):
    rows, columns = weight.shape
    head_count = rows // HD
    width = columns // group_count
    return pl.pallas_call(
        weight_kernel,
        grid_spec=pltpu.PrefetchScalarGridSpec(
            num_scalar_prefetch=2,
            grid=(group_count, head_count),
            in_specs=[
                pl.BlockSpec(
                    (HD, width),
                    lambda shift, slot, classes, place: (head_of(classes, slot, head_count), lax.rem(place[0] + shift, group_count)),
                )
            ],
            out_specs=pl.BlockSpec((1, HD, width), lambda shift, slot, classes, place: (shift, slot, 0)),
        ),
        out_shape=jax.ShapeDtypeStruct((group_count, rows, width), jnp.bfloat16),
        cost_estimate=pl.CostEstimate(flops=0, bytes_accessed=4 * rows * columns, transcendentals=0),
        name="weight_blocks",
    )(head_class, place, weight)


def project_kernel(with_sum, own, right, left, far_top, far_bottom, w_own, w_right, w_far, w_left, *rest):
    out = rest[-1]
    top = pl.program_id(0) < pl.num_programs(0) // 2
    far = jnp.where(top, far_top[...], far_bottom[...])
    total = jnp.dot(own[...], w_own[...], preferred_element_type=jnp.float32)
    total += jnp.dot(right[...], w_right[...], preferred_element_type=jnp.float32)
    total += jnp.dot(left[...], w_left[...], preferred_element_type=jnp.float32)
    total += jnp.dot(far, w_far[...], preferred_element_type=jnp.float32)
    if with_sum:
        total += rest[0][...]
    out[...] = total.astype(out.dtype)


def project(pieces, weights, row_block, total, out_dtype):
    own = pieces[0]
    tokens, depth = own.shape
    width = weights[0].shape[1]
    steps = 4
    block = tokens // steps
    row_spec = pl.BlockSpec((block, depth), lambda step: (step, 0))
    top_spec = pl.BlockSpec((block, depth), lambda step: (jnp.minimum(step, steps // 2 - 1), 0))
    bottom_spec = pl.BlockSpec((block, depth), lambda step: (jnp.maximum(step - steps // 2, 0), 0))
    weight_spec = pl.BlockSpec((depth, width), lambda step: (row_block, 0))
    sum_spec = pl.BlockSpec((block, width), lambda step: (step, 0))
    sums = [] if total is None else [total]
    return pl.pallas_call(
        functools.partial(project_kernel, total is not None),
        grid=(steps,),
        in_specs=[row_spec] * 3 + [top_spec, bottom_spec] + [weight_spec] * 4 + [sum_spec] * len(sums),
        out_specs=sum_spec,
        out_shape=jax.ShapeDtypeStruct((tokens, width), out_dtype),
        compiler_params=pltpu.CompilerParams(vmem_limit_bytes=VMEM_LIMIT),
        cost_estimate=pl.CostEstimate(
            flops=8 * tokens * depth * width, bytes_accessed=8 * tokens * depth + 8 * depth * width + 8 * tokens * width, transcendentals=0
        ),
        name="project",
    )(*pieces, *weights, *sums)


def shifted(block, by):
    count = lax.axis_size("head")
    return lax.ppermute(block, "head", [(at, (at + by) % count) for at in range(count)])


def ring(block):
    half = block.shape[0] // 2
    right, left = shifted(block, 1), shifted(block, -1)
    return block, right, left, shifted(right[:half], 1), shifted(left[half:], -1)


def other_core(block):
    count = lax.axis_size("seq")
    return lax.ppermute(block, "seq", [(at, at ^ 1) for at in range(count)])


def over_frames(blocks):
    count = lax.axis_size("seq")
    groups = [list(range(core, count, CORES)) for core in range(CORES)]
    return lax.all_to_all(blocks, "seq", 0, 0, axis_index_groups=groups)


def body(query_rows, key_rows, value_rows, query_gain, key_gain, head_class, out_weight):
    tokens = query_rows.shape[0]
    group_count = lax.axis_size("head")
    query_gain = query_gain.reshape(1, HD)
    key_gain = key_gain.reshape(1, HD)
    packed = pack(head_class, query_rows, key_rows, value_rows, query_gain, key_gain)
    arrived = over_frames(packed.reshape(FRAMES, tokens // FRAMES, TMAX * 3 * HD))

    other_keys, other_values = other_core(key_rows), other_core(value_rows)
    front, back = spatial(head_class, query_rows, key_rows, other_keys, value_rows, other_values, query_gain, key_gain)
    place = lax.axis_index("head").reshape(1).astype(jnp.int32)
    blocks = weight_blocks(head_class, place, out_weight, group_count)
    weights = [blocks[0]] + [shifted(blocks[by], by) for by in range(1, group_count)]
    total = project(ring(back), weights, TMAX // 2, None, jnp.float32)

    half = TMAX // 2
    temporal_slots = jnp.sum(head_class)
    for part in range(2):
        first = part * half
        returned = over_frames(temporal(head_class, arrived, first, half)).reshape(tokens, half * HD)
        slots = first + lax.broadcasted_iota(jnp.int32, (1, half * HD), 1) // HD
        chosen = jnp.where(slots < temporal_slots, returned, front[:, first * HD : (first + half) * HD])
        total = project(ring(chosen), weights, part, total, jnp.bfloat16 if part else jnp.float32)
    return total


def solution(mesh):
    return jax.shard_map(
        body,
        mesh=mesh,
        in_specs=(
            P("seq", "head"),
            P("seq", "head"),
            P("seq", "head"),
            P(),
            P(),
            P("head"),
            P("head", None),
        ),
        out_specs=P("seq", "head"),
        check_vma=False,
    )
```

time: 318 us -> 234 us (0.74)
  Pallas kernels: 0 us -> 53.7 us
  matrix products: 53 us -> 0 us
  local copies, waits for them, and re-layouts: 51.6 us -> 10.5 us
  waiting for transfers between devices: 144 us -> 109 us
  starting transfers between devices: 29.9 us -> 56 us
  other arithmetic: 23.4 us -> 2.47 us
  between operations: 13.6 us -> 0.24 us
    reduce_scatter x1 -> x0, waiting for transfers between devices: 62.9 us -> none  [body(): lax.psum_scatter(partial_value.astype(jnp.bfloat16), 'head', scatter_dime...]
    pallas_call x0 -> x8, Pallas kernels: none -> 53.7 us  [the longest x1 14.9 us: weight_blocks(): pl.pallas_call(weight_kernel, grid_spec=pltpu.PrefetchScalarGridSpec(num_...]
    dot_general x15 -> x0, matrix products: 53 us -> none  [the longest x6 21.4 us: attend_head(): jnp.einsum('nqk,nkd->nqd', spatial_weights, value_part, preferred_element...]
    ppermute x2 -> x17, waiting for transfers between devices: 0.01 us -> 37.9 us  [the longest x15 37.9 us: shifted(): lax.ppermute(block, 'head', [(at, (at + by) % count) for at in range(coun...]
    ppermute x2 -> x17, starting transfers between devices: 0.54 us -> 27 us  [the longest x15 26.4 us: shifted(): lax.ppermute(block, 'head', [(at, (at + by) % count) for at in range(coun...]
    convert_element_type x5 -> x0, other arithmetic: 12.9 us -> none  [the longest x3 7.66 us: normed(): return scaled.astype(jnp.bfloat16)]
    convert_element_type x5 -> x0, local copies, waits for them, and re-layouts: 12.2 us -> none  [the longest x2 5.96 us: normed(): return scaled.astype(jnp.bfloat16)]
    reshape x3 -> x0, local copies, waits for them, and re-layouts: 11.7 us -> none  [the longest x2 9.26 us: normed(): row_block.astype(jnp.float32).reshape(row_block.shape[0], head_count, -1)]
  transfers between devices with their start and end apart: 7 -> 20, of which waited for: 5 -> 10; matrix products, arithmetic and copies ran while one was open for 28% -> 3% of each run, Pallas kernels for 0% -> 18%
where the time goes in v1:
time: 234 us; the launch traced here: 231 us
  waiting for transfers between devices  109 us (47%)
  starting transfers between devices  56 us (24%)
  Pallas kernels  53.7 us (23%)
  local copies, waits for them, and re-layouts  10.5 us (4%)
  other arithmetic  2.47 us (1%)
    all_to_all x3, waiting for transfers between devices, over_frames(): return lax.all_to_all(blocks, 'seq', 0, 0, axis_index_groups=groups)  70.7 us
    ppermute x15, waiting for transfers between devices, shifted(): lax.ppermute(block, 'head', [(at, (at + by) % count) for at in range(coun...  37.9 us
    all_to_all x3, starting transfers between devices, over_frames(): return lax.all_to_all(blocks, 'seq', 0, 0, axis_index_groups=groups)  29 us
    ppermute x15, starting transfers between devices, shifted(): lax.ppermute(block, 'head', [(at, (at + by) % count) for at in range(coun...  26.4 us
    pallas_call x1, Pallas kernels, weight_blocks(): pl.pallas_call(weight_kernel, grid_spec=pltpu.PrefetchScalarGridSpec(num_...  14.9 us
    pallas_call x1, Pallas kernels, spatial(): pl.pallas_call(functools.partial(spatial_kernel, head_count), grid_spec=p...  12.8 us
    pallas_call x3, Pallas kernels, project(): pl.pallas_call(functools.partial(project_kernel, total is not None), grid...  11.7 us
    pallas_call x1, Pallas kernels, pack(): pl.pallas_call(pack_kernel, grid_spec=pltpu.PrefetchScalarGridSpec(num_sc...  7.82 us
  transfers between devices with their start and end apart: 20, of which 10 were waited for; matrix products, arithmetic and copies ran while one was open for 3% of the time, Pallas kernels for 18%

profile of v1, /device:TPU:8, one launch (start us, length us, event | category | flops | bytes accessed | tf_op | source)
XLA Modules:
  0.0 231.4 jit_solution(13111269544122439808)
XLA Ops:
  0.0 7.8 %pack.1 = bf16[1024,1536]{1,0:T(8,128)(2,1)} custom-call(s32[6]{0:T(128)} %classes.9, bf16[1024,768]{1,0:T(8,128)(2,1)} %query.3, bf16[1024,768]{1,0:T(8,128)(2,1)} %key.3, bf16[1024,768]{1,0:T(8,128)(2,1)} %value.3, f32[1,128]{1,0:T(1,128)} %bitcast.16, f32[1,128]{1,0:T(1,128)} %bitcast.18), custom_call_target="tpu_custom_call" | custom-call | flops 4194304 | bytes 6291456 | tf_op jit(solution)/shard_map/pack/pallas_call | solution.py:66
  7.8 11.8 %all-to-all-start = ((bf16[32,32,1536]{2,1,0:T(8,128)(2,1)}), bf16[32,32,1536]{2,1,0:T(8,128)(2,1)S(1)}, u32[]{:S(2)}, u32[]{:S(2)}) async-start(bf16[32,32,1536]{2,1,0:T(8,128)(2,1)} %bitcast.20), calls=%async_computation | async-start | bytes 6291456 | tf_op jit(solution)/shard_map/all_to_all | solution.py:286
  20.3 70.7 %all-to-all-done.packed = bf16[32,32,1536]{2,1,0:T(8,128)(2,1)S(1)} async-done(((bf16[32,32,1536]{2,1,0:T(8,128)(2,1)}), bf16[32,32,1536]{2,1,0:T(8,128)(2,1)S(1)}, u32[]{:S(2)}, u32[]{:S(2)}) %all-to-all-start) | async-done | bytes 3145760 | tf_op jit(solution)/shard_map/all_to_all | solution.py:286
  90.9 3.2 %temporal.3 = bf16[32,32,256]{2,1,0:T(8,128)(2,1)S(1)} custom-call(s32[6]{0:T(128)S(1)} %copy-done.6, bf16[32,32,1536]{2,1,0:T(8,128)(2,1)S(1)} %all-to-all-done.packed), custom_call_target="tpu_custom_call" | custom-call | flops 805306368 | bytes 2097152 | tf_op jit(solution)/shard_map/temporal/pallas_call | solution.py:182
  94.9 7.4 %all-to-all-start.2 = ((bf16[32,32,256]{2,1,0:T(8,128)(2,1)}), bf16[32,32,256]{2,1,0:T(8,128)(2,1)}, u32[]{:S(2)}, u32[]{:S(2)}) async-start(bf16[32,32,256]{2,1,0:T(8,128)(2,1)} %copy-done.1), calls=%async_computation.2 | async-start | bytes 1048576 | tf_op jit(solution)/shard_map/all_to_all | solution.py:286
  102.3 14.9 %weight_blocks.1 = bf16[4,768,768]{2,1,0:T(8,128)(2,1)} custom-call(s32[6]{0:T(128)} %classes.9, s32[1]{0:T(128)} %bitcast.4.place, bf16[768,3072]{1,0:T(8,128)(2,1)} %weight.1), custom_call_target="tpu_custom_call" | custom-call | bytes 9437184 | tf_op jit(solution)/shard_map/weight_blocks/pallas_call | solution.py:209
  117.2 4.6 %slice_bitcast_fusion = (bf16[768,768]{1,0:T(8,128)(2,1)}, bf16[768,768]{1,0:T(8,128)(2,1)}, bf16[768,768]{1,0:T(8,128)(2,1)}, bf16[768,768]{1,0:T(8,128)(2,1)}) fusion(bf16[4,768,768]{2,1,0:T(8,128)(2,1)} %weight_blocks.1), kind=kLoop, calls=%fused_computation | loop fusion | bytes 9437184 | tf_op jit(solution)/shard_map/squeeze | solution.py:301
  121.9 1.5 collective-permute-start.6
  123.4 2.7 %collective-permute-start.7 = (bf16[768,768]{1,0:T(8,128)(2,1)}, bf16[768,768]{1,0:T(8,128)(2,1)}, u32[]{:S(2)}, u32[]{:S(2)}) collective-permute-start(bf16[768,768]{1,0:T(8,128)(2,1)} %get-tuple-element.10), channel_id=1, source_target_pairs={{0,2},{1,3},{2,0},{3,1},{4,6},{5,7},{6,4},{7,5},{8,10},{9,11},{10,... | collective-permute-start | bytes 3538952 | tf_op jit(solution)/shard_map/ppermute | solution.py:269
  127.1 3.2 %temporal.2 = bf16[32,32,256]{2,1,0:T(8,128)(2,1)S(1)} custom-call(s32[6]{0:T(128)S(1)} %copy-done.7, bf16[32,32,1536]{2,1,0:T(8,128)(2,1)S(1)} %all-to-all-done.packed), custom_call_target="tpu_custom_call" | custom-call | flops 805306368 | bytes 2097152 | tf_op jit(solution)/shard_map/temporal/pallas_call | solution.py:182
  131.1 9.8 %all-to-all-start.1 = ((bf16[32,32,256]{2,1,0:T(8,128)(2,1)}), bf16[32,32,256]{2,1,0:T(8,128)(2,1)S(1)}, u32[]{:S(2)}, u32[]{:S(2)}) async-start(bf16[32,32,256]{2,1,0:T(8,128)(2,1)} %copy-done.2), calls=%async_computation.1 | async-start | bytes 1048576 | tf_op jit(solution)/shard_map/all_to_all | solution.py:286
  142.4 1.4 copy-done.4
  145.2 12.8 %spatial.1 = (bf16[1024,512]{1,0:T(8,128)(2,1)S(1)}, bf16[1024,256]{1,0:T(8,128)(2,1)S(1)}) custom-call(s32[6]{0:T(128)S(1)} %copy-done.7, bf16[1024,768]{1,0:T(8,128)(2,1)S(1)} %copy-done.3, bf16[1024,768]{1,0:T(8,128)(2,1)S(1)} %copy-done.4, bf16[1024,768]{1,0:T(8,128)(2,1)} %collective-permute-done.other_key, bf16[1024,768]{1,0:T(8,128)(2,1)S(1)} %copy-done.5, ...), custom_call_target="tpu_custom_call" | custom-call | flops 12884901888 | bytes 9437184 | tf_op jit(solution)/shard_map/spatial/pallas_call | solution.py:127
  158.0 4.1 %collective-permute-start.13 = (bf16[1024,256]{1,0:T(8,128)(2,1)S(1)}, bf16[1024,256]{1,0:T(8,128)(2,1)S(1)}, u32[]{:S(2)}, u32[]{:S(2)}) collective-permute-start(bf16[1024,256]{1,0:T(8,128)(2,1)S(1)} %get-tuple-element.8.own), channel_id=1, source_target_pairs={{0,1},{1,2},{2,3},{3,0},{4,5},{5,6},{6,7},{7,4},{8,9},{9,10},{10,1... | collective-permute-start | bytes 1572872 | tf_op jit(solution)/shard_map/ppermute | solution.py:269
  163.9 6.3 %collective-permute-start.9 = (bf16[1024,256]{1,0:T(8,128)(2,1)S(1)}, bf16[1024,256]{1,0:T(8,128)(2,1)S(1)}, u32[]{:S(2)}, u32[]{:S(2)}) collective-permute-start(bf16[1024,256]{1,0:T(8,128)(2,1)S(1)} %get-tuple-element.13.own), channel_id=1, source_target_pairs={{0,1},{1,2},{2,3},{3,0},{4,5},{5,6},{6,7},{7,4},{8,9},{9,10},{10,1... | collective-permute-start | bytes 1572872 | tf_op jit(solution)/shard_map/ppermute | solution.py:269
  170.2 8.4 %collective-permute-done.7.w_far = bf16[768,768]{1,0:T(8,128)(2,1)} collective-permute-done((bf16[768,768]{1,0:T(8,128)(2,1)}, bf16[768,768]{1,0:T(8,128)(2,1)}, u32[]{:S(2)}, u32[]{:S(2)}) %collective-permute-start.7) | collective-permute-done | bytes 1179680 | tf_op jit(solution)/shard_map/ppermute | solution.py:269
  178.6 9.1 %collective-permute-done.13.right = bf16[1024,256]{1,0:T(8,128)(2,1)S(1)} collective-permute-done((bf16[1024,256]{1,0:T(8,128)(2,1)S(1)}, bf16[1024,256]{1,0:T(8,128)(2,1)S(1)}, u32[]{:S(2)}, u32[]{:S(2)}) %collective-permute-start.13) | collective-permute-done | bytes 524320 | tf_op jit(solution)/shard_map/ppermute | solution.py:269
  191.0 7.9 %collective-permute-done.9.right = bf16[1024,256]{1,0:T(8,128)(2,1)S(1)} collective-permute-done((bf16[1024,256]{1,0:T(8,128)(2,1)S(1)}, bf16[1024,256]{1,0:T(8,128)(2,1)S(1)}, u32[]{:S(2)}, u32[]{:S(2)}) %collective-permute-start.9) | collective-permute-done | bytes 524320 | tf_op jit(solution)/shard_map/ppermute | solution.py:269
  202.2 7.9 %collective-permute-done.2.right = bf16[1024,256]{1,0:T(8,128)(2,1)S(1)} collective-permute-done((bf16[1024,256]{1,0:T(8,128)(2,1)S(1)}, bf16[1024,256]{1,0:T(8,128)(2,1)S(1)}, u32[]{:S(2)}, u32[]{:S(2)}) %collective-permute-start.2) | collective-permute-done | bytes 524320 | tf_op jit(solution)/shard_map/ppermute | solution.py:269
  214.2 1.5 collective-permute-done.15.far_top
  215.8 2.6 %collective-permute-start.5 = (bf16[512,256]{1,0:T(8,128)(2,1)S(1)}, bf16[512,256]{1,0:T(8,128)(2,1)S(1)}, u32[]{:S(2)}, u32[]{:S(2)}) collective-permute-start(bf16[512,256]{1,0:T(8,128)(2,1)S(1)} %slice.49), channel_id=1, source_target_pairs={{0,3},{1,0},{2,1},{3,2},{4,7},{5,4},{6,5},{7,6},{8,11},{9,8},{10,9... | collective-permute-start | bytes 786440 | tf_op jit(solution)/shard_map/ppermute | solution.py:269
  218.4 3.6 %project.3.rest_0_ = f32[1024,768]{1,0:T(8,128)S(1)} custom-call(bf16[1024,256]{1,0:T(8,128)(2,1)S(1)} %get-tuple-element.8.own, bf16[1024,256]{1,0:T(8,128)(2,1)S(1)} %collective-permute-done.13.right, bf16[1024,256]{1,0:T(8,128)(2,1)S(1)} %collective-permute-done.14.left, bf16[512,256]{1,0:T(8,128)(2,1)S(1)} %collective-permute-done.15.far_top, ...), custom_call_target="tpu_custom_call" | custom-call | flops 1610612736 | bytes 9961472 | tf_op jit(solution)/shard_map/project/pallas_call | solution.py:253
  223.3 3.6 %project.4.rest_0_ = f32[1024,768]{1,0:T(8,128)S(1)} custom-call(bf16[1024,256]{1,0:T(8,128)(2,1)S(1)} %get-tuple-element.13.own, bf16[1024,256]{1,0:T(8,128)(2,1)S(1)} %collective-permute-done.9.right, bf16[1024,256]{1,0:T(8,128)(2,1)S(1)} %collective-permute-done.10.left, bf16[512,256]{1,0:T(8,128)(2,1)S(1)} %collective-permute-done.11.far_top, ...), custom_call_target="tpu_custom_call" | custom-call | flops 1610612736 | bytes 9961472 | tf_op jit(solution)/shard_map/project/pallas_call | solution.py:253
  226.9 4.5 %project.5 = bf16[1024,768]{1,0:T(8,128)(2,1)} custom-call(bf16[1024,256]{1,0:T(8,128)(2,1)S(1)} %get-tuple-element.14.own, bf16[1024,256]{1,0:T(8,128)(2,1)S(1)} %collective-permute-done.2.right, bf16[1024,256]{1,0:T(8,128)(2,1)S(1)} %collective-permute-done.3.left, bf16[512,256]{1,0:T(8,128)(2,1)S(1)} %collective-permute-done.4.far_top, ...), custom_call_target="tpu_custom_call" | custom-call | flops 1610612736 | bytes 9961472 | tf_op jit(solution)/shard_map/project/pallas_call | solution.py:253
  (54 shorter events, 19.8 us)
Async XLA Ops:
  7.8 83.1 %copy-start.6 = (s32[6]{0:T(128)S(1)}, s32[6]{0:T(128)}, u32[]{:S(2)}) copy-start(s32[6]{0:T(128)} %classes.9) | copy-start | bytes 76
  7.8 83.1 %all-to-all-start = ((bf16[32,32,1536]{2,1,0:T(8,128)(2,1)}), bf16[32,32,1536]{2,1,0:T(8,128)(2,1)S(1)}, u32[]{:S(2)}, u32[]{:S(2)}) async-start(bf16[32,32,1536]{2,1,0:T(8,128)(2,1)} %bitcast.20), calls=%async_computation | async-start | bytes 6291456 | tf_op jit(solution)/shard_map/all_to_all | solution.py:286
  19.7 121.3 %collective-permute-start = (bf16[1024,768]{1,0:T(8,128)(2,1)}, bf16[1024,768]{1,0:T(8,128)(2,1)}, u32[]{:S(2)}, u32[]{:S(2)}) collective-permute-start(bf16[1024,768]{1,0:T(8,128)(2,1)} %key.3), channel_id=1, source_target_pairs={{0,4},{4,0},{8,12},{12,8},{16,20},{20,16},{24,28},{28,24},{32,36},... | collective-permute-start | bytes 4718600 | tf_op jit(solution)/shard_map/ppermute | solution.py:280
  19.8 121.2 %collective-permute-start.1 = (bf16[1024,768]{1,0:T(8,128)(2,1)}, bf16[1024,768]{1,0:T(8,128)(2,1)}, u32[]{:S(2)}, u32[]{:S(2)}) collective-permute-start(bf16[1024,768]{1,0:T(8,128)(2,1)} %value.3), channel_id=1, source_target_pairs={{0,4},{4,0},{8,12},{12,8},{16,20},{20,16},{24,28},{28,24},{32,36},... | collective-permute-start | bytes 4718600 | tf_op jit(solution)/shard_map/ppermute | solution.py:280
  94.9 36.2 %all-to-all-start.2 = ((bf16[32,32,256]{2,1,0:T(8,128)(2,1)}), bf16[32,32,256]{2,1,0:T(8,128)(2,1)}, u32[]{:S(2)}, u32[]{:S(2)}) async-start(bf16[32,32,256]{2,1,0:T(8,128)(2,1)} %copy-done.1), calls=%async_computation.2 | async-start | bytes 1048576 | tf_op jit(solution)/shard_map/all_to_all | solution.py:286
  121.9 42.1 %collective-permute-start.6 = (bf16[768,768]{1,0:T(8,128)(2,1)}, bf16[768,768]{1,0:T(8,128)(2,1)}, u32[]{:S(2)}, u32[]{:S(2)}) collective-permute-start(bf16[768,768]{1,0:T(8,128)(2,1)} %get-tuple-element.11), channel_id=1, source_target_pairs={{0,1},{1,2},{2,3},{3,0},{4,5},{5,6},{6,7},{7,4},{8,9},{9,10},{10,1... | collective-permute-start | bytes 3538952 | tf_op jit(solution)/shard_map/ppermute | solution.py:269
  123.4 55.3 %collective-permute-start.7 = (bf16[768,768]{1,0:T(8,128)(2,1)}, bf16[768,768]{1,0:T(8,128)(2,1)}, u32[]{:S(2)}, u32[]{:S(2)}) collective-permute-start(bf16[768,768]{1,0:T(8,128)(2,1)} %get-tuple-element.10), channel_id=1, source_target_pairs={{0,2},{1,3},{2,0},{3,1},{4,6},{5,7},{6,4},{7,5},{8,10},{9,11},{10,... | collective-permute-start | bytes 3538952 | tf_op jit(solution)/shard_map/ppermute | solution.py:269
  126.1 87.4 %collective-permute-start.8 = (bf16[768,768]{1,0:T(8,128)(2,1)}, bf16[768,768]{1,0:T(8,128)(2,1)}, u32[]{:S(2)}, u32[]{:S(2)}) collective-permute-start(bf16[768,768]{1,0:T(8,128)(2,1)} %get-tuple-element.9), channel_id=1, source_target_pairs={{0,3},{1,0},{2,1},{3,2},{4,7},{5,4},{6,5},{7,6},{8,11},{9,8},{10,9... | collective-permute-start | bytes 3538952 | tf_op jit(solution)/shard_map/ppermute | solution.py:269
  127.1 13.8 %copy-start.8 = (f32[128]{0:T(128)S(1)}, f32[128]{0:T(128)}, u32[]{:S(2)}) copy-start(f32[128]{0:T(128)} %param.10) | copy-start | bytes 1540
  127.1 13.8 %copy-start.9 = (f32[128]{0:T(128)S(1)}, f32[128]{0:T(128)}, u32[]{:S(2)}) copy-start(f32[128]{0:T(128)} %param.11) | copy-start | bytes 1540
  131.1 31.6 %all-to-all-start.1 = ((bf16[32,32,256]{2,1,0:T(8,128)(2,1)}), bf16[32,32,256]{2,1,0:T(8,128)(2,1)S(1)}, u32[]{:S(2)}, u32[]{:S(2)}) async-start(bf16[32,32,256]{2,1,0:T(8,128)(2,1)} %copy-done.2), calls=%async_computation.1 | async-start | bytes 1048576 | tf_op jit(solution)/shard_map/all_to_all | solution.py:286
  158.0 29.7 %collective-permute-start.13 = (bf16[1024,256]{1,0:T(8,128)(2,1)S(1)}, bf16[1024,256]{1,0:T(8,128)(2,1)S(1)}, u32[]{:S(2)}, u32[]{:S(2)}) collective-permute-start(bf16[1024,256]{1,0:T(8,128)(2,1)S(1)} %get-tuple-element.8.own), channel_id=1, source_target_pairs={{0,1},{1,2},{2,3},{3,0},{4,5},{5,6},{6,7},{7,4},{8,9},{9,10},{10,1... | collective-permute-start | bytes 1572872 | tf_op jit(solution)/shard_map/ppermute | solution.py:269
  162.1 27.5 %collective-permute-start.14 = (bf16[1024,256]{1,0:T(8,128)(2,1)S(1)}, bf16[1024,256]{1,0:T(8,128)(2,1)S(1)}, u32[]{:S(2)}, u32[]{:S(2)}) collective-permute-start(bf16[1024,256]{1,0:T(8,128)(2,1)S(1)} %get-tuple-element.8.own), channel_id=1, source_target_pairs={{0,3},{1,0},{2,1},{3,2},{4,7},{5,4},{6,5},{7,6},{8,11},{9,8},{10,9... | collective-permute-start | bytes 1572872 | tf_op jit(solution)/shard_map/ppermute | solution.py:269
  163.9 35.0 %collective-permute-start.9 = (bf16[1024,256]{1,0:T(8,128)(2,1)S(1)}, bf16[1024,256]{1,0:T(8,128)(2,1)S(1)}, u32[]{:S(2)}, u32[]{:S(2)}) collective-permute-start(bf16[1024,256]{1,0:T(8,128)(2,1)S(1)} %get-tuple-element.13.own), channel_id=1, source_target_pairs={{0,1},{1,2},{2,3},{3,0},{4,5},{5,6},{6,7},{7,4},{8,9},{9,10},{10,1... | collective-permute-start | bytes 1572872 | tf_op jit(solution)/shard_map/ppermute | solution.py:269
  178.6 22.2 %collective-permute-start.10 = (bf16[1024,256]{1,0:T(8,128)(2,1)S(1)}, bf16[1024,256]{1,0:T(8,128)(2,1)S(1)}, u32[]{:S(2)}, u32[]{:S(2)}) collective-permute-start(bf16[1024,256]{1,0:T(8,128)(2,1)S(1)} %get-tuple-element.13.own), channel_id=1, source_target_pairs={{0,3},{1,0},{2,1},{3,2},{4,7},{5,4},{6,5},{7,6},{8,11},{9,8},{10,9... | collective-permute-start | bytes 1572872 | tf_op jit(solution)/shard_map/ppermute | solution.py:269
  187.7 30.7 %copy-start = (bf16[768,768]{1,0:T(8,128)(2,1)S(1)}, bf16[768,768]{1,0:T(8,128)(2,1)}, u32[]{:S(2)}) copy-start(bf16[768,768]{1,0:T(8,128)(2,1)} %get-tuple-element.12.w_own) | copy-start | bytes 3538948
  187.7 22.5 %collective-permute-start.2 = (bf16[1024,256]{1,0:T(8,128)(2,1)S(1)}, bf16[1024,256]{1,0:T(8,128)(2,1)S(1)}, u32[]{:S(2)}, u32[]{:S(2)}) collective-permute-start(bf16[1024,256]{1,0:T(8,128)(2,1)S(1)} %get-tuple-element.14.own), channel_id=1, source_target_pairs={{0,1},{1,2},{2,3},{3,0},{4,5},{5,6},{6,7},{7,4},{8,9},{9,10},{10,1... | collective-permute-start | bytes 1572872 | tf_op jit(solution)/shard_map/ppermute | solution.py:269
  189.6 22.5 %collective-permute-start.3 = (bf16[1024,256]{1,0:T(8,128)(2,1)S(1)}, bf16[1024,256]{1,0:T(8,128)(2,1)S(1)}, u32[]{:S(2)}, u32[]{:S(2)}) collective-permute-start(bf16[1024,256]{1,0:T(8,128)(2,1)S(1)} %get-tuple-element.14.own), channel_id=1, source_target_pairs={{0,3},{1,0},{2,1},{3,2},{4,7},{5,4},{6,5},{7,6},{8,11},{9,8},{10,9... | collective-permute-start | bytes 1572872 | tf_op jit(solution)/shard_map/ppermute | solution.py:269
  198.9 16.9 %collective-permute-start.15 = (bf16[512,256]{1,0:T(8,128)(2,1)S(1)}, bf16[512,256]{1,0:T(8,128)(2,1)S(1)}, u32[]{:S(2)}, u32[]{:S(2)}) collective-permute-start(bf16[512,256]{1,0:T(8,128)(2,1)S(1)} %slice.56), channel_id=1, source_target_pairs={{0,1},{1,2},{2,3},{3,0},{4,5},{5,6},{6,7},{7,4},{8,9},{9,10},{10,1... | collective-permute-start | bytes 786440 | tf_op jit(solution)/shard_map/ppermute | solution.py:269
  200.8 17.6 %collective-permute-start.16 = (bf16[512,256]{1,0:T(8,128)(2,1)S(1)}, bf16[512,256]{1,0:T(8,128)(2,1)S(1)}, u32[]{:S(2)}, u32[]{:S(2)}) collective-permute-start(bf16[512,256]{1,0:T(8,128)(2,1)S(1)} %slice.57), channel_id=1, source_target_pairs={{0,3},{1,0},{2,1},{3,2},{4,7},{5,4},{6,5},{7,6},{8,11},{9,8},{10,9... | collective-permute-start | bytes 786440 | tf_op jit(solution)/shard_map/ppermute | solution.py:269
  210.2 11.8 %collective-permute-start.11 = (bf16[512,256]{1,0:T(8,128)(2,1)S(1)}, bf16[512,256]{1,0:T(8,128)(2,1)S(1)}, u32[]{:S(2)}, u32[]{:S(2)}) collective-permute-start(bf16[512,256]{1,0:T(8,128)(2,1)S(1)} %slice.54), channel_id=1, source_target_pairs={{0,1},{1,2},{2,3},{3,0},{4,5},{5,6},{6,7},{7,4},{8,9},{9,10},{10,1... | collective-permute-start | bytes 786440 | tf_op jit(solution)/shard_map/ppermute | solution.py:269
  212.1 11.2 %collective-permute-start.12 = (bf16[512,256]{1,0:T(8,128)(2,1)S(1)}, bf16[512,256]{1,0:T(8,128)(2,1)S(1)}, u32[]{:S(2)}, u32[]{:S(2)}) collective-permute-start(bf16[512,256]{1,0:T(8,128)(2,1)S(1)} %slice.55), channel_id=1, source_target_pairs={{0,3},{1,0},{2,1},{3,2},{4,7},{5,4},{6,5},{7,6},{8,11},{9,8},{10,9... | collective-permute-start | bytes 786440 | tf_op jit(solution)/shard_map/ppermute | solution.py:269
  213.5 13.5 %collective-permute-start.4 = (bf16[512,256]{1,0:T(8,128)(2,1)S(1)}, bf16[512,256]{1,0:T(8,128)(2,1)S(1)}, u32[]{:S(2)}, u32[]{:S(2)}) collective-permute-start(bf16[512,256]{1,0:T(8,128)(2,1)S(1)} %slice.48), channel_id=1, source_target_pairs={{0,1},{1,2},{2,3},{3,0},{4,5},{5,6},{6,7},{7,4},{8,9},{9,10},{10,1... | collective-permute-start | bytes 786440 | tf_op jit(solution)/shard_map/ppermute | solution.py:269
  215.8 11.1 %collective-permute-start.5 = (bf16[512,256]{1,0:T(8,128)(2,1)S(1)}, bf16[512,256]{1,0:T(8,128)(2,1)S(1)}, u32[]{:S(2)}, u32[]{:S(2)}) collective-permute-start(bf16[512,256]{1,0:T(8,128)(2,1)S(1)} %slice.49), channel_id=1, source_target_pairs={{0,3},{1,0},{2,1},{3,2},{4,7},{5,4},{6,5},{7,6},{8,11},{9,8},{10,9... | collective-permute-start | bytes 786440 | tf_op jit(solution)/shard_map/ppermute | solution.py:269
  (6 other events, 15.0 us)

commit v2 on v1

--- a/solution.py
+++ b/solution.py
@@ -10,11 +10,23 @@
 
 FRAMES = 32
 TMAX = 4
+SMALL_VMEM = 16 * 1024 * 1024
 CORES = 2
 HD = 128
 EPSILON = 1e-06
 LOG2_SCALE = math.log2(math.e) / math.sqrt(HD)
-VMEM_LIMIT = 40 * 1024 * 1024
+
+
+def in_hbm(shape, dtype):
+    return pltpu.HBM(shape, dtype)
+
+
+def from_hbm(array):
+    return pltpu.with_memory_space_constraint(array, pltpu.HBM)
+
+
+def from_vmem(array):
+    return pltpu.with_memory_space_constraint(array, pltpu.VMEM)
 
 
 def temporal_count(classes, head_count):
@@ -47,34 +59,57 @@
     return lax.dot_general(queries, keys, (((1,), (1,)), ((), ())), preferred_element_type=jnp.float32)
 
 
-def pack_kernel(classes, query, key, value, query_gain, key_gain, out):
-    out[:, :HD] = normed(query[...], query_gain[...])
-    out[:, HD : 2 * HD] = normed(key[...], key_gain[...])
-    out[:, 2 * HD :] = value[...]
+def pack_kernel(head_count, classes, query, key, value, query_gain, key_gain, out, raw, ready, in_sems, out_sems):
+    tokens = query.shape[0]
+    heads = [head_of(classes, slot, head_count) for slot in range(TMAX)]
+
+    def columns(slot):
+        return pl.ds(pl.multiple_of(heads[slot] * HD, HD), HD)
+
+    loads, moves = [], []
+    for slot in range(TMAX):
+        for which, source in enumerate((query, key)):
+            at = 2 * slot + which
+            loads.append(pltpu.make_async_copy(source.at[:, columns(slot)], raw.at[at], in_sems.at[at]))
+            loads[-1].start()
+    for slot in range(TMAX):
+        target = out.at[:, pl.ds((3 * slot + 2) * HD, HD)]
+        moves.append(pltpu.make_async_copy(value.at[:, columns(slot)], target, out_sems.at[2 * TMAX + slot]))
+        moves[-1].start()
+    for slot in range(TMAX):
+        for which, gain in enumerate((query_gain, key_gain)):
+            at = 2 * slot + which
+            loads[at].wait()
+            ready[at] = normed(raw[at], gain[...])
+            target = out.at[:, pl.ds((3 * slot + which) * HD, HD)]
+            moves.append(pltpu.make_async_copy(ready.at[at], target, out_sems.at[at]))
+            moves[-1].start()
+    for move in moves:
+        move.wait()
 
 
 def pack(head_class, query_rows, key_rows, value_rows, query_gain, key_gain):
     tokens, width = query_rows.shape
-    head_count = width // HD
-    block = tokens // 2
-
-    def rows(slot, row, classes):
-        return row, head_of(classes, slot, head_count)
-
-    row_spec = pl.BlockSpec((block, HD), rows)
-    gain_spec = pl.BlockSpec((1, HD), lambda slot, row, classes: (0, 0))
-    return pl.pallas_call(
-        pack_kernel,
+    anywhere = pl.BlockSpec(memory_space=pl.ANY)
+    gain_spec = pl.BlockSpec((1, HD), lambda step, classes: (0, 0))
+    return pl.pallas_call(
+        functools.partial(pack_kernel, width // HD),
         grid_spec=pltpu.PrefetchScalarGridSpec(
             num_scalar_prefetch=1,
-            grid=(TMAX, tokens // block),
-            in_specs=[row_spec, row_spec, row_spec, gain_spec, gain_spec],
-            out_specs=pl.BlockSpec((block, 3 * HD), lambda slot, row, classes: (row, slot)),
-        ),
-        out_shape=jax.ShapeDtypeStruct((tokens, TMAX * 3 * HD), jnp.bfloat16),
+            grid=(1,),
+            in_specs=[anywhere] * 3 + [gain_spec] * 2,
+            out_specs=anywhere,
+            scratch_shapes=[
+                pltpu.VMEM((2 * TMAX, tokens, HD), jnp.bfloat16),
+                pltpu.VMEM((2 * TMAX, tokens, HD), jnp.bfloat16),
+                pltpu.SemaphoreType.DMA((2 * TMAX,)),
+                pltpu.SemaphoreType.DMA((3 * TMAX,)),
+            ],
+        ),
+        out_shape=in_hbm((tokens, TMAX * 3 * HD), jnp.bfloat16),
         cost_estimate=pl.CostEstimate(flops=8 * tokens * TMAX * HD, bytes_accessed=12 * tokens * TMAX * HD, transcendentals=0),
         name="pack",
-    )(head_class, query_rows, key_rows, value_rows, query_gain, key_gain)
+    )(head_class, from_hbm(query_rows), from_hbm(key_rows), from_hbm(value_rows), query_gain, key_gain)
 
 
 def spatial_kernel(head_count, classes, query, key, other_key, value, other_value, query_gain, key_gain, front, back, keys, values):
@@ -140,18 +175,17 @@
             ],
         ),
         out_shape=[
-            jax.ShapeDtypeStruct((tokens, TMAX * HD), jnp.bfloat16),
-            jax.ShapeDtypeStruct((tokens, width - TMAX * HD), jnp.bfloat16),
+            in_hbm((tokens, TMAX * HD), jnp.bfloat16),
+            in_hbm((tokens, width - TMAX * HD), jnp.bfloat16),
         ],
-        compiler_params=pltpu.CompilerParams(vmem_limit_bytes=VMEM_LIMIT),
         cost_estimate=pl.CostEstimate(
             flops=16 * tokens * tokens * width, bytes_accessed=12 * tokens * width, transcendentals=2 * tokens * tokens * head_count
         ),
         name="spatial",
-    )(head_class, query_rows, key_rows, other_keys, value_rows, other_values, query_gain, key_gain)
-
-
-def temporal_kernel(head_count, first, classes, packed, out):
+    )(head_class, query_rows, key_rows, from_hbm(other_keys), value_rows, from_hbm(other_values), query_gain, key_gain)
+
+
+def temporal_kernel(head_count, first, classes, packed, after, out):
     slot = first + pl.program_id(0)
     frames, places = packed.shape[0], packed.shape[1]
     count = frames * places
@@ -176,7 +210,7 @@
         out[...] = jnp.zeros_like(out)
 
 
-def temporal(head_class, packed, first, slots):
+def temporal(head_class, packed, first, slots, after):
     frames, positions, _ = packed.shape
     places = 16
     return pl.pallas_call(
@@ -184,22 +218,28 @@
         grid_spec=pltpu.PrefetchScalarGridSpec(
             num_scalar_prefetch=1,
             grid=(slots, positions // places),
-            in_specs=[pl.BlockSpec((frames, places, 3 * HD), lambda slot, part, classes: (0, part, slot + first))],
+            in_specs=[
+                pl.BlockSpec((frames, places, 3 * HD), lambda slot, part, classes: (0, part, slot + first)),
+                pl.BlockSpec(memory_space=pl.ANY),
+            ],
             out_specs=pl.BlockSpec((frames, places, HD), lambda slot, part, classes: (0, part, slot)),
         ),
-        out_shape=jax.ShapeDtypeStruct((frames, positions, slots * HD), jnp.bfloat16),
-        compiler_params=pltpu.CompilerParams(vmem_limit_bytes=VMEM_LIMIT),
+        out_shape=in_hbm((frames, positions, slots * HD), jnp.bfloat16),
         cost_estimate=pl.CostEstimate(
             flops=6 * frames * frames * places * positions * slots * HD,
             bytes_accessed=8 * frames * positions * slots * HD,
             transcendentals=frames * frames * places * positions * slots,
         ),
+        compiler_params=pltpu.CompilerParams(vmem_limit_bytes=SMALL_VMEM),
         name="temporal",
-    )(head_class, packed)
+    )(head_class, from_vmem(packed), from_hbm(after))
 
 
 def weight_kernel(classes, place, weight, out):
-    out[...] = weight[...][None]
+    group_count, _, width = out.shape
+    for shift in range(group_count):
+        block = lax.rem(place[0] + shift, group_count)
+        out[shift] = weight[:, pl.ds(pl.multiple_of(block * width, width), width)]
 
 
 def weight_blocks(head_class, place, weight, group_count):
@@ -210,38 +250,73 @@
         weight_kernel,
         grid_spec=pltpu.PrefetchScalarGridSpec(
             num_scalar_prefetch=2,
-            grid=(group_count, head_count),
-            in_specs=[
-                pl.BlockSpec(
-                    (HD, width),
-                    lambda shift, slot, classes, place: (head_of(classes, slot, head_count), lax.rem(place[0] + shift, group_count)),
-                )
-            ],
-            out_specs=pl.BlockSpec((1, HD, width), lambda shift, slot, classes, place: (shift, slot, 0)),
-        ),
-        out_shape=jax.ShapeDtypeStruct((group_count, rows, width), jnp.bfloat16),
+            grid=(head_count,),
+            in_specs=[pl.BlockSpec((HD, columns), lambda slot, classes, place: (head_of(classes, slot, head_count), 0))],
+            out_specs=pl.BlockSpec((group_count, HD, width), lambda slot, classes, place: (0, slot, 0)),
+        ),
+        out_shape=in_hbm((group_count, rows, width), jnp.bfloat16),
         cost_estimate=pl.CostEstimate(flops=0, bytes_accessed=4 * rows * columns, transcendentals=0),
         name="weight_blocks",
     )(head_class, place, weight)
 
 
-def project_kernel(with_sum, own, right, left, far_top, far_bottom, w_own, w_right, w_far, w_left, *rest):
+def choose_kernel(head_count, first, classes, returned, front, later, out, later_out):
+    count = temporal_count(classes, head_count)
+    for slot in range(out.shape[1] // HD):
+        columns = slice(slot * HD, (slot + 1) * HD)
+
+        @pl.when(first + slot < count)
+        def _(columns=columns):
+            out[:, columns] = returned[:, columns]
+
+        @pl.when(first + slot >= count)
+        def _(columns=columns):
+            out[:, columns] = front[:, columns]
+
+
+def choose(head_class, returned, front, first, later):
+    tokens, width = returned.shape
+    steps = 2
+    spec = pl.BlockSpec((tokens // steps, width), lambda step, classes: (step, 0))
+    front_spec = pl.BlockSpec((tokens // steps, width), lambda step, classes: (step, first * HD // width))
+    anywhere = pl.BlockSpec(memory_space=pl.ANY)
+    return pl.pallas_call(
+        functools.partial(choose_kernel, head_class.shape[0], first),
+        grid_spec=pltpu.PrefetchScalarGridSpec(
+            num_scalar_prefetch=1,
+            grid=(steps,),
+            in_specs=[spec, front_spec, anywhere],
+            out_specs=[spec, anywhere],
+        ),
+        out_shape=[in_hbm(returned.shape, returned.dtype), in_hbm(later.shape, later.dtype)],
+        input_output_aliases={3: 1},
+        cost_estimate=pl.CostEstimate(flops=0, bytes_accessed=6 * tokens * width, transcendentals=0),
+        compiler_params=pltpu.CompilerParams(vmem_limit_bytes=SMALL_VMEM),
+        name="choose",
+    )(head_class, from_vmem(returned), from_hbm(front), from_hbm(later))
+
+
+def near_kernel(with_sum, own, right, left, w_own, w_right, w_left, *rest):
     out = rest[-1]
-    top = pl.program_id(0) < pl.num_programs(0) // 2
-    far = jnp.where(top, far_top[...], far_bottom[...])
     total = jnp.dot(own[...], w_own[...], preferred_element_type=jnp.float32)
     total += jnp.dot(right[...], w_right[...], preferred_element_type=jnp.float32)
     total += jnp.dot(left[...], w_left[...], preferred_element_type=jnp.float32)
-    total += jnp.dot(far, w_far[...], preferred_element_type=jnp.float32)
     if with_sum:
         total += rest[0][...]
     out[...] = total.astype(out.dtype)
 
 
-def project(pieces, weights, row_block, total, out_dtype):
-    own = pieces[0]
+def far_kernel(far_top, far_bottom, w_far, total, out):
+    top = pl.program_id(0) < pl.num_programs(0) // 2
+    far = jnp.where(top, far_top[...], far_bottom[...])
+    out[...] = (jnp.dot(far, w_far[...], preferred_element_type=jnp.float32) + total[...]).astype(out.dtype)
+
+
+def project_ring(pieces, weights, row_block, total, out_dtype):
+    own, right, left, far_top, far_bottom = pieces
+    w_own, w_right, w_far, w_left = weights
     tokens, depth = own.shape
-    width = weights[0].shape[1]
+    width = w_own.shape[1]
     steps = 4
     block = tokens // steps
     row_spec = pl.BlockSpec((block, depth), lambda step: (step, 0))
@@ -250,18 +325,67 @@
     weight_spec = pl.BlockSpec((depth, width), lambda step: (row_block, 0))
     sum_spec = pl.BlockSpec((block, width), lambda step: (step, 0))
     sums = [] if total is None else [total]
-    return pl.pallas_call(
-        functools.partial(project_kernel, total is not None),
+    near = pl.pallas_call(
+        functools.partial(near_kernel, total is not None),
         grid=(steps,),
-        in_specs=[row_spec] * 3 + [top_spec, bottom_spec] + [weight_spec] * 4 + [sum_spec] * len(sums),
+        in_specs=[row_spec] * 3 + [weight_spec] * 3 + [sum_spec] * len(sums),
         out_specs=sum_spec,
-        out_shape=jax.ShapeDtypeStruct((tokens, width), out_dtype),
-        compiler_params=pltpu.CompilerParams(vmem_limit_bytes=VMEM_LIMIT),
+        out_shape=in_hbm((tokens, width), jnp.float32),
+        cost_estimate=pl.CostEstimate(
+            flops=6 * tokens * depth * width, bytes_accessed=6 * tokens * depth + 6 * depth * width + 8 * tokens * width, transcendentals=0
+        ),
+        compiler_params=pltpu.CompilerParams(vmem_limit_bytes=SMALL_VMEM),
+        name="near",
+    )(from_hbm(own), from_vmem(right), from_vmem(left), *[from_hbm(array) for array in (w_own, w_right, w_left, *sums)])
+    return pl.pallas_call(
+        far_kernel,
+        grid=(steps,),
+        in_specs=[top_spec, bottom_spec, weight_spec, sum_spec],
+        out_specs=sum_spec,
+        out_shape=in_hbm((tokens, width), out_dtype),
+        cost_estimate=pl.CostEstimate(
+            flops=2 * tokens * depth * width, bytes_accessed=2 * tokens * depth + 2 * depth * width + 8 * tokens * width, transcendentals=0
+        ),
+        compiler_params=pltpu.CompilerParams(vmem_limit_bytes=SMALL_VMEM),
+        name="far",
+    )(from_vmem(far_top), from_vmem(far_bottom), from_hbm(w_far), from_hbm(near))
+
+
+def gathered_kernel(with_sum, place, *refs):
+    out = refs[-1]
+    group_count = (len(refs) - 1 - with_sum) // 2
+    total = refs[2 * group_count][...] if with_sum else jnp.zeros(out.shape, jnp.float32)
+    for by in range(group_count):
+        total += jnp.dot(refs[by][0], refs[group_count + by][...], preferred_element_type=jnp.float32)
+    out[...] = total
+
+
+def project_gathered(place, gathered, weights, row_block, total):
+    group_count, tokens, depth = gathered.shape
+    width = weights[0].shape[1]
+    steps = 4
+    block = tokens // steps
+
+    def rows(by):
+        return pl.BlockSpec((1, block, depth), lambda step, place: (lax.rem(place[0] + group_count - by, group_count), step, 0))
+
+    weight_spec = pl.BlockSpec((depth, width), lambda step, place: (row_block, 0))
+    sum_spec = pl.BlockSpec((block, width), lambda step, place: (step, 0))
+    sums = [] if total is None else [total]
+    return pl.pallas_call(
+        functools.partial(gathered_kernel, len(sums)),
+        grid_spec=pltpu.PrefetchScalarGridSpec(
+            num_scalar_prefetch=1,
+            grid=(steps,),
+            in_specs=[rows(by) for by in range(group_count)] + [weight_spec] * group_count + [sum_spec] * len(sums),
+            out_specs=sum_spec,
+        ),
+        out_shape=in_hbm((tokens, width), jnp.float32),
         cost_estimate=pl.CostEstimate(
             flops=8 * tokens * depth * width, bytes_accessed=8 * tokens * depth + 8 * depth * width + 8 * tokens * width, transcendentals=0
         ),
         name="project",
-    )(*pieces, *weights, *sums)
+    )(place, *[from_hbm(gathered)] * group_count, *[from_hbm(array) for array in (*weights, *sums)])
 
 
 def shifted(block, by):
@@ -299,17 +423,16 @@
     place = lax.axis_index("head").reshape(1).astype(jnp.int32)
     blocks = weight_blocks(head_class, place, out_weight, group_count)
     weights = [blocks[0]] + [shifted(blocks[by], by) for by in range(1, group_count)]
-    total = project(ring(back), weights, TMAX // 2, None, jnp.float32)
+    early = project_gathered(place, lax.all_gather(back, "head"), weights, TMAX // 2, None)
 
     half = TMAX // 2
-    temporal_slots = jnp.sum(head_class)
-    for part in range(2):
-        first = part * half
-        returned = over_frames(temporal(head_class, arrived, first, half)).reshape(tokens, half * HD)
-        slots = first + lax.broadcasted_iota(jnp.int32, (1, half * HD), 1) // HD
-        chosen = jnp.where(slots < temporal_slots, returned, front[:, first * HD : (first + half) * HD])
-        total = project(ring(chosen), weights, part, total, jnp.bfloat16 if part else jnp.float32)
-    return total
+    sent = [temporal(head_class, arrived, part * half, half, early) for part in range(2)]
+    returned = over_frames(sent[0]).reshape(tokens, half * HD)
+    chosen, later = choose(head_class, returned, front, 0, sent[1])
+    total = project_gathered(place, lax.all_gather(chosen, "head"), weights, 0, early)
+    returned = over_frames(later).reshape(tokens, half * HD)
+    chosen, _ = choose(head_class, returned, front, half, jnp.zeros((8, HD), jnp.float32))
+    return project_ring(ring(chosen), weights, 1, total, jnp.bfloat16)
 
 
 def solution(mesh):

time: 234 us -> 274 us (1.17); the launches traced: 231 us -> 275 us
  Pallas kernels: 53.7 us -> 90.3 us
  blocking collectives: 0 us -> 21.6 us
  between operations: 0.24 us -> 13.5 us
  starting transfers between devices: 56 us -> 43 us
  waiting for transfers between devices: 109 us -> 102 us
  local copies, waits for them, and re-layouts: 10.5 us -> 4.29 us
    all_to_all x3 -> x2, waiting for transfers between devices: 70.7 us -> 13.2 us  [over_frames(): return lax.all_to_all(blocks, 'seq', 0, 0, axis_index_groups=groups)]
    pallas_call x4 -> x7, Pallas kernels: 19.5 us -> 61.8 us  [the longest x1 34.4 us: pack(): pl.pallas_call(functools.partial(pack_kernel, width // HD), grid_spec=plt...]
    ppermute x15 -> x7, waiting for transfers between devices: 37.9 us -> 79.1 us  [shifted(): lax.ppermute(block, 'head', [(at, (at + by) % count) for at in range(coun...]
    all_to_all x0 -> x1, blocking collectives: none -> 21.6 us  [over_frames(): return lax.all_to_all(blocks, 'seq', 0, 0, axis_index_groups=groups)]
    pallas_call x1, Pallas kernels: 14.9 us -> 6.72 us  [weight_blocks(): pl.pallas_call(weight_kernel, grid_spec=pltpu.PrefetchScalarGridSpec(num_...]
    all_to_all x3 -> x2, starting transfers between devices: 29 us -> 21.5 us  [over_frames(): return lax.all_to_all(blocks, 'seq', 0, 0, axis_index_groups=groups)]
    unnamed x20 -> x2, local copies, waits for them, and re-layouts: 5.81 us -> 0.01 us
    ppermute x15 -> x7, starting transfers between devices: 26.4 us -> 20.8 us  [shifted(): lax.ppermute(block, 'head', [(at, (at + by) % count) for at in range(coun...]
  transfers between devices with their start and end apart: 20 -> 13, of which waited for: 10 -> 7; matrix products, arithmetic and copies ran while one was open for 3% -> 2% of each run, Pallas kernels for 18% -> 16%
where the time goes in v2:
time: 274 us; the launch traced here: 275 us
  waiting for transfers between devices  102 us (37%)
  Pallas kernels  90.3 us (33%)
  starting transfers between devices  43 us (16%)
  blocking collectives  21.6 us (8%)
  between operations  13.5 us (5%)
  local copies, waits for them, and re-layouts  4.29 us (2%)
    ppermute x7, waiting for transfers between devices, shifted(): lax.ppermute(block, 'head', [(at, (at + by) % count) for at in range(coun...  79.1 us
    pallas_call x1, Pallas kernels, pack(): pl.pallas_call(functools.partial(pack_kernel, width // HD), grid_spec=plt...  34.4 us
    all_to_all x1, blocking collectives, over_frames(): return lax.all_to_all(blocks, 'seq', 0, 0, axis_index_groups=groups)  21.6 us
    all_to_all x2, starting transfers between devices, over_frames(): return lax.all_to_all(blocks, 'seq', 0, 0, axis_index_groups=groups)  21.5 us
    ppermute x7, starting transfers between devices, shifted(): lax.ppermute(block, 'head', [(at, (at + by) % count) for at in range(coun...  20.8 us
    pallas_call x1, Pallas kernels, spatial(): pl.pallas_call(functools.partial(spatial_kernel, head_count), grid_spec=p...  14.3 us
    all_to_all x2, waiting for transfers between devices, over_frames(): return lax.all_to_all(blocks, 'seq', 0, 0, axis_index_groups=groups)  13.2 us
    pallas_call x2, Pallas kernels, project_gathered(): pl.pallas_call(functools.partial(gathered_kernel, len(sums)), grid_spec=p...  12.4 us
  transfers between devices with their start and end apart: 13, of which 7 were waited for; matrix products, arithmetic and copies ran while one was open for 2% of the time, Pallas kernels for 16%

profile of v2, /device:TPU:8, one launch (start us, length us, event | category | flops | bytes accessed | tf_op | source)
XLA Modules:
  0.0 274.9 jit_solution(9045262205172817511)
XLA Ops:
  6.5 34.4 %pack.1 = bf16[1024,1536]{1,0:T(8,128)(2,1)} custom-call(s32[6]{0:T(128)} %classes.13, bf16[1024,768]{1,0:T(8,128)(2,1)} %query.3, bf16[1024,768]{1,0:T(8,128)(2,1)} %key.3, bf16[1024,768]{1,0:T(8,128)(2,1)} %value.3, f32[1,128]{1,0:T(1,128)} %bitcast.26, f32[1,128]{1,0:T(1,128)} %bitcast.28), custom_call_target="tpu_custom_call" | custom-call | flops 4194304 | bytes 6291456 | tf_op jit(solution)/shard_map/pack/pallas_call | solution.py:95
  40.9 11.7 %all-to-all-start = ((bf16[32,32,1536]{2,1,0:T(8,128)(2,1)}), bf16[32,32,1536]{2,1,0:T(8,128)(2,1)S(1)}, u32[]{:S(2)}, u32[]{:S(2)}) async-start(bf16[32,32,1536]{2,1,0:T(8,128)(2,1)} %bitcast.25), calls=%async_computation | async-start | bytes 6291456 | tf_op jit(solution)/shard_map/all_to_all | solution.py:410
  53.3 3.2 %collective-permute-done.other_key = bf16[1024,768]{1,0:T(8,128)(2,1)} collective-permute-done((bf16[1024,768]{1,0:T(8,128)(2,1)}, bf16[1024,768]{1,0:T(8,128)(2,1)}, u32[]{:S(2)}, u32[]{:S(2)}) %collective-permute-start) | collective-permute-done | bytes 1572896 | tf_op jit(solution)/shard_map/ppermute | solution.py:404
  58.8 14.3 %spatial.1 = (bf16[1024,512]{1,0:T(8,128)(2,1)}, bf16[1024,256]{1,0:T(8,128)(2,1)}) custom-call(s32[6]{0:T(128)} %classes.13, bf16[1024,768]{1,0:T(8,128)(2,1)} %query.3, bf16[1024,768]{1,0:T(8,128)(2,1)} %key.3, bf16[1024,768]{1,0:T(8,128)(2,1)} %collective-permute-done.other_key, bf16[1024,768]{1,0:T(8,128)(2,1)} %value.3, ...), custom_call_target="tpu_custom_call" | custom-call | flops 12884901888 | bytes 9437184 | tf_op jit(solution)/shard_map/spatial/pallas_call | solution.py:162
  73.1 6.7 %weight_blocks.1 = bf16[4,768,768]{2,1,0:T(8,128)(2,1)} custom-call(s32[6]{0:T(128)} %classes.13, s32[1]{0:T(128)} %bitcast.3.place, bf16[768,3072]{1,0:T(8,128)(2,1)} %weight.1), custom_call_target="tpu_custom_call" | custom-call | bytes 9437184 | tf_op jit(solution)/shard_map/weight_blocks/pallas_call | solution.py:249
  79.8 3.7 %slice_bitcast_fusion = (bf16[768,768]{1,0:T(8,128)(2,1)S(1)}, bf16[768,768]{1,0:T(8,128)(2,1)S(1)}, bf16[768,768]{1,0:T(8,128)(2,1)S(1)}, bf16[768,768]{1,0:T(8,128)(2,1)}) fusion(bf16[4,768,768]{2,1,0:T(8,128)(2,1)} %weight_blocks.1), kind=kLoop, calls=%fused_computation | loop fusion | bytes 9437184 | tf_op jit(solution)/shard_map/squeeze | solution.py:425
  85.0 12.7 %collective-permute-start.3 = (bf16[768,768]{1,0:T(8,128)(2,1)S(1)}, bf16[768,768]{1,0:T(8,128)(2,1)}, u32[]{:S(2)}, u32[]{:S(2)}) collective-permute-start(bf16[768,768]{1,0:T(8,128)(2,1)S(1)} %get-tuple-element.16), channel_id=1, source_target_pairs={{0,2},{1,3},{2,0},{3,1},{4,6},{5,7},{6,4},{7,5},{8,10},{9,11},{10,... | collective-permute-start | bytes 3538952 | tf_op jit(solution)/shard_map/ppermute | solution.py:393
  97.6 36.1 %collective-permute-done.2.refs_5_.w_right = bf16[768,768]{1,0:T(8,128)(2,1)} collective-permute-done((bf16[768,768]{1,0:T(8,128)(2,1)S(1)}, bf16[768,768]{1,0:T(8,128)(2,1)}, u32[]{:S(2)}, u32[]{:S(2)}) %collective-permute-start.2) | collective-permute-done | bytes 1179680 | tf_op jit(solution)/shard_map/ppermute | solution.py:393
  133.8 32.2 %collective-permute-done.3.refs_6_.w_far = bf16[768,768]{1,0:T(8,128)(2,1)} collective-permute-done((bf16[768,768]{1,0:T(8,128)(2,1)S(1)}, bf16[768,768]{1,0:T(8,128)(2,1)}, u32[]{:S(2)}, u32[]{:S(2)}) %collective-permute-start.3) | collective-permute-done | bytes 1179680 | tf_op jit(solution)/shard_map/ppermute | solution.py:393
  166.0 4.3 %all-gather.5.cloned.1.call-done = bf16[4096,256]{1,0:T(8,128)(2,1)} async-done(((bf16[1024,256]{1,0:T(8,128)(2,1)}), bf16[4096,256]{1,0:T(8,128)(2,1)}) %all-gather.5.cloned.1.call-update) | async-done | bytes 2097168 | tf_op jit(solution)/shard_map/all_gather | solution.py:426
  170.2 5.8 %project.2.after.refs_8_ = f32[1024,768]{1,0:T(8,128)} custom-call(s32[1]{0:T(128)} %bitcast.3.place, bf16[4,1024,256]{2,1,0:T(8,128)(2,1)} %bitcast.17, bf16[4,1024,256]{2,1,0:T(8,128)(2,1)} %bitcast.18, bf16[4,1024,256]{2,1,0:T(8,128)(2,1)} %bitcast.19, bf16[4,1024,256]{2,1,0:T(8,128)(2,1)} %bitcast.20, bf16[768,768]{1,0:T(8,128)(2,1)} %get-tuple-element.18.refs_4_.w_own, ...), custom_call_target="tpu_custom_call" | custom-call | flops 1610612736 | bytes 9961472 | tf_op jit(solution)/shard_map/project/pallas_call | solution.py:375
  176.0 3.8 %temporal.2 = bf16[32,32,256]{2,1,0:T(8,128)(2,1)} custom-call(s32[6]{0:T(128)S(1)} %copy-done, bf16[32,32,1536]{2,1,0:T(8,128)(2,1)S(1)} %all-to-all-done.packed, f32[1024,768]{1,0:T(8,128)} %project.2.after.refs_8_), custom_call_target="tpu_custom_call" | custom-call | flops 805306368 | bytes 2097152 | tf_op jit(solution)/shard_map/temporal/pallas_call | solution.py:216
  179.8 9.8 %all-to-all-start.1 = ((bf16[32,32,256]{2,1,0:T(8,128)(2,1)}), bf16[32,32,256]{2,1,0:T(8,128)(2,1)}, u32[]{:S(2)}, u32[]{:S(2)}) async-start(bf16[32,32,256]{2,1,0:T(8,128)(2,1)} %temporal.2), calls=%async_computation.1 | async-start | bytes 1048576 | tf_op jit(solution)/shard_map/all_to_all | solution.py:410
  189.7 3.8 %temporal.3.later = bf16[32,32,256]{2,1,0:T(8,128)(2,1)} custom-call(s32[6]{0:T(128)S(1)} %copy-done, bf16[32,32,1536]{2,1,0:T(8,128)(2,1)S(1)} %all-to-all-done.packed, f32[1024,768]{1,0:T(8,128)} %project.2.after.refs_8_), custom_call_target="tpu_custom_call" | custom-call | flops 805306368 | bytes 2097152 | tf_op jit(solution)/shard_map/temporal/pallas_call | solution.py:216
  193.5 13.2 %all-to-all-done.1 = bf16[32,32,256]{2,1,0:T(8,128)(2,1)} async-done(((bf16[32,32,256]{2,1,0:T(8,128)(2,1)}), bf16[32,32,256]{2,1,0:T(8,128)(2,1)}, u32[]{:S(2)}, u32[]{:S(2)}) %all-to-all-start.1) | async-done | bytes 524320 | tf_op jit(solution)/shard_map/all_to_all | solution.py:410
  206.8 2.5 choose.2
  209.3 21.6 %all_to_all.15 = bf16[32,32,256]{2,1,0:T(8,128)(2,1)S(1)} all-to-all(bf16[32,32,256]{2,1,0:T(8,128)(2,1)} %get-tuple-element.12), channel_id=1, replica_groups={{0,8,16,24,32,40,48,56,64,72,80,88,96,104,112,120,128,136,144,152,160,1..., dimensions={0} | all-to-all | bytes 1048576 | tf_op jit(solution)/shard_map/all_to_all | solution.py:410
  231.5 2.4 choose.3
  233.9 3.2 %collective-permute-start.7 = (bf16[1024,256]{1,0:T(8,128)(2,1)}, bf16[1024,256]{1,0:T(8,128)(2,1)S(1)}, u32[]{:S(2)}, u32[]{:S(2)}) collective-permute-start(bf16[1024,256]{1,0:T(8,128)(2,1)} %get-tuple-element.13.own), channel_id=1, source_target_pairs={{0,3},{1,0},{2,1},{3,2},{4,7},{5,4},{6,5},{7,6},{8,11},{9,8},{10,9... | collective-permute-start | bytes 1572872 | tf_op jit(solution)/shard_map/ppermute | solution.py:393
  237.1 10.8 %collective-permute-done.5.right = bf16[1024,256]{1,0:T(8,128)(2,1)S(1)} collective-permute-done((bf16[1024,256]{1,0:T(8,128)(2,1)}, bf16[1024,256]{1,0:T(8,128)(2,1)S(1)}, u32[]{:S(2)}, u32[]{:S(2)}) %collective-permute-start.5) | collective-permute-done | bytes 524320 | tf_op jit(solution)/shard_map/ppermute | solution.py:393
  248.0 3.3 %collective-permute-start.8 = (bf16[512,256]{1,0:T(8,128)(2,1)S(1)}, bf16[512,256]{1,0:T(8,128)(2,1)S(1)}, u32[]{:S(2)}, u32[]{:S(2)}) collective-permute-start(bf16[512,256]{1,0:T(8,128)(2,1)S(1)} %slice.29), channel_id=1, source_target_pairs={{0,3},{1,0},{2,1},{3,2},{4,7},{5,4},{6,5},{7,6},{8,11},{9,8},{10,9... | collective-permute-start | bytes 786440 | tf_op jit(solution)/shard_map/ppermute | solution.py:393
  251.3 6.6 %project.3.rest_0_ = f32[1024,768]{1,0:T(8,128)} custom-call(s32[1]{0:T(128)} %bitcast.3.place, bf16[4,1024,256]{2,1,0:T(8,128)(2,1)} %bitcast.21, bf16[4,1024,256]{2,1,0:T(8,128)(2,1)} %bitcast.22, bf16[4,1024,256]{2,1,0:T(8,128)(2,1)} %bitcast.23, bf16[4,1024,256]{2,1,0:T(8,128)(2,1)} %bitcast.24, bf16[768,768]{1,0:T(8,128)(2,1)} %get-tuple-element.18.refs_4_.w_own, ...), custom_call_target="tpu_custom_call" | custom-call | flops 1610612736 | bytes 9961472 | tf_op jit(solution)/shard_map/project/pallas_call | solution.py:375
  258.0 5.6 %near.1.total = f32[1024,768]{1,0:T(8,128)} custom-call(bf16[1024,256]{1,0:T(8,128)(2,1)} %get-tuple-element.13.own, bf16[1024,256]{1,0:T(8,128)(2,1)S(1)} %collective-permute-done.5.right, bf16[1024,256]{1,0:T(8,128)(2,1)S(1)} %collective-permute-done.7.left, bf16[768,768]{1,0:T(8,128)(2,1)} %get-tuple-element.18.refs_4_.w_own, ...), custom_call_target="tpu_custom_call" | custom-call | flops 1207959552 | bytes 9043968 | tf_op jit(solution)/shard_map/near/pallas_call | solution.py:328
  263.6 4.5 %far.1 = bf16[1024,768]{1,0:T(8,128)(2,1)} custom-call(bf16[512,256]{1,0:T(8,128)(2,1)S(1)} %collective-permute-done.6.far_top, bf16[512,256]{1,0:T(8,128)(2,1)S(1)} %collective-permute-done.8.far_bottom, bf16[768,768]{1,0:T(8,128)(2,1)} %collective-permute-done.3.refs_6_.w_far, f32[1024,768]{1,0:T(8,128)} %near.1.total), custom_call_target="tpu_custom_call" | custom-call | flops 402653184 | bytes 7208960 | tf_op jit(solution)/shard_map/far/pallas_call | solution.py:340
  (22 shorter events, 5.2 us)
Async XLA Ops:
  40.9 135.1 %all-to-all-start = ((bf16[32,32,1536]{2,1,0:T(8,128)(2,1)}), bf16[32,32,1536]{2,1,0:T(8,128)(2,1)S(1)}, u32[]{:S(2)}, u32[]{:S(2)}) async-start(bf16[32,32,1536]{2,1,0:T(8,128)(2,1)} %bitcast.25), calls=%async_computation | async-start | bytes 6291456 | tf_op jit(solution)/shard_map/all_to_all | solution.py:410
  52.7 117.6 %all-gather.5.cloned.1.call-start = ((), (), s32[]{:S(2)}) async-start(), calls=%async_computation.3 | async-start | bytes 2621440 | tf_op jit(solution)/shard_map/all_gather | solution.py:426
  52.7 3.8 %collective-permute-start = (bf16[1024,768]{1,0:T(8,128)(2,1)}, bf16[1024,768]{1,0:T(8,128)(2,1)}, u32[]{:S(2)}, u32[]{:S(2)}) collective-permute-start(bf16[1024,768]{1,0:T(8,128)(2,1)} %key.3), channel_id=1, source_target_pairs={{0,4},{4,0},{8,12},{12,8},{16,20},{20,16},{24,28},{28,24},{32,36},... | collective-permute-start | bytes 4718600 | tf_op jit(solution)/shard_map/ppermute | solution.py:404
  52.8 6.0 %collective-permute-start.1 = (bf16[1024,768]{1,0:T(8,128)(2,1)}, bf16[1024,768]{1,0:T(8,128)(2,1)}, u32[]{:S(2)}, u32[]{:S(2)}) collective-permute-start(bf16[1024,768]{1,0:T(8,128)(2,1)} %value.3), channel_id=1, source_target_pairs={{0,4},{4,0},{8,12},{12,8},{16,20},{20,16},{24,28},{28,24},{32,36},... | collective-permute-start | bytes 4718600 | tf_op jit(solution)/shard_map/ppermute | solution.py:404
  83.5 50.3 %collective-permute-start.2 = (bf16[768,768]{1,0:T(8,128)(2,1)S(1)}, bf16[768,768]{1,0:T(8,128)(2,1)}, u32[]{:S(2)}, u32[]{:S(2)}) collective-permute-start(bf16[768,768]{1,0:T(8,128)(2,1)S(1)} %get-tuple-element.17), channel_id=1, source_target_pairs={{0,1},{1,2},{2,3},{3,0},{4,5},{5,6},{6,7},{7,4},{8,9},{9,10},{10,1... | collective-permute-start | bytes 3538952 | tf_op jit(solution)/shard_map/ppermute | solution.py:393
  85.0 81.0 %collective-permute-start.3 = (bf16[768,768]{1,0:T(8,128)(2,1)S(1)}, bf16[768,768]{1,0:T(8,128)(2,1)}, u32[]{:S(2)}, u32[]{:S(2)}) collective-permute-start(bf16[768,768]{1,0:T(8,128)(2,1)S(1)} %get-tuple-element.16), channel_id=1, source_target_pairs={{0,2},{1,3},{2,0},{3,1},{4,6},{5,7},{6,4},{7,5},{8,10},{9,11},{10,... | collective-permute-start | bytes 3538952 | tf_op jit(solution)/shard_map/ppermute | solution.py:393
  97.6 68.3 %collective-permute-start.4 = (bf16[768,768]{1,0:T(8,128)(2,1)S(1)}, bf16[768,768]{1,0:T(8,128)(2,1)}, u32[]{:S(2)}, u32[]{:S(2)}) collective-permute-start(bf16[768,768]{1,0:T(8,128)(2,1)S(1)} %get-tuple-element.15), channel_id=1, source_target_pairs={{0,3},{1,0},{2,1},{3,2},{4,7},{5,4},{6,5},{7,6},{8,11},{9,8},{10,9... | collective-permute-start | bytes 3538952 | tf_op jit(solution)/shard_map/ppermute | solution.py:393
  170.2 5.8 %copy-start = (s32[6]{0:T(128)S(1)}, s32[6]{0:T(128)}, u32[]{:S(2)}) copy-start(s32[6]{0:T(128)} %classes.13) | copy-start | bytes 76
  179.8 26.9 %all-to-all-start.1 = ((bf16[32,32,256]{2,1,0:T(8,128)(2,1)}), bf16[32,32,256]{2,1,0:T(8,128)(2,1)}, u32[]{:S(2)}, u32[]{:S(2)}) async-start(bf16[32,32,256]{2,1,0:T(8,128)(2,1)} %temporal.2), calls=%async_computation.1 | async-start | bytes 1048576 | tf_op jit(solution)/shard_map/all_to_all | solution.py:410
  189.7 61.7 %all-gather.7.cloned.1.call-start = ((), (), s32[]{:S(2)}) async-start(), calls=%async_computation.4 | async-start | bytes 2621440 | tf_op jit(solution)/shard_map/all_gather | solution.py:432
  233.9 14.0 %collective-permute-start.5 = (bf16[1024,256]{1,0:T(8,128)(2,1)}, bf16[1024,256]{1,0:T(8,128)(2,1)S(1)}, u32[]{:S(2)}, u32[]{:S(2)}) collective-permute-start(bf16[1024,256]{1,0:T(8,128)(2,1)} %get-tuple-element.13.own), channel_id=1, source_target_pairs={{0,1},{1,2},{2,3},{3,0},{4,5},{5,6},{6,7},{7,4},{8,9},{9,10},{10,1... | collective-permute-start | bytes 1572872 | tf_op jit(solution)/shard_map/ppermute | solution.py:393
  233.9 14.1 %collective-permute-start.7 = (bf16[1024,256]{1,0:T(8,128)(2,1)}, bf16[1024,256]{1,0:T(8,128)(2,1)S(1)}, u32[]{:S(2)}, u32[]{:S(2)}) collective-permute-start(bf16[1024,256]{1,0:T(8,128)(2,1)} %get-tuple-element.13.own), channel_id=1, source_target_pairs={{0,3},{1,0},{2,1},{3,2},{4,7},{5,4},{6,5},{7,6},{8,11},{9,8},{10,9... | collective-permute-start | bytes 1572872 | tf_op jit(solution)/shard_map/ppermute | solution.py:393
  247.9 15.7 %collective-permute-start.6 = (bf16[512,256]{1,0:T(8,128)(2,1)S(1)}, bf16[512,256]{1,0:T(8,128)(2,1)S(1)}, u32[]{:S(2)}, u32[]{:S(2)}) collective-permute-start(bf16[512,256]{1,0:T(8,128)(2,1)S(1)} %slice.28), channel_id=1, source_target_pairs={{0,1},{1,2},{2,3},{3,0},{4,5},{5,6},{6,7},{7,4},{8,9},{9,10},{10,1... | collective-permute-start | bytes 786440 | tf_op jit(solution)/shard_map/ppermute | solution.py:393
  248.0 15.5 %collective-permute-start.8 = (bf16[512,256]{1,0:T(8,128)(2,1)S(1)}, bf16[512,256]{1,0:T(8,128)(2,1)S(1)}, u32[]{:S(2)}, u32[]{:S(2)}) collective-permute-start(bf16[512,256]{1,0:T(8,128)(2,1)S(1)} %slice.29), channel_id=1, source_target_pairs={{0,3},{1,0},{2,1},{3,2},{4,7},{5,4},{6,5},{7,6},{8,11},{9,8},{10,9... | collective-permute-start | bytes 786440 | tf_op jit(solution)/shard_map/ppermute | solution.py:393
Sparse Core Ops, SparseCore 0:
  73.2 96.9 all-gather.4
  209.4 28.6 all-gather.6

commit v3 on v1

v3 whole, which is shorter than its diff:
```python
import functools
import math

import jax
import jax.numpy as jnp
from jax import lax
from jax.experimental import pallas as pl
from jax.experimental.pallas import tpu as pltpu
from jax.sharding import PartitionSpec as P

FRAMES = 32
TMAX = 4
SMALL_VMEM = 16 * 1024 * 1024
CORES = 2
HD = 128
EPSILON = 1e-06
LOG2_SCALE = math.log2(math.e) / math.sqrt(HD)


def in_hbm(shape, dtype):
    return pltpu.HBM(shape, dtype)


def from_hbm(array):
    return pltpu.with_memory_space_constraint(array, pltpu.HBM)


def from_vmem(array):
    return pltpu.with_memory_space_constraint(array, pltpu.VMEM)


def temporal_count(classes, head_count):
    total = classes[0]
    for head in range(1, head_count):
        total = total + classes[head]
    return total


def head_of(classes, slot, head_count):
    temporal_seen = jnp.int32(0)
    spatial_seen = temporal_count(classes, head_count)
    found = jnp.int32(0)
    for head in range(head_count):
        kind = classes[head]
        rank = jnp.where(kind == 1, temporal_seen, spatial_seen)
        found = jnp.where(rank == slot, jnp.int32(head), found)
        temporal_seen = temporal_seen + kind
        spatial_seen = spatial_seen + 1 - kind
    return found


def normed(rows, gain):
    widened = rows.astype(jnp.float32)
    mean = jnp.mean(widened * widened, axis=-1, keepdims=True)
    return (widened * lax.rsqrt(mean + EPSILON) * gain).astype(jnp.bfloat16)


def scores_of(queries, keys):
    return lax.dot_general(queries, keys, (((1,), (1,)), ((), ())), preferred_element_type=jnp.float32)


def pack_kernel(head_count, classes, query, key, value, query_gain, key_gain, out, raw, ready, in_sems, out_sems):
    heads = [head_of(classes, slot, head_count) for slot in range(TMAX)]
    gains = (query_gain, key_gain, None)
    loads, stores = [], []
    for at in range(3 * TMAX):
        slot, which = divmod(at, 3)
        source = (query, key, value)[which].at[:, pl.ds(pl.multiple_of(heads[slot] * HD, HD), HD)]
        landing = raw if gains[which] is not None else ready
        loads.append(pltpu.make_async_copy(source, landing.at[at], in_sems.at[at]))
        loads[-1].start()
    for at in range(3 * TMAX):
        gain = gains[at % 3]
        loads[at].wait()
        if gain is not None:
            ready[at] = normed(raw[at], gain[...])
        stores.append(pltpu.make_async_copy(ready.at[at], out.at[:, pl.ds(at * HD, HD)], out_sems.at[at]))
        stores[-1].start()
    for store in stores:
        store.wait()


def pack(head_class, query_rows, key_rows, value_rows, query_gain, key_gain):
    tokens, width = query_rows.shape
    anywhere = pl.BlockSpec(memory_space=pl.ANY)
    gain_spec = pl.BlockSpec((1, HD), lambda step, classes: (0, 0))
    return pl.pallas_call(
        functools.partial(pack_kernel, width // HD),
        grid_spec=pltpu.PrefetchScalarGridSpec(
            num_scalar_prefetch=1,
            grid=(1,),
            in_specs=[anywhere] * 3 + [gain_spec] * 2,
            out_specs=anywhere,
            scratch_shapes=[
                pltpu.VMEM((3 * TMAX, tokens, HD), jnp.bfloat16),
                pltpu.VMEM((3 * TMAX, tokens, HD), jnp.bfloat16),
                pltpu.SemaphoreType.DMA((3 * TMAX,)),
                pltpu.SemaphoreType.DMA((3 * TMAX,)),
            ],
        ),
        out_shape=in_hbm((tokens, TMAX * 3 * HD), jnp.bfloat16),
        cost_estimate=pl.CostEstimate(flops=8 * tokens * TMAX * HD, bytes_accessed=12 * tokens * TMAX * HD, transcendentals=0),
        name="pack",
    )(head_class, from_hbm(query_rows), from_hbm(key_rows), from_hbm(value_rows), query_gain, key_gain)


def spatial_kernel(head_count, classes, query, key, other_key, value, other_value, query_gain, key_gain, out, keys, values):
    slot = pl.program_id(0)
    tokens = query.shape[0]
    chunk = tokens // 4

    @pl.when(slot >= temporal_count(classes, head_count))
    def _():
        keys[:tokens] = normed(key[...], key_gain[...])
        keys[tokens:] = normed(other_key[...], key_gain[...])
        values[:tokens, :HD] = value[...]
        values[tokens:, :HD] = other_value[...]
        values[:, HD:] = jnp.ones((2 * tokens, HD), jnp.bfloat16)

        def step(index, carry):
            rows = pl.ds(pl.multiple_of(index * chunk, chunk), chunk)
            queries = normed(query[rows, :], query_gain[...])
            weights = jnp.exp2(scores_of(queries, keys[...]) * LOG2_SCALE).astype(jnp.bfloat16)
            summed = jnp.dot(weights, values[...], preferred_element_type=jnp.float32)
            out[rows, :] = (summed[:, :HD] / summed[:, HD:]).astype(jnp.bfloat16)
            return carry

        lax.fori_loop(0, tokens // chunk, step, 0)

    @pl.when(slot < temporal_count(classes, head_count))
    def _():
        out[...] = jnp.zeros_like(out)


def spatial(head_class, query_rows, key_rows, other_keys, value_rows, other_values, query_gain, key_gain):
    tokens, width = query_rows.shape
    head_count = width // HD

    def rows(slot, classes):
        return 0, head_of(classes, slot, head_count)

    row_spec = pl.BlockSpec((tokens, HD), rows)
    gain_spec = pl.BlockSpec((1, HD), lambda slot, classes: (0, 0))
    return pl.pallas_call(
        functools.partial(spatial_kernel, head_count),
        grid_spec=pltpu.PrefetchScalarGridSpec(
            num_scalar_prefetch=1,
            grid=(head_count,),
            in_specs=[row_spec] * 5 + [gain_spec] * 2,
            out_specs=pl.BlockSpec((tokens, HD), lambda slot, classes: (0, slot)),
            scratch_shapes=[
                pltpu.VMEM((2 * tokens, HD), jnp.bfloat16),
                pltpu.VMEM((2 * tokens, 2 * HD), jnp.bfloat16),
            ],
        ),
        out_shape=in_hbm((tokens, width), jnp.bfloat16),
        cost_estimate=pl.CostEstimate(
            flops=16 * tokens * tokens * width, bytes_accessed=12 * tokens * width, transcendentals=2 * tokens * tokens * head_count
        ),
        name="spatial",
    )(head_class, query_rows, key_rows, from_hbm(other_keys), value_rows, from_hbm(other_values), query_gain, key_gain)


def temporal_kernel(head_count, classes, packed, *rest):
    out = rest[-1]
    slot = pl.program_id(0)
    frames, positions, _ = packed.shape
    places = 16
    count = frames * places

    @pl.when(slot < temporal_count(classes, head_count))
    def _():
        row = lax.broadcasted_iota(jnp.int32, (count, count), 0)
        column = lax.broadcasted_iota(jnp.int32, (count, count), 1)
        same = (row & (places - 1)) == (column & (places - 1))
        base = pl.multiple_of(slot * 3 * HD, HD)
        for part in range(positions // places):
            at = slice(part * places, (part + 1) * places)
            queries, keys, values = (packed[:, at, pl.ds(base + which * HD, HD)].reshape(count, HD) for which in range(3))
            scaled = jnp.where(same, scores_of(queries, keys) * LOG2_SCALE, -1e30)
            weights = jnp.exp2(scaled).astype(jnp.bfloat16)
            both = jnp.concatenate([values, jnp.ones_like(values)], axis=1)
            summed = jnp.dot(weights, both, preferred_element_type=jnp.float32)
            out[:, at, :] = (summed[:, :HD] / summed[:, HD:]).astype(jnp.bfloat16).reshape(frames, places, HD)

    @pl.when(slot >= temporal_count(classes, head_count))
    def _():
        out[...] = jnp.zeros_like(out)


def temporal(head_class, packed, after):
    frames, positions, _ = packed.shape
    return pl.pallas_call(
        functools.partial(temporal_kernel, head_class.shape[0]),
        grid_spec=pltpu.PrefetchScalarGridSpec(
            num_scalar_prefetch=1,
            grid=(TMAX,),
            in_specs=[pl.BlockSpec(memory_space=pltpu.VMEM)] + [pl.BlockSpec(memory_space=pl.ANY)] * len(after),
            out_specs=pl.BlockSpec((frames, positions, HD), lambda slot, classes: (0, 0, slot)),
        ),
        out_shape=in_hbm((frames, positions, TMAX * HD), jnp.bfloat16),
        compiler_params=pltpu.CompilerParams(vmem_limit_bytes=SMALL_VMEM),
        cost_estimate=pl.CostEstimate(
            flops=64 * frames * frames * positions * TMAX * HD,
            bytes_accessed=8 * frames * positions * TMAX * HD,
            transcendentals=16 * frames * frames * positions * TMAX,
        ),
        name="temporal",
    )(head_class, from_vmem(packed), *[from_hbm(array) for array in after])


def weight_kernel(classes, place, weight, out):
    group_count, _, width = out.shape
    for shift in range(group_count):
        block = lax.rem(place[0] + shift, group_count)
        out[shift] = weight[:, pl.ds(pl.multiple_of(block * width, width), width)]


def weight_blocks(head_class, place, weight, group_count):
    rows, columns = weight.shape
    head_count = rows // HD
    width = columns // group_count
    return pl.pallas_call(
        weight_kernel,
        grid_spec=pltpu.PrefetchScalarGridSpec(
            num_scalar_prefetch=2,
            grid=(head_count,),
            in_specs=[pl.BlockSpec((HD, columns), lambda slot, classes, place: (head_of(classes, slot, head_count), 0))],
            out_specs=pl.BlockSpec((group_count, HD, width), lambda slot, classes, place: (0, slot, 0)),
        ),
        out_shape=in_hbm((group_count, rows, width), jnp.bfloat16),
        cost_estimate=pl.CostEstimate(flops=0, bytes_accessed=4 * rows * columns, transcendentals=0),
        name="weight_blocks",
    )(head_class, place, weight)


def early_kernel(own, right_top, right_bottom, left_top, left_bottom, far_top, far_bottom, w_own, w_right, w_far, w_left, out):
    top = pl.program_id(0) < pl.num_programs(0) // 2
    total = jnp.dot(own[...], w_own[...], preferred_element_type=jnp.float32)
    for upper, lower, weight in ((right_top, right_bottom, w_right), (left_top, left_bottom, w_left), (far_top, far_bottom, w_far)):
        rows = jnp.where(top, upper[...], lower[...])
        total += jnp.dot(rows, weight[...], preferred_element_type=jnp.float32)
    out[...] = total


def project_early(pieces, weights):
    tokens, depth = pieces[0].shape
    width = weights[0].shape[1]
    steps = 4
    block = tokens // steps
    row_spec = pl.BlockSpec((block, depth), lambda step: (step, 0))
    top_spec = pl.BlockSpec((block, depth), lambda step: (jnp.minimum(step, steps // 2 - 1), 0))
    bottom_spec = pl.BlockSpec((block, depth), lambda step: (jnp.maximum(step - steps // 2, 0), 0))
    weight_spec = pl.BlockSpec((depth, width), lambda step: (0, 0))
    return pl.pallas_call(
        early_kernel,
        grid=(steps,),
        in_specs=[row_spec] + [top_spec, bottom_spec] * 3 + [weight_spec] * 4,
        out_specs=pl.BlockSpec((block, width), lambda step: (step, 0)),
        out_shape=in_hbm((tokens, width), jnp.float32),
        compiler_params=pltpu.CompilerParams(vmem_limit_bytes=2 * SMALL_VMEM),
        cost_estimate=pl.CostEstimate(
            flops=8 * tokens * depth * width, bytes_accessed=8 * tokens * depth + 8 * depth * width + 4 * tokens * width, transcendentals=0
        ),
        name="project_early",
    )(*[from_hbm(array) for array in (*pieces, *weights)])


def near_kernel(own, right_top, right_bottom, left_top, left_bottom, w_own, w_right, w_left, total, out):
    depth = own.shape[1]
    half = own.shape[0] // 2
    for part, right, left in ((0, right_top, left_top), (1, right_bottom, left_bottom)):
        rows = slice(part * half, (part + 1) * half)
        summed = total[rows] + jnp.dot(own[rows], w_own[:depth], preferred_element_type=jnp.float32)
        summed += jnp.dot(right[...], w_right[:depth], preferred_element_type=jnp.float32)
        summed += jnp.dot(left[...], w_left[:depth], preferred_element_type=jnp.float32)
        out[rows] = summed


def far_kernel(far_top, far_bottom, w_far, total, out):
    depth = far_top.shape[1]

    @pl.when(pl.program_id(0) == 0)
    def _():
        out[...] = (jnp.dot(far_top[...], w_far[:depth], preferred_element_type=jnp.float32) + total[...]).astype(out.dtype)

    @pl.when(pl.program_id(0) == 1)
    def _():
        out[...] = (jnp.dot(far_bottom[...], w_far[:depth], preferred_element_type=jnp.float32) + total[...]).astype(out.dtype)


def project_late(pieces, weights, total):
    tokens, depth = pieces[0].shape
    rows, width = weights[0].shape
    half = tokens // 2
    whole = pl.BlockSpec(memory_space=pltpu.VMEM)
    w_own, w_right, w_far, w_left = weights
    near = pl.pallas_call(
        near_kernel,
        in_specs=[whole] * 9,
        out_specs=whole,
        out_shape=pltpu.VMEM((tokens, width), jnp.float32),
        compiler_params=pltpu.CompilerParams(vmem_limit_bytes=SMALL_VMEM),
        cost_estimate=pl.CostEstimate(
            flops=6 * tokens * depth * width, bytes_accessed=6 * tokens * depth + 6 * depth * width + 8 * tokens * width, transcendentals=0
        ),
        name="near",
    )(*[from_vmem(array) for array in (*pieces[:5], w_own, w_right, w_left, total)])
    sum_spec = pl.BlockSpec((half, width), lambda step: (step, 0))
    return pl.pallas_call(
        far_kernel,
        grid=(2,),
        in_specs=[whole] * 3 + [sum_spec],
        out_specs=sum_spec,
        out_shape=in_hbm((tokens, width), jnp.bfloat16),
        compiler_params=pltpu.CompilerParams(vmem_limit_bytes=SMALL_VMEM),
        cost_estimate=pl.CostEstimate(
            flops=2 * tokens * depth * width, bytes_accessed=2 * tokens * depth + 2 * depth * width + 8 * tokens * width, transcendentals=0
        ),
        name="far",
    )(*[from_vmem(array) for array in (*pieces[5:], w_far, near)])


def shifted(block, by):
    count = lax.axis_size("head")
    return lax.ppermute(block, "head", [(at, (at + by) % count) for at in range(count)])


def ring(block):
    half = block.shape[0] // 2
    top, bottom = block[:half], block[half:]
    right_top, left_bottom = shifted(top, 1), shifted(bottom, -1)
    right_bottom, left_top = shifted(bottom, 1), shifted(top, -1)
    far_top, far_bottom = shifted(right_top, 1), shifted(left_bottom, -1)
    return block, right_top, right_bottom, left_top, left_bottom, far_top, far_bottom


def other_core(block):
    count = lax.axis_size("seq")
    return lax.ppermute(block, "seq", [(at, at ^ 1) for at in range(count)])


def over_frames(blocks):
    count = lax.axis_size("seq")
    groups = [list(range(core, count, CORES)) for core in range(CORES)]
    return lax.all_to_all(blocks, "seq", 0, 0, axis_index_groups=groups)


def body(query_rows, key_rows, value_rows, query_gain, key_gain, head_class, out_weight):
    tokens = query_rows.shape[0]
    group_count = lax.axis_size("head")
    query_gain = query_gain.reshape(1, HD)
    key_gain = key_gain.reshape(1, HD)
    packed = pack(head_class, query_rows, key_rows, value_rows, query_gain, key_gain)
    arrived = over_frames(packed.reshape(FRAMES, tokens // FRAMES, TMAX * 3 * HD))

    other_keys, other_values = other_core(key_rows), other_core(value_rows)
    near_out = spatial(head_class, query_rows, key_rows, other_keys, value_rows, other_values, query_gain, key_gain)
    place = lax.axis_index("head").reshape(1).astype(jnp.int32)
    blocks = weight_blocks(head_class, place, out_weight, group_count)

    core = lax.rem(lax.axis_index("seq"), CORES)
    half = blocks.shape[1] // CORES
    mine = lax.dynamic_slice_in_dim(blocks, core * half, half, axis=1)
    fetched = jnp.stack([shifted(mine[by], by) for by in range(1, group_count)])
    rest = other_core(fetched)
    others = jnp.where(core == 0, jnp.concatenate([fetched, rest], axis=1), jnp.concatenate([rest, fetched], axis=1))
    weights = [blocks[0]] + [others[by] for by in range(group_count - 1)]

    pieces = ring(near_out)
    returned = over_frames(temporal(head_class, arrived, (*pieces[1:5], others))).reshape(tokens, TMAX * HD)
    early = project_early(pieces, weights)
    return project_late(ring(returned), weights, early)


def solution(mesh):
    return jax.shard_map(
        body,
        mesh=mesh,
        in_specs=(
            P("seq", "head"),
            P("seq", "head"),
            P("seq", "head"),
            P(),
            P(),
            P("head"),
            P("head", None),
        ),
        out_specs=P("seq", "head"),
        check_vma=False,
    )
```

time: 234 us -> 199 us (0.85); the launches traced: 231 us -> 201 us
  waiting for transfers between devices: 109 us -> 86.3 us
  starting transfers between devices: 56 us -> 45.2 us
  other arithmetic: 2.47 us -> 6.6 us
    all_to_all x3 -> x2, waiting for transfers between devices: 70.7 us -> 25.2 us  [over_frames(): return lax.all_to_all(blocks, 'seq', 0, 0, axis_index_groups=groups)]
    ppermute x15, waiting for transfers between devices: 37.9 us -> 61.1 us  [shifted(): lax.ppermute(block, 'head', [(at, (at + by) % count) for at in range(coun...]
    pallas_call x1, Pallas kernels: 14.9 us -> 6.71 us  [weight_blocks(): pl.pallas_call(weight_kernel, grid_spec=pltpu.PrefetchScalarGridSpec(num_...]
    pallas_call x1, Pallas kernels: 12.8 us -> 20.8 us  [spatial(): pl.pallas_call(functools.partial(spatial_kernel, head_count), grid_spec=p...]
    all_to_all x3 -> x2, starting transfers between devices: 29 us -> 21.5 us  [over_frames(): return lax.all_to_all(blocks, 'seq', 0, 0, axis_index_groups=groups)]
    select_n x1, other arithmetic: 1.15 us -> 5.03 us  [body(): jnp.where(core == 0, jnp.concatenate([fetched, rest], axis=1), jnp.concat...]
    ppermute x15, starting transfers between devices: 26.4 us -> 23.1 us  [shifted(): lax.ppermute(block, 'head', [(at, (at + by) % count) for at in range(coun...]
    unnamed x20 -> x24, local copies, waits for them, and re-layouts: 5.81 us -> 2.8 us
  transfers between devices with their start and end apart: 20 -> 20, of which waited for: 10 -> 8; matrix products, arithmetic and copies ran while one was open for 3% -> 8% of each run, Pallas kernels for 18% -> 20%
where the time goes in v3:
time: 199 us; the launch traced here: 201 us
  waiting for transfers between devices  86.3 us (43%)
  Pallas kernels  51.6 us (26%)
  starting transfers between devices  45.2 us (23%)
  local copies, waits for them, and re-layouts  11.4 us (6%)
  other arithmetic  6.6 us (3%)
    ppermute x15, waiting for transfers between devices, shifted(): lax.ppermute(block, 'head', [(at, (at + by) % count) for at in range(coun...  61.1 us
    all_to_all x2, waiting for transfers between devices, over_frames(): return lax.all_to_all(blocks, 'seq', 0, 0, axis_index_groups=groups)  25.2 us
    ppermute x15, starting transfers between devices, shifted(): lax.ppermute(block, 'head', [(at, (at + by) % count) for at in range(coun...  23.1 us
    all_to_all x2, starting transfers between devices, over_frames(): return lax.all_to_all(blocks, 'seq', 0, 0, axis_index_groups=groups)  21.5 us
    pallas_call x1, Pallas kernels, spatial(): pl.pallas_call(functools.partial(spatial_kernel, head_count), grid_spec=p...  20.8 us
    pallas_call x1, Pallas kernels, project_early(): pl.pallas_call(early_kernel, grid=(steps,), in_specs=[row_spec] + [top_sp...  10.4 us
    pallas_call x1, Pallas kernels, weight_blocks(): pl.pallas_call(weight_kernel, grid_spec=pltpu.PrefetchScalarGridSpec(num_...  6.71 us
    pallas_call x1, Pallas kernels, pack(): pl.pallas_call(functools.partial(pack_kernel, width // HD), grid_spec=plt...  5.18 us
  transfers between devices with their start and end apart: 20, of which 8 were waited for; matrix products, arithmetic and copies ran while one was open for 8% of the time, Pallas kernels for 20%

profile of v3, /device:TPU:8, one launch (start us, length us, event | category | flops | bytes accessed | tf_op | source)
XLA Modules:
  0.0 201.2 jit_solution(11517320635233027983)
XLA Ops:
  0.0 5.2 %pack.1 = bf16[1024,1536]{1,0:T(8,128)(2,1)} custom-call(s32[6]{0:T(128)} %classes.7, bf16[1024,768]{1,0:T(8,128)(2,1)} %query.3, bf16[1024,768]{1,0:T(8,128)(2,1)} %key.3, bf16[1024,768]{1,0:T(8,128)(2,1)} %value.3, f32[1,128]{1,0:T(1,128)} %bitcast.36, f32[1,128]{1,0:T(1,128)} %bitcast.38), custom_call_target="tpu_custom_call" | custom-call | flops 4194304 | bytes 6291456 | tf_op jit(solution)/shard_map/pack/pallas_call | solution.py:87
  5.2 11.7 %all-to-all-start = ((bf16[32,32,1536]{2,1,0:T(8,128)(2,1)}), bf16[32,32,1536]{2,1,0:T(8,128)(2,1)S(1)}, u32[]{:S(2)}, u32[]{:S(2)}) async-start(bf16[32,32,1536]{2,1,0:T(8,128)(2,1)} %bitcast.25), calls=%async_computation | async-start | bytes 6291456 | tf_op jit(solution)/shard_map/all_to_all | solution.py:346
  17.5 6.7 %weight_blocks.1 = bf16[4,768,768]{2,1,0:T(8,128)(2,1)} custom-call(s32[6]{0:T(128)} %classes.7, s32[1]{0:T(128)} %bitcast.3.place, bf16[768,3072]{1,0:T(8,128)(2,1)} %weight.1), custom_call_target="tpu_custom_call" | custom-call | bytes 9437184 | tf_op jit(solution)/shard_map/weight_blocks/pallas_call | solution.py:223
  27.3 2.7 %collective-permute-start.7 = (bf16[384,768]{1,0:T(8,128)(2,1)S(1)}, bf16[384,768]{1,0:T(8,128)(2,1)S(1)}, u32[]{:S(2)}, u32[]{:S(2)}) collective-permute-start(bf16[384,768]{1,0:T(8,128)(2,1)S(1)} %get-tuple-element.6), channel_id=1, source_target_pairs={{0,2},{1,3},{2,0},{3,1},{4,6},{5,7},{6,4},{7,5},{8,10},{9,11},{10,... | collective-permute-start | bytes 1769480 | tf_op jit(solution)/shard_map/ppermute | solution.py:326
  31.5 10.9 %collective-permute-done.6 = bf16[384,768]{1,0:T(8,128)(2,1)S(1)} collective-permute-done((bf16[384,768]{1,0:T(8,128)(2,1)S(1)}, bf16[384,768]{1,0:T(8,128)(2,1)S(1)}, u32[]{:S(2)}, u32[]{:S(2)}) %collective-permute-start.6) | collective-permute-done | bytes 589856 | tf_op jit(solution)/shard_map/ppermute | solution.py:326
  42.4 13.6 %collective-permute-done.7 = bf16[384,768]{1,0:T(8,128)(2,1)S(1)} collective-permute-done((bf16[384,768]{1,0:T(8,128)(2,1)S(1)}, bf16[384,768]{1,0:T(8,128)(2,1)S(1)}, u32[]{:S(2)}, u32[]{:S(2)}) %collective-permute-start.7) | collective-permute-done | bytes 589856 | tf_op jit(solution)/shard_map/ppermute | solution.py:326
  57.6 20.8 %spatial.1.own = bf16[1024,768]{1,0:T(8,128)(2,1)} custom-call(s32[6]{0:T(128)} %classes.7, bf16[1024,768]{1,0:T(8,128)(2,1)} %query.3, bf16[1024,768]{1,0:T(8,128)(2,1)} %key.3, bf16[1024,768]{1,0:T(8,128)(2,1)} %collective-permute-done.other_key, bf16[1024,768]{1,0:T(8,128)(2,1)} %value.3, bf16[1024,768]{1,0:T(8,128)(2,1)} %collective-permute-done.1.other_value, ...), custom_call_target="tpu_custom_call" | custom-call | flops 12884901888 | bytes 9437184 | tf_op jit(solution)/shard_map/spatial/pallas_call | solution.py:144
  78.4 2.6 %fusion = (bf16[512,768]{1,0:T(8,128)(2,1)}, bf16[512,768]{1,0:T(8,128)(2,1)}) fusion(bf16[1024,768]{1,0:T(8,128)(2,1)} %spatial.1.own), kind=kLoop, calls=%fused_computation.9 | loop fusion | bytes 3145728 | tf_op jit(solution)/shard_map/slice | solution.py:331
  83.1 4.1 %collective-permute-start.4 = (bf16[512,768]{1,0:T(8,128)(2,1)}, bf16[512,768]{1,0:T(8,128)(2,1)}, u32[]{:S(2)}, u32[]{:S(2)}) collective-permute-start(bf16[512,768]{1,0:T(8,128)(2,1)} %get-tuple-element.12), channel_id=1, source_target_pairs={{0,3},{1,0},{2,1},{3,2},{4,7},{5,4},{6,5},{7,6},{8,11},{9,8},{10,9... | collective-permute-start | bytes 2359304 | tf_op jit(solution)/shard_map/ppermute | solution.py:326
  87.1 5.0 %maximum_select_fusion.rest_4_ = bf16[3,768,768]{2,1,0:T(8,128)(2,1)} fusion(bf16[3,384,768]{2,1,0:T(8,128)(2,1)} %collective-permute-done.9, bf16[1,384,768]{2,1,0:T(8,128)(2,1)} %bitcast.31, bf16[1,384,768]{2,1,0:T(8,128)(2,1)} %bitcast.29, bf16[1,384,768]{2,1,0:T(8,128)(2,1)} %bitcast.27, pred[]{:T(512)S(6)} %eq.3), kind=kLoop, calls=%fused_computation | loop fusion | flops 30081024 | bytes 7077889 | tf_op jit(solution)/shard_map/jit(_where)/select_n | solution.py:367
  92.2 9.5 %collective-permute-done.5.rest_3_.left_bottom = bf16[512,768]{1,0:T(8,128)(2,1)} collective-permute-done((bf16[512,768]{1,0:T(8,128)(2,1)}, bf16[512,768]{1,0:T(8,128)(2,1)}, u32[]{:S(2)}, u32[]{:S(2)}) %collective-permute-start.5) | collective-permute-done | bytes 786464 | tf_op jit(solution)/shard_map/ppermute | solution.py:326
  101.7 4.1 %collective-permute-done.3.rest_1_.right_bottom = bf16[512,768]{1,0:T(8,128)(2,1)} collective-permute-done((bf16[512,768]{1,0:T(8,128)(2,1)}, bf16[512,768]{1,0:T(8,128)(2,1)}, u32[]{:S(2)}, u32[]{:S(2)}) %collective-permute-start.3) | collective-permute-done | bytes 786464 | tf_op jit(solution)/shard_map/ppermute | solution.py:326
  105.8 12.4 %collective-permute-done.4.rest_2_.left_top = bf16[512,768]{1,0:T(8,128)(2,1)} collective-permute-done((bf16[512,768]{1,0:T(8,128)(2,1)}, bf16[512,768]{1,0:T(8,128)(2,1)}, u32[]{:S(2)}, u32[]{:S(2)}) %collective-permute-start.4) | collective-permute-done | bytes 786464 | tf_op jit(solution)/shard_map/ppermute | solution.py:326
  118.1 4.1 %collective-permute-done.2.rest_0_.right_top = bf16[512,768]{1,0:T(8,128)(2,1)} collective-permute-done((bf16[512,768]{1,0:T(8,128)(2,1)}, bf16[512,768]{1,0:T(8,128)(2,1)}, u32[]{:S(2)}, u32[]{:S(2)}) %collective-permute-start.2) | collective-permute-done | bytes 786464 | tf_op jit(solution)/shard_map/ppermute | solution.py:326
  122.2 3.8 %temporal.1 = bf16[32,32,512]{2,1,0:T(8,128)(2,1)} custom-call(s32[6]{0:T(128)S(1)} %copy-done.5, bf16[32,32,1536]{2,1,0:T(8,128)(2,1)S(1)} %all-to-all-done.packed, bf16[512,768]{1,0:T(8,128)(2,1)} %collective-permute-done.2.rest_0_.right_top, bf16[512,768]{1,0:T(8,128)(2,1)} %collective-permute-done.3.rest_1_.right_bottom, ...), custom_call_target="tpu_custom_call" | custom-call | flops 1073741824 | bytes 4194304 | tf_op jit(solution)/shard_map/temporal/pallas_call | solution.py:193
  126.1 9.8 %all-to-all-start.1 = ((bf16[32,32,512]{2,1,0:T(8,128)(2,1)}), bf16[32,32,512]{2,1,0:T(8,128)(2,1)S(1)}, u32[]{:S(2)}, u32[]{:S(2)}) async-start(bf16[32,32,512]{2,1,0:T(8,128)(2,1)} %temporal.1), calls=%async_computation.1 | async-start | bytes 2097152 | tf_op jit(solution)/shard_map/all_to_all | solution.py:346
  135.8 2.7 %collective-permute-start.17 = (bf16[512,768]{1,0:T(8,128)(2,1)}, bf16[512,768]{1,0:T(8,128)(2,1)S(1)}, u32[]{:S(2)}, u32[]{:S(2)}) collective-permute-start(bf16[512,768]{1,0:T(8,128)(2,1)} %collective-permute-done.5.rest_3_.left_bottom), channel_id=1, source_target_pairs={{0,3},{1,0},{2,1},{3,2},{4,7},{5,4},{6,5},{7,6},{8,11},{9,8},{10,9... | collective-permute-start | bytes 2359304 | tf_op jit(solution)/shard_map/ppermute | solution.py:326
  138.5 25.2 %all-to-all-done.1 = bf16[32,32,512]{2,1,0:T(8,128)(2,1)S(1)} async-done(((bf16[32,32,512]{2,1,0:T(8,128)(2,1)}), bf16[32,32,512]{2,1,0:T(8,128)(2,1)S(1)}, u32[]{:S(2)}, u32[]{:S(2)}) %all-to-all-start.1) | async-done | bytes 1048608 | tf_op jit(solution)/shard_map/all_to_all | solution.py:346
  164.0 3.2 %collective-permute-start.12 = (bf16[512,512]{1,0:T(8,128)(2,1)S(1)}, bf16[512,512]{1,0:T(8,128)(2,1)S(1)}, u32[]{:S(2)}, u32[]{:S(2)}) collective-permute-start(bf16[512,512]{1,0:T(8,128)(2,1)S(1)} %bitcast.32), channel_id=1, source_target_pairs={{0,3},{1,0},{2,1},{3,2},{4,7},{5,4},{6,5},{7,6},{8,11},{9,8},{10,9... | collective-permute-start | bytes 1572872 | tf_op jit(solution)/shard_map/ppermute | solution.py:326
  167.2 2.4 %slice_bitcast_fusion.2.w_own = bf16[768,768]{1,0:T(8,128)(2,1)} fusion(bf16[4,768,768]{2,1,0:T(8,128)(2,1)} %weight_blocks.1), kind=kLoop, calls=%fused_computation.4 | loop fusion | bytes 2359296 | tf_op jit(solution)/shard_map/squeeze | solution.py:368
  173.5 6.5 %collective-permute-done.10.right_top = bf16[512,512]{1,0:T(8,128)(2,1)S(1)} collective-permute-done((bf16[512,512]{1,0:T(8,128)(2,1)S(1)}, bf16[512,512]{1,0:T(8,128)(2,1)S(1)}, u32[]{:S(2)}, u32[]{:S(2)}) %collective-permute-start.10) | collective-permute-done | bytes 524320 | tf_op jit(solution)/shard_map/ppermute | solution.py:326
  180.0 3.2 %collective-permute-start.13 = (bf16[512,512]{1,0:T(8,128)(2,1)S(1)}, bf16[512,512]{1,0:T(8,128)(2,1)S(1)}, u32[]{:S(2)}, u32[]{:S(2)}) collective-permute-start(bf16[512,512]{1,0:T(8,128)(2,1)S(1)} %collective-permute-done.12.left_bottom), channel_id=1, source_target_pairs={{0,3},{1,0},{2,1},{3,2},{4,7},{5,4},{6,5},{7,6},{8,11},{9,8},{10,9... | collective-permute-start | bytes 1572872 | tf_op jit(solution)/shard_map/ppermute | solution.py:326
  184.1 10.4 %project_early.1.total = f32[1024,768]{1,0:T(8,128)} custom-call(bf16[1024,768]{1,0:T(8,128)(2,1)} %spatial.1.own, bf16[512,768]{1,0:T(8,128)(2,1)} %collective-permute-done.2.rest_0_.right_top, bf16[512,768]{1,0:T(8,128)(2,1)} %collective-permute-done.3.rest_1_.right_bottom, bf16[512,768]{1,0:T(8,128)(2,1)} %collective-permute-done.4.rest_2_.left_top, ...), custom_call_target="tpu_custom_call" | custom-call | flops 4831838208 | bytes 14155776 | tf_op jit(solution)/shard_map/project_early/pallas_call | solution.py:255
  196.5 2.6 %near.1.total = f32[1024,768]{1,0:T(8,128)S(1)} custom-call(bf16[1024,512]{1,0:T(8,128)(2,1)S(1)} %bitcast.24, bf16[512,512]{1,0:T(8,128)(2,1)S(1)} %collective-permute-done.10.right_top, bf16[512,512]{1,0:T(8,128)(2,1)S(1)} %collective-permute-done.14.right_bottom, bf16[512,512]{1,0:T(8,128)(2,1)S(1)} %collective-permute-done.15.left_top, ...), custom_call_target="tpu_custom_call" | custom-call | flops 2415919104 | bytes 11796480 | tf_op jit(solution)/shard_map/near/pallas_call | solution.py:298
  (54 shorter events, 17.7 us)
Async XLA Ops:
  5.2 117.1 %all-to-all-start = ((bf16[32,32,1536]{2,1,0:T(8,128)(2,1)}), bf16[32,32,1536]{2,1,0:T(8,128)(2,1)S(1)}, u32[]{:S(2)}, u32[]{:S(2)}) async-start(bf16[32,32,1536]{2,1,0:T(8,128)(2,1)} %bitcast.25), calls=%async_computation | async-start | bytes 6291456 | tf_op jit(solution)/shard_map/all_to_all | solution.py:346
  16.9 40.7 %collective-permute-start = (bf16[1024,768]{1,0:T(8,128)(2,1)}, bf16[1024,768]{1,0:T(8,128)(2,1)}, u32[]{:S(2)}, u32[]{:S(2)}) collective-permute-start(bf16[1024,768]{1,0:T(8,128)(2,1)} %key.3), channel_id=1, source_target_pairs={{0,4},{4,0},{8,12},{12,8},{16,20},{20,16},{24,28},{28,24},{32,36},... | collective-permute-start | bytes 4718600 | tf_op jit(solution)/shard_map/ppermute | solution.py:340
  17.0 40.6 %collective-permute-start.1 = (bf16[1024,768]{1,0:T(8,128)(2,1)}, bf16[1024,768]{1,0:T(8,128)(2,1)}, u32[]{:S(2)}, u32[]{:S(2)}) collective-permute-start(bf16[1024,768]{1,0:T(8,128)(2,1)} %value.3), channel_id=1, source_target_pairs={{0,4},{4,0},{8,12},{12,8},{16,20},{20,16},{24,28},{28,24},{32,36},... | collective-permute-start | bytes 4718600 | tf_op jit(solution)/shard_map/ppermute | solution.py:340
  25.7 16.6 %collective-permute-start.6 = (bf16[384,768]{1,0:T(8,128)(2,1)S(1)}, bf16[384,768]{1,0:T(8,128)(2,1)S(1)}, u32[]{:S(2)}, u32[]{:S(2)}) collective-permute-start(bf16[384,768]{1,0:T(8,128)(2,1)S(1)} %get-tuple-element.5), channel_id=1, source_target_pairs={{0,1},{1,2},{2,3},{3,0},{4,5},{5,6},{6,7},{7,4},{8,9},{9,10},{10,1... | collective-permute-start | bytes 1769480 | tf_op jit(solution)/shard_map/ppermute | solution.py:326
  27.3 28.7 %collective-permute-start.7 = (bf16[384,768]{1,0:T(8,128)(2,1)S(1)}, bf16[384,768]{1,0:T(8,128)(2,1)S(1)}, u32[]{:S(2)}, u32[]{:S(2)}) collective-permute-start(bf16[384,768]{1,0:T(8,128)(2,1)S(1)} %get-tuple-element.6), channel_id=1, source_target_pairs={{0,2},{1,3},{2,0},{3,1},{4,6},{5,7},{6,4},{7,5},{8,10},{9,11},{10,... | collective-permute-start | bytes 1769480 | tf_op jit(solution)/shard_map/ppermute | solution.py:326
  30.0 26.0 %collective-permute-start.8 = (bf16[384,768]{1,0:T(8,128)(2,1)S(1)}, bf16[384,768]{1,0:T(8,128)(2,1)S(1)}, u32[]{:S(2)}, u32[]{:S(2)}) collective-permute-start(bf16[384,768]{1,0:T(8,128)(2,1)S(1)} %get-tuple-element.7), channel_id=1, source_target_pairs={{0,3},{1,0},{2,1},{3,2},{4,7},{5,4},{6,5},{7,6},{8,11},{9,8},{10,9... | collective-permute-start | bytes 1769480 | tf_op jit(solution)/shard_map/ppermute | solution.py:326
  42.4 13.6 %copy-start.7 = (bf16[384,768]{1,0:T(8,128)(2,1)}, bf16[384,768]{1,0:T(8,128)(2,1)S(1)}, u32[]{:S(2)}) copy-start(bf16[384,768]{1,0:T(8,128)(2,1)S(1)} %collective-permute-done.6) | copy-start | bytes 1769476
  57.6 29.6 %collective-permute-start.9 = (bf16[3,384,768]{2,1,0:T(8,128)(2,1)}, bf16[3,384,768]{2,1,0:T(8,128)(2,1)}, u32[]{:S(2)}, u32[]{:S(2)}) collective-permute-start(bf16[3,384,768]{2,1,0:T(8,128)(2,1)} %pad_maximum_fusion), channel_id=1, source_target_pairs={{0,4},{4,0},{8,12},{12,8},{16,20},{20,16},{24,28},{28,24},{32,36},... | collective-permute-start | bytes 5308424 | tf_op jit(solution)/shard_map/ppermute | solution.py:340
  81.0 20.7 %collective-permute-start.5 = (bf16[512,768]{1,0:T(8,128)(2,1)}, bf16[512,768]{1,0:T(8,128)(2,1)}, u32[]{:S(2)}, u32[]{:S(2)}) collective-permute-start(bf16[512,768]{1,0:T(8,128)(2,1)} %get-tuple-element.11), channel_id=1, source_target_pairs={{0,3},{1,0},{2,1},{3,2},{4,7},{5,4},{6,5},{7,6},{8,11},{9,8},{10,9... | collective-permute-start | bytes 2359304 | tf_op jit(solution)/shard_map/ppermute | solution.py:326
  81.0 24.7 %collective-permute-start.3 = (bf16[512,768]{1,0:T(8,128)(2,1)}, bf16[512,768]{1,0:T(8,128)(2,1)}, u32[]{:S(2)}, u32[]{:S(2)}) collective-permute-start(bf16[512,768]{1,0:T(8,128)(2,1)} %get-tuple-element.11), channel_id=1, source_target_pairs={{0,1},{1,2},{2,3},{3,0},{4,5},{5,6},{6,7},{7,4},{8,9},{9,10},{10,1... | collective-permute-start | bytes 2359304 | tf_op jit(solution)/shard_map/ppermute | solution.py:326
  83.1 35.1 %collective-permute-start.4 = (bf16[512,768]{1,0:T(8,128)(2,1)}, bf16[512,768]{1,0:T(8,128)(2,1)}, u32[]{:S(2)}, u32[]{:S(2)}) collective-permute-start(bf16[512,768]{1,0:T(8,128)(2,1)} %get-tuple-element.12), channel_id=1, source_target_pairs={{0,3},{1,0},{2,1},{3,2},{4,7},{5,4},{6,5},{7,6},{8,11},{9,8},{10,9... | collective-permute-start | bytes 2359304 | tf_op jit(solution)/shard_map/ppermute | solution.py:326
  87.1 35.1 %collective-permute-start.2 = (bf16[512,768]{1,0:T(8,128)(2,1)}, bf16[512,768]{1,0:T(8,128)(2,1)}, u32[]{:S(2)}, u32[]{:S(2)}) collective-permute-start(bf16[512,768]{1,0:T(8,128)(2,1)} %get-tuple-element.12), channel_id=1, source_target_pairs={{0,1},{1,2},{2,3},{3,0},{4,5},{5,6},{6,7},{7,4},{8,9},{9,10},{10,1... | collective-permute-start | bytes 2359304 | tf_op jit(solution)/shard_map/ppermute | solution.py:326
  87.1 35.1 %copy-start.5 = (s32[6]{0:T(128)S(1)}, s32[6]{0:T(128)}, u32[]{:S(2)}) copy-start(s32[6]{0:T(128)} %classes.7) | copy-start | bytes 76
  126.1 37.7 %all-to-all-start.1 = ((bf16[32,32,512]{2,1,0:T(8,128)(2,1)}), bf16[32,32,512]{2,1,0:T(8,128)(2,1)S(1)}, u32[]{:S(2)}, u32[]{:S(2)}) async-start(bf16[32,32,512]{2,1,0:T(8,128)(2,1)} %temporal.1), calls=%async_computation.1 | async-start | bytes 2097152 | tf_op jit(solution)/shard_map/all_to_all | solution.py:346
  135.8 34.9 %collective-permute-start.17 = (bf16[512,768]{1,0:T(8,128)(2,1)}, bf16[512,768]{1,0:T(8,128)(2,1)S(1)}, u32[]{:S(2)}, u32[]{:S(2)}) collective-permute-start(bf16[512,768]{1,0:T(8,128)(2,1)} %collective-permute-done.5.rest_3_.left_bottom), channel_id=1, source_target_pairs={{0,3},{1,0},{2,1},{3,2},{4,7},{5,4},{6,5},{7,6},{8,11},{9,8},{10,9... | collective-permute-start | bytes 2359304 | tf_op jit(solution)/shard_map/ppermute | solution.py:326
  138.5 44.7 %collective-permute-start.16 = (bf16[512,768]{1,0:T(8,128)(2,1)}, bf16[512,768]{1,0:T(8,128)(2,1)S(1)}, u32[]{:S(2)}, u32[]{:S(2)}) collective-permute-start(bf16[512,768]{1,0:T(8,128)(2,1)} %collective-permute-done.2.rest_0_.right_top), channel_id=1, source_target_pairs={{0,1},{1,2},{2,3},{3,0},{4,5},{5,6},{6,7},{7,4},{8,9},{9,10},{10,1... | collective-permute-start | bytes 2359304 | tf_op jit(solution)/shard_map/ppermute | solution.py:326
  163.9 16.1 %collective-permute-start.10 = (bf16[512,512]{1,0:T(8,128)(2,1)S(1)}, bf16[512,512]{1,0:T(8,128)(2,1)S(1)}, u32[]{:S(2)}, u32[]{:S(2)}) collective-permute-start(bf16[512,512]{1,0:T(8,128)(2,1)S(1)} %bitcast.34), channel_id=1, source_target_pairs={{0,1},{1,2},{2,3},{3,0},{4,5},{5,6},{6,7},{7,4},{8,9},{9,10},{10,1... | collective-permute-start | bytes 1572872 | tf_op jit(solution)/shard_map/ppermute | solution.py:326
  164.0 16.1 %collective-permute-start.12 = (bf16[512,512]{1,0:T(8,128)(2,1)S(1)}, bf16[512,512]{1,0:T(8,128)(2,1)S(1)}, u32[]{:S(2)}, u32[]{:S(2)}) collective-permute-start(bf16[512,512]{1,0:T(8,128)(2,1)S(1)} %bitcast.32), channel_id=1, source_target_pairs={{0,3},{1,0},{2,1},{3,2},{4,7},{5,4},{6,5},{7,6},{8,11},{9,8},{10,9... | collective-permute-start | bytes 1572872 | tf_op jit(solution)/shard_map/ppermute | solution.py:326
  169.6 25.0 %collective-permute-start.15 = (bf16[512,512]{1,0:T(8,128)(2,1)S(1)}, bf16[512,512]{1,0:T(8,128)(2,1)S(1)}, u32[]{:S(2)}, u32[]{:S(2)}) collective-permute-start(bf16[512,512]{1,0:T(8,128)(2,1)S(1)} %bitcast.35), channel_id=1, source_target_pairs={{0,3},{1,0},{2,1},{3,2},{4,7},{5,4},{6,5},{7,6},{8,11},{9,8},{10,9... | collective-permute-start | bytes 1572872 | tf_op jit(solution)/shard_map/ppermute | solution.py:326
  170.7 23.9 %collective-permute-start.14 = (bf16[512,512]{1,0:T(8,128)(2,1)S(1)}, bf16[512,512]{1,0:T(8,128)(2,1)S(1)}, u32[]{:S(2)}, u32[]{:S(2)}) collective-permute-start(bf16[512,512]{1,0:T(8,128)(2,1)S(1)} %bitcast.33), channel_id=1, source_target_pairs={{0,1},{1,2},{2,3},{3,0},{4,5},{5,6},{6,7},{7,4},{8,9},{9,10},{10,1... | collective-permute-start | bytes 1572872 | tf_op jit(solution)/shard_map/ppermute | solution.py:326
  180.0 19.1 %collective-permute-start.11 = (bf16[512,512]{1,0:T(8,128)(2,1)S(1)}, bf16[512,512]{1,0:T(8,128)(2,1)S(1)}, u32[]{:S(2)}, u32[]{:S(2)}) collective-permute-start(bf16[512,512]{1,0:T(8,128)(2,1)S(1)} %collective-permute-done.10.right_top), channel_id=1, source_target_pairs={{0,1},{1,2},{2,3},{3,0},{4,5},{5,6},{6,7},{7,4},{8,9},{9,10},{10,1... | collective-permute-start | bytes 1572872 | tf_op jit(solution)/shard_map/ppermute | solution.py:326
  180.0 19.1 %collective-permute-start.13 = (bf16[512,512]{1,0:T(8,128)(2,1)S(1)}, bf16[512,512]{1,0:T(8,128)(2,1)S(1)}, u32[]{:S(2)}, u32[]{:S(2)}) collective-permute-start(bf16[512,512]{1,0:T(8,128)(2,1)S(1)} %collective-permute-done.12.left_bottom), channel_id=1, source_target_pairs={{0,3},{1,0},{2,1},{3,2},{4,7},{5,4},{6,5},{7,6},{8,11},{9,8},{10,9... | collective-permute-start | bytes 1572872 | tf_op jit(solution)/shard_map/ppermute | solution.py:326
  184.1 10.4 %copy-start.1 = (bf16[768,768]{1,0:T(8,128)(2,1)S(1)}, bf16[768,768]{1,0:T(8,128)(2,1)}, u32[]{:S(2)}) copy-start(bf16[768,768]{1,0:T(8,128)(2,1)} %get-tuple-element.9.w_right) | copy-start | bytes 3538948
  184.1 10.5 %copy-start.2 = (bf16[768,768]{1,0:T(8,128)(2,1)S(1)}, bf16[768,768]{1,0:T(8,128)(2,1)}, u32[]{:S(2)}) copy-start(bf16[768,768]{1,0:T(8,128)(2,1)} %slice_bitcast_fusion.2.w_own) | copy-start | bytes 3538948
  (8 other events, 29.7 us)

commit v4 on v3

--- a/solution.py
+++ b/solution.py
@@ -57,6 +57,23 @@
 
 def scores_of(queries, keys):
     return lax.dot_general(queries, keys, (((1,), (1,)), ((), ())), preferred_element_type=jnp.float32)
+
+
+def hold_kernel(*refs):
+    pass
+
+
+def hold(arrays, after):
+    anywhere = pl.BlockSpec(memory_space=pl.ANY)
+    return pl.pallas_call(
+        hold_kernel,
+        in_specs=[anywhere] * (len(arrays) + len(after)),
+        out_specs=[anywhere] * len(arrays),
+        out_shape=[in_hbm(array.shape, array.dtype) for array in arrays],
+        input_output_aliases={at: at for at in range(len(arrays))},
+        cost_estimate=pl.CostEstimate(flops=0, bytes_accessed=0, transcendentals=0),
+        name="hold",
+    )(*[from_hbm(array) for array in (*arrays, *after)])
 
 
 def pack_kernel(head_count, classes, query, key, value, query_gain, key_gain, out, raw, ready, in_sems, out_sems):
@@ -104,10 +121,11 @@
     )(head_class, from_hbm(query_rows), from_hbm(key_rows), from_hbm(value_rows), query_gain, key_gain)
 
 
-def spatial_kernel(head_count, classes, query, key, other_key, value, other_value, query_gain, key_gain, out, keys, values):
+def spatial_kernel(head_count, classes, query, key, other_key, value, other_value, query_gain, key_gain, front, back, keys, values):
     slot = pl.program_id(0)
     tokens = query.shape[0]
     chunk = tokens // 4
+    is_front = slot < TMAX
 
     @pl.when(slot >= temporal_count(classes, head_count))
     def _():
@@ -122,14 +140,23 @@
             queries = normed(query[rows, :], query_gain[...])
             weights = jnp.exp2(scores_of(queries, keys[...]) * LOG2_SCALE).astype(jnp.bfloat16)
             summed = jnp.dot(weights, values[...], preferred_element_type=jnp.float32)
-            out[rows, :] = (summed[:, :HD] / summed[:, HD:]).astype(jnp.bfloat16)
+            result = (summed[:, :HD] / summed[:, HD:]).astype(jnp.bfloat16)
+
+            @pl.when(is_front)
+            def _():
+                front[rows, :] = result
+
+            @pl.when(jnp.logical_not(is_front))
+            def _():
+                back[rows, :] = result
+
             return carry
 
         lax.fori_loop(0, tokens // chunk, step, 0)
 
     @pl.when(slot < temporal_count(classes, head_count))
     def _():
-        out[...] = jnp.zeros_like(out)
+        front[...] = jnp.zeros_like(front)
 
 
 def spatial(head_class, query_rows, key_rows, other_keys, value_rows, other_values, query_gain, key_gain):
@@ -147,13 +174,19 @@
             num_scalar_prefetch=1,
             grid=(head_count,),
             in_specs=[row_spec] * 5 + [gain_spec] * 2,
-            out_specs=pl.BlockSpec((tokens, HD), lambda slot, classes: (0, slot)),
+            out_specs=[
+                pl.BlockSpec((tokens, HD), lambda slot, classes: (0, jnp.minimum(slot, TMAX - 1))),
+                pl.BlockSpec((tokens, HD), lambda slot, classes: (0, jnp.maximum(slot - TMAX, 0))),
+            ],
             scratch_shapes=[
                 pltpu.VMEM((2 * tokens, HD), jnp.bfloat16),
                 pltpu.VMEM((2 * tokens, 2 * HD), jnp.bfloat16),
             ],
         ),
-        out_shape=in_hbm((tokens, width), jnp.bfloat16),
+        out_shape=[
+            in_hbm((tokens, TMAX * HD), jnp.bfloat16),
+            in_hbm((tokens, width - TMAX * HD), jnp.bfloat16),
+        ],
         cost_estimate=pl.CostEstimate(
             flops=16 * tokens * tokens * width, bytes_accessed=12 * tokens * width, transcendentals=2 * tokens * tokens * head_count
         ),
@@ -209,103 +242,104 @@
     )(head_class, from_vmem(packed), *[from_hbm(array) for array in after])
 
 
-def weight_kernel(classes, place, weight, out):
-    group_count, _, width = out.shape
-    for shift in range(group_count):
+def weight_kernel(classes, place, weight, own, *others):
+    width = own.shape[1]
+    group_count = len(others) + 1
+
+    def columns(shift):
         block = lax.rem(place[0] + shift, group_count)
-        out[shift] = weight[:, pl.ds(pl.multiple_of(block * width, width), width)]
+        return weight[:, pl.ds(pl.multiple_of(block * width, width), width)]
+
+    own[...] = columns(0)
+
+    @pl.when(pl.program_id(0) // (pl.num_programs(0) // CORES) == place[1])
+    def _():
+        for shift, other in enumerate(others):
+            other[...] = columns(shift + 1)
 
 
 def weight_blocks(head_class, place, weight, group_count):
     rows, columns = weight.shape
     head_count = rows // HD
+    share = head_count // CORES
     width = columns // group_count
+
+    def half_rows(slot, classes, place):
+        return jnp.clip(slot - place[1] * share, 0, share - 1), 0
+
     return pl.pallas_call(
         weight_kernel,
         grid_spec=pltpu.PrefetchScalarGridSpec(
             num_scalar_prefetch=2,
             grid=(head_count,),
             in_specs=[pl.BlockSpec((HD, columns), lambda slot, classes, place: (head_of(classes, slot, head_count), 0))],
-            out_specs=pl.BlockSpec((group_count, HD, width), lambda slot, classes, place: (0, slot, 0)),
-        ),
-        out_shape=in_hbm((group_count, rows, width), jnp.bfloat16),
+            out_specs=[pl.BlockSpec((HD, width), lambda slot, classes, place: (slot, 0))]
+            + [pl.BlockSpec((HD, width), half_rows)] * (group_count - 1),
+        ),
+        out_shape=[in_hbm((rows, width), jnp.bfloat16)] + [in_hbm((rows // CORES, width), jnp.bfloat16)] * (group_count - 1),
         cost_estimate=pl.CostEstimate(flops=0, bytes_accessed=4 * rows * columns, transcendentals=0),
         name="weight_blocks",
     )(head_class, place, weight)
 
 
-def early_kernel(own, right_top, right_bottom, left_top, left_bottom, far_top, far_bottom, w_own, w_right, w_far, w_left, out):
-    top = pl.program_id(0) < pl.num_programs(0) // 2
-    total = jnp.dot(own[...], w_own[...], preferred_element_type=jnp.float32)
-    for upper, lower, weight in ((right_top, right_bottom, w_right), (left_top, left_bottom, w_left), (far_top, far_bottom, w_far)):
-        rows = jnp.where(top, upper[...], lower[...])
-        total += jnp.dot(rows, weight[...], preferred_element_type=jnp.float32)
-    out[...] = total
-
-
-def project_early(pieces, weights):
-    tokens, depth = pieces[0].shape
-    width = weights[0].shape[1]
-    steps = 4
-    block = tokens // steps
-    row_spec = pl.BlockSpec((block, depth), lambda step: (step, 0))
-    top_spec = pl.BlockSpec((block, depth), lambda step: (jnp.minimum(step, steps // 2 - 1), 0))
-    bottom_spec = pl.BlockSpec((block, depth), lambda step: (jnp.maximum(step - steps // 2, 0), 0))
-    weight_spec = pl.BlockSpec((depth, width), lambda step: (0, 0))
-    return pl.pallas_call(
-        early_kernel,
-        grid=(steps,),
-        in_specs=[row_spec] + [top_spec, bottom_spec] * 3 + [weight_spec] * 4,
-        out_specs=pl.BlockSpec((block, width), lambda step: (step, 0)),
-        out_shape=in_hbm((tokens, width), jnp.float32),
-        compiler_params=pltpu.CompilerParams(vmem_limit_bytes=2 * SMALL_VMEM),
-        cost_estimate=pl.CostEstimate(
-            flops=8 * tokens * depth * width, bytes_accessed=8 * tokens * depth + 8 * depth * width + 4 * tokens * width, transcendentals=0
-        ),
-        name="project_early",
-    )(*[from_hbm(array) for array in (*pieces, *weights)])
-
-
-def near_kernel(own, right_top, right_bottom, left_top, left_bottom, w_own, w_right, w_left, total, out):
-    depth = own.shape[1]
-    half = own.shape[0] // 2
-    for part, right, left in ((0, right_top, left_top), (1, right_bottom, left_bottom)):
+def product(rows, weight, first):
+    return jnp.dot(rows, weight[first : first + rows.shape[1]], preferred_element_type=jnp.float32)
+
+
+def near_sum(own, right, left, w_own, w_others, first):
+    return product(own[...], w_own, first) + product(right[...], w_others.at[0], first) + product(left[...], w_others.at[2], first)
+
+
+def early_kernel(first, own_top, own_bottom, right_top, right_bottom, left_top, left_bottom, far_top, far_bottom, w_own, w_others, out):
+    half = own_top.shape[0]
+    parts = ((own_top, right_top, left_top, far_top), (own_bottom, right_bottom, left_bottom, far_bottom))
+    for part, (own, right, left, far) in enumerate(parts):
+        total = near_sum(own, right, left, w_own, w_others, first) + product(far[...], w_others.at[1], first)
+        out[part * half : (part + 1) * half] = total
+
+
+def near_kernel(own_top, own_bottom, right_top, right_bottom, left_top, left_bottom, w_own, w_others, total, out):
+    half = own_top.shape[0]
+    for part, (own, right, left) in enumerate(((own_top, right_top, left_top), (own_bottom, right_bottom, left_bottom))):
         rows = slice(part * half, (part + 1) * half)
-        summed = total[rows] + jnp.dot(own[rows], w_own[:depth], preferred_element_type=jnp.float32)
-        summed += jnp.dot(right[...], w_right[:depth], preferred_element_type=jnp.float32)
-        summed += jnp.dot(left[...], w_left[:depth], preferred_element_type=jnp.float32)
-        out[rows] = summed
-
-
-def far_kernel(far_top, far_bottom, w_far, total, out):
-    depth = far_top.shape[1]
-
-    @pl.when(pl.program_id(0) == 0)
-    def _():
-        out[...] = (jnp.dot(far_top[...], w_far[:depth], preferred_element_type=jnp.float32) + total[...]).astype(out.dtype)
-
-    @pl.when(pl.program_id(0) == 1)
-    def _():
-        out[...] = (jnp.dot(far_bottom[...], w_far[:depth], preferred_element_type=jnp.float32) + total[...]).astype(out.dtype)
-
-
-def project_late(pieces, weights, total):
-    tokens, depth = pieces[0].shape
-    rows, width = weights[0].shape
-    half = tokens // 2
+        out[rows] = total[rows] + near_sum(own, right, left, w_own, w_others, 0)
+
+
+def far_kernel(far_top, far_bottom, w_others, total, out):
+    for part, far in enumerate((far_top, far_bottom)):
+
+        @pl.when(pl.program_id(0) == part)
+        def _(far=far):
+            out[...] = (product(far[...], w_others.at[1], 0) + total[...]).astype(out.dtype)
+
+
+def summing(kernel, name, operands, depth_terms):
+    tokens, width = 2 * operands[0].shape[0], operands[-1].shape[-1]
+    depth = operands[0].shape[1]
     whole = pl.BlockSpec(memory_space=pltpu.VMEM)
-    w_own, w_right, w_far, w_left = weights
-    near = pl.pallas_call(
-        near_kernel,
-        in_specs=[whole] * 9,
+    return pl.pallas_call(
+        kernel,
+        in_specs=[whole] * len(operands),
         out_specs=whole,
         out_shape=pltpu.VMEM((tokens, width), jnp.float32),
         compiler_params=pltpu.CompilerParams(vmem_limit_bytes=SMALL_VMEM),
         cost_estimate=pl.CostEstimate(
-            flops=6 * tokens * depth * width, bytes_accessed=6 * tokens * depth + 6 * depth * width + 8 * tokens * width, transcendentals=0
-        ),
-        name="near",
-    )(*[from_vmem(array) for array in (*pieces[:5], w_own, w_right, w_left, total)])
+            flops=2 * depth_terms * tokens * depth * width, bytes_accessed=8 * tokens * width, transcendentals=0
+        ),
+        name=name,
+    )(*[from_vmem(array) for array in operands])
+
+
+def project_early(pieces, w_own, w_others):
+    first = TMAX * HD
+    return summing(functools.partial(early_kernel, first), "project_early", (*pieces, w_own, w_others), 4)
+
+
+def project_late(pieces, w_own, w_others, total):
+    near = summing(near_kernel, "near", (*pieces[:6], w_own, w_others, total), 3)
+    tokens, width = near.shape
+    half, depth = pieces[0].shape
+    whole = pl.BlockSpec(memory_space=pltpu.VMEM)
     sum_spec = pl.BlockSpec((half, width), lambda step: (step, 0))
     return pl.pallas_call(
         far_kernel,
@@ -314,11 +348,9 @@
         out_specs=sum_spec,
         out_shape=in_hbm((tokens, width), jnp.bfloat16),
         compiler_params=pltpu.CompilerParams(vmem_limit_bytes=SMALL_VMEM),
-        cost_estimate=pl.CostEstimate(
-            flops=2 * tokens * depth * width, bytes_accessed=2 * tokens * depth + 2 * depth * width + 8 * tokens * width, transcendentals=0
-        ),
+        cost_estimate=pl.CostEstimate(flops=2 * tokens * depth * width, bytes_accessed=8 * tokens * width, transcendentals=0),
         name="far",
-    )(*[from_vmem(array) for array in (*pieces[5:], w_far, near)])
+    )(*[from_vmem(array) for array in (*pieces[6:], w_others, near)])
 
 
 def shifted(block, by):
@@ -326,13 +358,11 @@
     return lax.ppermute(block, "head", [(at, (at + by) % count) for at in range(count)])
 
 
-def ring(block):
-    half = block.shape[0] // 2
-    top, bottom = block[:half], block[half:]
+def ring(top, bottom):
     right_top, left_bottom = shifted(top, 1), shifted(bottom, -1)
     right_bottom, left_top = shifted(bottom, 1), shifted(top, -1)
     far_top, far_bottom = shifted(right_top, 1), shifted(left_bottom, -1)
-    return block, right_top, right_bottom, left_top, left_bottom, far_top, far_bottom
+    return top, bottom, right_top, right_bottom, left_top, left_bottom, far_top, far_bottom
 
 
 def other_core(block):
@@ -355,22 +385,22 @@
     arrived = over_frames(packed.reshape(FRAMES, tokens // FRAMES, TMAX * 3 * HD))
 
     other_keys, other_values = other_core(key_rows), other_core(value_rows)
-    near_out = spatial(head_class, query_rows, key_rows, other_keys, value_rows, other_values, query_gain, key_gain)
-    place = lax.axis_index("head").reshape(1).astype(jnp.int32)
-    blocks = weight_blocks(head_class, place, out_weight, group_count)
-
+    front, back = spatial(head_class, query_rows, key_rows, other_keys, value_rows, other_values, query_gain, key_gain)
     core = lax.rem(lax.axis_index("seq"), CORES)
-    half = blocks.shape[1] // CORES
-    mine = lax.dynamic_slice_in_dim(blocks, core * half, half, axis=1)
-    fetched = jnp.stack([shifted(mine[by], by) for by in range(1, group_count)])
+    place = jnp.stack([lax.axis_index("head"), core]).astype(jnp.int32)
+    w_own, *halves = weight_blocks(head_class, place, out_weight, group_count)
+
+    fetched = [shifted(half, by + 1) for by, half in enumerate(halves)]
+    fetched = jnp.stack(hold(fetched, (back,)))
     rest = other_core(fetched)
-    others = jnp.where(core == 0, jnp.concatenate([fetched, rest], axis=1), jnp.concatenate([rest, fetched], axis=1))
-    weights = [blocks[0]] + [others[by] for by in range(group_count - 1)]
-
-    pieces = ring(near_out)
-    returned = over_frames(temporal(head_class, arrived, (*pieces[1:5], others))).reshape(tokens, TMAX * HD)
-    early = project_early(pieces, weights)
-    return project_late(ring(returned), weights, early)
+    w_others = jnp.where(core == 0, jnp.concatenate([fetched, rest], axis=1), jnp.concatenate([rest, fetched], axis=1))
+
+    middle = tokens // 2
+    pieces = ring(back[:middle], back[middle:])
+    returned = over_frames(temporal(head_class, arrived, (*pieces[2:], w_others))).reshape(tokens, TMAX * HD)
+    early = project_early(pieces, w_own, w_others)
+    pieces = ring(returned[:middle] + front[:middle], returned[middle:] + front[middle:])
+    return project_late(pieces, w_own, w_others, early)
 
 
 def solution(mesh):

time: 199 us -> 167 us (0.84); the launches traced: 201 us -> 166 us
  waiting for transfers between devices: 86.3 us -> 44 us
  blocking collectives: 0 us -> 35.3 us
  Pallas kernels: 51.6 us -> 38.4 us
  local copies, waits for them, and re-layouts: 11.4 us -> 1.68 us
  starting transfers between devices: 45.2 us -> 37.4 us
  other arithmetic: 6.6 us -> 8.76 us
    all_to_all x0 -> x1, blocking collectives: none -> 35.3 us  [over_frames(): return lax.all_to_all(blocks, 'seq', 0, 0, axis_index_groups=groups)]
    ppermute x15, waiting for transfers between devices: 61.1 us -> 36.5 us  [shifted(): lax.ppermute(block, 'head', [(at, (at + by) % count) for at in range(coun...]
    all_to_all x2 -> x1, waiting for transfers between devices: 25.2 us -> 7.48 us  [over_frames(): return lax.all_to_all(blocks, 'seq', 0, 0, axis_index_groups=groups)]
    all_to_all x2 -> x1, starting transfers between devices: 21.5 us -> 11.7 us  [over_frames(): return lax.all_to_all(blocks, 'seq', 0, 0, axis_index_groups=groups)]
    pallas_call x2 -> x3, Pallas kernels: 13 us -> 5.75 us  [the longest x2 5.75 us: summing(): pl.pallas_call(kernel, in_specs=[whole] * len(operands), out_specs=whole,...]
    pallas_call x1, Pallas kernels: 20.8 us -> 14.3 us  [spatial(): pl.pallas_call(functools.partial(spatial_kernel, head_count), grid_spec=p...]
    squeeze x3 -> x0, local copies, waits for them, and re-layouts: 5.86 us -> none  [the longest x2 4.32 us: body(): weights = [blocks[0]] + [others[by] for by in range(group_count - 1)]]
    unnamed x24 -> x26, local copies, waits for them, and re-layouts: 2.8 us -> 0.75 us
  transfers between devices with their start and end apart: 20 -> 19, of which waited for: 8 -> 8; matrix products, arithmetic and copies ran while one was open for 8% -> 6% of each run, Pallas kernels for 20% -> 16%
where the time goes in v4:
time: 167 us; the launch traced here: 166 us
  waiting for transfers between devices  44 us (26%)
  Pallas kernels  38.4 us (23%)
  starting transfers between devices  37.4 us (22%)
  blocking collectives  35.3 us (21%)
  other arithmetic  8.76 us (5%)
  local copies, waits for them, and re-layouts  1.68 us (1%)
    ppermute x15, waiting for transfers between devices, shifted(): lax.ppermute(block, 'head', [(at, (at + by) % count) for at in range(coun...  36.5 us
    all_to_all x1, blocking collectives, over_frames(): return lax.all_to_all(blocks, 'seq', 0, 0, axis_index_groups=groups)  35.3 us
    ppermute x15, starting transfers between devices, shifted(): lax.ppermute(block, 'head', [(at, (at + by) % count) for at in range(coun...  25.1 us
    pallas_call x1, Pallas kernels, spatial(): pl.pallas_call(functools.partial(spatial_kernel, head_count), grid_spec=p...  14.3 us
    all_to_all x1, starting transfers between devices, over_frames(): return lax.all_to_all(blocks, 'seq', 0, 0, axis_index_groups=groups)  11.7 us
    all_to_all x1, waiting for transfers between devices, over_frames(): return lax.all_to_all(blocks, 'seq', 0, 0, axis_index_groups=groups)  7.48 us
    pallas_call x1, Pallas kernels, weight_blocks(): pl.pallas_call(weight_kernel, grid_spec=pltpu.PrefetchScalarGridSpec(num_...  6.46 us
    pallas_call x2, Pallas kernels, summing(): pl.pallas_call(kernel, in_specs=[whole] * len(operands), out_specs=whole,...  5.75 us
  transfers between devices with their start and end apart: 19, of which 8 were waited for; matrix products, arithmetic and copies ran while one was open for 6% of the time, Pallas kernels for 16%

profile of v4, /device:TPU:8, one launch (start us, length us, event | category | flops | bytes accessed | tf_op | source)
XLA Modules:
  0.0 165.8 jit_solution(12578335904292895629)
XLA Ops:
  0.0 5.2 %pack.1 = bf16[1024,1536]{1,0:T(8,128)(2,1)} custom-call(s32[6]{0:T(128)} %classes.7, bf16[1024,768]{1,0:T(8,128)(2,1)} %query.3, bf16[1024,768]{1,0:T(8,128)(2,1)} %key.3, bf16[1024,768]{1,0:T(8,128)(2,1)} %value.3, f32[1,128]{1,0:T(1,128)} %bitcast.13, f32[1,128]{1,0:T(1,128)} %bitcast.15), custom_call_target="tpu_custom_call" | custom-call | flops 4194304 | bytes 6291456 | tf_op jit(solution)/shard_map/pack/pallas_call | solution.py:104
  5.2 11.7 %all-to-all-start = ((bf16[32,32,1536]{2,1,0:T(8,128)(2,1)}), bf16[32,32,1536]{2,1,0:T(8,128)(2,1)S(1)}, u32[]{:S(2)}, u32[]{:S(2)}) async-start(bf16[32,32,1536]{2,1,0:T(8,128)(2,1)} %bitcast.12), calls=%async_computation | async-start | bytes 6291456 | tf_op jit(solution)/shard_map/all_to_all | solution.py:376
  18.1 6.5 %weight_blocks.1 = (bf16[768,768]{1,0:T(8,128)(2,1)}, bf16[384,768]{1,0:T(8,128)(2,1)}, bf16[384,768]{1,0:T(8,128)(2,1)}, bf16[384,768]{1,0:T(8,128)(2,1)}) custom-call(s32[6]{0:T(128)} %classes.7, s32[2]{0:T(128)} %pad_add_fusion.place, bf16[768,3072]{1,0:T(8,128)(2,1)} %weight.1), custom_call_target="tpu_custom_call" | custom-call | bytes 9437184 | tf_op jit(solution)/shard_map/weight_blocks/pallas_call | solution.py:270
  26.1 2.7 %collective-permute-start.9 = (bf16[384,768]{1,0:T(8,128)(2,1)}, bf16[384,768]{1,0:T(8,128)(2,1)}, u32[]{:S(2)}, u32[]{:S(2)}) collective-permute-start(bf16[384,768]{1,0:T(8,128)(2,1)} %get-tuple-element.16), channel_id=1, source_target_pairs={{0,2},{1,3},{2,0},{3,1},{4,6},{5,7},{6,4},{7,5},{8,10},{9,11},{10,... | collective-permute-start | bytes 1769480 | tf_op jit(solution)/shard_map/ppermute | solution.py:358
  30.3 14.3 %spatial.1 = (bf16[1024,512]{1,0:T(8,128)(2,1)}, bf16[1024,256]{1,0:T(8,128)(2,1)}) custom-call(s32[6]{0:T(128)} %classes.7, bf16[1024,768]{1,0:T(8,128)(2,1)} %query.3, bf16[1024,768]{1,0:T(8,128)(2,1)} %key.3, bf16[1024,768]{1,0:T(8,128)(2,1)} %collective-permute-done.other_key, bf16[1024,768]{1,0:T(8,128)(2,1)} %value.3, ...), custom_call_target="tpu_custom_call" | custom-call | flops 12884901888 | bytes 9437184 | tf_op jit(solution)/shard_map/spatial/pallas_call | solution.py:171
  44.5 10.3 %collective-permute-done.9.refs_1_ = bf16[384,768]{1,0:T(8,128)(2,1)} collective-permute-done((bf16[384,768]{1,0:T(8,128)(2,1)}, bf16[384,768]{1,0:T(8,128)(2,1)}, u32[]{:S(2)}, u32[]{:S(2)}) %collective-permute-start.9) | collective-permute-done | bytes 589856 | tf_op jit(solution)/shard_map/ppermute | solution.py:358
  54.9 2.9 %pad_maximum_fusion = bf16[3,384,768]{2,1,0:T(8,128)(2,1)} fusion(bf16[1,384,768]{2,1,0:T(8,128)(2,1)} %bitcast.7, bf16[1,384,768]{2,1,0:T(8,128)(2,1)} %bitcast.6, bf16[1,384,768]{2,1,0:T(8,128)(2,1)} %bitcast.5), kind=kLoop, calls=%fused_computation.1 | loop fusion | flops 1769472 | bytes 3538944 | tf_op jit(solution)/shard_map/stack | solution.py:394
  62.0 3.1 %collective-permute-start.4 = (bf16[512,256]{1,0:T(8,128)(2,1)}, bf16[512,256]{1,0:T(8,128)(2,1)S(1)}, u32[]{:S(2)}, u32[]{:S(2)}) collective-permute-start(bf16[512,256]{1,0:T(8,128)(2,1)} %get-tuple-element.28.own_top), channel_id=1, source_target_pairs={{0,3},{1,0},{2,1},{3,2},{4,7},{5,4},{6,5},{7,6},{8,11},{9,8},{10,9... | collective-permute-start | bytes 786440 | tf_op jit(solution)/shard_map/ppermute | solution.py:358
  65.1 4.0 %collective-permute-done.2.rest_0_.right_top = bf16[512,256]{1,0:T(8,128)(2,1)S(1)} collective-permute-done((bf16[512,256]{1,0:T(8,128)(2,1)}, bf16[512,256]{1,0:T(8,128)(2,1)S(1)}, u32[]{:S(2)}, u32[]{:S(2)}) %collective-permute-start.2) | collective-permute-done | bytes 262176 | tf_op jit(solution)/shard_map/ppermute | solution.py:358
  69.4 3.1 %collective-permute-start.7 = (bf16[512,256]{1,0:T(8,128)(2,1)}, bf16[512,256]{1,0:T(8,128)(2,1)}, u32[]{:S(2)}, u32[]{:S(2)}) collective-permute-start(bf16[512,256]{1,0:T(8,128)(2,1)} %collective-permute-done.5.rest_3_.left_bottom), channel_id=1, source_target_pairs={{0,3},{1,0},{2,1},{3,2},{4,7},{5,4},{6,5},{7,6},{8,11},{9,8},{10,9... | collective-permute-start | bytes 786440 | tf_op jit(solution)/shard_map/ppermute | solution.py:358
  72.5 5.0 %maximum_select_fusion.rest_6_.w_others = bf16[3,768,768]{2,1,0:T(8,128)(2,1)} fusion(bf16[3,384,768]{2,1,0:T(8,128)(2,1)} %collective-permute-done.11, bf16[1,384,768]{2,1,0:T(8,128)(2,1)} %bitcast.7, bf16[1,384,768]{2,1,0:T(8,128)(2,1)} %bitcast.6, bf16[1,384,768]{2,1,0:T(8,128)(2,1)} %bitcast.5, pred[]{:T(512)S(6)} %eq.3), kind=kLoop, calls=%fused_computation | loop fusion | flops 30081024 | bytes 7077889 | tf_op jit(solution)/shard_map/jit(_where)/select_n | solution.py:396
  77.6 2.4 %collective-permute-done.6.rest_4_.far_top = bf16[512,256]{1,0:T(8,128)(2,1)S(1)} collective-permute-done((bf16[512,256]{1,0:T(8,128)(2,1)S(1)}, bf16[512,256]{1,0:T(8,128)(2,1)S(1)}, u32[]{:S(2)}, u32[]{:S(2)}) %collective-permute-start.6) | collective-permute-done | bytes 262176 | tf_op jit(solution)/shard_map/ppermute | solution.py:358
  80.7 7.5 %all-to-all-done.packed = bf16[32,32,1536]{2,1,0:T(8,128)(2,1)S(1)} async-done(((bf16[32,32,1536]{2,1,0:T(8,128)(2,1)}), bf16[32,32,1536]{2,1,0:T(8,128)(2,1)S(1)}, u32[]{:S(2)}, u32[]{:S(2)}) %all-to-all-start) | async-done | bytes 3145760 | tf_op jit(solution)/shard_map/all_to_all | solution.py:376
  88.2 4.7 %temporal.1 = bf16[32,32,512]{2,1,0:T(8,128)(2,1)} custom-call(s32[6]{0:T(128)S(1)} %copy-done.10, bf16[32,32,1536]{2,1,0:T(8,128)(2,1)S(1)} %all-to-all-done.packed, bf16[512,256]{1,0:T(8,128)(2,1)} %copy-done.2, bf16[512,256]{1,0:T(8,128)(2,1)} %copy-done.4, bf16[512,256]{1,0:T(8,128)(2,1)} %copy-done.6, ...), custom_call_target="tpu_custom_call" | custom-call | flops 1073741824 | bytes 4194304 | tf_op jit(solution)/shard_map/temporal/pallas_call | solution.py:226
  92.9 35.3 %all_to_all.10 = bf16[32,32,512]{2,1,0:T(8,128)(2,1)S(1)} all-to-all(bf16[32,32,512]{2,1,0:T(8,128)(2,1)} %temporal.1), channel_id=1, replica_groups={{0,8,16,24,32,40,48,56,64,72,80,88,96,104,112,120,128,136,144,152,160,1..., dimensions={0} | all-to-all | bytes 2097152 | tf_op jit(solution)/shard_map/all_to_all | solution.py:376
  128.6 3.2 %collective-permute-start.14 = (bf16[512,512]{1,0:T(8,128)(2,1)S(1)}, bf16[512,512]{1,0:T(8,128)(2,1)S(1)}, u32[]{:S(2)}, u32[]{:S(2)}) collective-permute-start(bf16[512,512]{1,0:T(8,128)(2,1)S(1)} %get-tuple-element.23.own_bottom), channel_id=1, source_target_pairs={{0,3},{1,0},{2,1},{3,2},{4,7},{5,4},{6,5},{7,6},{8,11},{9,8},{10,9... | collective-permute-start | bytes 1572872 | tf_op jit(solution)/shard_map/ppermute | solution.py:358
  131.9 3.2 %collective-permute-start.17 = (bf16[512,512]{1,0:T(8,128)(2,1)S(1)}, bf16[512,512]{1,0:T(8,128)(2,1)S(1)}, u32[]{:S(2)}, u32[]{:S(2)}) collective-permute-start(bf16[512,512]{1,0:T(8,128)(2,1)S(1)} %get-tuple-element.24.own_top), channel_id=1, source_target_pairs={{0,3},{1,0},{2,1},{3,2},{4,7},{5,4},{6,5},{7,6},{8,11},{9,8},{10,9... | collective-permute-start | bytes 1572872 | tf_op jit(solution)/shard_map/ppermute | solution.py:358
  135.1 9.6 %collective-permute-done.12.right_top = bf16[512,512]{1,0:T(8,128)(2,1)S(1)} collective-permute-done((bf16[512,512]{1,0:T(8,128)(2,1)S(1)}, bf16[512,512]{1,0:T(8,128)(2,1)S(1)}, u32[]{:S(2)}, u32[]{:S(2)}) %collective-permute-start.12) | collective-permute-done | bytes 524320 | tf_op jit(solution)/shard_map/ppermute | solution.py:358
  144.7 3.2 %collective-permute-start.15 = (bf16[512,512]{1,0:T(8,128)(2,1)S(1)}, bf16[512,512]{1,0:T(8,128)(2,1)S(1)}, u32[]{:S(2)}, u32[]{:S(2)}) collective-permute-start(bf16[512,512]{1,0:T(8,128)(2,1)S(1)} %collective-permute-done.14.left_bottom), channel_id=1, source_target_pairs={{0,3},{1,0},{2,1},{3,2},{4,7},{5,4},{6,5},{7,6},{8,11},{9,8},{10,9... | collective-permute-start | bytes 1572872 | tf_op jit(solution)/shard_map/ppermute | solution.py:358
  148.0 3.0 %project_early.1.total = f32[1024,768]{1,0:T(8,128)S(1)} custom-call(bf16[512,256]{1,0:T(8,128)(2,1)} %get-tuple-element.28.own_top, bf16[512,256]{1,0:T(8,128)(2,1)} %get-tuple-element.27.own_bottom, bf16[512,256]{1,0:T(8,128)(2,1)S(1)} %copy-done.3, bf16[512,256]{1,0:T(8,128)(2,1)S(1)} %copy-done.5, bf16[512,256]{1,0:T(8,128)(2,1)S(1)} %copy-done.7, ...), custom_call_target="tpu_custom_call" | custom-call | flops 1610612736 | bytes 6291456 | tf_op jit(solution)/shard_map/project_early/pallas_call | solution.py:320
  151.0 4.9 %collective-permute-done.16.right_bottom = bf16[512,512]{1,0:T(8,128)(2,1)S(1)} collective-permute-done((bf16[512,512]{1,0:T(8,128)(2,1)S(1)}, bf16[512,512]{1,0:T(8,128)(2,1)S(1)}, u32[]{:S(2)}, u32[]{:S(2)}) %collective-permute-start.16) | collective-permute-done | bytes 524320 | tf_op jit(solution)/shard_map/ppermute | solution.py:358
  155.9 2.7 %near.1.total = f32[1024,768]{1,0:T(8,128)S(1)} custom-call(bf16[512,512]{1,0:T(8,128)(2,1)S(1)} %get-tuple-element.24.own_top, bf16[512,512]{1,0:T(8,128)(2,1)S(1)} %get-tuple-element.23.own_bottom, bf16[512,512]{1,0:T(8,128)(2,1)S(1)} %collective-permute-done.12.right_top, bf16[512,512]{1,0:T(8,128)(2,1)S(1)} %collective-permute-done.16.right_bottom, ...), custom_call_target="tpu_custom_call" | custom-call | flops 2415919104 | bytes 6291456 | tf_op jit(solution)/shard_map/near/pallas_call | solution.py:320
  158.7 5.1 %collective-permute-done.13.far_top = bf16[512,512]{1,0:T(8,128)(2,1)S(1)} collective-permute-done((bf16[512,512]{1,0:T(8,128)(2,1)S(1)}, bf16[512,512]{1,0:T(8,128)(2,1)S(1)}, u32[]{:S(2)}, u32[]{:S(2)}) %collective-permute-start.13) | collective-permute-done | bytes 524320 | tf_op jit(solution)/shard_map/ppermute | solution.py:358
  163.8 2.1 %far.1 = bf16[1024,768]{1,0:T(8,128)(2,1)} custom-call(bf16[512,512]{1,0:T(8,128)(2,1)S(1)} %collective-permute-done.13.far_top, bf16[512,512]{1,0:T(8,128)(2,1)S(1)} %collective-permute-done.15.far_bottom, bf16[3,768,768]{2,1,0:T(8,128)(2,1)S(1)} %copy-done, f32[1024,768]{1,0:T(8,128)S(1)} %near.1.total), custom_call_target="tpu_custom_call" | custom-call | flops 805306368 | bytes 6291456 | tf_op jit(solution)/shard_map/far/pallas_call | solution.py:344
  (55 shorter events, 9.8 us)
Async XLA Ops:
  5.2 83.0 %all-to-all-start = ((bf16[32,32,1536]{2,1,0:T(8,128)(2,1)}), bf16[32,32,1536]{2,1,0:T(8,128)(2,1)S(1)}, u32[]{:S(2)}, u32[]{:S(2)}) async-start(bf16[32,32,1536]{2,1,0:T(8,128)(2,1)} %bitcast.12), calls=%async_computation | async-start | bytes 6291456 | tf_op jit(solution)/shard_map/all_to_all | solution.py:376
  16.9 13.4 %collective-permute-start = (bf16[1024,768]{1,0:T(8,128)(2,1)}, bf16[1024,768]{1,0:T(8,128)(2,1)}, u32[]{:S(2)}, u32[]{:S(2)}) collective-permute-start(bf16[1024,768]{1,0:T(8,128)(2,1)} %key.3), channel_id=1, source_target_pairs={{0,4},{4,0},{8,12},{12,8},{16,20},{20,16},{24,28},{28,24},{32,36},... | collective-permute-start | bytes 4718600 | tf_op jit(solution)/shard_map/ppermute | solution.py:370
  17.0 13.3 %collective-permute-start.1 = (bf16[1024,768]{1,0:T(8,128)(2,1)}, bf16[1024,768]{1,0:T(8,128)(2,1)}, u32[]{:S(2)}, u32[]{:S(2)}) collective-permute-start(bf16[1024,768]{1,0:T(8,128)(2,1)} %value.3), channel_id=1, source_target_pairs={{0,4},{4,0},{8,12},{12,8},{16,20},{20,16},{24,28},{28,24},{32,36},... | collective-permute-start | bytes 4718600 | tf_op jit(solution)/shard_map/ppermute | solution.py:370
  24.6 19.9 %collective-permute-start.8 = (bf16[384,768]{1,0:T(8,128)(2,1)}, bf16[384,768]{1,0:T(8,128)(2,1)}, u32[]{:S(2)}, u32[]{:S(2)}) collective-permute-start(bf16[384,768]{1,0:T(8,128)(2,1)} %get-tuple-element.15), channel_id=1, source_target_pairs={{0,1},{1,2},{2,3},{3,0},{4,5},{5,6},{6,7},{7,4},{8,9},{9,10},{10,1... | collective-permute-start | bytes 1769480 | tf_op jit(solution)/shard_map/ppermute | solution.py:358
  26.1 28.7 %collective-permute-start.9 = (bf16[384,768]{1,0:T(8,128)(2,1)}, bf16[384,768]{1,0:T(8,128)(2,1)}, u32[]{:S(2)}, u32[]{:S(2)}) collective-permute-start(bf16[384,768]{1,0:T(8,128)(2,1)} %get-tuple-element.16), channel_id=1, source_target_pairs={{0,2},{1,3},{2,0},{3,1},{4,6},{5,7},{6,4},{7,5},{8,10},{9,11},{10,... | collective-permute-start | bytes 1769480 | tf_op jit(solution)/shard_map/ppermute | solution.py:358
  28.8 26.0 %collective-permute-start.10 = (bf16[384,768]{1,0:T(8,128)(2,1)}, bf16[384,768]{1,0:T(8,128)(2,1)}, u32[]{:S(2)}, u32[]{:S(2)}) collective-permute-start(bf16[384,768]{1,0:T(8,128)(2,1)} %get-tuple-element.17), channel_id=1, source_target_pairs={{0,3},{1,0},{2,1},{3,2},{4,7},{5,4},{6,5},{7,6},{8,11},{9,8},{10,9... | collective-permute-start | bytes 1769480 | tf_op jit(solution)/shard_map/ppermute | solution.py:358
  57.8 14.7 %collective-permute-start.11 = (bf16[3,384,768]{2,1,0:T(8,128)(2,1)}, bf16[3,384,768]{2,1,0:T(8,128)(2,1)}, u32[]{:S(2)}, u32[]{:S(2)}) collective-permute-start(bf16[3,384,768]{2,1,0:T(8,128)(2,1)} %pad_maximum_fusion), channel_id=1, source_target_pairs={{0,4},{4,0},{8,12},{12,8},{16,20},{20,16},{24,28},{28,24},{32,36},... | collective-permute-start | bytes 5308424 | tf_op jit(solution)/shard_map/ppermute | solution.py:370
  58.6 10.5 %collective-permute-start.2 = (bf16[512,256]{1,0:T(8,128)(2,1)}, bf16[512,256]{1,0:T(8,128)(2,1)S(1)}, u32[]{:S(2)}, u32[]{:S(2)}) collective-permute-start(bf16[512,256]{1,0:T(8,128)(2,1)} %get-tuple-element.28.own_top), channel_id=1, source_target_pairs={{0,1},{1,2},{2,3},{3,0},{4,5},{5,6},{6,7},{7,4},{8,9},{9,10},{10,1... | collective-permute-start | bytes 786440 | tf_op jit(solution)/shard_map/ppermute | solution.py:358
  59.9 9.5 %collective-permute-start.5 = (bf16[512,256]{1,0:T(8,128)(2,1)}, bf16[512,256]{1,0:T(8,128)(2,1)}, u32[]{:S(2)}, u32[]{:S(2)}) collective-permute-start(bf16[512,256]{1,0:T(8,128)(2,1)} %get-tuple-element.27.own_bottom), channel_id=1, source_target_pairs={{0,3},{1,0},{2,1},{3,2},{4,7},{5,4},{6,5},{7,6},{8,11},{9,8},{10,9... | collective-permute-start | bytes 786440 | tf_op jit(solution)/shard_map/ppermute | solution.py:358
  61.8 15.7 %collective-permute-start.3 = (bf16[512,256]{1,0:T(8,128)(2,1)}, bf16[512,256]{1,0:T(8,128)(2,1)S(1)}, u32[]{:S(2)}, u32[]{:S(2)}) collective-permute-start(bf16[512,256]{1,0:T(8,128)(2,1)} %get-tuple-element.27.own_bottom), channel_id=1, source_target_pairs={{0,1},{1,2},{2,3},{3,0},{4,5},{5,6},{6,7},{7,4},{8,9},{9,10},{10,1... | collective-permute-start | bytes 786440 | tf_op jit(solution)/shard_map/ppermute | solution.py:358
  62.0 15.6 %collective-permute-start.4 = (bf16[512,256]{1,0:T(8,128)(2,1)}, bf16[512,256]{1,0:T(8,128)(2,1)S(1)}, u32[]{:S(2)}, u32[]{:S(2)}) collective-permute-start(bf16[512,256]{1,0:T(8,128)(2,1)} %get-tuple-element.28.own_top), channel_id=1, source_target_pairs={{0,3},{1,0},{2,1},{3,2},{4,7},{5,4},{6,5},{7,6},{8,11},{9,8},{10,9... | collective-permute-start | bytes 786440 | tf_op jit(solution)/shard_map/ppermute | solution.py:358
  69.1 10.8 %collective-permute-start.6 = (bf16[512,256]{1,0:T(8,128)(2,1)S(1)}, bf16[512,256]{1,0:T(8,128)(2,1)S(1)}, u32[]{:S(2)}, u32[]{:S(2)}) collective-permute-start(bf16[512,256]{1,0:T(8,128)(2,1)S(1)} %collective-permute-done.2.rest_0_.right_top), channel_id=1, source_target_pairs={{0,1},{1,2},{2,3},{3,0},{4,5},{5,6},{6,7},{7,4},{8,9},{9,10},{10,1... | collective-permute-start | bytes 786440 | tf_op jit(solution)/shard_map/ppermute | solution.py:358
  69.4 11.3 %collective-permute-start.7 = (bf16[512,256]{1,0:T(8,128)(2,1)}, bf16[512,256]{1,0:T(8,128)(2,1)}, u32[]{:S(2)}, u32[]{:S(2)}) collective-permute-start(bf16[512,256]{1,0:T(8,128)(2,1)} %collective-permute-done.5.rest_3_.left_bottom), channel_id=1, source_target_pairs={{0,3},{1,0},{2,1},{3,2},{4,7},{5,4},{6,5},{7,6},{8,11},{9,8},{10,9... | collective-permute-start | bytes 786440 | tf_op jit(solution)/shard_map/ppermute | solution.py:358
  92.9 55.1 %copy-start.1 = (bf16[768,768]{1,0:T(8,128)(2,1)S(1)}, bf16[768,768]{1,0:T(8,128)(2,1)}, u32[]{:S(2)}) copy-start(bf16[768,768]{1,0:T(8,128)(2,1)} %get-tuple-element.22.w_own) | copy-start | bytes 3538948
  92.9 55.1 %copy-start.3 = (bf16[512,256]{1,0:T(8,128)(2,1)S(1)}, bf16[512,256]{1,0:T(8,128)(2,1)}, u32[]{:S(2)}) copy-start(bf16[512,256]{1,0:T(8,128)(2,1)} %copy-done.2) | copy-start | bytes 786436
  92.9 55.1 %copy-start.5 = (bf16[512,256]{1,0:T(8,128)(2,1)S(1)}, bf16[512,256]{1,0:T(8,128)(2,1)}, u32[]{:S(2)}) copy-start(bf16[512,256]{1,0:T(8,128)(2,1)} %copy-done.4) | copy-start | bytes 786436
  92.9 55.1 %copy-start.7 = (bf16[512,256]{1,0:T(8,128)(2,1)S(1)}, bf16[512,256]{1,0:T(8,128)(2,1)}, u32[]{:S(2)}) copy-start(bf16[512,256]{1,0:T(8,128)(2,1)} %copy-done.6) | copy-start | bytes 786436
  92.9 55.1 %copy-start.9 = (bf16[512,256]{1,0:T(8,128)(2,1)S(1)}, bf16[512,256]{1,0:T(8,128)(2,1)}, u32[]{:S(2)}) copy-start(bf16[512,256]{1,0:T(8,128)(2,1)} %copy-done.8) | copy-start | bytes 786436
  128.5 16.1 %collective-permute-start.12 = (bf16[512,512]{1,0:T(8,128)(2,1)S(1)}, bf16[512,512]{1,0:T(8,128)(2,1)S(1)}, u32[]{:S(2)}, u32[]{:S(2)}) collective-permute-start(bf16[512,512]{1,0:T(8,128)(2,1)S(1)} %get-tuple-element.24.own_top), channel_id=1, source_target_pairs={{0,1},{1,2},{2,3},{3,0},{4,5},{5,6},{6,7},{7,4},{8,9},{9,10},{10,1... | collective-permute-start | bytes 1572872 | tf_op jit(solution)/shard_map/ppermute | solution.py:358
  128.6 16.1 %collective-permute-start.14 = (bf16[512,512]{1,0:T(8,128)(2,1)S(1)}, bf16[512,512]{1,0:T(8,128)(2,1)S(1)}, u32[]{:S(2)}, u32[]{:S(2)}) collective-permute-start(bf16[512,512]{1,0:T(8,128)(2,1)S(1)} %get-tuple-element.23.own_bottom), channel_id=1, source_target_pairs={{0,3},{1,0},{2,1},{3,2},{4,7},{5,4},{6,5},{7,6},{8,11},{9,8},{10,9... | collective-permute-start | bytes 1572872 | tf_op jit(solution)/shard_map/ppermute | solution.py:358
  131.9 24.1 %collective-permute-start.16 = (bf16[512,512]{1,0:T(8,128)(2,1)S(1)}, bf16[512,512]{1,0:T(8,128)(2,1)S(1)}, u32[]{:S(2)}, u32[]{:S(2)}) collective-permute-start(bf16[512,512]{1,0:T(8,128)(2,1)S(1)} %get-tuple-element.23.own_bottom), channel_id=1, source_target_pairs={{0,1},{1,2},{2,3},{3,0},{4,5},{5,6},{6,7},{7,4},{8,9},{9,10},{10,1... | collective-permute-start | bytes 1572872 | tf_op jit(solution)/shard_map/ppermute | solution.py:358
  131.9 24.1 %collective-permute-start.17 = (bf16[512,512]{1,0:T(8,128)(2,1)S(1)}, bf16[512,512]{1,0:T(8,128)(2,1)S(1)}, u32[]{:S(2)}, u32[]{:S(2)}) collective-permute-start(bf16[512,512]{1,0:T(8,128)(2,1)S(1)} %get-tuple-element.24.own_top), channel_id=1, source_target_pairs={{0,3},{1,0},{2,1},{3,2},{4,7},{5,4},{6,5},{7,6},{8,11},{9,8},{10,9... | collective-permute-start | bytes 1572872 | tf_op jit(solution)/shard_map/ppermute | solution.py:358
  144.7 19.1 %collective-permute-start.13 = (bf16[512,512]{1,0:T(8,128)(2,1)S(1)}, bf16[512,512]{1,0:T(8,128)(2,1)S(1)}, u32[]{:S(2)}, u32[]{:S(2)}) collective-permute-start(bf16[512,512]{1,0:T(8,128)(2,1)S(1)} %collective-permute-done.12.right_top), channel_id=1, source_target_pairs={{0,1},{1,2},{2,3},{3,0},{4,5},{5,6},{6,7},{7,4},{8,9},{9,10},{10,1... | collective-permute-start | bytes 1572872 | tf_op jit(solution)/shard_map/ppermute | solution.py:358
  144.7 19.1 %collective-permute-start.15 = (bf16[512,512]{1,0:T(8,128)(2,1)S(1)}, bf16[512,512]{1,0:T(8,128)(2,1)S(1)}, u32[]{:S(2)}, u32[]{:S(2)}) collective-permute-start(bf16[512,512]{1,0:T(8,128)(2,1)S(1)} %collective-permute-done.14.left_bottom), channel_id=1, source_target_pairs={{0,3},{1,0},{2,1},{3,2},{4,7},{5,4},{6,5},{7,6},{8,11},{9,8},{10,9... | collective-permute-start | bytes 1572872 | tf_op jit(solution)/shard_map/ppermute | solution.py:358
  (8 other events, 138.4 us)

commit v5 on v4

v5 whole, which is shorter than its diff:
```python
import functools
import math

import jax
import jax.numpy as jnp
from jax import lax
from jax.experimental import pallas as pl
from jax.experimental.pallas import tpu as pltpu
from jax.sharding import Mesh
from jax.sharding import PartitionSpec as P

TMAX = 4
SMALL_VMEM = 16 * 1024 * 1024
CORES = 2
ROWS = 8
HD = 128
EPSILON = 1e-06
LOG2_SCALE = math.log2(math.e) / math.sqrt(HD)


def in_hbm(shape, dtype):
    return pltpu.HBM(shape, dtype)


def from_hbm(array):
    return pltpu.with_memory_space_constraint(array, pltpu.HBM)


def from_vmem(array):
    return pltpu.with_memory_space_constraint(array, pltpu.VMEM)


def temporal_count(classes, head_count):
    total = classes[0]
    for head in range(1, head_count):
        total = total + classes[head]
    return total


def head_of(classes, slot, head_count):
    temporal_seen = jnp.int32(0)
    spatial_seen = temporal_count(classes, head_count)
    found = jnp.int32(0)
    for head in range(head_count):
        kind = classes[head]
        rank = jnp.where(kind == 1, temporal_seen, spatial_seen)
        found = jnp.where(rank == slot, jnp.int32(head), found)
        temporal_seen = temporal_seen + kind
        spatial_seen = spatial_seen + 1 - kind
    return found


def scaled(widened, gain):
    mean = jnp.mean(widened * widened, axis=-1, keepdims=True)
    return widened * lax.rsqrt(mean + EPSILON) * gain


def normed(rows, gain):
    return scaled(rows.astype(jnp.float32), gain).astype(jnp.bfloat16)


def scores_of(queries, keys):
    return lax.dot_general(queries, keys, (((1,), (1,)), ((), ())), preferred_element_type=jnp.float32)


def hold_kernel(*refs):
    pass


def hold(arrays, after):
    anywhere = pl.BlockSpec(memory_space=pl.ANY)
    return pl.pallas_call(
        hold_kernel,
        in_specs=[anywhere] * (len(arrays) + len(after)),
        out_specs=[anywhere] * len(arrays),
        out_shape=[in_hbm(array.shape, array.dtype) for array in arrays],
        input_output_aliases={at: at for at in range(len(arrays))},
        cost_estimate=pl.CostEstimate(flops=0, bytes_accessed=0, transcendentals=0),
        name="hold",
    )(*[from_hbm(array) for array in (*arrays, *after)])


def pack_kernel(head_count, classes, query, key, value, query_gain, key_gain, out, raw, ready, in_sems, out_sems):
    heads = [head_of(classes, slot, head_count) for slot in range(TMAX)]
    gains = (query_gain, key_gain, None)
    frames, positions, _ = out.shape
    quarters = positions // ROWS
    tokens = frames * positions
    chunk = 8
    loads, stores = [], []
    for at in range(3 * TMAX):
        slot, which = divmod(at, 3)
        source = (query, key, value)[which].at[:, pl.ds(pl.multiple_of(heads[slot] * HD, HD), HD)]
        loads.append(pltpu.make_async_copy(source, raw.at[at], in_sems.at[at]))
        loads[-1].start()
    for at in range(3 * TMAX):
        gain = gains[at % 3]
        loads[at].wait()
        for first in range(0, frames, chunk):
            blocks = []
            for quarter in range(quarters):
                begin = quarter * (tokens // quarters) + first * ROWS
                rows = raw[at, begin : begin + chunk * ROWS].astype(jnp.float32)
                if gain is not None:
                    rows = scaled(rows, gain[...])
                blocks.append(rows.reshape(chunk, ROWS, HD))
            ready[at, first : first + chunk] = jnp.concatenate(blocks, axis=1).astype(jnp.bfloat16)
        stores.append(pltpu.make_async_copy(ready.at[at], out.at[:, :, pl.ds(at * HD, HD)], out_sems.at[at]))
        stores[-1].start()
    for store in stores:
        store.wait()


def pack(head_class, query_rows, key_rows, value_rows, query_gain, key_gain, frames):
    tokens, width = query_rows.shape
    positions = tokens // frames
    anywhere = pl.BlockSpec(memory_space=pl.ANY)
    gain_spec = pl.BlockSpec((1, HD), lambda step, classes: (0, 0))
    return pl.pallas_call(
        functools.partial(pack_kernel, width // HD),
        grid_spec=pltpu.PrefetchScalarGridSpec(
            num_scalar_prefetch=1,
            grid=(1,),
            in_specs=[anywhere] * 3 + [gain_spec] * 2,
            out_specs=anywhere,
            scratch_shapes=[
                pltpu.VMEM((3 * TMAX, tokens, HD), jnp.bfloat16),
                pltpu.VMEM((3 * TMAX, frames, positions, HD), jnp.bfloat16),
                pltpu.SemaphoreType.DMA((3 * TMAX,)),
                pltpu.SemaphoreType.DMA((3 * TMAX,)),
            ],
        ),
        out_shape=in_hbm((frames, positions, TMAX * 3 * HD), jnp.bfloat16),
        cost_estimate=pl.CostEstimate(flops=8 * tokens * TMAX * HD, bytes_accessed=12 * tokens * TMAX * HD, transcendentals=0),
        name="pack",
    )(head_class, from_hbm(query_rows), from_hbm(key_rows), from_hbm(value_rows), query_gain, key_gain)


def spatial_kernel(head_count, classes, query, key, other_key, value, other_value, query_gain, key_gain, out, keys, values):
    slot = pl.program_id(0)
    tokens = query.shape[0]
    chunk = tokens // 4

    @pl.when(slot >= temporal_count(classes, head_count))
    def _():
        keys[:tokens] = normed(key[...], key_gain[...])
        keys[tokens:] = normed(other_key[...], key_gain[...])
        values[:tokens, :HD] = value[...]
        values[tokens:, :HD] = other_value[...]
        values[:, HD:] = jnp.ones((2 * tokens, HD), jnp.bfloat16)

        def step(index, carry):
            rows = pl.ds(pl.multiple_of(index * chunk, chunk), chunk)
            queries = normed(query[rows, :], query_gain[...])
            weights = jnp.exp2(scores_of(queries, keys[...]) * LOG2_SCALE).astype(jnp.bfloat16)
            summed = jnp.dot(weights, values[...], preferred_element_type=jnp.float32)
            out[rows, :] = (summed[:, :HD] / summed[:, HD:]).astype(jnp.bfloat16)
            return carry

        lax.fori_loop(0, tokens // chunk, step, 0)

    @pl.when(slot < temporal_count(classes, head_count))
    def _():
        out[...] = jnp.zeros_like(out)


def spatial(head_class, query_rows, key_rows, other_keys, value_rows, other_values, query_gain, key_gain):
    tokens, width = query_rows.shape
    head_count = width // HD

    def rows(slot, classes):
        return 0, head_of(classes, slot, head_count)

    row_spec = pl.BlockSpec((tokens, HD), rows)
    gain_spec = pl.BlockSpec((1, HD), lambda slot, classes: (0, 0))
    return pl.pallas_call(
        functools.partial(spatial_kernel, head_count),
        grid_spec=pltpu.PrefetchScalarGridSpec(
            num_scalar_prefetch=1,
            grid=(head_count,),
            in_specs=[row_spec] * 5 + [gain_spec] * 2,
            out_specs=pl.BlockSpec((tokens, HD), lambda slot, classes: (0, slot)),
            scratch_shapes=[
                pltpu.VMEM((2 * tokens, HD), jnp.bfloat16),
                pltpu.VMEM((2 * tokens, 2 * HD), jnp.bfloat16),
            ],
        ),
        out_shape=in_hbm((tokens, width), jnp.bfloat16),
        cost_estimate=pl.CostEstimate(
            flops=16 * tokens * tokens * width, bytes_accessed=12 * tokens * width, transcendentals=2 * tokens * tokens * head_count
        ),
        name="spatial",
    )(head_class, query_rows, key_rows, from_hbm(other_keys), value_rows, from_hbm(other_values), query_gain, key_gain)


def temporal_kernel(head_count, classes, packed, *rest):
    out = rest[-1]
    slot = pl.program_id(0)
    frames, positions, _ = packed.shape
    places = 2 * ROWS
    count = frames * places

    @pl.when(slot < temporal_count(classes, head_count))
    def _():
        row = lax.broadcasted_iota(jnp.int32, (count, count), 0)
        column = lax.broadcasted_iota(jnp.int32, (count, count), 1)
        same = (row & (places - 1)) == (column & (places - 1))
        base = pl.multiple_of(slot * 3 * HD, HD)
        for part in range(positions // places):
            at = slice(part * places, (part + 1) * places)
            queries, keys, values = (packed[:, at, pl.ds(base + which * HD, HD)].reshape(count, HD) for which in range(3))
            exponents = jnp.where(same, scores_of(queries, keys) * LOG2_SCALE, -1e30)
            weights = jnp.exp2(exponents).astype(jnp.bfloat16)
            both = jnp.concatenate([values, jnp.ones_like(values)], axis=1)
            summed = jnp.dot(weights, both, preferred_element_type=jnp.float32)
            result = (summed[:, :HD] / summed[:, HD:]).reshape(frames, 2, ROWS, HD)
            out[:, 2 * part : 2 * part + 2] = result.astype(jnp.bfloat16)

    @pl.when(slot >= temporal_count(classes, head_count))
    def _():
        out[...] = jnp.zeros_like(out)


def temporal(head_class, packed, after):
    frames, positions, _ = packed.shape
    quarters = positions // ROWS
    return pl.pallas_call(
        functools.partial(temporal_kernel, head_class.shape[0]),
        grid_spec=pltpu.PrefetchScalarGridSpec(
            num_scalar_prefetch=1,
            grid=(TMAX,),
            in_specs=[pl.BlockSpec(memory_space=pltpu.VMEM)] + [pl.BlockSpec(memory_space=pl.ANY)] * len(after),
            out_specs=pl.BlockSpec((frames, quarters, ROWS, HD), lambda slot, classes: (0, 0, 0, slot)),
        ),
        out_shape=in_hbm((frames, quarters, ROWS, TMAX * HD), jnp.bfloat16),
        compiler_params=pltpu.CompilerParams(vmem_limit_bytes=SMALL_VMEM),
        cost_estimate=pl.CostEstimate(
            flops=64 * frames * frames * positions * TMAX * HD,
            bytes_accessed=8 * frames * positions * TMAX * HD,
            transcendentals=16 * frames * frames * positions * TMAX,
        ),
        name="temporal",
    )(head_class, from_vmem(packed), *[from_hbm(array) for array in after])


def weight_kernel(classes, place, weight, left, right):
    width = left.shape[1]
    left[...] = weight[:, :width]
    right[...] = weight[:, width:]


def weight_half(head_class, place, weight):
    rows, columns = weight.shape
    head_count = rows // HD
    share = head_count // CORES
    spec = pl.BlockSpec((HD, columns // 2), lambda step, classes, place: (step, 0))

    def source(step, classes, place):
        return head_of(classes, place[1] * share + step, head_count), 0

    return pl.pallas_call(
        weight_kernel,
        grid_spec=pltpu.PrefetchScalarGridSpec(
            num_scalar_prefetch=2,
            grid=(share,),
            in_specs=[pl.BlockSpec((HD, columns), source)],
            out_specs=[spec, spec],
        ),
        out_shape=[in_hbm((rows // CORES, columns // 2), jnp.bfloat16)] * 2,
        cost_estimate=pl.CostEstimate(flops=0, bytes_accessed=2 * rows * columns, transcendentals=0),
        name="weight_half",
    )(head_class, place, weight)


def combine_kernel(place, returned, *refs):
    out = refs[-1]
    group_count = out.shape[0]
    width = returned.shape[-1]
    rows = out.shape[1]
    for by in range(group_count):
        group = lax.rem(place[0] + group_count - by, group_count)
        temporal_rows = returned[:, pl.ds(group, 1)].astype(jnp.float32).reshape(rows, width)
        out[by, :, :width] = (temporal_rows + refs[by][:, :width].astype(jnp.float32)).astype(jnp.bfloat16)
        out[by, :, width:] = refs[by][:, width:]


def combine(place, returned, pieces):
    rows, width = pieces[0].shape
    whole = pl.BlockSpec(memory_space=pltpu.VMEM)
    return pl.pallas_call(
        combine_kernel,
        grid_spec=pltpu.PrefetchScalarGridSpec(
            num_scalar_prefetch=1, grid=(1,), in_specs=[whole] * (1 + len(pieces)), out_specs=whole
        ),
        out_shape=pltpu.VMEM((len(pieces), rows, width), jnp.bfloat16),
        compiler_params=pltpu.CompilerParams(vmem_limit_bytes=SMALL_VMEM),
        cost_estimate=pl.CostEstimate(flops=0, bytes_accessed=8 * len(pieces) * rows * width, transcendentals=0),
        name="combine",
    )(place, from_vmem(returned), *[from_vmem(piece) for piece in pieces])


def project_kernel(by, place, heads, *refs):
    out = refs[-1]
    group_count = heads.shape[0]
    block = lax.rem(place[0] + by, group_count)
    width = out.shape[1]
    share = refs[0].shape[0]
    columns = pl.ds(pl.multiple_of(lax.rem(block, 2) * width, HD), width)
    for side in range(2):

        @pl.when(block // 2 == side)
        def _(side=side):
            total = jnp.zeros(out.shape, jnp.float32)
            for group in range(group_count):
                for core in range(CORES):
                    weight = refs[(core * group_count + group) * 2 + side]
                    first = (place[1] if core == 0 else 1 - place[1]) * share
                    rows = heads[group, :, pl.ds(pl.multiple_of(first, HD), share)]
                    total += jnp.dot(rows, weight[:, columns], preferred_element_type=jnp.float32)
            out[...] = total.astype(out.dtype)


def project(place, heads, weights, by):
    group_count, rows, depth = heads.shape
    width = weights[0].shape[1] * 2 // group_count
    whole = pl.BlockSpec(memory_space=pltpu.VMEM)
    return pl.pallas_call(
        functools.partial(project_kernel, by),
        grid_spec=pltpu.PrefetchScalarGridSpec(
            num_scalar_prefetch=1, grid=(1,), in_specs=[whole] * (1 + len(weights)), out_specs=whole
        ),
        out_shape=jax.ShapeDtypeStruct((rows, width), jnp.bfloat16),
        compiler_params=pltpu.CompilerParams(vmem_limit_bytes=SMALL_VMEM),
        cost_estimate=pl.CostEstimate(flops=2 * group_count * rows * depth * width, bytes_accessed=2 * rows * width, transcendentals=0),
        name="project",
    )(place, heads, *[from_vmem(weight) for weight in weights])


def join_kernel(place, *refs):
    *pieces, out, sems = refs
    rows = pieces[0].shape[0]
    group_count = len(pieces)
    copies = []
    for by, piece in enumerate(pieces):
        quarter = lax.rem(place[0] + group_count - by, group_count)
        target = out.at[pl.ds(pl.multiple_of(quarter * rows, rows), rows), :]
        copies.append(pltpu.make_async_copy(piece, target, sems.at[by]))
        copies[-1].start()
    for copy in copies:
        copy.wait()


def join(place, pieces):
    rows, width = pieces[0].shape
    return pl.pallas_call(
        join_kernel,
        grid_spec=pltpu.PrefetchScalarGridSpec(
            num_scalar_prefetch=1,
            grid=(1,),
            in_specs=[pl.BlockSpec(memory_space=pltpu.VMEM)] * len(pieces),
            out_specs=pl.BlockSpec(memory_space=pl.ANY),
            scratch_shapes=[pltpu.SemaphoreType.DMA((len(pieces),))],
        ),
        out_shape=in_hbm((len(pieces) * rows, width), jnp.bfloat16),
        compiler_params=pltpu.CompilerParams(vmem_limit_bytes=SMALL_VMEM),
        cost_estimate=pl.CostEstimate(flops=0, bytes_accessed=4 * len(pieces) * rows * width, transcendentals=0),
        name="join",
    )(place, *[from_vmem(piece) for piece in pieces])


def shifted(block, by):
    count = lax.axis_size("head")
    if by == 0:
        return block
    return lax.ppermute(block, "head", [(at, (at + by) % count) for at in range(count)])


def other_core(block):
    return lax.ppermute(block, "core", [(0, 1), (1, 0)])


def body(query_rows, key_rows, value_rows, query_gain, key_gain, head_class, out_weight):
    tokens = query_rows.shape[0]
    frames = lax.axis_size("frame")
    group_count = lax.axis_size("head")
    group = lax.axis_index("head")
    place = jnp.stack([group, lax.axis_index("core")]).astype(jnp.int32)
    query_gain = query_gain.reshape(1, HD)
    key_gain = key_gain.reshape(1, HD)
    packed = pack(head_class, query_rows, key_rows, value_rows, query_gain, key_gain, frames)
    arrived = lax.all_to_all(packed, "frame", 0, 0)

    w_left, w_right = weight_half(head_class, place, out_weight)
    right_of_left, left_of_right = shifted(w_left, 1), shifted(w_right, -1)
    right_of_right, left_of_left = shifted(w_right, 1), shifted(w_left, -1)

    other_keys, other_values = other_core(key_rows), other_core(value_rows)
    near_out = spatial(head_class, query_rows, key_rows, other_keys, value_rows, other_values, query_gain, key_gain)
    right_of_left, left_of_right = hold((right_of_left, left_of_right), (near_out,))
    far_of_left, far_of_right = shifted(right_of_left, 1), shifted(left_of_right, -1)
    mine = (w_left, w_right, right_of_left, right_of_right, far_of_left, far_of_right, left_of_left, left_of_right)
    weights = (*mine, *[other_core(array) for array in mine])

    quarter = tokens // group_count
    pieces = []
    for by in range(group_count):
        first = lax.rem(group + by, group_count) * quarter
        pieces.append(shifted(lax.dynamic_slice_in_dim(near_out, first, quarter), by))

    sent = temporal(head_class, arrived, (*pieces[1:], right_of_right, left_of_left))
    sent = sent.reshape(frames * group_count, ROWS, TMAX * HD)
    returned = lax.all_to_all(sent, ("frame", "head"), 0, 0).reshape(frames, group_count, ROWS, TMAX * HD)
    heads = combine(place, returned, pieces)
    results = {by: shifted(project(place, heads, weights, by), by) for by in (2, 1, 3, 0)}
    return join(place, [results[by] for by in range(group_count)])


def solution(mesh):
    seq, head = mesh.devices.shape
    split = Mesh(mesh.devices.reshape(seq // CORES, CORES, head), ("frame", "core", "head"))
    rows = P(("frame", "core"), "head")
    return jax.shard_map(
        body,
        mesh=split,
        in_specs=(rows, rows, rows, P(), P(), P("head"), P("head", None)),
        out_specs=rows,
        check_vma=False,
    )
```

time: 167 us -> 189 us (1.13)
  blocking collectives: 35.3 us -> 0 us
  waiting for transfers between devices: 44 us -> 73.9 us
  Pallas kernels: 38.4 us -> 65.4 us
  other arithmetic: 8.76 us -> 0.58 us
  starting transfers between devices: 37.4 us -> 44.6 us
    all_to_all x1 -> x0, blocking collectives: 35.3 us -> none  [over_frames(): return lax.all_to_all(blocks, 'seq', 0, 0, axis_index_groups=groups)]
    pallas_call x4 -> x7, Pallas kernels: 14.3 us -> 37.1 us  [the longest x4 28.2 us: project(): pl.pallas_call(functools.partial(project_kernel, by), grid_spec=pltpu.Pre...]
    ppermute x15 -> x12, waiting for transfers between devices: 36.5 us -> 58.1 us  [shifted(): lax.ppermute(block, 'head', [(at, (at + by) % count) for at in range(coun...]
    all_to_all x1 -> x2, starting transfers between devices: 11.7 us -> 23.5 us  [the longest x1 11.8 us: body(): lax.all_to_all(sent, ('frame', 'head'), 0, 0)]
    all_to_all x1 -> x2, waiting for transfers between devices: 7.48 us -> 15.8 us  [the longest x1 15.8 us: body(): lax.all_to_all(sent, ('frame', 'head'), 0, 0)]
    ppermute x15 -> x12, starting transfers between devices: 25.1 us -> 19.1 us  [shifted(): lax.ppermute(block, 'head', [(at, (at + by) % count) for at in range(coun...]
    select_n x1 -> x0, other arithmetic: 5.02 us -> none  [body(): jnp.where(core == 0, jnp.concatenate([fetched, rest], axis=1), jnp.concat...]
    another operation x2 -> x1, other arithmetic: 3.55 us -> 0.58 us  [body(): place = jnp.stack([group, lax.axis_index('core')]).astype(jnp.int32)]
  transfers between devices with their start and end apart: 19 -> 24, of which waited for: 8 -> 7; matrix products, arithmetic and copies ran while one was open for 6% -> 2% of each run, Pallas kernels for 16% -> 27%
where the time goes in v5:
time: 189 us
  waiting for transfers between devices  73.9 us (39%)
  Pallas kernels  65.4 us (35%)
  starting transfers between devices  44.6 us (24%)
  local copies, waits for them, and re-layouts  3.57 us (2%)
    ppermute x12, waiting for transfers between devices, shifted(): lax.ppermute(block, 'head', [(at, (at + by) % count) for at in range(coun...  58.1 us
    pallas_call x4, Pallas kernels, project(): pl.pallas_call(functools.partial(project_kernel, by), grid_spec=pltpu.Pre...  28.2 us
    ppermute x12, starting transfers between devices, shifted(): lax.ppermute(block, 'head', [(at, (at + by) % count) for at in range(coun...  19.1 us
    pallas_call x1, Pallas kernels, spatial(): pl.pallas_call(functools.partial(spatial_kernel, head_count), grid_spec=p...  17.1 us
    all_to_all x1, waiting for transfers between devices, body(): lax.all_to_all(sent, ('frame', 'head'), 0, 0)  15.8 us
    all_to_all x1, starting transfers between devices, body(): lax.all_to_all(sent, ('frame', 'head'), 0, 0)  11.8 us
    all_to_all x1, starting transfers between devices, body(): arrived = lax.all_to_all(packed, 'frame', 0, 0)  11.8 us
    pallas_call x1, Pallas kernels, temporal(): pl.pallas_call(functools.partial(temporal_kernel, head_class.shape[0]), g...  5.86 us
  transfers between devices with their start and end apart: 24, of which 7 were waited for; matrix products, arithmetic and copies ran while one was open for 2% of the time, Pallas kernels for 27%

profile of v5, /device:TPU:8, one launch (start us, length us, event | category | flops | bytes accessed | tf_op | source)
XLA Modules:
  0.0 188.5 jit_solution(7404287884536658678)
XLA Ops:
  0.0 5.3 %pack.1 = bf16[32,32,1536]{2,1,0:T(8,128)(2,1)} custom-call(s32[6]{0:T(128)} %classes.7, bf16[1024,768]{1,0:T(8,128)(2,1)} %query.3, bf16[1024,768]{1,0:T(8,128)(2,1)} %key.3, bf16[1024,768]{1,0:T(8,128)(2,1)} %value.3, f32[1,128]{1,0:T(1,128)} %bitcast.7, f32[1,128]{1,0:T(1,128)} %bitcast.9), custom_call_target="tpu_custom_call" | custom-call | flops 4194304 | bytes 6291456 | tf_op jit(solution)/shard_map/pack/pallas_call | solution.py:119
  5.3 11.8 %all-to-all-start = ((bf16[32,32,1536]{2,1,0:T(8,128)(2,1)}), bf16[32,32,1536]{2,1,0:T(8,128)(2,1)}, u32[]{:S(2)}, u32[]{:S(2)}) async-start(bf16[32,32,1536]{2,1,0:T(8,128)(2,1)} %pack.1), calls=%async_computation | async-start | bytes 6291456 | tf_op jit(solution)/shard_map/all_to_all | solution.py:391
  18.3 4.6 %weight_half.1 = (bf16[384,1536]{1,0:T(8,128)(2,1)}, bf16[384,1536]{1,0:T(8,128)(2,1)}) custom-call(s32[6]{0:T(128)} %classes.7, s32[2]{0:T(128)} %pad_add_fusion.place, bf16[768,3072]{1,0:T(8,128)(2,1)} %weight.1), custom_call_target="tpu_custom_call" | custom-call | bytes 4718592 | tf_op jit(solution)/shard_map/weight_half/pallas_call | solution.py:261
  22.9 2.8 %collective-permute-start.6 = (bf16[384,1536]{1,0:T(8,128)(2,1)}, bf16[384,1536]{1,0:T(8,128)(2,1)S(1)}, u32[]{:S(2)}, u32[]{:S(2)}) collective-permute-start(bf16[384,1536]{1,0:T(8,128)(2,1)} %get-tuple-element.10.refs_0_), channel_id=1, source_target_pairs={{0,3},{1,0},{2,1},{3,2},{4,7},{5,4},{6,5},{7,6},{8,11},{9,8},{10,9... | collective-permute-start | bytes 3538952 | tf_op jit(solution)/shard_map/ppermute | solution.py:375
  26.4 2.5 %collective-permute-start.8 = (bf16[384,1536]{1,0:T(8,128)(2,1)}, bf16[384,1536]{1,0:T(8,128)(2,1)}, u32[]{:S(2)}, u32[]{:S(2)}) collective-permute-start(bf16[384,1536]{1,0:T(8,128)(2,1)} %get-tuple-element.9.refs_1_), channel_id=1, source_target_pairs={{0,3},{1,0},{2,1},{3,2},{4,7},{5,4},{6,5},{7,6},{8,11},{9,8},{10,9... | collective-permute-start | bytes 3538952 | tf_op jit(solution)/shard_map/ppermute | solution.py:375
  28.9 17.1 %spatial.1.refs_2_ = bf16[1024,768]{1,0:T(8,128)(2,1)} custom-call(s32[6]{0:T(128)} %classes.7, bf16[1024,768]{1,0:T(8,128)(2,1)} %query.3, bf16[1024,768]{1,0:T(8,128)(2,1)} %key.3, bf16[1024,768]{1,0:T(8,128)(2,1)} %collective-permute-done.other_key, bf16[1024,768]{1,0:T(8,128)(2,1)} %value.3, bf16[1024,768]{1,0:T(8,128)(2,1)} %collective-permute-done.1.other_value, ...), custom_call_target="tpu_custom_call" | custom-call | flops 12884901888 | bytes 9437184 | tf_op jit(solution)/shard_map/spatial/pallas_call | solution.py:176
  46.0 2.5 %constant_dynamic-slice_fusion = (bf16[256,768]{1,0:T(8,128)(2,1)}, bf16[256,768]{1,0:T(8,128)(2,1)}, bf16[256,768]{1,0:T(8,128)(2,1)}, bf16[256,768]{1,0:T(8,128)(2,1)}) fusion(bf16[1024,768]{1,0:T(8,128)(2,1)} %spatial.1.refs_2_, s32[]{:T(128)S(6)} %select_n.15, s32[]{:T(128)S(6)} %select_n.14, s32[]{:T(128)S(6)} %select_n.13, s32[]{:T(128)S(6)} %select_n.12), kind=kLoop, calls=%fused_computation | loop fusion | bytes 3145744 | tf_op jit(solution)/shard_map/dynamic_slice | solution.py:408
  48.6 3.2 %collective-permute-start.2 = (bf16[256,768]{1,0:T(8,128)(2,1)}, bf16[256,768]{1,0:T(8,128)(2,1)}, u32[]{:S(2)}, u32[]{:S(2)}) collective-permute-start(bf16[256,768]{1,0:T(8,128)(2,1)} %get-tuple-element.16), channel_id=1, source_target_pairs={{0,1},{1,2},{2,3},{3,0},{4,5},{5,6},{6,7},{7,4},{8,9},{9,10},{10,1... | collective-permute-start | bytes 1179656 | tf_op jit(solution)/shard_map/ppermute | solution.py:375
  51.7 4.2 %collective-permute-done.7.refs_0_ = bf16[384,1536]{1,0:T(8,128)(2,1)S(1)} collective-permute-done((bf16[384,1536]{1,0:T(8,128)(2,1)}, bf16[384,1536]{1,0:T(8,128)(2,1)S(1)}, u32[]{:S(2)}, u32[]{:S(2)}) %collective-permute-start.7) | collective-permute-done | bytes 1179680 | tf_op jit(solution)/shard_map/ppermute | solution.py:375
  55.9 29.3 %collective-permute-done.8.refs_1_ = bf16[384,1536]{1,0:T(8,128)(2,1)} collective-permute-done((bf16[384,1536]{1,0:T(8,128)(2,1)}, bf16[384,1536]{1,0:T(8,128)(2,1)}, u32[]{:S(2)}, u32[]{:S(2)}) %collective-permute-start.8) | collective-permute-done | bytes 1179680 | tf_op jit(solution)/shard_map/ppermute | solution.py:375
  85.2 3.7 %collective-permute-start.4 = (bf16[256,768]{1,0:T(8,128)(2,1)}, bf16[256,768]{1,0:T(8,128)(2,1)}, u32[]{:S(2)}, u32[]{:S(2)}) collective-permute-start(bf16[256,768]{1,0:T(8,128)(2,1)} %get-tuple-element.14), channel_id=1, source_target_pairs={{0,3},{1,0},{2,1},{3,2},{4,7},{5,4},{6,5},{7,6},{8,11},{9,8},{10,9... | collective-permute-start | bytes 1179656 | tf_op jit(solution)/shard_map/ppermute | solution.py:375
  89.4 7.5 %collective-permute-done.2.rest_0_.refs_1_ = bf16[256,768]{1,0:T(8,128)(2,1)} collective-permute-done((bf16[256,768]{1,0:T(8,128)(2,1)}, bf16[256,768]{1,0:T(8,128)(2,1)}, u32[]{:S(2)}, u32[]{:S(2)}) %collective-permute-start.2) | collective-permute-done | bytes 393248 | tf_op jit(solution)/shard_map/ppermute | solution.py:375
  97.0 3.2 %collective-permute-start.10 = (bf16[384,1536]{1,0:T(8,128)(2,1)}, bf16[384,1536]{1,0:T(8,128)(2,1)}, u32[]{:S(2)}, u32[]{:S(2)}) collective-permute-start(bf16[384,1536]{1,0:T(8,128)(2,1)} %get-tuple-element.12.refs_7_), channel_id=1, source_target_pairs={{0,3},{1,0},{2,1},{3,2},{4,7},{5,4},{6,5},{7,6},{8,11},{9,8},{10,9... | collective-permute-start | bytes 3538952 | tf_op jit(solution)/shard_map/ppermute | solution.py:375
  100.2 5.9 %temporal.1 = bf16[32,4,8,512]{3,2,1,0:T(8,128)(2,1)} custom-call(s32[6]{0:T(128)S(1)} %copy-done.10, bf16[32,32,1536]{2,1,0:T(8,128)(2,1)} %all-to-all-done.packed, bf16[256,768]{1,0:T(8,128)(2,1)} %collective-permute-done.2.rest_0_.refs_1_, bf16[256,768]{1,0:T(8,128)(2,1)} %collective-permute-done.3.rest_1_.refs_2_, ...), custom_call_target="tpu_custom_call" | custom-call | flops 1073741824 | bytes 4194304 | tf_op jit(solution)/shard_map/temporal/pallas_call | solution.py:227
  106.1 11.8 %all-to-all-start.1 = ((bf16[128,8,512]{2,1,0:T(8,128)(2,1)}), bf16[128,8,512]{2,1,0:T(8,128)(2,1)}, u32[]{:S(2)}, u32[]{:S(2)}) async-start(bf16[128,8,512]{2,1,0:T(8,128)(2,1)} %bitcast.6), calls=%async_computation.1 | async-start | bytes 2097152 | tf_op jit(solution)/shard_map/all_to_all | solution.py:412
  118.7 13.4 %collective-permute-done.9.refs_4_ = bf16[384,1536]{1,0:T(8,128)(2,1)} collective-permute-done((bf16[384,1536]{1,0:T(8,128)(2,1)}, bf16[384,1536]{1,0:T(8,128)(2,1)}, u32[]{:S(2)}, u32[]{:S(2)}) %collective-permute-start.9) | collective-permute-done | bytes 1179680 | tf_op jit(solution)/shard_map/ppermute | solution.py:375
  133.0 15.8 %all-to-all-done.1 = bf16[128,8,512]{2,1,0:T(8,128)(2,1)} async-done(((bf16[128,8,512]{2,1,0:T(8,128)(2,1)}), bf16[128,8,512]{2,1,0:T(8,128)(2,1)}, u32[]{:S(2)}, u32[]{:S(2)}) %all-to-all-start.1) | async-done | bytes 1048608 | tf_op jit(solution)/shard_map/all_to_all | solution.py:412
  149.8 2.6 %combine.1.heads = bf16[4,256,768]{2,1,0:T(8,128)(2,1)S(1)} custom-call(s32[2]{0:T(128)S(1)} %copy-done.9, bf16[32,4,8,512]{3,2,1,0:T(8,128)(2,1)} %bitcast.5.returned, bf16[256,768]{1,0:T(8,128)(2,1)S(1)} %copy-done.8, bf16[256,768]{1,0:T(8,128)(2,1)} %collective-permute-done.2.rest_0_.refs_1_, bf16[256,768]{1,0:T(8,128)(2,1)} %collective-permute-done.3.rest_1_.refs_2_, ...), custom_call_target="tpu_custom_call" | custom-call | bytes 6291456 | tf_op jit(solution)/shard_map/combine/pallas_call | solution.py:290
  152.5 7.1 %project.7 = bf16[256,768]{1,0:T(8,128)(2,1)S(1)} custom-call(s32[2]{0:T(128)S(1)} %copy-done.9, bf16[4,256,768]{2,1,0:T(8,128)(2,1)S(1)} %combine.1.heads, bf16[384,1536]{1,0:T(8,128)(2,1)S(1)} %copy-done.6, bf16[384,1536]{1,0:T(8,128)(2,1)S(1)} %copy-done.7, bf16[384,1536]{1,0:T(8,128)(2,1)S(1)} %copy-done.5, bf16[384,1536]{1,0:T(8,128)(2,1)S(1)} %copy-done.3, ...), custom_call_target="tpu_custom_call" | custom-call | flops 1207959552 | bytes 393216 | tf_op jit(solution)/shard_map/project/pallas_call | solution.py:327
  159.7 7.1 %project.6 = bf16[256,768]{1,0:T(8,128)(2,1)S(1)} custom-call(s32[2]{0:T(128)S(1)} %copy-done.9, bf16[4,256,768]{2,1,0:T(8,128)(2,1)S(1)} %combine.1.heads, bf16[384,1536]{1,0:T(8,128)(2,1)S(1)} %copy-done.6, bf16[384,1536]{1,0:T(8,128)(2,1)S(1)} %copy-done.7, bf16[384,1536]{1,0:T(8,128)(2,1)S(1)} %copy-done.5, bf16[384,1536]{1,0:T(8,128)(2,1)S(1)} %copy-done.3, ...), custom_call_target="tpu_custom_call" | custom-call | flops 1207959552 | bytes 393216 | tf_op jit(solution)/shard_map/project/pallas_call | solution.py:327
  166.7 2.9 %collective-permute-start.20 = (bf16[256,768]{1,0:T(8,128)(2,1)S(1)}, bf16[256,768]{1,0:T(8,128)(2,1)S(1)}, u32[]{:S(2)}, u32[]{:S(2)}) collective-permute-start(bf16[256,768]{1,0:T(8,128)(2,1)S(1)} %project.6), channel_id=1, source_target_pairs={{0,2},{1,3},{2,0},{3,1},{4,6},{5,7},{6,4},{7,5},{8,10},{9,11},{10,... | collective-permute-start | bytes 1179656 | tf_op jit(solution)/shard_map/ppermute | solution.py:375
  169.6 7.1 %project.5 = bf16[256,768]{1,0:T(8,128)(2,1)S(1)} custom-call(s32[2]{0:T(128)S(1)} %copy-done.9, bf16[4,256,768]{2,1,0:T(8,128)(2,1)S(1)} %combine.1.heads, bf16[384,1536]{1,0:T(8,128)(2,1)S(1)} %copy-done.6, bf16[384,1536]{1,0:T(8,128)(2,1)S(1)} %copy-done.7, bf16[384,1536]{1,0:T(8,128)(2,1)S(1)} %copy-done.5, bf16[384,1536]{1,0:T(8,128)(2,1)S(1)} %copy-done.3, ...), custom_call_target="tpu_custom_call" | custom-call | flops 1207959552 | bytes 393216 | tf_op jit(solution)/shard_map/project/pallas_call | solution.py:327
  176.8 7.1 %project.4.refs_0_ = bf16[256,768]{1,0:T(8,128)(2,1)S(1)} custom-call(s32[2]{0:T(128)S(1)} %copy-done.9, bf16[4,256,768]{2,1,0:T(8,128)(2,1)S(1)} %combine.1.heads, bf16[384,1536]{1,0:T(8,128)(2,1)S(1)} %copy-done.6, bf16[384,1536]{1,0:T(8,128)(2,1)S(1)} %copy-done.7, bf16[384,1536]{1,0:T(8,128)(2,1)S(1)} %copy-done.5, bf16[384,1536]{1,0:T(8,128)(2,1)S(1)} %copy-done.3, ...), custom_call_target="tpu_custom_call" | custom-call | flops 1207959552 | bytes 393216 | tf_op jit(solution)/shard_map/project/pallas_call | solution.py:327
  183.9 2.7 %collective-permute-done.19.refs_1_ = bf16[256,768]{1,0:T(8,128)(2,1)S(1)} collective-permute-done((bf16[256,768]{1,0:T(8,128)(2,1)S(1)}, bf16[256,768]{1,0:T(8,128)(2,1)S(1)}, u32[]{:S(2)}, u32[]{:S(2)}) %collective-permute-start.19) | collective-permute-done | bytes 393248 | tf_op jit(solution)/shard_map/ppermute | solution.py:375
  (59 shorter events, 7.1 us)
Async XLA Ops:
  5.3 94.9 %all-to-all-start = ((bf16[32,32,1536]{2,1,0:T(8,128)(2,1)}), bf16[32,32,1536]{2,1,0:T(8,128)(2,1)}, u32[]{:S(2)}, u32[]{:S(2)}) async-start(bf16[32,32,1536]{2,1,0:T(8,128)(2,1)} %pack.1), calls=%async_computation | async-start | bytes 6291456 | tf_op jit(solution)/shard_map/all_to_all | solution.py:391
  17.1 9.3 %collective-permute-start = (bf16[1024,768]{1,0:T(8,128)(2,1)}, bf16[1024,768]{1,0:T(8,128)(2,1)}, u32[]{:S(2)}, u32[]{:S(2)}) collective-permute-start(bf16[1024,768]{1,0:T(8,128)(2,1)} %key.3), channel_id=1, source_target_pairs={{0,4},{4,0},{1,5},{5,1},{2,6},{6,2},{3,7},{7,3},{8,12},{12,8},{9,1... | collective-permute-start | bytes 4718600 | tf_op jit(solution)/shard_map/ppermute | solution.py:379
  17.2 11.7 %collective-permute-start.1 = (bf16[1024,768]{1,0:T(8,128)(2,1)}, bf16[1024,768]{1,0:T(8,128)(2,1)}, u32[]{:S(2)}, u32[]{:S(2)}) collective-permute-start(bf16[1024,768]{1,0:T(8,128)(2,1)} %value.3), channel_id=1, source_target_pairs={{0,4},{4,0},{1,5},{5,1},{2,6},{6,2},{3,7},{7,3},{8,12},{12,8},{9,1... | collective-permute-start | bytes 4718600 | tf_op jit(solution)/shard_map/ppermute | solution.py:379
  22.9 66.1 %collective-permute-start.6 = (bf16[384,1536]{1,0:T(8,128)(2,1)}, bf16[384,1536]{1,0:T(8,128)(2,1)S(1)}, u32[]{:S(2)}, u32[]{:S(2)}) collective-permute-start(bf16[384,1536]{1,0:T(8,128)(2,1)} %get-tuple-element.10.refs_0_), channel_id=1, source_target_pairs={{0,3},{1,0},{2,1},{3,2},{4,7},{5,4},{6,5},{7,6},{8,11},{9,8},{10,9... | collective-permute-start | bytes 3538952 | tf_op jit(solution)/shard_map/ppermute | solution.py:375
  25.6 30.3 %collective-permute-start.7 = (bf16[384,1536]{1,0:T(8,128)(2,1)}, bf16[384,1536]{1,0:T(8,128)(2,1)S(1)}, u32[]{:S(2)}, u32[]{:S(2)}) collective-permute-start(bf16[384,1536]{1,0:T(8,128)(2,1)} %get-tuple-element.10.refs_0_), channel_id=1, source_target_pairs={{0,1},{1,2},{2,3},{3,0},{4,5},{5,6},{6,7},{7,4},{8,9},{9,10},{10,1... | collective-permute-start | bytes 3538952 | tf_op jit(solution)/shard_map/ppermute | solution.py:375
  25.6 63.2 %collective-permute-start.5 = (bf16[384,1536]{1,0:T(8,128)(2,1)}, bf16[384,1536]{1,0:T(8,128)(2,1)S(1)}, u32[]{:S(2)}, u32[]{:S(2)}) collective-permute-start(bf16[384,1536]{1,0:T(8,128)(2,1)} %get-tuple-element.9.refs_1_), channel_id=1, source_target_pairs={{0,1},{1,2},{2,3},{3,0},{4,5},{5,6},{6,7},{7,4},{8,9},{9,10},{10,1... | collective-permute-start | bytes 3538952 | tf_op jit(solution)/shard_map/ppermute | solution.py:375
  26.4 58.8 %collective-permute-start.8 = (bf16[384,1536]{1,0:T(8,128)(2,1)}, bf16[384,1536]{1,0:T(8,128)(2,1)}, u32[]{:S(2)}, u32[]{:S(2)}) collective-permute-start(bf16[384,1536]{1,0:T(8,128)(2,1)} %get-tuple-element.9.refs_1_), channel_id=1, source_target_pairs={{0,3},{1,0},{2,1},{3,2},{4,7},{5,4},{6,5},{7,6},{8,11},{9,8},{10,9... | collective-permute-start | bytes 3538952 | tf_op jit(solution)/shard_map/ppermute | solution.py:375
  48.6 48.4 %collective-permute-start.2 = (bf16[256,768]{1,0:T(8,128)(2,1)}, bf16[256,768]{1,0:T(8,128)(2,1)}, u32[]{:S(2)}, u32[]{:S(2)}) collective-permute-start(bf16[256,768]{1,0:T(8,128)(2,1)} %get-tuple-element.16), channel_id=1, source_target_pairs={{0,1},{1,2},{2,3},{3,0},{4,5},{5,6},{6,7},{7,4},{8,9},{9,10},{10,1... | collective-permute-start | bytes 1179656 | tf_op jit(solution)/shard_map/ppermute | solution.py:375
  55.9 41.1 %collective-permute-start.3 = (bf16[256,768]{1,0:T(8,128)(2,1)}, bf16[256,768]{1,0:T(8,128)(2,1)}, u32[]{:S(2)}, u32[]{:S(2)}) collective-permute-start(bf16[256,768]{1,0:T(8,128)(2,1)} %get-tuple-element.15), channel_id=1, source_target_pairs={{0,2},{1,3},{2,0},{3,1},{4,6},{5,7},{6,4},{7,5},{8,10},{9,11},{10,... | collective-permute-start | bytes 1179656 | tf_op jit(solution)/shard_map/ppermute | solution.py:375
  85.2 11.8 %collective-permute-start.4 = (bf16[256,768]{1,0:T(8,128)(2,1)}, bf16[256,768]{1,0:T(8,128)(2,1)}, u32[]{:S(2)}, u32[]{:S(2)}) collective-permute-start(bf16[256,768]{1,0:T(8,128)(2,1)} %get-tuple-element.14), channel_id=1, source_target_pairs={{0,3},{1,0},{2,1},{3,2},{4,7},{5,4},{6,5},{7,6},{8,11},{9,8},{10,9... | collective-permute-start | bytes 1179656 | tf_op jit(solution)/shard_map/ppermute | solution.py:375
  88.8 29.1 %collective-permute-start.11 = (bf16[384,1536]{1,0:T(8,128)(2,1)}, bf16[384,1536]{1,0:T(8,128)(2,1)}, u32[]{:S(2)}, u32[]{:S(2)}) collective-permute-start(bf16[384,1536]{1,0:T(8,128)(2,1)} %get-tuple-element.10.refs_0_), channel_id=1, source_target_pairs={{0,4},{4,0},{1,5},{5,1},{2,6},{6,2},{3,7},{7,3},{8,12},{12,8},{9,1... | collective-permute-start | bytes 3538952 | tf_op jit(solution)/shard_map/ppermute | solution.py:379
  89.0 29.1 %collective-permute-start.12 = (bf16[384,1536]{1,0:T(8,128)(2,1)}, bf16[384,1536]{1,0:T(8,128)(2,1)}, u32[]{:S(2)}, u32[]{:S(2)}) collective-permute-start(bf16[384,1536]{1,0:T(8,128)(2,1)} %get-tuple-element.9.refs_1_), channel_id=1, source_target_pairs={{0,4},{4,0},{1,5},{5,1},{2,6},{6,2},{3,7},{7,3},{8,12},{12,8},{9,1... | collective-permute-start | bytes 3538952 | tf_op jit(solution)/shard_map/ppermute | solution.py:379
  97.0 21.6 %collective-permute-start.14 = (bf16[384,1536]{1,0:T(8,128)(2,1)S(1)}, bf16[384,1536]{1,0:T(8,128)(2,1)}, u32[]{:S(2)}, u32[]{:S(2)}) collective-permute-start(bf16[384,1536]{1,0:T(8,128)(2,1)S(1)} %collective-permute-done.5.rest_3_.refs_3_), channel_id=1, source_target_pairs={{0,4},{4,0},{1,5},{5,1},{2,6},{6,2},{3,7},{7,3},{8,12},{12,8},{9,1... | collective-permute-start | bytes 3538952 | tf_op jit(solution)/shard_map/ppermute | solution.py:379
  97.0 35.1 %collective-permute-start.9 = (bf16[384,1536]{1,0:T(8,128)(2,1)}, bf16[384,1536]{1,0:T(8,128)(2,1)}, u32[]{:S(2)}, u32[]{:S(2)}) collective-permute-start(bf16[384,1536]{1,0:T(8,128)(2,1)} %get-tuple-element.11.refs_2_), channel_id=1, source_target_pairs={{0,1},{1,2},{2,3},{3,0},{4,5},{5,6},{6,7},{7,4},{8,9},{9,10},{10,1... | collective-permute-start | bytes 3538952 | tf_op jit(solution)/shard_map/ppermute | solution.py:375
  97.0 36.0 %collective-permute-start.10 = (bf16[384,1536]{1,0:T(8,128)(2,1)}, bf16[384,1536]{1,0:T(8,128)(2,1)}, u32[]{:S(2)}, u32[]{:S(2)}) collective-permute-start(bf16[384,1536]{1,0:T(8,128)(2,1)} %get-tuple-element.12.refs_7_), channel_id=1, source_target_pairs={{0,3},{1,0},{2,1},{3,2},{4,7},{5,4},{6,5},{7,6},{8,11},{9,8},{10,9... | collective-permute-start | bytes 3538952 | tf_op jit(solution)/shard_map/ppermute | solution.py:375
  106.1 42.7 %all-to-all-start.1 = ((bf16[128,8,512]{2,1,0:T(8,128)(2,1)}), bf16[128,8,512]{2,1,0:T(8,128)(2,1)}, u32[]{:S(2)}, u32[]{:S(2)}) async-start(bf16[128,8,512]{2,1,0:T(8,128)(2,1)} %bitcast.6), calls=%async_computation.1 | async-start | bytes 2097152 | tf_op jit(solution)/shard_map/all_to_all | solution.py:412
  117.9 34.5 %collective-permute-start.17 = (bf16[384,1536]{1,0:T(8,128)(2,1)S(1)}, bf16[384,1536]{1,0:T(8,128)(2,1)}, u32[]{:S(2)}, u32[]{:S(2)}) collective-permute-start(bf16[384,1536]{1,0:T(8,128)(2,1)S(1)} %copy-done.1), channel_id=1, source_target_pairs={{0,4},{4,0},{1,5},{5,1},{2,6},{6,2},{3,7},{7,3},{8,12},{12,8},{9,1... | collective-permute-start | bytes 3538952 | tf_op jit(solution)/shard_map/ppermute | solution.py:379
  118.0 34.4 %collective-permute-start.13 = (bf16[384,1536]{1,0:T(8,128)(2,1)S(1)}, bf16[384,1536]{1,0:T(8,128)(2,1)}, u32[]{:S(2)}, u32[]{:S(2)}) collective-permute-start(bf16[384,1536]{1,0:T(8,128)(2,1)S(1)} %copy-done.5), channel_id=1, source_target_pairs={{0,4},{4,0},{1,5},{5,1},{2,6},{6,2},{3,7},{7,3},{8,12},{12,8},{9,1... | collective-permute-start | bytes 3538952 | tf_op jit(solution)/shard_map/ppermute | solution.py:379
  118.5 33.9 %collective-permute-start.18 = (bf16[384,1536]{1,0:T(8,128)(2,1)}, bf16[384,1536]{1,0:T(8,128)(2,1)}, u32[]{:S(2)}, u32[]{:S(2)}) collective-permute-start(bf16[384,1536]{1,0:T(8,128)(2,1)} %get-tuple-element.12.refs_7_), channel_id=1, source_target_pairs={{0,4},{4,0},{1,5},{5,1},{2,6},{6,2},{3,7},{7,3},{8,12},{12,8},{9,1... | collective-permute-start | bytes 3538952 | tf_op jit(solution)/shard_map/ppermute | solution.py:379
  132.1 20.4 %collective-permute-start.15 = (bf16[384,1536]{1,0:T(8,128)(2,1)}, bf16[384,1536]{1,0:T(8,128)(2,1)}, u32[]{:S(2)}, u32[]{:S(2)}) collective-permute-start(bf16[384,1536]{1,0:T(8,128)(2,1)} %collective-permute-done.9.refs_4_), channel_id=1, source_target_pairs={{0,4},{4,0},{1,5},{5,1},{2,6},{6,2},{3,7},{7,3},{8,12},{12,8},{9,1... | collective-permute-start | bytes 3538952 | tf_op jit(solution)/shard_map/ppermute | solution.py:379
  133.0 19.5 %collective-permute-start.16 = (bf16[384,1536]{1,0:T(8,128)(2,1)}, bf16[384,1536]{1,0:T(8,128)(2,1)}, u32[]{:S(2)}, u32[]{:S(2)}) collective-permute-start(bf16[384,1536]{1,0:T(8,128)(2,1)} %collective-permute-done.10.refs_5_), channel_id=1, source_target_pairs={{0,4},{4,0},{1,5},{5,1},{2,6},{6,2},{3,7},{7,3},{8,12},{12,8},{9,1... | collective-permute-start | bytes 3538952 | tf_op jit(solution)/shard_map/ppermute | solution.py:379
  159.6 24.3 %collective-permute-start.21 = (bf16[256,768]{1,0:T(8,128)(2,1)S(1)}, bf16[256,768]{1,0:T(8,128)(2,1)S(1)}, u32[]{:S(2)}, u32[]{:S(2)}) collective-permute-start(bf16[256,768]{1,0:T(8,128)(2,1)S(1)} %project.7), channel_id=1, source_target_pairs={{0,3},{1,0},{2,1},{3,2},{4,7},{5,4},{6,5},{7,6},{8,11},{9,8},{10,9... | collective-permute-start | bytes 1179656 | tf_op jit(solution)/shard_map/ppermute | solution.py:375
  166.7 17.1 %collective-permute-start.20 = (bf16[256,768]{1,0:T(8,128)(2,1)S(1)}, bf16[256,768]{1,0:T(8,128)(2,1)S(1)}, u32[]{:S(2)}, u32[]{:S(2)}) collective-permute-start(bf16[256,768]{1,0:T(8,128)(2,1)S(1)} %project.6), channel_id=1, source_target_pairs={{0,2},{1,3},{2,0},{3,1},{4,6},{5,7},{6,4},{7,5},{8,10},{9,11},{10,... | collective-permute-start | bytes 1179656 | tf_op jit(solution)/shard_map/ppermute | solution.py:375
  176.7 9.9 %collective-permute-start.19 = (bf16[256,768]{1,0:T(8,128)(2,1)S(1)}, bf16[256,768]{1,0:T(8,128)(2,1)S(1)}, u32[]{:S(2)}, u32[]{:S(2)}) collective-permute-start(bf16[256,768]{1,0:T(8,128)(2,1)S(1)} %project.5), channel_id=1, source_target_pairs={{0,1},{1,2},{2,3},{3,0},{4,5},{5,6},{6,7},{7,4},{8,9},{9,10},{10,1... | collective-permute-start | bytes 1179656 | tf_op jit(solution)/shard_map/ppermute | solution.py:375
  (11 other events, 152.0 us)

commit v6 on v5

--- a/solution.py
+++ b/solution.py
@@ -80,7 +80,7 @@
     )(*[from_hbm(array) for array in (*arrays, *after)])
 
 
-def pack_kernel(head_count, classes, query, key, value, query_gain, key_gain, out, raw, ready, in_sems, out_sems):
+def pack_kernel(head_count, classes, place, query, key, value, query_gain, key_gain, weight, out, left, right, raw, ready, rows_held, in_sems, out_sems, row_in_sems, row_out_sems):
     heads = [head_of(classes, slot, head_count) for slot in range(TMAX)]
     gains = (query_gain, key_gain, None)
     frames, positions, _ = out.shape
@@ -93,6 +93,13 @@
         source = (query, key, value)[which].at[:, pl.ds(pl.multiple_of(heads[slot] * HD, HD), HD)]
         loads.append(pltpu.make_async_copy(source, raw.at[at], in_sems.at[at]))
         loads[-1].start()
+    share = left.shape[0] // HD
+    row_loads = []
+    for step in range(share):
+        head = head_of(classes, place[1] * share + step, head_count)
+        source = weight.at[pl.ds(pl.multiple_of(head * HD, HD), HD), :]
+        row_loads.append(pltpu.make_async_copy(source, rows_held.at[step], row_in_sems.at[step]))
+        row_loads[-1].start()
     for at in range(3 * TMAX):
         gain = gains[at % 3]
         loads[at].wait()
@@ -107,33 +114,50 @@
             ready[at, first : first + chunk] = jnp.concatenate(blocks, axis=1).astype(jnp.bfloat16)
         stores.append(pltpu.make_async_copy(ready.at[at], out.at[:, :, pl.ds(at * HD, HD)], out_sems.at[at]))
         stores[-1].start()
+    half = left.shape[1]
+    for step in range(share):
+        row_loads[step].wait()
+        for side, target in enumerate((left, right)):
+            source = rows_held.at[step, :, pl.ds(side * half, half)]
+            target = target.at[pl.ds(step * HD, HD), :]
+            stores.append(pltpu.make_async_copy(source, target, row_out_sems.at[2 * step + side]))
+            stores[-1].start()
     for store in stores:
         store.wait()
 
 
-def pack(head_class, query_rows, key_rows, value_rows, query_gain, key_gain, frames):
+def pack(head_class, place, query_rows, key_rows, value_rows, query_gain, key_gain, weight, frames):
     tokens, width = query_rows.shape
     positions = tokens // frames
+    rows, columns = weight.shape
+    share = rows // HD // CORES
     anywhere = pl.BlockSpec(memory_space=pl.ANY)
-    gain_spec = pl.BlockSpec((1, HD), lambda step, classes: (0, 0))
+    gain_spec = pl.BlockSpec((1, HD), lambda step, classes, place: (0, 0))
     return pl.pallas_call(
         functools.partial(pack_kernel, width // HD),
         grid_spec=pltpu.PrefetchScalarGridSpec(
-            num_scalar_prefetch=1,
+            num_scalar_prefetch=2,
             grid=(1,),
-            in_specs=[anywhere] * 3 + [gain_spec] * 2,
-            out_specs=anywhere,
+            in_specs=[anywhere] * 3 + [gain_spec] * 2 + [anywhere],
+            out_specs=[anywhere] * 3,
             scratch_shapes=[
                 pltpu.VMEM((3 * TMAX, tokens, HD), jnp.bfloat16),
                 pltpu.VMEM((3 * TMAX, frames, positions, HD), jnp.bfloat16),
+                pltpu.VMEM((share, HD, columns), jnp.bfloat16),
                 pltpu.SemaphoreType.DMA((3 * TMAX,)),
                 pltpu.SemaphoreType.DMA((3 * TMAX,)),
+                pltpu.SemaphoreType.DMA((share,)),
+                pltpu.SemaphoreType.DMA((2 * share,)),
             ],
         ),
-        out_shape=in_hbm((frames, positions, TMAX * 3 * HD), jnp.bfloat16),
+        out_shape=[
+            in_hbm((frames, positions, TMAX * 3 * HD), jnp.bfloat16),
+            in_hbm((share * HD, columns // 2), jnp.bfloat16),
+            in_hbm((share * HD, columns // 2), jnp.bfloat16),
+        ],
         cost_estimate=pl.CostEstimate(flops=8 * tokens * TMAX * HD, bytes_accessed=12 * tokens * TMAX * HD, transcendentals=0),
         name="pack",
-    )(head_class, from_hbm(query_rows), from_hbm(key_rows), from_hbm(value_rows), query_gain, key_gain)
+    )(head_class, place, from_hbm(query_rows), from_hbm(key_rows), from_hbm(value_rows), query_gain, key_gain, from_hbm(weight))
 
 
 def spatial_kernel(head_count, classes, query, key, other_key, value, other_value, query_gain, key_gain, out, keys, values):
@@ -243,35 +267,6 @@
     )(head_class, from_vmem(packed), *[from_hbm(array) for array in after])
 
 
-def weight_kernel(classes, place, weight, left, right):
-    width = left.shape[1]
-    left[...] = weight[:, :width]
-    right[...] = weight[:, width:]
-
-
-def weight_half(head_class, place, weight):
-    rows, columns = weight.shape
-    head_count = rows // HD
-    share = head_count // CORES
-    spec = pl.BlockSpec((HD, columns // 2), lambda step, classes, place: (step, 0))
-
-    def source(step, classes, place):
-        return head_of(classes, place[1] * share + step, head_count), 0
-
-    return pl.pallas_call(
-        weight_kernel,
-        grid_spec=pltpu.PrefetchScalarGridSpec(
-            num_scalar_prefetch=2,
-            grid=(share,),
-            in_specs=[pl.BlockSpec((HD, columns), source)],
-            out_specs=[spec, spec],
-        ),
-        out_shape=[in_hbm((rows // CORES, columns // 2), jnp.bfloat16)] * 2,
-        cost_estimate=pl.CostEstimate(flops=0, bytes_accessed=2 * rows * columns, transcendentals=0),
-        name="weight_half",
-    )(head_class, place, weight)
-
-
 def combine_kernel(place, returned, *refs):
     out = refs[-1]
     group_count = out.shape[0]
@@ -300,40 +295,56 @@
 
 
 def project_kernel(by, place, heads, *refs):
-    out = refs[-1]
+    *weights, out, held, sems = refs
     group_count = heads.shape[0]
     block = lax.rem(place[0] + by, group_count)
     width = out.shape[1]
-    share = refs[0].shape[0]
-    columns = pl.ds(pl.multiple_of(lax.rem(block, 2) * width, HD), width)
+    columns = pl.ds(pl.multiple_of(lax.rem(block, 2) * width, width), width)
+    share = held.shape[1]
+
+    def load(at, side):
+        return pltpu.make_async_copy(weights[2 * at + side].at[:, columns], held.at[at], sems.at[at])
+
     for side in range(2):
 
         @pl.when(block // 2 == side)
         def _(side=side):
-            total = jnp.zeros(out.shape, jnp.float32)
-            for group in range(group_count):
-                for core in range(CORES):
-                    weight = refs[(core * group_count + group) * 2 + side]
-                    first = (place[1] if core == 0 else 1 - place[1]) * share
-                    rows = heads[group, :, pl.ds(pl.multiple_of(first, HD), share)]
-                    total += jnp.dot(rows, weight[:, columns], preferred_element_type=jnp.float32)
-            out[...] = total.astype(out.dtype)
+            for at in range(CORES * group_count):
+                load(at, side).start()
+
+    total = jnp.zeros(out.shape, jnp.float32)
+    for at in range(CORES * group_count):
+        core, group = divmod(at, group_count)
+        load(at, 0).wait()
+        first = (place[1] if core == 0 else 1 - place[1]) * share
+        rows = heads[group, :, pl.ds(pl.multiple_of(first, share), share)]
+        total += jnp.dot(rows, held[at], preferred_element_type=jnp.float32)
+    out[...] = total.astype(out.dtype)
 
 
 def project(place, heads, weights, by):
     group_count, rows, depth = heads.shape
-    width = weights[0].shape[1] * 2 // group_count
+    share, width = weights[0].shape[0], weights[0].shape[1] * 2 // group_count
     whole = pl.BlockSpec(memory_space=pltpu.VMEM)
     return pl.pallas_call(
         functools.partial(project_kernel, by),
         grid_spec=pltpu.PrefetchScalarGridSpec(
-            num_scalar_prefetch=1, grid=(1,), in_specs=[whole] * (1 + len(weights)), out_specs=whole
+            num_scalar_prefetch=1,
+            grid=(1,),
+            in_specs=[whole] + [pl.BlockSpec(memory_space=pl.ANY)] * len(weights),
+            out_specs=whole,
+            scratch_shapes=[
+                pltpu.VMEM((len(weights) // 2, share, width), jnp.bfloat16),
+                pltpu.SemaphoreType.DMA((len(weights) // 2,)),
+            ],
         ),
         out_shape=jax.ShapeDtypeStruct((rows, width), jnp.bfloat16),
         compiler_params=pltpu.CompilerParams(vmem_limit_bytes=SMALL_VMEM),
-        cost_estimate=pl.CostEstimate(flops=2 * group_count * rows * depth * width, bytes_accessed=2 * rows * width, transcendentals=0),
+        cost_estimate=pl.CostEstimate(
+            flops=2 * group_count * rows * depth * width, bytes_accessed=2 * group_count * depth * width, transcendentals=0
+        ),
         name="project",
-    )(place, heads, *[from_vmem(weight) for weight in weights])
+    )(place, heads, *[from_hbm(weight) for weight in weights])
 
 
 def join_kernel(place, *refs):
@@ -387,10 +398,9 @@
     place = jnp.stack([group, lax.axis_index("core")]).astype(jnp.int32)
     query_gain = query_gain.reshape(1, HD)
     key_gain = key_gain.reshape(1, HD)
-    packed = pack(head_class, query_rows, key_rows, value_rows, query_gain, key_gain, frames)
+    packed, w_left, w_right = pack(head_class, place, query_rows, key_rows, value_rows, query_gain, key_gain, out_weight, frames)
     arrived = lax.all_to_all(packed, "frame", 0, 0)
 
-    w_left, w_right = weight_half(head_class, place, out_weight)
     right_of_left, left_of_right = shifted(w_left, 1), shifted(w_right, -1)
     right_of_right, left_of_left = shifted(w_right, 1), shifted(w_left, -1)
 
@@ -407,7 +417,7 @@
         first = lax.rem(group + by, group_count) * quarter
         pieces.append(shifted(lax.dynamic_slice_in_dim(near_out, first, quarter), by))
 
-    sent = temporal(head_class, arrived, (*pieces[1:], right_of_right, left_of_left))
+    sent = temporal(head_class, arrived, (near_out, right_of_right, left_of_left, far_of_left, far_of_right))
     sent = sent.reshape(frames * group_count, ROWS, TMAX * HD)
     returned = lax.all_to_all(sent, ("frame", "head"), 0, 0).reshape(frames, group_count, ROWS, TMAX * HD)
     heads = combine(place, returned, pieces)

time: 189 us -> 195 us (1.032)
  waiting for transfers between devices: 73.9 us -> 102 us
  Pallas kernels: 65.4 us -> 46.3 us
  local copies, waits for them, and re-layouts: 3.57 us -> 0.13 us
    ppermute x12, waiting for transfers between devices: 58.1 us -> 97 us  [shifted(): lax.ppermute(block, 'head', [(at, (at + by) % count) for at in range(coun...]
    all_to_all x1, waiting for transfers between devices: 15.8 us -> 0.01 us  [body(): lax.all_to_all(sent, ('frame', 'head'), 0, 0)]
    pallas_call x4, Pallas kernels: 28.2 us -> 18.9 us  [project(): pl.pallas_call(functools.partial(project_kernel, by), grid_spec=pltpu.Pre...]
    ppermute x10, waiting for transfers between devices: 0.03 us -> 5.13 us  [other_core(): return lax.ppermute(block, 'core', [(0, 1), (1, 0)])]
    pallas_call x1 -> x0, Pallas kernels: 4.57 us -> none  [weight_half(): pl.pallas_call(weight_kernel, grid_spec=pltpu.PrefetchScalarGridSpec(num_...]
    pallas_call x1, Pallas kernels: 17.1 us -> 14.1 us  [spatial(): pl.pallas_call(functools.partial(spatial_kernel, head_count), grid_spec=p...]
    dynamic_slice x1, local copies, waits for them, and re-layouts: 2.54 us -> 0.11 us  [body(): lax.dynamic_slice_in_dim(near_out, first, quarter)]
  transfers between devices with their start and end apart: 24 -> 24, of which waited for: 7 -> 10; matrix products, arithmetic and copies ran while one was open for 2% -> 0% of each run, Pallas kernels for 27% -> 17%
where the time goes in v6:
time: 195 us
  waiting for transfers between devices  102 us (52%)
  Pallas kernels  46.3 us (24%)
  starting transfers between devices  45 us (23%)
    ppermute x12, waiting for transfers between devices, shifted(): lax.ppermute(block, 'head', [(at, (at + by) % count) for at in range(coun...  97 us
    pallas_call x4, Pallas kernels, project(): pl.pallas_call(functools.partial(project_kernel, by), grid_spec=pltpu.Pre...  18.9 us
    ppermute x12, starting transfers between devices, shifted(): lax.ppermute(block, 'head', [(at, (at + by) % count) for at in range(coun...  17.8 us
    pallas_call x1, Pallas kernels, spatial(): pl.pallas_call(functools.partial(spatial_kernel, head_count), grid_spec=p...  14.1 us
    all_to_all x1, starting transfers between devices, body(): lax.all_to_all(sent, ('frame', 'head'), 0, 0)  13.5 us
    all_to_all x1, starting transfers between devices, body(): arrived = lax.all_to_all(packed, 'frame', 0, 0)  11.7 us
    pallas_call x1, Pallas kernels, pack(): pl.pallas_call(functools.partial(pack_kernel, width // HD), grid_spec=plt...  6.13 us
    ppermute x10, waiting for transfers between devices, other_core(): return lax.ppermute(block, 'core', [(0, 1), (1, 0)])  5.13 us
  transfers between devices with their start and end apart: 24, of which 10 were waited for; matrix products, arithmetic and copies ran while one was open for 0% of the time, Pallas kernels for 17%

profile of v6, /device:TPU:8, one launch (start us, length us, event | category | flops | bytes accessed | tf_op | source)
XLA Modules:
  0.0 194.5 jit_solution(14242606407746897124)
XLA Ops:
  0.6 6.1 %pack.1 = (bf16[32,32,1536]{2,1,0:T(8,128)(2,1)}, bf16[384,1536]{1,0:T(8,128)(2,1)}, bf16[384,1536]{1,0:T(8,128)(2,1)}) custom-call(s32[6]{0:T(128)} %classes.5, s32[2]{0:T(128)} %pad_add_fusion.place, bf16[1024,768]{1,0:T(8,128)(2,1)} %query.3, bf16[1024,768]{1,0:T(8,128)(2,1)} %key.3, bf16[1024,768]{1,0:T(8,128)(2,1)} %value.3, f32[1,128]{1,0:T(1,128)} %bitcast.8, ...), custom_call_target="tpu_custom_call" | custom-call | flops 4194304 | bytes 6291456 | tf_op jit(solution)/shard_map/pack/pallas_call | solution.py:136
  6.8 11.7 %all-to-all-start = ((bf16[32,32,1536]{2,1,0:T(8,128)(2,1)}), bf16[32,32,1536]{2,1,0:T(8,128)(2,1)S(1)}, u32[]{:S(2)}, u32[]{:S(2)}) async-start(bf16[32,32,1536]{2,1,0:T(8,128)(2,1)} %get-tuple-element.10), calls=%async_computation | async-start | bytes 6291456 | tf_op jit(solution)/shard_map/all_to_all | solution.py:402
  19.1 2.8 %collective-permute-start.5 = (bf16[384,1536]{1,0:T(8,128)(2,1)}, bf16[384,1536]{1,0:T(8,128)(2,1)}, u32[]{:S(2)}, u32[]{:S(2)}) collective-permute-start(bf16[384,1536]{1,0:T(8,128)(2,1)} %get-tuple-element.11.refs_1_), channel_id=1, source_target_pairs={{0,3},{1,0},{2,1},{3,2},{4,7},{5,4},{6,5},{7,6},{8,11},{9,8},{10,9... | collective-permute-start | bytes 3538952 | tf_op jit(solution)/shard_map/ppermute | solution.py:386
  22.6 2.5 %collective-permute-start.3 = (bf16[384,1536]{1,0:T(8,128)(2,1)}, bf16[384,1536]{1,0:T(8,128)(2,1)}, u32[]{:S(2)}, u32[]{:S(2)}) collective-permute-start(bf16[384,1536]{1,0:T(8,128)(2,1)} %get-tuple-element.12.refs_0_), channel_id=1, source_target_pairs={{0,3},{1,0},{2,1},{3,2},{4,7},{5,4},{6,5},{7,6},{8,11},{9,8},{10,9... | collective-permute-start | bytes 3538952 | tf_op jit(solution)/shard_map/ppermute | solution.py:386
  25.1 14.1 %spatial.1.refs_2_.rest_0_ = bf16[1024,768]{1,0:T(8,128)(2,1)} custom-call(s32[6]{0:T(128)} %classes.5, bf16[1024,768]{1,0:T(8,128)(2,1)} %query.3, bf16[1024,768]{1,0:T(8,128)(2,1)} %key.3, bf16[1024,768]{1,0:T(8,128)(2,1)} %collective-permute-done.other_key, bf16[1024,768]{1,0:T(8,128)(2,1)} %value.3, ...), custom_call_target="tpu_custom_call" | custom-call | flops 12884901888 | bytes 9437184 | tf_op jit(solution)/shard_map/spatial/pallas_call | solution.py:200
  39.2 37.1 %collective-permute-done.4.refs_0_ = bf16[384,1536]{1,0:T(8,128)(2,1)} collective-permute-done((bf16[384,1536]{1,0:T(8,128)(2,1)}, bf16[384,1536]{1,0:T(8,128)(2,1)}, u32[]{:S(2)}, u32[]{:S(2)}) %collective-permute-start.4) | collective-permute-done | bytes 1179680 | tf_op jit(solution)/shard_map/ppermute | solution.py:386
  76.3 3.2 %collective-permute-start.7 = (bf16[384,1536]{1,0:T(8,128)(2,1)}, bf16[384,1536]{1,0:T(8,128)(2,1)}, u32[]{:S(2)}, u32[]{:S(2)}) collective-permute-start(bf16[384,1536]{1,0:T(8,128)(2,1)} %get-tuple-element.14.refs_7_), channel_id=1, source_target_pairs={{0,3},{1,0},{2,1},{3,2},{4,7},{5,4},{6,5},{7,6},{8,11},{9,8},{10,9... | collective-permute-start | bytes 3538952 | tf_op jit(solution)/shard_map/ppermute | solution.py:386
  80.4 24.3 %collective-permute-done.6.rest_3_.refs_4_ = bf16[384,1536]{1,0:T(8,128)(2,1)} collective-permute-done((bf16[384,1536]{1,0:T(8,128)(2,1)}, bf16[384,1536]{1,0:T(8,128)(2,1)}, u32[]{:S(2)}, u32[]{:S(2)}) %collective-permute-start.6) | collective-permute-done | bytes 1179680 | tf_op jit(solution)/shard_map/ppermute | solution.py:386
  104.7 4.7 %temporal.1 = bf16[32,4,8,512]{3,2,1,0:T(8,128)(2,1)} custom-call(s32[6]{0:T(128)S(1)} %copy-done.1, bf16[32,32,1536]{2,1,0:T(8,128)(2,1)S(1)} %all-to-all-done.packed, bf16[1024,768]{1,0:T(8,128)(2,1)} %spatial.1.refs_2_.rest_0_, bf16[384,1536]{1,0:T(8,128)(2,1)} %collective-permute-done.2.rest_1_.refs_3_, ...), custom_call_target="tpu_custom_call" | custom-call | flops 1073741824 | bytes 4194304 | tf_op jit(solution)/shard_map/temporal/pallas_call | solution.py:251
  109.4 13.5 %all-to-all-start.1 = ((bf16[128,8,512]{2,1,0:T(8,128)(2,1)}), bf16[128,8,512]{2,1,0:T(8,128)(2,1)S(1)}, u32[]{:S(2)}, u32[]{:S(2)}) async-start(bf16[128,8,512]{2,1,0:T(8,128)(2,1)} %bitcast.7), calls=%async_computation.1 | async-start | bytes 2097152 | tf_op jit(solution)/shard_map/all_to_all | solution.py:422
  123.1 2.8 %collective-permute-start.10 = (bf16[256,768]{1,0:T(8,128)(2,1)S(1)}, bf16[256,768]{1,0:T(8,128)(2,1)S(1)}, u32[]{:S(2)}, u32[]{:S(2)}) collective-permute-start(bf16[256,768]{1,0:T(8,128)(2,1)S(1)} %get-tuple-element.15), channel_id=1, source_target_pairs={{0,3},{1,0},{2,1},{3,2},{4,7},{5,4},{6,5},{7,6},{8,11},{9,8},{10,9... | collective-permute-start | bytes 1179656 | tf_op jit(solution)/shard_map/ppermute | solution.py:386
  125.8 2.3 %collective-permute-start.9 = (bf16[256,768]{1,0:T(8,128)(2,1)S(1)}, bf16[256,768]{1,0:T(8,128)(2,1)S(1)}, u32[]{:S(2)}, u32[]{:S(2)}) collective-permute-start(bf16[256,768]{1,0:T(8,128)(2,1)S(1)} %get-tuple-element.16), channel_id=1, source_target_pairs={{0,2},{1,3},{2,0},{3,1},{4,6},{5,7},{6,4},{7,5},{8,10},{9,11},{10,... | collective-permute-start | bytes 1179656 | tf_op jit(solution)/shard_map/ppermute | solution.py:386
  128.2 22.0 %collective-permute-done.10.refs_3_ = bf16[256,768]{1,0:T(8,128)(2,1)S(1)} collective-permute-done((bf16[256,768]{1,0:T(8,128)(2,1)S(1)}, bf16[256,768]{1,0:T(8,128)(2,1)S(1)}, u32[]{:S(2)}, u32[]{:S(2)}) %collective-permute-start.10) | collective-permute-done | bytes 393248 | tf_op jit(solution)/shard_map/ppermute | solution.py:386
  150.1 3.2 %collective-permute-done.8.refs_1_ = bf16[256,768]{1,0:T(8,128)(2,1)S(1)} collective-permute-done((bf16[256,768]{1,0:T(8,128)(2,1)S(1)}, bf16[256,768]{1,0:T(8,128)(2,1)S(1)}, u32[]{:S(2)}, u32[]{:S(2)}) %collective-permute-start.8) | collective-permute-done | bytes 393248 | tf_op jit(solution)/shard_map/ppermute | solution.py:386
  154.8 1.7 collective-permute-done.18.refs_15_
  156.5 1.7 collective-permute-done.15.refs_12_
  159.9 4.7 %project.7 = bf16[256,768]{1,0:T(8,128)(2,1)S(1)} custom-call(s32[2]{0:T(128)S(1)} %copy-done, bf16[4,256,768]{2,1,0:T(8,128)(2,1)S(1)} %combine.1.heads, bf16[384,1536]{1,0:T(8,128)(2,1)} %get-tuple-element.12.refs_0_, bf16[384,1536]{1,0:T(8,128)(2,1)} %get-tuple-element.11.refs_1_, bf16[384,1536]{1,0:T(8,128)(2,1)} %get-tuple-element.13.refs_2_, ...), custom_call_target="tpu_custom_call" | custom-call | flops 1207959552 | bytes 4718592 | tf_op jit(solution)/shard_map/project/pallas_call | solution.py:329
  164.6 2.2 %collective-permute-start.21 = (bf16[256,768]{1,0:T(8,128)(2,1)S(1)}, bf16[256,768]{1,0:T(8,128)(2,1)S(1)}, u32[]{:S(2)}, u32[]{:S(2)}) collective-permute-start(bf16[256,768]{1,0:T(8,128)(2,1)S(1)} %project.7), channel_id=1, source_target_pairs={{0,3},{1,0},{2,1},{3,2},{4,7},{5,4},{6,5},{7,6},{8,11},{9,8},{10,9... | collective-permute-start | bytes 1179656 | tf_op jit(solution)/shard_map/ppermute | solution.py:386
  166.8 4.7 %project.6 = bf16[256,768]{1,0:T(8,128)(2,1)S(1)} custom-call(s32[2]{0:T(128)S(1)} %copy-done, bf16[4,256,768]{2,1,0:T(8,128)(2,1)S(1)} %combine.1.heads, bf16[384,1536]{1,0:T(8,128)(2,1)} %get-tuple-element.12.refs_0_, bf16[384,1536]{1,0:T(8,128)(2,1)} %get-tuple-element.11.refs_1_, bf16[384,1536]{1,0:T(8,128)(2,1)} %get-tuple-element.13.refs_2_, ...), custom_call_target="tpu_custom_call" | custom-call | flops 1207959552 | bytes 4718592 | tf_op jit(solution)/shard_map/project/pallas_call | solution.py:329
  171.9 4.7 %project.5 = bf16[256,768]{1,0:T(8,128)(2,1)S(1)} custom-call(s32[2]{0:T(128)S(1)} %copy-done, bf16[4,256,768]{2,1,0:T(8,128)(2,1)S(1)} %combine.1.heads, bf16[384,1536]{1,0:T(8,128)(2,1)} %get-tuple-element.12.refs_0_, bf16[384,1536]{1,0:T(8,128)(2,1)} %get-tuple-element.11.refs_1_, bf16[384,1536]{1,0:T(8,128)(2,1)} %get-tuple-element.13.refs_2_, ...), custom_call_target="tpu_custom_call" | custom-call | flops 1207959552 | bytes 4718592 | tf_op jit(solution)/shard_map/project/pallas_call | solution.py:329
  177.5 4.7 %project.4.refs_0_ = bf16[256,768]{1,0:T(8,128)(2,1)S(1)} custom-call(s32[2]{0:T(128)S(1)} %copy-done, bf16[4,256,768]{2,1,0:T(8,128)(2,1)S(1)} %combine.1.heads, bf16[384,1536]{1,0:T(8,128)(2,1)} %get-tuple-element.12.refs_0_, bf16[384,1536]{1,0:T(8,128)(2,1)} %get-tuple-element.11.refs_1_, bf16[384,1536]{1,0:T(8,128)(2,1)} %get-tuple-element.13.refs_2_, ...), custom_call_target="tpu_custom_call" | custom-call | flops 1207959552 | bytes 4718592 | tf_op jit(solution)/shard_map/project/pallas_call | solution.py:329
  182.2 1.7 collective-permute-done.21.refs_3_
  185.4 7.2 %collective-permute-done.19.refs_1_ = bf16[256,768]{1,0:T(8,128)(2,1)S(1)} collective-permute-done((bf16[256,768]{1,0:T(8,128)(2,1)S(1)}, bf16[256,768]{1,0:T(8,128)(2,1)S(1)}, u32[]{:S(2)}, u32[]{:S(2)}) %collective-permute-start.19) | collective-permute-done | bytes 393248 | tf_op jit(solution)/shard_map/ppermute | solution.py:386
  192.6 1.7 join.1
  (42 shorter events, 8.7 us)
Async XLA Ops:
  6.8 97.9 %all-to-all-start = ((bf16[32,32,1536]{2,1,0:T(8,128)(2,1)}), bf16[32,32,1536]{2,1,0:T(8,128)(2,1)S(1)}, u32[]{:S(2)}, u32[]{:S(2)}) async-start(bf16[32,32,1536]{2,1,0:T(8,128)(2,1)} %get-tuple-element.10), calls=%async_computation | async-start | bytes 6291456 | tf_op jit(solution)/shard_map/all_to_all | solution.py:402
  18.5 4.1 %collective-permute-start = (bf16[1024,768]{1,0:T(8,128)(2,1)}, bf16[1024,768]{1,0:T(8,128)(2,1)}, u32[]{:S(2)}, u32[]{:S(2)}) collective-permute-start(bf16[1024,768]{1,0:T(8,128)(2,1)} %key.3), channel_id=1, source_target_pairs={{0,4},{4,0},{1,5},{5,1},{2,6},{6,2},{3,7},{7,3},{8,12},{12,8},{9,1... | collective-permute-start | bytes 4718600 | tf_op jit(solution)/shard_map/ppermute | solution.py:390
  18.6 6.5 %collective-permute-start.1 = (bf16[1024,768]{1,0:T(8,128)(2,1)}, bf16[1024,768]{1,0:T(8,128)(2,1)}, u32[]{:S(2)}, u32[]{:S(2)}) collective-permute-start(bf16[1024,768]{1,0:T(8,128)(2,1)} %value.3), channel_id=1, source_target_pairs={{0,4},{4,0},{1,5},{5,1},{2,6},{6,2},{3,7},{7,3},{8,12},{12,8},{9,1... | collective-permute-start | bytes 4718600 | tf_op jit(solution)/shard_map/ppermute | solution.py:390
  19.1 57.3 %collective-permute-start.5 = (bf16[384,1536]{1,0:T(8,128)(2,1)}, bf16[384,1536]{1,0:T(8,128)(2,1)}, u32[]{:S(2)}, u32[]{:S(2)}) collective-permute-start(bf16[384,1536]{1,0:T(8,128)(2,1)} %get-tuple-element.11.refs_1_), channel_id=1, source_target_pairs={{0,3},{1,0},{2,1},{3,2},{4,7},{5,4},{6,5},{7,6},{8,11},{9,8},{10,9... | collective-permute-start | bytes 3538952 | tf_op jit(solution)/shard_map/ppermute | solution.py:386
  21.8 57.8 %collective-permute-start.2 = (bf16[384,1536]{1,0:T(8,128)(2,1)}, bf16[384,1536]{1,0:T(8,128)(2,1)}, u32[]{:S(2)}, u32[]{:S(2)}) collective-permute-start(bf16[384,1536]{1,0:T(8,128)(2,1)} %get-tuple-element.11.refs_1_), channel_id=1, source_target_pairs={{0,1},{1,2},{2,3},{3,0},{4,5},{5,6},{6,7},{7,4},{8,9},{9,10},{10,1... | collective-permute-start | bytes 3538952 | tf_op jit(solution)/shard_map/ppermute | solution.py:386
  21.8 54.5 %collective-permute-start.4 = (bf16[384,1536]{1,0:T(8,128)(2,1)}, bf16[384,1536]{1,0:T(8,128)(2,1)}, u32[]{:S(2)}, u32[]{:S(2)}) collective-permute-start(bf16[384,1536]{1,0:T(8,128)(2,1)} %get-tuple-element.12.refs_0_), channel_id=1, source_target_pairs={{0,1},{1,2},{2,3},{3,0},{4,5},{5,6},{6,7},{7,4},{8,9},{9,10},{10,1... | collective-permute-start | bytes 3538952 | tf_op jit(solution)/shard_map/ppermute | solution.py:386
  22.6 57.5 %collective-permute-start.3 = (bf16[384,1536]{1,0:T(8,128)(2,1)}, bf16[384,1536]{1,0:T(8,128)(2,1)}, u32[]{:S(2)}, u32[]{:S(2)}) collective-permute-start(bf16[384,1536]{1,0:T(8,128)(2,1)} %get-tuple-element.12.refs_0_), channel_id=1, source_target_pairs={{0,3},{1,0},{2,1},{3,2},{4,7},{5,4},{6,5},{7,6},{8,11},{9,8},{10,9... | collective-permute-start | bytes 3538952 | tf_op jit(solution)/shard_map/ppermute | solution.py:386
  76.3 28.3 %collective-permute-start.6 = (bf16[384,1536]{1,0:T(8,128)(2,1)}, bf16[384,1536]{1,0:T(8,128)(2,1)}, u32[]{:S(2)}, u32[]{:S(2)}) collective-permute-start(bf16[384,1536]{1,0:T(8,128)(2,1)} %get-tuple-element.13.refs_2_), channel_id=1, source_target_pairs={{0,1},{1,2},{2,3},{3,0},{4,5},{5,6},{6,7},{7,4},{8,9},{9,10},{10,1... | collective-permute-start | bytes 3538952 | tf_op jit(solution)/shard_map/ppermute | solution.py:386
  76.3 28.3 %collective-permute-start.7 = (bf16[384,1536]{1,0:T(8,128)(2,1)}, bf16[384,1536]{1,0:T(8,128)(2,1)}, u32[]{:S(2)}, u32[]{:S(2)}) collective-permute-start(bf16[384,1536]{1,0:T(8,128)(2,1)} %get-tuple-element.14.refs_7_), channel_id=1, source_target_pairs={{0,3},{1,0},{2,1},{3,2},{4,7},{5,4},{6,5},{7,6},{8,11},{9,8},{10,9... | collective-permute-start | bytes 3538952 | tf_op jit(solution)/shard_map/ppermute | solution.py:386
  79.6 46.3 %collective-permute-start.11 = (bf16[384,1536]{1,0:T(8,128)(2,1)}, bf16[384,1536]{1,0:T(8,128)(2,1)}, u32[]{:S(2)}, u32[]{:S(2)}) collective-permute-start(bf16[384,1536]{1,0:T(8,128)(2,1)} %get-tuple-element.12.refs_0_), channel_id=1, source_target_pairs={{0,4},{4,0},{1,5},{5,1},{2,6},{6,2},{3,7},{7,3},{8,12},{12,8},{9,1... | collective-permute-start | bytes 3538952 | tf_op jit(solution)/shard_map/ppermute | solution.py:390
  79.6 48.6 %collective-permute-start.12 = (bf16[384,1536]{1,0:T(8,128)(2,1)}, bf16[384,1536]{1,0:T(8,128)(2,1)}, u32[]{:S(2)}, u32[]{:S(2)}) collective-permute-start(bf16[384,1536]{1,0:T(8,128)(2,1)} %get-tuple-element.11.refs_1_), channel_id=1, source_target_pairs={{0,4},{4,0},{1,5},{5,1},{2,6},{6,2},{3,7},{7,3},{8,12},{12,8},{9,1... | collective-permute-start | bytes 3538952 | tf_op jit(solution)/shard_map/ppermute | solution.py:390
  80.1 73.8 %collective-permute-start.14 = (bf16[384,1536]{1,0:T(8,128)(2,1)}, bf16[384,1536]{1,0:T(8,128)(2,1)}, u32[]{:S(2)}, u32[]{:S(2)}) collective-permute-start(bf16[384,1536]{1,0:T(8,128)(2,1)} %collective-permute-done.2.rest_1_.refs_3_), channel_id=1, source_target_pairs={{0,4},{4,0},{1,5},{5,1},{2,6},{6,2},{3,7},{7,3},{8,12},{12,8},{9,1... | collective-permute-start | bytes 3538952 | tf_op jit(solution)/shard_map/ppermute | solution.py:390
  109.4 44.5 %all-to-all-start.1 = ((bf16[128,8,512]{2,1,0:T(8,128)(2,1)}), bf16[128,8,512]{2,1,0:T(8,128)(2,1)S(1)}, u32[]{:S(2)}, u32[]{:S(2)}) async-start(bf16[128,8,512]{2,1,0:T(8,128)(2,1)} %bitcast.7), calls=%async_computation.1 | async-start | bytes 2097152 | tf_op jit(solution)/shard_map/all_to_all | solution.py:422
  123.1 27.0 %collective-permute-start.10 = (bf16[256,768]{1,0:T(8,128)(2,1)S(1)}, bf16[256,768]{1,0:T(8,128)(2,1)S(1)}, u32[]{:S(2)}, u32[]{:S(2)}) collective-permute-start(bf16[256,768]{1,0:T(8,128)(2,1)S(1)} %get-tuple-element.15), channel_id=1, source_target_pairs={{0,3},{1,0},{2,1},{3,2},{4,7},{5,4},{6,5},{7,6},{8,11},{9,8},{10,9... | collective-permute-start | bytes 1179656 | tf_op jit(solution)/shard_map/ppermute | solution.py:386
  125.8 27.5 %collective-permute-start.8 = (bf16[256,768]{1,0:T(8,128)(2,1)S(1)}, bf16[256,768]{1,0:T(8,128)(2,1)S(1)}, u32[]{:S(2)}, u32[]{:S(2)}) collective-permute-start(bf16[256,768]{1,0:T(8,128)(2,1)S(1)} %get-tuple-element.17), channel_id=1, source_target_pairs={{0,1},{1,2},{2,3},{3,0},{4,5},{5,6},{6,7},{7,4},{8,9},{9,10},{10,1... | collective-permute-start | bytes 1179656 | tf_op jit(solution)/shard_map/ppermute | solution.py:386
  125.8 27.5 %collective-permute-start.9 = (bf16[256,768]{1,0:T(8,128)(2,1)S(1)}, bf16[256,768]{1,0:T(8,128)(2,1)S(1)}, u32[]{:S(2)}, u32[]{:S(2)}) collective-permute-start(bf16[256,768]{1,0:T(8,128)(2,1)S(1)} %get-tuple-element.16), channel_id=1, source_target_pairs={{0,2},{1,3},{2,0},{3,1},{4,6},{5,7},{6,4},{7,5},{8,10},{9,11},{10,... | collective-permute-start | bytes 1179656 | tf_op jit(solution)/shard_map/ppermute | solution.py:386
  128.2 26.6 %collective-permute-start.17 = (bf16[384,1536]{1,0:T(8,128)(2,1)}, bf16[384,1536]{1,0:T(8,128)(2,1)}, u32[]{:S(2)}, u32[]{:S(2)}) collective-permute-start(bf16[384,1536]{1,0:T(8,128)(2,1)} %collective-permute-done.3.rest_2_.refs_6_), channel_id=1, source_target_pairs={{0,4},{4,0},{1,5},{5,1},{2,6},{6,2},{3,7},{7,3},{8,12},{12,8},{9,1... | collective-permute-start | bytes 3538952 | tf_op jit(solution)/shard_map/ppermute | solution.py:390
  150.1 4.7 %collective-permute-start.13 = (bf16[384,1536]{1,0:T(8,128)(2,1)}, bf16[384,1536]{1,0:T(8,128)(2,1)}, u32[]{:S(2)}, u32[]{:S(2)}) collective-permute-start(bf16[384,1536]{1,0:T(8,128)(2,1)} %get-tuple-element.13.refs_2_), channel_id=1, source_target_pairs={{0,4},{4,0},{1,5},{5,1},{2,6},{6,2},{3,7},{7,3},{8,12},{12,8},{9,1... | collective-permute-start | bytes 3538952 | tf_op jit(solution)/shard_map/ppermute | solution.py:390
  153.3 3.2 %collective-permute-start.18 = (bf16[384,1536]{1,0:T(8,128)(2,1)}, bf16[384,1536]{1,0:T(8,128)(2,1)}, u32[]{:S(2)}, u32[]{:S(2)}) collective-permute-start(bf16[384,1536]{1,0:T(8,128)(2,1)} %get-tuple-element.14.refs_7_), channel_id=1, source_target_pairs={{0,4},{4,0},{1,5},{5,1},{2,6},{6,2},{3,7},{7,3},{8,12},{12,8},{9,1... | collective-permute-start | bytes 3538952 | tf_op jit(solution)/shard_map/ppermute | solution.py:390
  153.3 4.9 %collective-permute-start.15 = (bf16[384,1536]{1,0:T(8,128)(2,1)}, bf16[384,1536]{1,0:T(8,128)(2,1)}, u32[]{:S(2)}, u32[]{:S(2)}) collective-permute-start(bf16[384,1536]{1,0:T(8,128)(2,1)} %collective-permute-done.6.rest_3_.refs_4_), channel_id=1, source_target_pairs={{0,4},{4,0},{1,5},{5,1},{2,6},{6,2},{3,7},{7,3},{8,12},{12,8},{9,1... | collective-permute-start | bytes 3538952 | tf_op jit(solution)/shard_map/ppermute | solution.py:390
  153.8 6.0 %collective-permute-start.16 = (bf16[384,1536]{1,0:T(8,128)(2,1)}, bf16[384,1536]{1,0:T(8,128)(2,1)}, u32[]{:S(2)}, u32[]{:S(2)}) collective-permute-start(bf16[384,1536]{1,0:T(8,128)(2,1)} %collective-permute-done.7.rest_4_.refs_5_), channel_id=1, source_target_pairs={{0,4},{4,0},{1,5},{5,1},{2,6},{6,2},{3,7},{7,3},{8,12},{12,8},{9,1... | collective-permute-start | bytes 3538952 | tf_op jit(solution)/shard_map/ppermute | solution.py:390
  164.6 19.3 %collective-permute-start.21 = (bf16[256,768]{1,0:T(8,128)(2,1)S(1)}, bf16[256,768]{1,0:T(8,128)(2,1)S(1)}, u32[]{:S(2)}, u32[]{:S(2)}) collective-permute-start(bf16[256,768]{1,0:T(8,128)(2,1)S(1)} %project.7), channel_id=1, source_target_pairs={{0,3},{1,0},{2,1},{3,2},{4,7},{5,4},{6,5},{7,6},{8,11},{9,8},{10,9... | collective-permute-start | bytes 1179656 | tf_op jit(solution)/shard_map/ppermute | solution.py:386
  171.5 13.9 %collective-permute-start.20 = (bf16[256,768]{1,0:T(8,128)(2,1)S(1)}, bf16[256,768]{1,0:T(8,128)(2,1)S(1)}, u32[]{:S(2)}, u32[]{:S(2)}) collective-permute-start(bf16[256,768]{1,0:T(8,128)(2,1)S(1)} %project.6), channel_id=1, source_target_pairs={{0,2},{1,3},{2,0},{3,1},{4,6},{5,7},{6,4},{7,5},{8,10},{9,11},{10,... | collective-permute-start | bytes 1179656 | tf_op jit(solution)/shard_map/ppermute | solution.py:386
  176.6 16.0 %collective-permute-start.19 = (bf16[256,768]{1,0:T(8,128)(2,1)S(1)}, bf16[256,768]{1,0:T(8,128)(2,1)S(1)}, u32[]{:S(2)}, u32[]{:S(2)}) collective-permute-start(bf16[256,768]{1,0:T(8,128)(2,1)S(1)} %project.5), channel_id=1, source_target_pairs={{0,1},{1,2},{2,3},{3,0},{4,5},{5,6},{6,7},{7,4},{8,9},{9,10},{10,1... | collective-permute-start | bytes 1179656 | tf_op jit(solution)/shard_map/ppermute | solution.py:386
  (3 other events, 110.0 us)

commit v7 on v4

--- a/solution.py
+++ b/solution.py
@@ -10,6 +10,7 @@
 
 FRAMES = 32
 TMAX = 4
+ORDER_WEIGHT = 20
 SMALL_VMEM = 16 * 1024 * 1024
 CORES = 2
 HD = 128
@@ -73,7 +74,7 @@
         input_output_aliases={at: at for at in range(len(arrays))},
         cost_estimate=pl.CostEstimate(flops=0, bytes_accessed=0, transcendentals=0),
         name="hold",
-    )(*[from_hbm(array) for array in (*arrays, *after)])
+    )(*[from_hbm(array) for array in arrays], *after)
 
 
 def pack_kernel(head_count, classes, query, key, value, query_gain, key_gain, out, raw, ready, in_sems, out_sems):
@@ -194,9 +195,9 @@
     )(head_class, query_rows, key_rows, from_hbm(other_keys), value_rows, from_hbm(other_values), query_gain, key_gain)
 
 
-def temporal_kernel(head_count, classes, packed, *rest):
+def temporal_kernel(head_count, begin, classes, packed, *rest):
     out = rest[-1]
-    slot = pl.program_id(0)
+    slot = begin + pl.program_id(0)
     frames, positions, _ = packed.shape
     places = 16
     count = frames * places
@@ -221,22 +222,22 @@
         out[...] = jnp.zeros_like(out)
 
 
-def temporal(head_class, packed, after):
+def temporal(head_class, packed, begin, slots, after):
     frames, positions, _ = packed.shape
     return pl.pallas_call(
-        functools.partial(temporal_kernel, head_class.shape[0]),
+        functools.partial(temporal_kernel, head_class.shape[0], begin),
         grid_spec=pltpu.PrefetchScalarGridSpec(
             num_scalar_prefetch=1,
-            grid=(TMAX,),
+            grid=(slots,),
             in_specs=[pl.BlockSpec(memory_space=pltpu.VMEM)] + [pl.BlockSpec(memory_space=pl.ANY)] * len(after),
             out_specs=pl.BlockSpec((frames, positions, HD), lambda slot, classes: (0, 0, slot)),
         ),
-        out_shape=in_hbm((frames, positions, TMAX * HD), jnp.bfloat16),
+        out_shape=in_hbm((frames, positions, slots * HD), jnp.bfloat16),
         compiler_params=pltpu.CompilerParams(vmem_limit_bytes=SMALL_VMEM),
         cost_estimate=pl.CostEstimate(
-            flops=64 * frames * frames * positions * TMAX * HD,
-            bytes_accessed=8 * frames * positions * TMAX * HD,
-            transcendentals=16 * frames * frames * positions * TMAX,
+            flops=64 * frames * frames * positions * slots * HD,
+            bytes_accessed=8 * frames * positions * slots * HD,
+            transcendentals=16 * frames * frames * positions * slots,
         ),
         name="temporal",
     )(head_class, from_vmem(packed), *[from_hbm(array) for array in after])
@@ -290,27 +291,29 @@
     return product(own[...], w_own, first) + product(right[...], w_others.at[0], first) + product(left[...], w_others.at[2], first)
 
 
-def early_kernel(first, own_top, own_bottom, right_top, right_bottom, left_top, left_bottom, far_top, far_bottom, w_own, w_others, out):
+def all_kernel(first, own_top, own_bottom, right_top, right_bottom, left_top, left_bottom, far_top, far_bottom, w_own, w_others, *rest):
+    out = rest[-1]
     half = own_top.shape[0]
     parts = ((own_top, right_top, left_top, far_top), (own_bottom, right_bottom, left_bottom, far_bottom))
     for part, (own, right, left, far) in enumerate(parts):
+        rows = slice(part * half, (part + 1) * half)
         total = near_sum(own, right, left, w_own, w_others, first) + product(far[...], w_others.at[1], first)
-        out[part * half : (part + 1) * half] = total
-
-
-def near_kernel(own_top, own_bottom, right_top, right_bottom, left_top, left_bottom, w_own, w_others, total, out):
+        out[rows] = total if len(rest) == 1 else total + rest[0][rows]
+
+
+def near_kernel(first, own_top, own_bottom, right_top, right_bottom, left_top, left_bottom, w_own, w_others, total, out):
     half = own_top.shape[0]
     for part, (own, right, left) in enumerate(((own_top, right_top, left_top), (own_bottom, right_bottom, left_bottom))):
         rows = slice(part * half, (part + 1) * half)
-        out[rows] = total[rows] + near_sum(own, right, left, w_own, w_others, 0)
-
-
-def far_kernel(far_top, far_bottom, w_others, total, out):
+        out[rows] = total[rows] + near_sum(own, right, left, w_own, w_others, first)
+
+
+def far_kernel(first, far_top, far_bottom, w_others, total, out):
     for part, far in enumerate((far_top, far_bottom)):
 
         @pl.when(pl.program_id(0) == part)
         def _(far=far):
-            out[...] = (product(far[...], w_others.at[1], 0) + total[...]).astype(out.dtype)
+            out[...] = (product(far[...], w_others.at[1], first) + total[...]).astype(out.dtype)
 
 
 def summing(kernel, name, operands, depth_terms):
@@ -324,25 +327,24 @@
         out_shape=pltpu.VMEM((tokens, width), jnp.float32),
         compiler_params=pltpu.CompilerParams(vmem_limit_bytes=SMALL_VMEM),
         cost_estimate=pl.CostEstimate(
-            flops=2 * depth_terms * tokens * depth * width, bytes_accessed=8 * tokens * width, transcendentals=0
+            flops=ORDER_WEIGHT * depth_terms * tokens * depth * width, bytes_accessed=8 * tokens * width, transcendentals=0
         ),
         name=name,
     )(*[from_vmem(array) for array in operands])
 
 
-def project_early(pieces, w_own, w_others):
-    first = TMAX * HD
-    return summing(functools.partial(early_kernel, first), "project_early", (*pieces, w_own, w_others), 4)
-
-
-def project_late(pieces, w_own, w_others, total):
-    near = summing(near_kernel, "near", (*pieces[:6], w_own, w_others, total), 3)
+def project_all(name, first, pieces, w_own, w_others, *total):
+    return summing(functools.partial(all_kernel, first), name, (*pieces, w_own, w_others, *total), 4)
+
+
+def project_last(first, pieces, w_own, w_others, total):
+    near = summing(functools.partial(near_kernel, first), "near", (*pieces[:6], w_own, w_others, total), 3)
     tokens, width = near.shape
     half, depth = pieces[0].shape
     whole = pl.BlockSpec(memory_space=pltpu.VMEM)
     sum_spec = pl.BlockSpec((half, width), lambda step: (step, 0))
     return pl.pallas_call(
-        far_kernel,
+        functools.partial(far_kernel, first),
         grid=(2,),
         in_specs=[whole] * 3 + [sum_spec],
         out_specs=sum_spec,
@@ -396,11 +398,22 @@
     w_others = jnp.where(core == 0, jnp.concatenate([fetched, rest], axis=1), jnp.concatenate([rest, fetched], axis=1))
 
     middle = tokens // 2
-    pieces = ring(back[:middle], back[middle:])
-    returned = over_frames(temporal(head_class, arrived, (*pieces[2:], w_others))).reshape(tokens, TMAX * HD)
-    early = project_early(pieces, w_own, w_others)
-    pieces = ring(returned[:middle] + front[:middle], returned[middle:] + front[middle:])
-    return project_late(pieces, w_own, w_others, early)
+    early = ring(back[:middle], back[middle:])
+    half = TMAX // 2
+    width = half * HD
+    sent = [temporal(head_class, arrived, part * half, half, (*early[2:], w_others)) for part in range(2)]
+
+    returned = over_frames(sent[0]).reshape(tokens, width)
+    (front,) = hold((front,), (sent[1],))
+    first = ring(returned[:middle] + front[:middle, :width], returned[middle:] + front[middle:, :width])
+    (later,) = hold((sent[1],), first[:2])
+    returned = over_frames(later).reshape(tokens, width)
+    total = project_all("early", TMAX * HD, early, w_own, w_others)
+    (rest,) = hold((front,), (*first[2:], total))
+    last = ring(returned[:middle] + rest[:middle, width:], returned[middle:] + rest[middle:, width:])
+
+    total = project_all("first", 0, first, w_own, w_others, total)
+    return project_last(width, last, w_own, w_others, total)
 
 
 def solution(mesh):

time: 167 us -> 171 us (1.024)
  blocking collectives: 35.3 us -> 0 us
  starting transfers between devices: 37.4 us -> 59 us
  local copies, waits for them, and re-layouts: 1.68 us -> 13.5 us
  Pallas kernels: 38.4 us -> 43.6 us
  waiting for transfers between devices: 44 us -> 41.2 us
  other arithmetic: 8.76 us -> 11.3 us
    all_to_all x1 -> x0, blocking collectives: 35.3 us -> none  [over_frames(): return lax.all_to_all(blocks, 'seq', 0, 0, axis_index_groups=groups)]
    ppermute x15 -> x21, waiting for transfers between devices: 36.5 us -> 17.7 us  [shifted(): lax.ppermute(block, 'head', [(at, (at + by) % count) for at in range(coun...]
    all_to_all x1 -> x3, waiting for transfers between devices: 7.48 us -> 23.5 us  [over_frames(): return lax.all_to_all(blocks, 'seq', 0, 0, axis_index_groups=groups)]
    all_to_all x1 -> x3, starting transfers between devices: 11.7 us -> 24.7 us  [over_frames(): return lax.all_to_all(blocks, 'seq', 0, 0, axis_index_groups=groups)]
    unnamed x26 -> x30, local copies, waits for them, and re-layouts: 0.75 us -> 10.6 us
    ppermute x15 -> x21, starting transfers between devices: 25.1 us -> 33.7 us  [shifted(): lax.ppermute(block, 'head', [(at, (at + by) % count) for at in range(coun...]
    pallas_call x1, Pallas kernels: 14.3 us -> 17.5 us  [spatial(): pl.pallas_call(functools.partial(spatial_kernel, head_count), grid_spec=p...]
    add x1 -> x2, other arithmetic: 0.2 us -> 3 us  [the longest x1 1.91 us: body(): returned[middle:] + front[middle:, :width]]
  transfers between devices with their start and end apart: 19 -> 27, of which waited for: 8 -> 10; matrix products, arithmetic and copies ran while one was open for 6% -> 5% of each run, Pallas kernels for 16% -> 20%
where the time goes in v7:
time: 171 us; the launch traced here: 169 us
  starting transfers between devices  59 us (35%)
  Pallas kernels  43.6 us (25%)
  waiting for transfers between devices  41.2 us (24%)
  local copies, waits for them, and re-layouts  13.5 us (8%)
  other arithmetic  11.3 us (7%)
    ppermute x21, starting transfers between devices, shifted(): lax.ppermute(block, 'head', [(at, (at + by) % count) for at in range(coun...  33.7 us
    all_to_all x3, starting transfers between devices, over_frames(): return lax.all_to_all(blocks, 'seq', 0, 0, axis_index_groups=groups)  24.7 us
    all_to_all x3, waiting for transfers between devices, over_frames(): return lax.all_to_all(blocks, 'seq', 0, 0, axis_index_groups=groups)  23.5 us
    ppermute x21, waiting for transfers between devices, shifted(): lax.ppermute(block, 'head', [(at, (at + by) % count) for at in range(coun...  17.7 us
    pallas_call x1, Pallas kernels, spatial(): pl.pallas_call(functools.partial(spatial_kernel, head_count), grid_spec=p...  17.5 us
    unnamed x30, local copies, waits for them, and re-layouts  10.6 us
    pallas_call x3, Pallas kernels, summing(): pl.pallas_call(kernel, in_specs=[whole] * len(operands), out_specs=whole,...  7.68 us
    pallas_call x1, Pallas kernels, weight_blocks(): pl.pallas_call(weight_kernel, grid_spec=pltpu.PrefetchScalarGridSpec(num_...  6.47 us
  transfers between devices with their start and end apart: 27, of which 10 were waited for; matrix products, arithmetic and copies ran while one was open for 5% of the time, Pallas kernels for 20%

profile of v7, /device:TPU:8, one launch (start us, length us, event | category | flops | bytes accessed | tf_op | source)
XLA Modules:
  0.0 168.9 jit_solution(9256031752757840038)
XLA Ops:
  0.0 5.1 %pack.1 = bf16[1024,1536]{1,0:T(8,128)(2,1)} custom-call(s32[6]{0:T(128)} %classes.9, bf16[1024,768]{1,0:T(8,128)(2,1)} %query.3, bf16[1024,768]{1,0:T(8,128)(2,1)} %key.3, bf16[1024,768]{1,0:T(8,128)(2,1)} %value.3, f32[1,128]{1,0:T(1,128)} %bitcast.17, f32[1,128]{1,0:T(1,128)} %bitcast.19), custom_call_target="tpu_custom_call" | custom-call | flops 4194304 | bytes 6291456 | tf_op jit(solution)/shard_map/pack/pallas_call | solution.py:105
  5.2 11.7 %all-to-all-start = ((bf16[32,32,1536]{2,1,0:T(8,128)(2,1)}), bf16[32,32,1536]{2,1,0:T(8,128)(2,1)S(1)}, u32[]{:S(2)}, u32[]{:S(2)}) async-start(bf16[32,32,1536]{2,1,0:T(8,128)(2,1)} %bitcast.16), calls=%async_computation | async-start | bytes 6291456 | tf_op jit(solution)/shard_map/all_to_all | solution.py:378
  18.1 6.5 %weight_blocks.1 = (bf16[768,768]{1,0:T(8,128)(2,1)}, bf16[384,768]{1,0:T(8,128)(2,1)}, bf16[384,768]{1,0:T(8,128)(2,1)}, bf16[384,768]{1,0:T(8,128)(2,1)}) custom-call(s32[6]{0:T(128)} %classes.9, s32[2]{0:T(128)} %pad_add_fusion.place, bf16[768,3072]{1,0:T(8,128)(2,1)} %weight.1), custom_call_target="tpu_custom_call" | custom-call | bytes 9437184 | tf_op jit(solution)/shard_map/weight_blocks/pallas_call | solution.py:271
  26.1 2.7 %collective-permute-start.9 = (bf16[384,768]{1,0:T(8,128)(2,1)}, bf16[384,768]{1,0:T(8,128)(2,1)}, u32[]{:S(2)}, u32[]{:S(2)}) collective-permute-start(bf16[384,768]{1,0:T(8,128)(2,1)} %get-tuple-element.16), channel_id=1, source_target_pairs={{0,2},{1,3},{2,0},{3,1},{4,6},{5,7},{6,4},{7,5},{8,10},{9,11},{10,... | collective-permute-start | bytes 1769480 | tf_op jit(solution)/shard_map/ppermute | solution.py:360
  30.3 17.5 %spatial.1 = (bf16[1024,512]{1,0:T(8,128)(2,1)}, bf16[1024,256]{1,0:T(8,128)(2,1)}) custom-call(s32[6]{0:T(128)} %classes.9, bf16[1024,768]{1,0:T(8,128)(2,1)} %query.3, bf16[1024,768]{1,0:T(8,128)(2,1)} %key.3, bf16[1024,768]{1,0:T(8,128)(2,1)} %collective-permute-done.other_key, bf16[1024,768]{1,0:T(8,128)(2,1)} %value.3, ...), custom_call_target="tpu_custom_call" | custom-call | flops 12884901888 | bytes 9437184 | tf_op jit(solution)/shard_map/spatial/pallas_call | solution.py:172
  47.7 7.1 %collective-permute-done.9.refs_1_ = bf16[384,768]{1,0:T(8,128)(2,1)} collective-permute-done((bf16[384,768]{1,0:T(8,128)(2,1)}, bf16[384,768]{1,0:T(8,128)(2,1)}, u32[]{:S(2)}, u32[]{:S(2)}) %collective-permute-start.9) | collective-permute-done | bytes 589856 | tf_op jit(solution)/shard_map/ppermute | solution.py:360
  54.8 2.9 %pad_maximum_fusion = bf16[3,384,768]{2,1,0:T(8,128)(2,1)} fusion(bf16[1,384,768]{2,1,0:T(8,128)(2,1)} %bitcast.7, bf16[1,384,768]{2,1,0:T(8,128)(2,1)} %bitcast.6, bf16[1,384,768]{2,1,0:T(8,128)(2,1)} %bitcast.5), kind=kLoop, calls=%fused_computation.1 | loop fusion | flops 1769472 | bytes 3538944 | tf_op jit(solution)/shard_map/stack | solution.py:396
  62.0 3.1 %collective-permute-start.4 = (bf16[512,256]{1,0:T(8,128)(2,1)}, bf16[512,256]{1,0:T(8,128)(2,1)S(1)}, u32[]{:S(2)}, u32[]{:S(2)}) collective-permute-start(bf16[512,256]{1,0:T(8,128)(2,1)} %get-tuple-element.32.own_top), channel_id=1, source_target_pairs={{0,3},{1,0},{2,1},{3,2},{4,7},{5,4},{6,5},{7,6},{8,11},{9,8},{10,9... | collective-permute-start | bytes 786440 | tf_op jit(solution)/shard_map/ppermute | solution.py:360
  65.1 4.0 %collective-permute-done.2.rest_0_.right_top = bf16[512,256]{1,0:T(8,128)(2,1)S(1)} collective-permute-done((bf16[512,256]{1,0:T(8,128)(2,1)}, bf16[512,256]{1,0:T(8,128)(2,1)S(1)}, u32[]{:S(2)}, u32[]{:S(2)}) %collective-permute-start.2) | collective-permute-done | bytes 262176 | tf_op jit(solution)/shard_map/ppermute | solution.py:360
  69.4 3.1 %collective-permute-start.7 = (bf16[512,256]{1,0:T(8,128)(2,1)}, bf16[512,256]{1,0:T(8,128)(2,1)}, u32[]{:S(2)}, u32[]{:S(2)}) collective-permute-start(bf16[512,256]{1,0:T(8,128)(2,1)} %collective-permute-done.5.rest_3_.left_bottom), channel_id=1, source_target_pairs={{0,3},{1,0},{2,1},{3,2},{4,7},{5,4},{6,5},{7,6},{8,11},{9,8},{10,9... | collective-permute-start | bytes 786440 | tf_op jit(solution)/shard_map/ppermute | solution.py:360
  72.5 4.7 %maximum_select_fusion.rest_6_.w_others = bf16[3,768,768]{2,1,0:T(8,128)(2,1)} fusion(bf16[3,384,768]{2,1,0:T(8,128)(2,1)} %collective-permute-done.11, bf16[1,384,768]{2,1,0:T(8,128)(2,1)} %bitcast.7, bf16[1,384,768]{2,1,0:T(8,128)(2,1)} %bitcast.6, bf16[1,384,768]{2,1,0:T(8,128)(2,1)} %bitcast.5, pred[]{:T(512)S(6)} %eq.3), kind=kLoop, calls=%fused_computation | loop fusion | flops 30081024 | bytes 7077889 | tf_op jit(solution)/shard_map/jit(_where)/select_n | solution.py:398
  77.3 2.7 %collective-permute-done.6.rest_4_.far_top = bf16[512,256]{1,0:T(8,128)(2,1)S(1)} collective-permute-done((bf16[512,256]{1,0:T(8,128)(2,1)S(1)}, bf16[512,256]{1,0:T(8,128)(2,1)S(1)}, u32[]{:S(2)}, u32[]{:S(2)}) %collective-permute-start.6) | collective-permute-done | bytes 262176 | tf_op jit(solution)/shard_map/ppermute | solution.py:360
  80.7 7.4 %all-to-all-done.packed = bf16[32,32,1536]{2,1,0:T(8,128)(2,1)S(1)} async-done(((bf16[32,32,1536]{2,1,0:T(8,128)(2,1)}), bf16[32,32,1536]{2,1,0:T(8,128)(2,1)S(1)}, u32[]{:S(2)}, u32[]{:S(2)}) %all-to-all-start) | async-done | bytes 3145760 | tf_op jit(solution)/shard_map/all_to_all | solution.py:378
  88.1 3.0 %temporal.3 = bf16[32,32,256]{2,1,0:T(8,128)(2,1)} custom-call(s32[6]{0:T(128)S(1)} %copy-done.11, bf16[32,32,1536]{2,1,0:T(8,128)(2,1)S(1)} %all-to-all-done.packed, bf16[512,256]{1,0:T(8,128)(2,1)} %copy-done.3, bf16[512,256]{1,0:T(8,128)(2,1)} %copy-done.5, bf16[512,256]{1,0:T(8,128)(2,1)} %copy-done.7, ...), custom_call_target="tpu_custom_call" | custom-call | flops 536870912 | bytes 2097152 | tf_op jit(solution)/shard_map/temporal/pallas_call | solution.py:227
  91.1 7.4 %all-to-all-start.1 = ((bf16[32,32,256]{2,1,0:T(8,128)(2,1)}), bf16[32,32,256]{2,1,0:T(8,128)(2,1)}, u32[]{:S(2)}, u32[]{:S(2)}) async-start(bf16[32,32,256]{2,1,0:T(8,128)(2,1)} %temporal.3), calls=%async_computation.1 | async-start | bytes 1048576 | tf_op jit(solution)/shard_map/all_to_all | solution.py:378
  98.5 2.2 %temporal.2.refs_1_.refs_0_ = bf16[32,32,256]{2,1,0:T(8,128)(2,1)} custom-call(s32[6]{0:T(128)S(1)} %copy-done.11, bf16[32,32,1536]{2,1,0:T(8,128)(2,1)S(1)} %all-to-all-done.packed, bf16[512,256]{1,0:T(8,128)(2,1)} %copy-done.3, bf16[512,256]{1,0:T(8,128)(2,1)} %copy-done.5, bf16[512,256]{1,0:T(8,128)(2,1)} %copy-done.7, ...), custom_call_target="tpu_custom_call" | custom-call | flops 536870912 | bytes 2097152 | tf_op jit(solution)/shard_map/temporal/pallas_call | solution.py:227
  100.8 14.3 %all-to-all-done.1 = bf16[32,32,256]{2,1,0:T(8,128)(2,1)} async-done(((bf16[32,32,256]{2,1,0:T(8,128)(2,1)}), bf16[32,32,256]{2,1,0:T(8,128)(2,1)}, u32[]{:S(2)}, u32[]{:S(2)}) %all-to-all-start.1) | async-done | bytes 524320 | tf_op jit(solution)/shard_map/all_to_all | solution.py:378
  121.5 3.0 %collective-permute-start.14 = (bf16[512,256]{1,0:T(8,128)(2,1)}, bf16[512,256]{1,0:T(8,128)(2,1)}, u32[]{:S(2)}, u32[]{:S(2)}) collective-permute-start(bf16[512,256]{1,0:T(8,128)(2,1)} %get-tuple-element.26.refs_1_.own_top), channel_id=1, source_target_pairs={{0,3},{1,0},{2,1},{3,2},{4,7},{5,4},{6,5},{7,6},{8,11},{9,8},{10,9... | collective-permute-start | bytes 786440 | tf_op jit(solution)/shard_map/ppermute | solution.py:360
  124.5 5.6 %all-to-all-start.2 = ((bf16[32,32,256]{2,1,0:T(8,128)(2,1)}), bf16[32,32,256]{2,1,0:T(8,128)(2,1)}, u32[]{:S(2)}, u32[]{:S(2)}) async-start(bf16[32,32,256]{2,1,0:T(8,128)(2,1)} %hold.6), calls=%async_computation.2 | async-start | bytes 1048576 | tf_op jit(solution)/shard_map/all_to_all | solution.py:378
  130.3 3.2 %collective-permute-start.17 = (bf16[512,256]{1,0:T(8,128)(2,1)}, bf16[512,256]{1,0:T(8,128)(2,1)}, u32[]{:S(2)}, u32[]{:S(2)}) collective-permute-start(bf16[512,256]{1,0:T(8,128)(2,1)} %collective-permute-done.15.refs_4_.left_bottom), channel_id=1, source_target_pairs={{0,3},{1,0},{2,1},{3,2},{4,7},{5,4},{6,5},{7,6},{8,11},{9,8},{10,9... | collective-permute-start | bytes 786440 | tf_op jit(solution)/shard_map/ppermute | solution.py:360
  138.6 3.0 %early.1.refs_7_.rest_0_ = f32[1024,768]{1,0:T(8,128)S(1)} custom-call(bf16[512,256]{1,0:T(8,128)(2,1)} %get-tuple-element.32.own_top, bf16[512,256]{1,0:T(8,128)(2,1)} %get-tuple-element.31.own_bottom, bf16[512,256]{1,0:T(8,128)(2,1)S(1)} %copy-done.4, bf16[512,256]{1,0:T(8,128)(2,1)S(1)} %copy-done.6, bf16[512,256]{1,0:T(8,128)(2,1)S(1)} %copy-done.8, ...), custom_call_target="tpu_custom_call" | custom-call | flops 16106127360 | bytes 6291456 | tf_op jit(solution)/shard_map/early/pallas_call | solution.py:323
  149.3 3.2 %collective-permute-start.23 = (bf16[512,256]{1,0:T(8,128)(2,1)S(1)}, bf16[512,256]{1,0:T(8,128)(2,1)S(1)}, u32[]{:S(2)}, u32[]{:S(2)}) collective-permute-start(bf16[512,256]{1,0:T(8,128)(2,1)S(1)} %get-tuple-element.24.own_top), channel_id=1, source_target_pairs={{0,3},{1,0},{2,1},{3,2},{4,7},{5,4},{6,5},{7,6},{8,11},{9,8},{10,9... | collective-permute-start | bytes 786440 | tf_op jit(solution)/shard_map/ppermute | solution.py:360
  155.6 3.3 %first.1.total = f32[1024,768]{1,0:T(8,128)S(1)} custom-call(bf16[512,256]{1,0:T(8,128)(2,1)} %get-tuple-element.26.refs_1_.own_top, bf16[512,256]{1,0:T(8,128)(2,1)} %get-tuple-element.25.refs_2_.own_bottom, bf16[512,256]{1,0:T(8,128)(2,1)} %collective-permute-done.12.refs_1_.right_top, bf16[512,256]{1,0:T(8,128)(2,1)} %collective-permute-done.13.refs_2_.right_bottom, ...), custom_call_target="tpu_custom_call" | custom-call | flops 16106127360 | bytes 6291456 | tf_op jit(solution)/shard_map/first/pallas_call | solution.py:323
  163.8 2.9 %collective-permute-done.19.far_top = bf16[512,256]{1,0:T(8,128)(2,1)S(1)} collective-permute-done((bf16[512,256]{1,0:T(8,128)(2,1)S(1)}, bf16[512,256]{1,0:T(8,128)(2,1)S(1)}, u32[]{:S(2)}, u32[]{:S(2)}) %collective-permute-start.19) | collective-permute-done | bytes 262176 | tf_op jit(solution)/shard_map/ppermute | solution.py:360
  (81 shorter events, 38.9 us)
Async XLA Ops:
  5.2 83.0 %all-to-all-start = ((bf16[32,32,1536]{2,1,0:T(8,128)(2,1)}), bf16[32,32,1536]{2,1,0:T(8,128)(2,1)S(1)}, u32[]{:S(2)}, u32[]{:S(2)}) async-start(bf16[32,32,1536]{2,1,0:T(8,128)(2,1)} %bitcast.16), calls=%async_computation | async-start | bytes 6291456 | tf_op jit(solution)/shard_map/all_to_all | solution.py:378
  16.9 13.4 %collective-permute-start = (bf16[1024,768]{1,0:T(8,128)(2,1)}, bf16[1024,768]{1,0:T(8,128)(2,1)}, u32[]{:S(2)}, u32[]{:S(2)}) collective-permute-start(bf16[1024,768]{1,0:T(8,128)(2,1)} %key.3), channel_id=1, source_target_pairs={{0,4},{4,0},{8,12},{12,8},{16,20},{20,16},{24,28},{28,24},{32,36},... | collective-permute-start | bytes 4718600 | tf_op jit(solution)/shard_map/ppermute | solution.py:372
  17.0 13.3 %collective-permute-start.1 = (bf16[1024,768]{1,0:T(8,128)(2,1)}, bf16[1024,768]{1,0:T(8,128)(2,1)}, u32[]{:S(2)}, u32[]{:S(2)}) collective-permute-start(bf16[1024,768]{1,0:T(8,128)(2,1)} %value.3), channel_id=1, source_target_pairs={{0,4},{4,0},{8,12},{12,8},{16,20},{20,16},{24,28},{28,24},{32,36},... | collective-permute-start | bytes 4718600 | tf_op jit(solution)/shard_map/ppermute | solution.py:372
  24.6 23.1 %collective-permute-start.8 = (bf16[384,768]{1,0:T(8,128)(2,1)}, bf16[384,768]{1,0:T(8,128)(2,1)}, u32[]{:S(2)}, u32[]{:S(2)}) collective-permute-start(bf16[384,768]{1,0:T(8,128)(2,1)} %get-tuple-element.15), channel_id=1, source_target_pairs={{0,1},{1,2},{2,3},{3,0},{4,5},{5,6},{6,7},{7,4},{8,9},{9,10},{10,1... | collective-permute-start | bytes 1769480 | tf_op jit(solution)/shard_map/ppermute | solution.py:360
  26.1 28.7 %collective-permute-start.9 = (bf16[384,768]{1,0:T(8,128)(2,1)}, bf16[384,768]{1,0:T(8,128)(2,1)}, u32[]{:S(2)}, u32[]{:S(2)}) collective-permute-start(bf16[384,768]{1,0:T(8,128)(2,1)} %get-tuple-element.16), channel_id=1, source_target_pairs={{0,2},{1,3},{2,0},{3,1},{4,6},{5,7},{6,4},{7,5},{8,10},{9,11},{10,... | collective-permute-start | bytes 1769480 | tf_op jit(solution)/shard_map/ppermute | solution.py:360
  28.8 26.0 %collective-permute-start.10 = (bf16[384,768]{1,0:T(8,128)(2,1)}, bf16[384,768]{1,0:T(8,128)(2,1)}, u32[]{:S(2)}, u32[]{:S(2)}) collective-permute-start(bf16[384,768]{1,0:T(8,128)(2,1)} %get-tuple-element.17), channel_id=1, source_target_pairs={{0,3},{1,0},{2,1},{3,2},{4,7},{5,4},{6,5},{7,6},{8,11},{9,8},{10,9... | collective-permute-start | bytes 1769480 | tf_op jit(solution)/shard_map/ppermute | solution.py:360
  57.8 14.7 %collective-permute-start.11 = (bf16[3,384,768]{2,1,0:T(8,128)(2,1)}, bf16[3,384,768]{2,1,0:T(8,128)(2,1)}, u32[]{:S(2)}, u32[]{:S(2)}) collective-permute-start(bf16[3,384,768]{2,1,0:T(8,128)(2,1)} %pad_maximum_fusion), channel_id=1, source_target_pairs={{0,4},{4,0},{8,12},{12,8},{16,20},{20,16},{24,28},{28,24},{32,36},... | collective-permute-start | bytes 5308424 | tf_op jit(solution)/shard_map/ppermute | solution.py:372
  58.6 10.5 %collective-permute-start.2 = (bf16[512,256]{1,0:T(8,128)(2,1)}, bf16[512,256]{1,0:T(8,128)(2,1)S(1)}, u32[]{:S(2)}, u32[]{:S(2)}) collective-permute-start(bf16[512,256]{1,0:T(8,128)(2,1)} %get-tuple-element.32.own_top), channel_id=1, source_target_pairs={{0,1},{1,2},{2,3},{3,0},{4,5},{5,6},{6,7},{7,4},{8,9},{9,10},{10,1... | collective-permute-start | bytes 786440 | tf_op jit(solution)/shard_map/ppermute | solution.py:360
  61.8 15.4 %collective-permute-start.3 = (bf16[512,256]{1,0:T(8,128)(2,1)}, bf16[512,256]{1,0:T(8,128)(2,1)S(1)}, u32[]{:S(2)}, u32[]{:S(2)}) collective-permute-start(bf16[512,256]{1,0:T(8,128)(2,1)} %get-tuple-element.31.own_bottom), channel_id=1, source_target_pairs={{0,1},{1,2},{2,3},{3,0},{4,5},{5,6},{6,7},{7,4},{8,9},{9,10},{10,1... | collective-permute-start | bytes 786440 | tf_op jit(solution)/shard_map/ppermute | solution.py:360
  62.0 15.3 %collective-permute-start.4 = (bf16[512,256]{1,0:T(8,128)(2,1)}, bf16[512,256]{1,0:T(8,128)(2,1)S(1)}, u32[]{:S(2)}, u32[]{:S(2)}) collective-permute-start(bf16[512,256]{1,0:T(8,128)(2,1)} %get-tuple-element.32.own_top), channel_id=1, source_target_pairs={{0,3},{1,0},{2,1},{3,2},{4,7},{5,4},{6,5},{7,6},{8,11},{9,8},{10,9... | collective-permute-start | bytes 786440 | tf_op jit(solution)/shard_map/ppermute | solution.py:360
  69.1 10.8 %collective-permute-start.6 = (bf16[512,256]{1,0:T(8,128)(2,1)S(1)}, bf16[512,256]{1,0:T(8,128)(2,1)S(1)}, u32[]{:S(2)}, u32[]{:S(2)}) collective-permute-start(bf16[512,256]{1,0:T(8,128)(2,1)S(1)} %collective-permute-done.2.rest_0_.right_top), channel_id=1, source_target_pairs={{0,1},{1,2},{2,3},{3,0},{4,5},{5,6},{6,7},{7,4},{8,9},{9,10},{10,1... | collective-permute-start | bytes 786440 | tf_op jit(solution)/shard_map/ppermute | solution.py:360
  69.4 11.3 %collective-permute-start.7 = (bf16[512,256]{1,0:T(8,128)(2,1)}, bf16[512,256]{1,0:T(8,128)(2,1)}, u32[]{:S(2)}, u32[]{:S(2)}) collective-permute-start(bf16[512,256]{1,0:T(8,128)(2,1)} %collective-permute-done.5.rest_3_.left_bottom), channel_id=1, source_target_pairs={{0,3},{1,0},{2,1},{3,2},{4,7},{5,4},{6,5},{7,6},{8,11},{9,8},{10,9... | collective-permute-start | bytes 786440 | tf_op jit(solution)/shard_map/ppermute | solution.py:360
  91.1 23.9 %all-to-all-start.1 = ((bf16[32,32,256]{2,1,0:T(8,128)(2,1)}), bf16[32,32,256]{2,1,0:T(8,128)(2,1)}, u32[]{:S(2)}, u32[]{:S(2)}) async-start(bf16[32,32,256]{2,1,0:T(8,128)(2,1)} %temporal.3), calls=%async_computation.1 | async-start | bytes 1048576 | tf_op jit(solution)/shard_map/all_to_all | solution.py:378
  118.0 12.1 %collective-permute-start.12 = (bf16[512,256]{1,0:T(8,128)(2,1)}, bf16[512,256]{1,0:T(8,128)(2,1)}, u32[]{:S(2)}, u32[]{:S(2)}) collective-permute-start(bf16[512,256]{1,0:T(8,128)(2,1)} %get-tuple-element.26.refs_1_.own_top), channel_id=1, source_target_pairs={{0,1},{1,2},{2,3},{3,0},{4,5},{5,6},{6,7},{7,4},{8,9},{9,10},{10,1... | collective-permute-start | bytes 786440 | tf_op jit(solution)/shard_map/ppermute | solution.py:360
  119.5 10.8 %collective-permute-start.15 = (bf16[512,256]{1,0:T(8,128)(2,1)}, bf16[512,256]{1,0:T(8,128)(2,1)}, u32[]{:S(2)}, u32[]{:S(2)}) collective-permute-start(bf16[512,256]{1,0:T(8,128)(2,1)} %get-tuple-element.25.refs_2_.own_bottom), channel_id=1, source_target_pairs={{0,3},{1,0},{2,1},{3,2},{4,7},{5,4},{6,5},{7,6},{8,11},{9,8},{10,9... | collective-permute-start | bytes 786440 | tf_op jit(solution)/shard_map/ppermute | solution.py:360
  121.3 21.9 %collective-permute-start.13 = (bf16[512,256]{1,0:T(8,128)(2,1)}, bf16[512,256]{1,0:T(8,128)(2,1)}, u32[]{:S(2)}, u32[]{:S(2)}) collective-permute-start(bf16[512,256]{1,0:T(8,128)(2,1)} %get-tuple-element.25.refs_2_.own_bottom), channel_id=1, source_target_pairs={{0,1},{1,2},{2,3},{3,0},{4,5},{5,6},{6,7},{7,4},{8,9},{9,10},{10,1... | collective-permute-start | bytes 786440 | tf_op jit(solution)/shard_map/ppermute | solution.py:360
  121.5 21.6 %collective-permute-start.14 = (bf16[512,256]{1,0:T(8,128)(2,1)}, bf16[512,256]{1,0:T(8,128)(2,1)}, u32[]{:S(2)}, u32[]{:S(2)}) collective-permute-start(bf16[512,256]{1,0:T(8,128)(2,1)} %get-tuple-element.26.refs_1_.own_top), channel_id=1, source_target_pairs={{0,3},{1,0},{2,1},{3,2},{4,7},{5,4},{6,5},{7,6},{8,11},{9,8},{10,9... | collective-permute-start | bytes 786440 | tf_op jit(solution)/shard_map/ppermute | solution.py:360
  124.5 20.5 %all-to-all-start.2 = ((bf16[32,32,256]{2,1,0:T(8,128)(2,1)}), bf16[32,32,256]{2,1,0:T(8,128)(2,1)}, u32[]{:S(2)}, u32[]{:S(2)}) async-start(bf16[32,32,256]{2,1,0:T(8,128)(2,1)} %hold.6), calls=%async_computation.2 | async-start | bytes 1048576 | tf_op jit(solution)/shard_map/all_to_all | solution.py:378
  130.2 13.0 %collective-permute-start.16 = (bf16[512,256]{1,0:T(8,128)(2,1)}, bf16[512,256]{1,0:T(8,128)(2,1)}, u32[]{:S(2)}, u32[]{:S(2)}) collective-permute-start(bf16[512,256]{1,0:T(8,128)(2,1)} %collective-permute-done.12.refs_1_.right_top), channel_id=1, source_target_pairs={{0,1},{1,2},{2,3},{3,0},{4,5},{5,6},{6,7},{7,4},{8,9},{9,10},{10,1... | collective-permute-start | bytes 786440 | tf_op jit(solution)/shard_map/ppermute | solution.py:360
  130.3 12.9 %collective-permute-start.17 = (bf16[512,256]{1,0:T(8,128)(2,1)}, bf16[512,256]{1,0:T(8,128)(2,1)}, u32[]{:S(2)}, u32[]{:S(2)}) collective-permute-start(bf16[512,256]{1,0:T(8,128)(2,1)} %collective-permute-done.15.refs_4_.left_bottom), channel_id=1, source_target_pairs={{0,3},{1,0},{2,1},{3,2},{4,7},{5,4},{6,5},{7,6},{8,11},{9,8},{10,9... | collective-permute-start | bytes 786440 | tf_op jit(solution)/shard_map/ppermute | solution.py:360
  147.1 13.8 %collective-permute-start.20 = (bf16[512,256]{1,0:T(8,128)(2,1)S(1)}, bf16[512,256]{1,0:T(8,128)(2,1)S(1)}, u32[]{:S(2)}, u32[]{:S(2)}) collective-permute-start(bf16[512,256]{1,0:T(8,128)(2,1)S(1)} %get-tuple-element.23.own_bottom), channel_id=1, source_target_pairs={{0,3},{1,0},{2,1},{3,2},{4,7},{5,4},{6,5},{7,6},{8,11},{9,8},{10,9... | collective-permute-start | bytes 786440 | tf_op jit(solution)/shard_map/ppermute | solution.py:360
  147.6 14.8 %collective-permute-start.22 = (bf16[512,256]{1,0:T(8,128)(2,1)S(1)}, bf16[512,256]{1,0:T(8,128)(2,1)S(1)}, u32[]{:S(2)}, u32[]{:S(2)}) collective-permute-start(bf16[512,256]{1,0:T(8,128)(2,1)S(1)} %get-tuple-element.23.own_bottom), channel_id=1, source_target_pairs={{0,1},{1,2},{2,3},{3,0},{4,5},{5,6},{6,7},{7,4},{8,9},{9,10},{10,1... | collective-permute-start | bytes 786440 | tf_op jit(solution)/shard_map/ppermute | solution.py:360
  149.2 9.9 %collective-permute-start.18 = (bf16[512,256]{1,0:T(8,128)(2,1)S(1)}, bf16[512,256]{1,0:T(8,128)(2,1)S(1)}, u32[]{:S(2)}, u32[]{:S(2)}) collective-permute-start(bf16[512,256]{1,0:T(8,128)(2,1)S(1)} %get-tuple-element.24.own_top), channel_id=1, source_target_pairs={{0,1},{1,2},{2,3},{3,0},{4,5},{5,6},{6,7},{7,4},{8,9},{9,10},{10,1... | collective-permute-start | bytes 786440 | tf_op jit(solution)/shard_map/ppermute | solution.py:360
  149.3 13.1 %collective-permute-start.23 = (bf16[512,256]{1,0:T(8,128)(2,1)S(1)}, bf16[512,256]{1,0:T(8,128)(2,1)S(1)}, u32[]{:S(2)}, u32[]{:S(2)}) collective-permute-start(bf16[512,256]{1,0:T(8,128)(2,1)S(1)} %get-tuple-element.24.own_top), channel_id=1, source_target_pairs={{0,3},{1,0},{2,1},{3,2},{4,7},{5,4},{6,5},{7,6},{8,11},{9,8},{10,9... | collective-permute-start | bytes 786440 | tf_op jit(solution)/shard_map/ppermute | solution.py:360
  (18 other events, 109.5 us)

commit v8 on v7

--- a/solution.py
+++ b/solution.py
@@ -122,11 +122,10 @@
     )(head_class, from_hbm(query_rows), from_hbm(key_rows), from_hbm(value_rows), query_gain, key_gain)
 
 
-def spatial_kernel(head_count, classes, query, key, other_key, value, other_value, query_gain, key_gain, front, back, keys, values):
+def spatial_kernel(head_count, classes, query, key, other_key, value, other_value, query_gain, key_gain, out, keys, values):
     slot = pl.program_id(0)
     tokens = query.shape[0]
     chunk = tokens // 4
-    is_front = slot < TMAX
 
     @pl.when(slot >= temporal_count(classes, head_count))
     def _():
@@ -141,23 +140,14 @@
             queries = normed(query[rows, :], query_gain[...])
             weights = jnp.exp2(scores_of(queries, keys[...]) * LOG2_SCALE).astype(jnp.bfloat16)
             summed = jnp.dot(weights, values[...], preferred_element_type=jnp.float32)
-            result = (summed[:, :HD] / summed[:, HD:]).astype(jnp.bfloat16)
-
-            @pl.when(is_front)
-            def _():
-                front[rows, :] = result
-
-            @pl.when(jnp.logical_not(is_front))
-            def _():
-                back[rows, :] = result
-
+            out[rows, :] = (summed[:, :HD] / summed[:, HD:]).astype(jnp.bfloat16)
             return carry
 
         lax.fori_loop(0, tokens // chunk, step, 0)
 
     @pl.when(slot < temporal_count(classes, head_count))
     def _():
-        front[...] = jnp.zeros_like(front)
+        out[...] = jnp.zeros_like(out)
 
 
 def spatial(head_class, query_rows, key_rows, other_keys, value_rows, other_values, query_gain, key_gain):
@@ -175,19 +165,13 @@
             num_scalar_prefetch=1,
             grid=(head_count,),
             in_specs=[row_spec] * 5 + [gain_spec] * 2,
-            out_specs=[
-                pl.BlockSpec((tokens, HD), lambda slot, classes: (0, jnp.minimum(slot, TMAX - 1))),
-                pl.BlockSpec((tokens, HD), lambda slot, classes: (0, jnp.maximum(slot - TMAX, 0))),
-            ],
+            out_specs=pl.BlockSpec((tokens, HD), lambda slot, classes: (0, slot)),
             scratch_shapes=[
                 pltpu.VMEM((2 * tokens, HD), jnp.bfloat16),
                 pltpu.VMEM((2 * tokens, 2 * HD), jnp.bfloat16),
             ],
         ),
-        out_shape=[
-            in_hbm((tokens, TMAX * HD), jnp.bfloat16),
-            in_hbm((tokens, width - TMAX * HD), jnp.bfloat16),
-        ],
+        out_shape=in_hbm((tokens, width), jnp.bfloat16),
         cost_estimate=pl.CostEstimate(
             flops=16 * tokens * tokens * width, bytes_accessed=12 * tokens * width, transcendentals=2 * tokens * tokens * head_count
         ),
@@ -287,25 +271,25 @@
     return jnp.dot(rows, weight[first : first + rows.shape[1]], preferred_element_type=jnp.float32)
 
 
-def near_sum(own, right, left, w_own, w_others, first):
-    return product(own[...], w_own, first) + product(right[...], w_others.at[0], first) + product(left[...], w_others.at[2], first)
-
-
-def all_kernel(first, own_top, own_bottom, right_top, right_bottom, left_top, left_bottom, far_top, far_bottom, w_own, w_others, *rest):
+def near_sum(own, right, left, w_own, w_others, first, rows):
+    total = product(own[rows], w_own, first)
+    return total + product(right[rows], w_others.at[0], first) + product(left[rows], w_others.at[2], first)
+
+
+def halves(tokens):
+    return slice(0, tokens // 2), slice(tokens // 2, tokens)
+
+
+def all_kernel(first, own, right, left, far_top, far_bottom, w_own, w_others, *rest):
     out = rest[-1]
-    half = own_top.shape[0]
-    parts = ((own_top, right_top, left_top, far_top), (own_bottom, right_bottom, left_bottom, far_bottom))
-    for part, (own, right, left, far) in enumerate(parts):
-        rows = slice(part * half, (part + 1) * half)
-        total = near_sum(own, right, left, w_own, w_others, first) + product(far[...], w_others.at[1], first)
+    for rows, far in zip(halves(own.shape[0]), (far_top, far_bottom), strict=True):
+        total = near_sum(own, right, left, w_own, w_others, first, rows) + product(far[...], w_others.at[1], first)
         out[rows] = total if len(rest) == 1 else total + rest[0][rows]
 
 
-def near_kernel(first, own_top, own_bottom, right_top, right_bottom, left_top, left_bottom, w_own, w_others, total, out):
-    half = own_top.shape[0]
-    for part, (own, right, left) in enumerate(((own_top, right_top, left_top), (own_bottom, right_bottom, left_bottom))):
-        rows = slice(part * half, (part + 1) * half)
-        out[rows] = total[rows] + near_sum(own, right, left, w_own, w_others, first)
+def near_kernel(first, own, right, left, w_own, w_others, total, out):
+    for rows in halves(own.shape[0]):
+        out[rows] = total[rows] + near_sum(own, right, left, w_own, w_others, first, rows)
 
 
 def far_kernel(first, far_top, far_bottom, w_others, total, out):
@@ -317,7 +301,7 @@
 
 
 def summing(kernel, name, operands, depth_terms):
-    tokens, width = 2 * operands[0].shape[0], operands[-1].shape[-1]
+    tokens, width = operands[0].shape[0], operands[-1].shape[-1]
     depth = operands[0].shape[1]
     whole = pl.BlockSpec(memory_space=pltpu.VMEM)
     return pl.pallas_call(
@@ -338,9 +322,9 @@
 
 
 def project_last(first, pieces, w_own, w_others, total):
-    near = summing(functools.partial(near_kernel, first), "near", (*pieces[:6], w_own, w_others, total), 3)
+    near = summing(functools.partial(near_kernel, first), "near", (*pieces[:3], w_own, w_others, total), 3)
     tokens, width = near.shape
-    half, depth = pieces[0].shape
+    half, depth = pieces[3].shape
     whole = pl.BlockSpec(memory_space=pltpu.VMEM)
     sum_spec = pl.BlockSpec((half, width), lambda step: (step, 0))
     return pl.pallas_call(
@@ -352,7 +336,7 @@
         compiler_params=pltpu.CompilerParams(vmem_limit_bytes=SMALL_VMEM),
         cost_estimate=pl.CostEstimate(flops=2 * tokens * depth * width, bytes_accessed=8 * tokens * width, transcendentals=0),
         name="far",
-    )(*[from_vmem(array) for array in (*pieces[6:], w_others, near)])
+    )(*[from_vmem(array) for array in (*pieces[3:], w_others, near)])
 
 
 def shifted(block, by):
@@ -360,11 +344,10 @@
     return lax.ppermute(block, "head", [(at, (at + by) % count) for at in range(count)])
 
 
-def ring(top, bottom):
-    right_top, left_bottom = shifted(top, 1), shifted(bottom, -1)
-    right_bottom, left_top = shifted(bottom, 1), shifted(top, -1)
-    far_top, far_bottom = shifted(right_top, 1), shifted(left_bottom, -1)
-    return top, bottom, right_top, right_bottom, left_top, left_bottom, far_top, far_bottom
+def ring(block):
+    half = block.shape[0] // 2
+    right, left = shifted(block, 1), shifted(block, -1)
+    return block, right, left, shifted(right[:half], 1), shifted(left[half:], -1)
 
 
 def other_core(block):
@@ -386,31 +369,31 @@
     packed = pack(head_class, query_rows, key_rows, value_rows, query_gain, key_gain)
     arrived = over_frames(packed.reshape(FRAMES, tokens // FRAMES, TMAX * 3 * HD))
 
-    other_keys, other_values = other_core(key_rows), other_core(value_rows)
-    front, back = spatial(head_class, query_rows, key_rows, other_keys, value_rows, other_values, query_gain, key_gain)
     core = lax.rem(lax.axis_index("seq"), CORES)
     place = jnp.stack([lax.axis_index("head"), core]).astype(jnp.int32)
-    w_own, *halves = weight_blocks(head_class, place, out_weight, group_count)
-
-    fetched = [shifted(half, by + 1) for by, half in enumerate(halves)]
-    fetched = jnp.stack(hold(fetched, (back,)))
+    w_own, *halves_of_others = weight_blocks(head_class, place, out_weight, group_count)
+    (other_keys,) = hold((other_core(key_rows),), halves_of_others)
+    other_values = other_core(value_rows)
+    near_out = spatial(head_class, query_rows, key_rows, other_keys, value_rows, other_values, query_gain, key_gain)
+
+    fetched = [shifted(half, by + 1) for by, half in enumerate(halves_of_others)]
+    fetched = jnp.stack(hold(fetched, (near_out,)))
     rest = other_core(fetched)
     w_others = jnp.where(core == 0, jnp.concatenate([fetched, rest], axis=1), jnp.concatenate([rest, fetched], axis=1))
 
-    middle = tokens // 2
-    early = ring(back[:middle], back[middle:])
+    early = ring(near_out)
     half = TMAX // 2
     width = half * HD
-    sent = [temporal(head_class, arrived, part * half, half, (*early[2:], w_others)) for part in range(2)]
-
-    returned = over_frames(sent[0]).reshape(tokens, width)
-    (front,) = hold((front,), (sent[1],))
-    first = ring(returned[:middle] + front[:middle, :width], returned[middle:] + front[middle:, :width])
-    (later,) = hold((sent[1],), first[:2])
-    returned = over_frames(later).reshape(tokens, width)
-    total = project_all("early", TMAX * HD, early, w_own, w_others)
-    (rest,) = hold((front,), (*first[2:], total))
-    last = ring(returned[:middle] + rest[:middle, width:], returned[middle:] + rest[middle:, width:])
+    sent = [temporal(head_class, arrived, part * half, half, (*early[1:3], w_others)) for part in range(2)]
+
+    returned = over_frames(sent[0])
+    (later,) = hold((sent[1],), (returned,))
+    (returned,) = hold((returned,), (later,))
+    first = ring(returned.reshape(tokens, width))
+    total = project_all("early", 0, early, w_own, w_others)
+    returned = over_frames(later)
+    (returned,) = hold((returned,), (*first[1:], total))
+    last = ring(returned.reshape(tokens, width))
 
     total = project_all("first", 0, first, w_own, w_others, total)
     return project_last(width, last, w_own, w_others, total)

time: 171 us -> 183 us (1.070)
  waiting for transfers between devices: 41.2 us -> 60.2 us
  starting transfers between devices: 59 us -> 53.7 us
  Pallas kernels: 43.6 us -> 46.8 us
  other arithmetic: 11.3 us -> 8.4 us
    ppermute x21 -> x15, waiting for transfers between devices: 17.7 us -> 53 us  [shifted(): lax.ppermute(block, 'head', [(at, (at + by) % count) for at in range(coun...]
    all_to_all x3, waiting for transfers between devices: 23.5 us -> 6.42 us  [over_frames(): return lax.all_to_all(blocks, 'seq', 0, 0, axis_index_groups=groups)]
    ppermute x21 -> x15, starting transfers between devices: 33.7 us -> 25.9 us  [shifted(): lax.ppermute(block, 'head', [(at, (at + by) % count) for at in range(coun...]
    pallas_call x3, Pallas kernels: 7.68 us -> 13.5 us  [summing(): pl.pallas_call(kernel, in_specs=[whole] * len(operands), out_specs=whole,...]
    unnamed x30 -> x12, local copies, waits for them, and re-layouts: 10.6 us -> 6.06 us
    pallas_call x1, Pallas kernels: 17.5 us -> 14.1 us  [spatial(): pl.pallas_call(functools.partial(spatial_kernel, head_count), grid_spec=p...]
    slice x3 -> x6, local copies, waits for them, and re-layouts: 2.95 us -> 6.12 us  [the longest x3 3.06 us: ring(): right[:half]]
    add x2 -> x0, other arithmetic: 3 us -> none  [the longest x1 1.91 us: body(): returned[middle:] + front[middle:, :width]]
  transfers between devices with their start and end apart: 27 -> 21, of which waited for: 10 -> 8; matrix products, arithmetic and copies ran while one was open for 5% -> 8% of each run, Pallas kernels for 20% -> 20%
where the time goes in v8:
time: 183 us; the launch traced here: 182 us
  waiting for transfers between devices  60.2 us (33%)
  starting transfers between devices  53.7 us (29%)
  Pallas kernels  46.8 us (26%)
  local copies, waits for them, and re-layouts  12.2 us (7%)
  other arithmetic  8.4 us (5%)
    ppermute x15, waiting for transfers between devices, shifted(): lax.ppermute(block, 'head', [(at, (at + by) % count) for at in range(coun...  53 us
    all_to_all x3, starting transfers between devices, over_frames(): return lax.all_to_all(blocks, 'seq', 0, 0, axis_index_groups=groups)  27.2 us
    ppermute x15, starting transfers between devices, shifted(): lax.ppermute(block, 'head', [(at, (at + by) % count) for at in range(coun...  25.9 us
    pallas_call x1, Pallas kernels, spatial(): pl.pallas_call(functools.partial(spatial_kernel, head_count), grid_spec=p...  14.1 us
    pallas_call x3, Pallas kernels, summing(): pl.pallas_call(kernel, in_specs=[whole] * len(operands), out_specs=whole,...  13.5 us
    pallas_call x1, Pallas kernels, weight_blocks(): pl.pallas_call(weight_kernel, grid_spec=pltpu.PrefetchScalarGridSpec(num_...  6.46 us
    all_to_all x3, waiting for transfers between devices, over_frames(): return lax.all_to_all(blocks, 'seq', 0, 0, axis_index_groups=groups)  6.42 us
    unnamed x12, local copies, waits for them, and re-layouts  6.06 us
  transfers between devices with their start and end apart: 21, of which 8 were waited for; matrix products, arithmetic and copies ran while one was open for 8% of the time, Pallas kernels for 20%

profile of v8, /device:TPU:8, one launch (start us, length us, event | category | flops | bytes accessed | tf_op | source)
XLA Modules:
  0.0 181.5 jit_solution(14257233605548099765)
XLA Ops:
  0.0 5.2 %pack.1 = bf16[1024,1536]{1,0:T(8,128)(2,1)} custom-call(s32[6]{0:T(128)} %classes.9, bf16[1024,768]{1,0:T(8,128)(2,1)} %query.3, bf16[1024,768]{1,0:T(8,128)(2,1)} %key.3, bf16[1024,768]{1,0:T(8,128)(2,1)} %value.3, f32[1,128]{1,0:T(1,128)} %bitcast.11, f32[1,128]{1,0:T(1,128)} %bitcast.13), custom_call_target="tpu_custom_call" | custom-call | flops 4194304 | bytes 6291456 | tf_op jit(solution)/shard_map/pack/pallas_call | solution.py:105
  5.2 11.7 %all-to-all-start = ((bf16[32,32,1536]{2,1,0:T(8,128)(2,1)}), bf16[32,32,1536]{2,1,0:T(8,128)(2,1)S(1)}, u32[]{:S(2)}, u32[]{:S(2)}) async-start(bf16[32,32,1536]{2,1,0:T(8,128)(2,1)} %bitcast.10), calls=%async_computation | async-start | bytes 6291456 | tf_op jit(solution)/shard_map/all_to_all | solution.py:361
  18.1 6.5 %weight_blocks.1 = (bf16[768,768]{1,0:T(8,128)(2,1)}, bf16[384,768]{1,0:T(8,128)(2,1)}, bf16[384,768]{1,0:T(8,128)(2,1)}, bf16[384,768]{1,0:T(8,128)(2,1)}) custom-call(s32[6]{0:T(128)} %classes.9, s32[2]{0:T(128)} %pad_add_fusion.place, bf16[768,3072]{1,0:T(8,128)(2,1)} %weight.1), custom_call_target="tpu_custom_call" | custom-call | bytes 9437184 | tf_op jit(solution)/shard_map/weight_blocks/pallas_call | solution.py:255
  26.1 2.7 %collective-permute-start.5 = (bf16[384,768]{1,0:T(8,128)(2,1)}, bf16[384,768]{1,0:T(8,128)(2,1)}, u32[]{:S(2)}, u32[]{:S(2)}) collective-permute-start(bf16[384,768]{1,0:T(8,128)(2,1)} %get-tuple-element.13.refs_2_), channel_id=1, source_target_pairs={{0,2},{1,3},{2,0},{3,1},{4,6},{5,7},{6,4},{7,5},{8,10},{9,11},{10,... | collective-permute-start | bytes 1769480 | tf_op jit(solution)/shard_map/ppermute | solution.py:344
  30.3 14.1 %spatial.1.refs_3_.own = bf16[1024,768]{1,0:T(8,128)(2,1)} custom-call(s32[6]{0:T(128)} %classes.9, bf16[1024,768]{1,0:T(8,128)(2,1)} %query.3, bf16[1024,768]{1,0:T(8,128)(2,1)} %key.3, bf16[1024,768]{1,0:T(8,128)(2,1)} %hold.5.other_key, bf16[1024,768]{1,0:T(8,128)(2,1)} %value.3, bf16[1024,768]{1,0:T(8,128)(2,1)} %collective-permute-done.1.other_value, ...), custom_call_target="tpu_custom_call" | custom-call | flops 12884901888 | bytes 9437184 | tf_op jit(solution)/shard_map/spatial/pallas_call | solution.py:162
  44.3 10.5 %collective-permute-done.5.refs_1_ = bf16[384,768]{1,0:T(8,128)(2,1)} collective-permute-done((bf16[384,768]{1,0:T(8,128)(2,1)}, bf16[384,768]{1,0:T(8,128)(2,1)}, u32[]{:S(2)}, u32[]{:S(2)}) %collective-permute-start.5) | collective-permute-done | bytes 589856 | tf_op jit(solution)/shard_map/ppermute | solution.py:344
  54.8 2.8 %pad_maximum_fusion = bf16[3,384,768]{2,1,0:T(8,128)(2,1)} fusion(bf16[1,384,768]{2,1,0:T(8,128)(2,1)} %bitcast.7, bf16[1,384,768]{2,1,0:T(8,128)(2,1)} %bitcast.6, bf16[1,384,768]{2,1,0:T(8,128)(2,1)} %bitcast.5), kind=kLoop, calls=%fused_computation.1 | loop fusion | flops 1769472 | bytes 3538944 | tf_op jit(solution)/shard_map/stack | solution.py:380
  61.7 4.9 %maximum_select_fusion.rest_2_.w_others = bf16[3,768,768]{2,1,0:T(8,128)(2,1)} fusion(bf16[3,384,768]{2,1,0:T(8,128)(2,1)} %collective-permute-done.7, bf16[1,384,768]{2,1,0:T(8,128)(2,1)} %bitcast.7, bf16[1,384,768]{2,1,0:T(8,128)(2,1)} %bitcast.6, bf16[1,384,768]{2,1,0:T(8,128)(2,1)} %bitcast.5, pred[]{:T(512)S(6)} %eq.3), kind=kLoop, calls=%fused_computation | loop fusion | flops 30081024 | bytes 7077889 | tf_op jit(solution)/shard_map/jit(_where)/select_n | solution.py:382
  66.6 29.4 %collective-permute-done.2.rest_0_.right = bf16[1024,768]{1,0:T(8,128)(2,1)} collective-permute-done((bf16[1024,768]{1,0:T(8,128)(2,1)}, bf16[1024,768]{1,0:T(8,128)(2,1)}, u32[]{:S(2)}, u32[]{:S(2)}) %collective-permute-start.2) | collective-permute-done | bytes 1572896 | tf_op jit(solution)/shard_map/ppermute | solution.py:344
  96.0 3.0 %temporal.3 = bf16[32,32,256]{2,1,0:T(8,128)(2,1)} custom-call(s32[6]{0:T(128)S(1)} %copy-done.3, bf16[32,32,1536]{2,1,0:T(8,128)(2,1)S(1)} %all-to-all-done.packed, bf16[1024,768]{1,0:T(8,128)(2,1)} %collective-permute-done.2.rest_0_.right, bf16[1024,768]{1,0:T(8,128)(2,1)} %collective-permute-done.3.rest_1_.left, ...), custom_call_target="tpu_custom_call" | custom-call | flops 536870912 | bytes 2097152 | tf_op jit(solution)/shard_map/temporal/pallas_call | solution.py:211
  99.0 9.8 %all-to-all-start.1 = ((bf16[32,32,256]{2,1,0:T(8,128)(2,1)}), bf16[32,32,256]{2,1,0:T(8,128)(2,1)}, u32[]{:S(2)}, u32[]{:S(2)}) async-start(bf16[32,32,256]{2,1,0:T(8,128)(2,1)} %temporal.3), calls=%async_computation.1 | async-start | bytes 1048576 | tf_op jit(solution)/shard_map/all_to_all | solution.py:361
  113.4 2.9 %collective-permute-start.13 = (bf16[512,768]{1,0:T(8,128)(2,1)}, bf16[512,768]{1,0:T(8,128)(2,1)}, u32[]{:S(2)}, u32[]{:S(2)}) collective-permute-start(bf16[512,768]{1,0:T(8,128)(2,1)} %slice.27), channel_id=1, source_target_pairs={{0,3},{1,0},{2,1},{3,2},{4,7},{5,4},{6,5},{7,6},{8,11},{9,8},{10,9... | collective-permute-start | bytes 2359304 | tf_op jit(solution)/shard_map/ppermute | solution.py:344
  116.3 3.0 %temporal.2.refs_0_ = bf16[32,32,256]{2,1,0:T(8,128)(2,1)} custom-call(s32[6]{0:T(128)S(1)} %copy-done.3, bf16[32,32,1536]{2,1,0:T(8,128)(2,1)S(1)} %all-to-all-done.packed, bf16[1024,768]{1,0:T(8,128)(2,1)} %collective-permute-done.2.rest_0_.right, bf16[1024,768]{1,0:T(8,128)(2,1)} %collective-permute-done.3.rest_1_.left, ...), custom_call_target="tpu_custom_call" | custom-call | flops 536870912 | bytes 2097152 | tf_op jit(solution)/shard_map/temporal/pallas_call | solution.py:211
  119.2 6.4 %all-to-all-done.1.refs_1_.refs_0_ = bf16[32,32,256]{2,1,0:T(8,128)(2,1)} async-done(((bf16[32,32,256]{2,1,0:T(8,128)(2,1)}), bf16[32,32,256]{2,1,0:T(8,128)(2,1)}, u32[]{:S(2)}, u32[]{:S(2)}) %all-to-all-start.1) | async-done | bytes 524320 | tf_op jit(solution)/shard_map/all_to_all | solution.py:361
  125.7 3.2 %collective-permute-start.9 = (bf16[1024,256]{1,0:T(8,128)(2,1)}, bf16[1024,256]{1,0:T(8,128)(2,1)}, u32[]{:S(2)}, u32[]{:S(2)}) collective-permute-start(bf16[1024,256]{1,0:T(8,128)(2,1)} %bitcast.8.own), channel_id=1, source_target_pairs={{0,3},{1,0},{2,1},{3,2},{4,7},{5,4},{6,5},{7,6},{8,11},{9,8},{10,9... | collective-permute-start | bytes 1572872 | tf_op jit(solution)/shard_map/ppermute | solution.py:344
  128.9 5.6 %all-to-all-start.2 = ((bf16[32,32,256]{2,1,0:T(8,128)(2,1)}), bf16[32,32,256]{2,1,0:T(8,128)(2,1)}, u32[]{:S(2)}, u32[]{:S(2)}) async-start(bf16[32,32,256]{2,1,0:T(8,128)(2,1)} %hold.7.refs_1_), calls=%async_computation.2 | async-start | bytes 1048576 | tf_op jit(solution)/shard_map/all_to_all | solution.py:361
  134.5 7.8 %collective-permute-done.8.refs_1_.right = bf16[1024,256]{1,0:T(8,128)(2,1)} collective-permute-done((bf16[1024,256]{1,0:T(8,128)(2,1)}, bf16[1024,256]{1,0:T(8,128)(2,1)}, u32[]{:S(2)}, u32[]{:S(2)}) %collective-permute-start.8) | collective-permute-done | bytes 524320 | tf_op jit(solution)/shard_map/ppermute | solution.py:344
  144.6 3.8 %collective-permute-start.11 = (bf16[512,256]{1,0:T(8,128)(2,1)S(1)}, bf16[512,256]{1,0:T(8,128)(2,1)}, u32[]{:S(2)}, u32[]{:S(2)}) collective-permute-start(bf16[512,256]{1,0:T(8,128)(2,1)S(1)} %slice.25), channel_id=1, source_target_pairs={{0,3},{1,0},{2,1},{3,2},{4,7},{5,4},{6,5},{7,6},{8,11},{9,8},{10,9... | collective-permute-start | bytes 786440 | tf_op jit(solution)/shard_map/ppermute | solution.py:344
  149.7 7.8 %early.1.refs_5_.rest_0_ = f32[1024,768]{1,0:T(8,128)S(1)} custom-call(bf16[1024,768]{1,0:T(8,128)(2,1)} %spatial.1.refs_3_.own, bf16[1024,768]{1,0:T(8,128)(2,1)} %collective-permute-done.2.rest_0_.right, bf16[1024,768]{1,0:T(8,128)(2,1)} %collective-permute-done.3.rest_1_.left, bf16[512,768]{1,0:T(8,128)(2,1)} %collective-permute-done.12.far_top, ...), custom_call_target="tpu_custom_call" | custom-call | flops 48318382080 | bytes 6291456 | tf_op jit(solution)/shard_map/early/pallas_call | solution.py:307
  159.3 3.2 %collective-permute-start.16 = (bf16[1024,256]{1,0:T(8,128)(2,1)}, bf16[1024,256]{1,0:T(8,128)(2,1)S(1)}, u32[]{:S(2)}, u32[]{:S(2)}) collective-permute-start(bf16[1024,256]{1,0:T(8,128)(2,1)} %bitcast.9.own), channel_id=1, source_target_pairs={{0,3},{1,0},{2,1},{3,2},{4,7},{5,4},{6,5},{7,6},{8,11},{9,8},{10,9... | collective-permute-start | bytes 1572872 | tf_op jit(solution)/shard_map/ppermute | solution.py:344
  165.6 3.3 %first.1.total = f32[1024,768]{1,0:T(8,128)S(1)} custom-call(bf16[1024,256]{1,0:T(8,128)(2,1)} %bitcast.8.own, bf16[1024,256]{1,0:T(8,128)(2,1)} %collective-permute-done.8.refs_1_.right, bf16[1024,256]{1,0:T(8,128)(2,1)} %collective-permute-done.9.refs_2_.left, bf16[512,256]{1,0:T(8,128)(2,1)} %collective-permute-done.10.refs_3_.far_top, ...), custom_call_target="tpu_custom_call" | custom-call | flops 16106127360 | bytes 6291456 | tf_op jit(solution)/shard_map/first/pallas_call | solution.py:307
  169.0 3.2 %collective-permute-done.14.right = bf16[1024,256]{1,0:T(8,128)(2,1)S(1)} collective-permute-done((bf16[1024,256]{1,0:T(8,128)(2,1)}, bf16[1024,256]{1,0:T(8,128)(2,1)S(1)}, u32[]{:S(2)}, u32[]{:S(2)}) %collective-permute-start.14) | collective-permute-done | bytes 524320 | tf_op jit(solution)/shard_map/ppermute | solution.py:344
  172.3 3.3 %collective-permute-start.17 = (bf16[512,256]{1,0:T(8,128)(2,1)S(1)}, bf16[512,256]{1,0:T(8,128)(2,1)S(1)}, u32[]{:S(2)}, u32[]{:S(2)}) collective-permute-start(bf16[512,256]{1,0:T(8,128)(2,1)S(1)} %slice.29), channel_id=1, source_target_pairs={{0,3},{1,0},{2,1},{3,2},{4,7},{5,4},{6,5},{7,6},{8,11},{9,8},{10,9... | collective-permute-start | bytes 786440 | tf_op jit(solution)/shard_map/ppermute | solution.py:344
  175.6 2.4 %near.1.total = f32[1024,768]{1,0:T(8,128)S(1)} custom-call(bf16[1024,256]{1,0:T(8,128)(2,1)} %bitcast.9.own, bf16[1024,256]{1,0:T(8,128)(2,1)S(1)} %collective-permute-done.14.right, bf16[1024,256]{1,0:T(8,128)(2,1)S(1)} %collective-permute-done.16.left, bf16[768,768]{1,0:T(8,128)(2,1)S(1)} %copy-done.5, bf16[3,768,768]{2,1,0:T(8,128)(2,1)S(1)} %copy-done, ...), custom_call_target="tpu_custom_call" | custom-call | flops 12079595520 | bytes 6291456 | tf_op jit(solution)/shard_map/near/pallas_call | solution.py:307
  (53 shorter events, 24.8 us)
Async XLA Ops:
  5.2 90.9 %all-to-all-start = ((bf16[32,32,1536]{2,1,0:T(8,128)(2,1)}), bf16[32,32,1536]{2,1,0:T(8,128)(2,1)S(1)}, u32[]{:S(2)}, u32[]{:S(2)}) async-start(bf16[32,32,1536]{2,1,0:T(8,128)(2,1)} %bitcast.10), calls=%async_computation | async-start | bytes 6291456 | tf_op jit(solution)/shard_map/all_to_all | solution.py:361
  16.9 13.4 %collective-permute-start = (bf16[1024,768]{1,0:T(8,128)(2,1)}, bf16[1024,768]{1,0:T(8,128)(2,1)}, u32[]{:S(2)}, u32[]{:S(2)}) collective-permute-start(bf16[1024,768]{1,0:T(8,128)(2,1)} %key.3), channel_id=1, source_target_pairs={{0,4},{4,0},{8,12},{12,8},{16,20},{20,16},{24,28},{28,24},{32,36},... | collective-permute-start | bytes 4718600 | tf_op jit(solution)/shard_map/ppermute | solution.py:355
  17.0 13.3 %collective-permute-start.1 = (bf16[1024,768]{1,0:T(8,128)(2,1)}, bf16[1024,768]{1,0:T(8,128)(2,1)}, u32[]{:S(2)}, u32[]{:S(2)}) collective-permute-start(bf16[1024,768]{1,0:T(8,128)(2,1)} %value.3), channel_id=1, source_target_pairs={{0,4},{4,0},{8,12},{12,8},{16,20},{20,16},{24,28},{28,24},{32,36},... | collective-permute-start | bytes 4718600 | tf_op jit(solution)/shard_map/ppermute | solution.py:355
  24.6 19.7 %collective-permute-start.4 = (bf16[384,768]{1,0:T(8,128)(2,1)}, bf16[384,768]{1,0:T(8,128)(2,1)}, u32[]{:S(2)}, u32[]{:S(2)}) collective-permute-start(bf16[384,768]{1,0:T(8,128)(2,1)} %get-tuple-element.12.refs_1_), channel_id=1, source_target_pairs={{0,1},{1,2},{2,3},{3,0},{4,5},{5,6},{6,7},{7,4},{8,9},{9,10},{10,1... | collective-permute-start | bytes 1769480 | tf_op jit(solution)/shard_map/ppermute | solution.py:344
  26.1 28.7 %collective-permute-start.5 = (bf16[384,768]{1,0:T(8,128)(2,1)}, bf16[384,768]{1,0:T(8,128)(2,1)}, u32[]{:S(2)}, u32[]{:S(2)}) collective-permute-start(bf16[384,768]{1,0:T(8,128)(2,1)} %get-tuple-element.13.refs_2_), channel_id=1, source_target_pairs={{0,2},{1,3},{2,0},{3,1},{4,6},{5,7},{6,4},{7,5},{8,10},{9,11},{10,... | collective-permute-start | bytes 1769480 | tf_op jit(solution)/shard_map/ppermute | solution.py:344
  28.8 26.0 %collective-permute-start.6 = (bf16[384,768]{1,0:T(8,128)(2,1)}, bf16[384,768]{1,0:T(8,128)(2,1)}, u32[]{:S(2)}, u32[]{:S(2)}) collective-permute-start(bf16[384,768]{1,0:T(8,128)(2,1)} %get-tuple-element.14.refs_3_), channel_id=1, source_target_pairs={{0,3},{1,0},{2,1},{3,2},{4,7},{5,4},{6,5},{7,6},{8,11},{9,8},{10,9... | collective-permute-start | bytes 1769480 | tf_op jit(solution)/shard_map/ppermute | solution.py:344
  57.7 4.0 %collective-permute-start.7 = (bf16[3,384,768]{2,1,0:T(8,128)(2,1)}, bf16[3,384,768]{2,1,0:T(8,128)(2,1)}, u32[]{:S(2)}, u32[]{:S(2)}) collective-permute-start(bf16[3,384,768]{2,1,0:T(8,128)(2,1)} %pad_maximum_fusion), channel_id=1, source_target_pairs={{0,4},{4,0},{8,12},{12,8},{16,20},{20,16},{24,28},{28,24},{32,36},... | collective-permute-start | bytes 5308424 | tf_op jit(solution)/shard_map/ppermute | solution.py:355
  57.7 38.3 %collective-permute-start.2 = (bf16[1024,768]{1,0:T(8,128)(2,1)}, bf16[1024,768]{1,0:T(8,128)(2,1)}, u32[]{:S(2)}, u32[]{:S(2)}) collective-permute-start(bf16[1024,768]{1,0:T(8,128)(2,1)} %spatial.1.refs_3_.own), channel_id=1, source_target_pairs={{0,1},{1,2},{2,3},{3,0},{4,5},{5,6},{6,7},{7,4},{8,9},{9,10},{10,1... | collective-permute-start | bytes 4718600 | tf_op jit(solution)/shard_map/ppermute | solution.py:344
  59.0 37.0 %collective-permute-start.3 = (bf16[1024,768]{1,0:T(8,128)(2,1)}, bf16[1024,768]{1,0:T(8,128)(2,1)}, u32[]{:S(2)}, u32[]{:S(2)}) collective-permute-start(bf16[1024,768]{1,0:T(8,128)(2,1)} %spatial.1.refs_3_.own), channel_id=1, source_target_pairs={{0,3},{1,0},{2,1},{3,2},{4,7},{5,4},{6,5},{7,6},{8,11},{9,8},{10,9... | collective-permute-start | bytes 4718600 | tf_op jit(solution)/shard_map/ppermute | solution.py:344
  60.9 35.1 %copy-start.3 = (s32[6]{0:T(128)S(1)}, s32[6]{0:T(128)}, u32[]{:S(2)}) copy-start(s32[6]{0:T(128)} %classes.9) | copy-start | bytes 76
  99.0 26.6 %all-to-all-start.1 = ((bf16[32,32,256]{2,1,0:T(8,128)(2,1)}), bf16[32,32,256]{2,1,0:T(8,128)(2,1)}, u32[]{:S(2)}, u32[]{:S(2)}) async-start(bf16[32,32,256]{2,1,0:T(8,128)(2,1)} %temporal.3), calls=%async_computation.1 | async-start | bytes 1048576 | tf_op jit(solution)/shard_map/all_to_all | solution.py:361
  110.9 37.5 %collective-permute-start.12 = (bf16[512,768]{1,0:T(8,128)(2,1)}, bf16[512,768]{1,0:T(8,128)(2,1)}, u32[]{:S(2)}, u32[]{:S(2)}) collective-permute-start(bf16[512,768]{1,0:T(8,128)(2,1)} %slice.26), channel_id=1, source_target_pairs={{0,1},{1,2},{2,3},{3,0},{4,5},{5,6},{6,7},{7,4},{8,9},{9,10},{10,1... | collective-permute-start | bytes 2359304 | tf_op jit(solution)/shard_map/ppermute | solution.py:344
  113.4 35.1 %collective-permute-start.13 = (bf16[512,768]{1,0:T(8,128)(2,1)}, bf16[512,768]{1,0:T(8,128)(2,1)}, u32[]{:S(2)}, u32[]{:S(2)}) collective-permute-start(bf16[512,768]{1,0:T(8,128)(2,1)} %slice.27), channel_id=1, source_target_pairs={{0,3},{1,0},{2,1},{3,2},{4,7},{5,4},{6,5},{7,6},{8,11},{9,8},{10,9... | collective-permute-start | bytes 2359304 | tf_op jit(solution)/shard_map/ppermute | solution.py:344
  119.2 29.2 %copy-start = (bf16[3,768,768]{2,1,0:T(8,128)(2,1)S(1)}, bf16[3,768,768]{2,1,0:T(8,128)(2,1)}, u32[]{:S(2)}) copy-start(bf16[3,768,768]{2,1,0:T(8,128)(2,1)} %maximum_select_fusion.rest_2_.w_others) | copy-start | bytes 10616836
  125.6 16.7 %collective-permute-start.8 = (bf16[1024,256]{1,0:T(8,128)(2,1)}, bf16[1024,256]{1,0:T(8,128)(2,1)}, u32[]{:S(2)}, u32[]{:S(2)}) collective-permute-start(bf16[1024,256]{1,0:T(8,128)(2,1)} %bitcast.8.own), channel_id=1, source_target_pairs={{0,1},{1,2},{2,3},{3,0},{4,5},{5,6},{6,7},{7,4},{8,9},{9,10},{10,1... | collective-permute-start | bytes 1572872 | tf_op jit(solution)/shard_map/ppermute | solution.py:344
  125.7 18.0 %collective-permute-start.9 = (bf16[1024,256]{1,0:T(8,128)(2,1)}, bf16[1024,256]{1,0:T(8,128)(2,1)}, u32[]{:S(2)}, u32[]{:S(2)}) collective-permute-start(bf16[1024,256]{1,0:T(8,128)(2,1)} %bitcast.8.own), channel_id=1, source_target_pairs={{0,3},{1,0},{2,1},{3,2},{4,7},{5,4},{6,5},{7,6},{8,11},{9,8},{10,9... | collective-permute-start | bytes 1572872 | tf_op jit(solution)/shard_map/ppermute | solution.py:344
  128.9 30.3 %all-to-all-start.2 = ((bf16[32,32,256]{2,1,0:T(8,128)(2,1)}), bf16[32,32,256]{2,1,0:T(8,128)(2,1)}, u32[]{:S(2)}, u32[]{:S(2)}) async-start(bf16[32,32,256]{2,1,0:T(8,128)(2,1)} %hold.7.refs_1_), calls=%async_computation.2 | async-start | bytes 1048576 | tf_op jit(solution)/shard_map/all_to_all | solution.py:361
  143.3 15.9 %collective-permute-start.10 = (bf16[512,256]{1,0:T(8,128)(2,1)S(1)}, bf16[512,256]{1,0:T(8,128)(2,1)}, u32[]{:S(2)}, u32[]{:S(2)}) collective-permute-start(bf16[512,256]{1,0:T(8,128)(2,1)S(1)} %slice.24), channel_id=1, source_target_pairs={{0,1},{1,2},{2,3},{3,0},{4,5},{5,6},{6,7},{7,4},{8,9},{9,10},{10,1... | collective-permute-start | bytes 786440 | tf_op jit(solution)/shard_map/ppermute | solution.py:344
  144.6 14.5 %collective-permute-start.11 = (bf16[512,256]{1,0:T(8,128)(2,1)S(1)}, bf16[512,256]{1,0:T(8,128)(2,1)}, u32[]{:S(2)}, u32[]{:S(2)}) collective-permute-start(bf16[512,256]{1,0:T(8,128)(2,1)S(1)} %slice.25), channel_id=1, source_target_pairs={{0,3},{1,0},{2,1},{3,2},{4,7},{5,4},{6,5},{7,6},{8,11},{9,8},{10,9... | collective-permute-start | bytes 786440 | tf_op jit(solution)/shard_map/ppermute | solution.py:344
  159.2 13.0 %collective-permute-start.14 = (bf16[1024,256]{1,0:T(8,128)(2,1)}, bf16[1024,256]{1,0:T(8,128)(2,1)S(1)}, u32[]{:S(2)}, u32[]{:S(2)}) collective-permute-start(bf16[1024,256]{1,0:T(8,128)(2,1)} %bitcast.9.own), channel_id=1, source_target_pairs={{0,1},{1,2},{2,3},{3,0},{4,5},{5,6},{6,7},{7,4},{8,9},{9,10},{10,1... | collective-permute-start | bytes 1572872 | tf_op jit(solution)/shard_map/ppermute | solution.py:344
  159.3 13.0 %collective-permute-start.16 = (bf16[1024,256]{1,0:T(8,128)(2,1)}, bf16[1024,256]{1,0:T(8,128)(2,1)S(1)}, u32[]{:S(2)}, u32[]{:S(2)}) collective-permute-start(bf16[1024,256]{1,0:T(8,128)(2,1)} %bitcast.9.own), channel_id=1, source_target_pairs={{0,3},{1,0},{2,1},{3,2},{4,7},{5,4},{6,5},{7,6},{8,11},{9,8},{10,9... | collective-permute-start | bytes 1572872 | tf_op jit(solution)/shard_map/ppermute | solution.py:344
  162.5 1.9 %copy-start.2 = (f32[1024,768]{1,0:T(8,128)S(1)}, f32[1024,768]{1,0:T(8,128)}, u32[]{:S(2)}) copy-start(f32[1024,768]{1,0:T(8,128)} %copy-done.1) | copy-start | bytes 9437188
  172.2 7.7 %collective-permute-start.15 = (bf16[512,256]{1,0:T(8,128)(2,1)S(1)}, bf16[512,256]{1,0:T(8,128)(2,1)S(1)}, u32[]{:S(2)}, u32[]{:S(2)}) collective-permute-start(bf16[512,256]{1,0:T(8,128)(2,1)S(1)} %slice.28), channel_id=1, source_target_pairs={{0,1},{1,2},{2,3},{3,0},{4,5},{5,6},{6,7},{7,4},{8,9},{9,10},{10,1... | collective-permute-start | bytes 786440 | tf_op jit(solution)/shard_map/ppermute | solution.py:344
  172.3 7.5 %collective-permute-start.17 = (bf16[512,256]{1,0:T(8,128)(2,1)S(1)}, bf16[512,256]{1,0:T(8,128)(2,1)S(1)}, u32[]{:S(2)}, u32[]{:S(2)}) collective-permute-start(bf16[512,256]{1,0:T(8,128)(2,1)S(1)} %slice.29), channel_id=1, source_target_pairs={{0,3},{1,0},{2,1},{3,2},{4,7},{5,4},{6,5},{7,6},{8,11},{9,8},{10,9... | collective-permute-start | bytes 786440 | tf_op jit(solution)/shard_map/ppermute | solution.py:344
  (3 other events, 4.2 us)

commit v9 on v4

--- a/solution.py
+++ b/solution.py
@@ -12,6 +12,7 @@
 TMAX = 4
 SMALL_VMEM = 16 * 1024 * 1024
 CORES = 2
+ROWS = 8
 HD = 128
 EPSILON = 1e-06
 LOG2_SCALE = math.log2(math.e) / math.sqrt(HD)
@@ -195,30 +196,45 @@
 
 
 def temporal_kernel(head_count, classes, packed, *rest):
-    out = rest[-1]
-    slot = pl.program_id(0)
+    out, held, sems = rest[-3:]
     frames, positions, _ = packed.shape
-    places = 16
-    count = frames * places
-
-    @pl.when(slot < temporal_count(classes, head_count))
-    def _():
-        row = lax.broadcasted_iota(jnp.int32, (count, count), 0)
-        column = lax.broadcasted_iota(jnp.int32, (count, count), 1)
-        same = (row & (places - 1)) == (column & (places - 1))
-        base = pl.multiple_of(slot * 3 * HD, HD)
-        for part in range(positions // places):
-            at = slice(part * places, (part + 1) * places)
-            queries, keys, values = (packed[:, at, pl.ds(base + which * HD, HD)].reshape(count, HD) for which in range(3))
-            scaled = jnp.where(same, scores_of(queries, keys) * LOG2_SCALE, -1e30)
-            weights = jnp.exp2(scaled).astype(jnp.bfloat16)
-            both = jnp.concatenate([values, jnp.ones_like(values)], axis=1)
-            summed = jnp.dot(weights, both, preferred_element_type=jnp.float32)
-            out[:, at, :] = (summed[:, :HD] / summed[:, HD:]).astype(jnp.bfloat16).reshape(frames, places, HD)
-
-    @pl.when(slot >= temporal_count(classes, head_count))
-    def _():
-        out[...] = jnp.zeros_like(out)
+    count = frames * ROWS
+    row = lax.broadcasted_iota(jnp.int32, (count, count), 0)
+    column = lax.broadcasted_iota(jnp.int32, (count, count), 1)
+    same = (row & (ROWS - 1)) == (column & (ROWS - 1))
+    total = temporal_count(classes, head_count)
+
+    def attend(queries, keys, values):
+        exponents = jnp.where(same, scores_of(queries, keys) * LOG2_SCALE, -1e30)
+        weights = jnp.exp2(exponents).astype(jnp.bfloat16)
+        both = jnp.concatenate([values, jnp.ones_like(values)], axis=1)
+        summed = jnp.dot(weights, both, preferred_element_type=jnp.float32)
+        return (summed[:, :HD] / summed[:, HD:]).reshape(frames, ROWS, HD)
+
+    def store(slot):
+        return pltpu.make_async_copy(held.at[slot], out.at[:, :, pl.ds(slot * HD, HD)], sems.at[slot])
+
+    for slot in range(TMAX):
+
+        @pl.when(slot < total)
+        def _(slot=slot):
+            for begin in range(0, positions, 2 * ROWS):
+                at = slice(begin, begin + 2 * ROWS)
+                columns = [slice((3 * slot + which) * HD, (3 * slot + which + 1) * HD) for which in range(3)]
+                wide = [packed[:, at, column].astype(jnp.float32) for column in columns]
+                results = []
+                for first in (0, ROWS):
+                    parts = [array[:, first : first + ROWS].reshape(count, HD).astype(jnp.bfloat16) for array in wide]
+                    results.append(attend(*parts))
+                held[slot, :, at] = jnp.concatenate(results, axis=1).astype(jnp.bfloat16)
+
+        @pl.when(slot >= total)
+        def _(slot=slot):
+            held[slot] = jnp.zeros(held.shape[1:], held.dtype)
+
+        store(slot).start()
+    for slot in range(TMAX):
+        store(slot).wait()
 
 
 def temporal(head_class, packed, after):
@@ -227,16 +243,20 @@
         functools.partial(temporal_kernel, head_class.shape[0]),
         grid_spec=pltpu.PrefetchScalarGridSpec(
             num_scalar_prefetch=1,
-            grid=(TMAX,),
+            grid=(1,),
             in_specs=[pl.BlockSpec(memory_space=pltpu.VMEM)] + [pl.BlockSpec(memory_space=pl.ANY)] * len(after),
-            out_specs=pl.BlockSpec((frames, positions, HD), lambda slot, classes: (0, 0, slot)),
+            out_specs=pl.BlockSpec(memory_space=pl.ANY),
+            scratch_shapes=[
+                pltpu.VMEM((TMAX, frames, positions, HD), jnp.bfloat16),
+                pltpu.SemaphoreType.DMA((TMAX,)),
+            ],
         ),
         out_shape=in_hbm((frames, positions, TMAX * HD), jnp.bfloat16),
         compiler_params=pltpu.CompilerParams(vmem_limit_bytes=SMALL_VMEM),
         cost_estimate=pl.CostEstimate(
-            flops=64 * frames * frames * positions * TMAX * HD,
+            flops=32 * frames * frames * positions * TMAX * HD,
             bytes_accessed=8 * frames * positions * TMAX * HD,
-            transcendentals=16 * frames * frames * positions * TMAX,
+            transcendentals=8 * frames * frames * positions * TMAX,
         ),
         name="temporal",
     )(head_class, from_vmem(packed), *[from_hbm(array) for array in after])
@@ -305,12 +325,18 @@
         out[rows] = total[rows] + near_sum(own, right, left, w_own, w_others, 0)
 
 
-def far_kernel(far_top, far_bottom, w_others, total, out):
-    for part, far in enumerate((far_top, far_bottom)):
-
-        @pl.when(pl.program_id(0) == part)
-        def _(far=far):
-            out[...] = (product(far[...], w_others.at[1], 0) + total[...]).astype(out.dtype)
+def far_kernel(far_top, far_bottom, w_others, total, out, held, sems):
+    steps, rows, _ = held.shape
+    stores = []
+    for step in range(steps):
+        far = (far_top, far_bottom)[2 * step // steps]
+        begin = step * rows % far.shape[0]
+        summed = product(far[begin : begin + rows], w_others.at[1], 0) + total[step * rows : (step + 1) * rows]
+        held[step] = summed.astype(held.dtype)
+        stores.append(pltpu.make_async_copy(held.at[step], out.at[pl.ds(step * rows, rows)], sems.at[step]))
+        stores[-1].start()
+    for store in stores:
+        store.wait()
 
 
 def summing(kernel, name, operands, depth_terms):
@@ -338,15 +364,14 @@
 def project_late(pieces, w_own, w_others, total):
     near = summing(near_kernel, "near", (*pieces[:6], w_own, w_others, total), 3)
     tokens, width = near.shape
-    half, depth = pieces[0].shape
-    whole = pl.BlockSpec(memory_space=pltpu.VMEM)
-    sum_spec = pl.BlockSpec((half, width), lambda step: (step, 0))
+    depth = pieces[0].shape[1]
+    steps = 4
     return pl.pallas_call(
         far_kernel,
-        grid=(2,),
-        in_specs=[whole] * 3 + [sum_spec],
-        out_specs=sum_spec,
+        in_specs=[pl.BlockSpec(memory_space=pltpu.VMEM)] * 4,
+        out_specs=pl.BlockSpec(memory_space=pl.ANY),
         out_shape=in_hbm((tokens, width), jnp.bfloat16),
+        scratch_shapes=[pltpu.VMEM((steps, tokens // steps, width), jnp.bfloat16), pltpu.SemaphoreType.DMA((steps,))],
         compiler_params=pltpu.CompilerParams(vmem_limit_bytes=SMALL_VMEM),
         cost_estimate=pl.CostEstimate(flops=2 * tokens * depth * width, bytes_accessed=8 * tokens * width, transcendentals=0),
         name="far",

time: 167 us -> 165 us (0.988)
  no operation moved by 1% of the time
where the time goes in v9:
time: 165 us
  waiting for transfers between devices  44 us (27%)
  starting transfers between devices  37.5 us (23%)
  Pallas kernels  37 us (22%)
  blocking collectives  35.3 us (21%)
  other arithmetic  8.76 us (5%)
  local copies, waits for them, and re-layouts  1.69 us (1%)
    ppermute x15, waiting for transfers between devices, shifted(): lax.ppermute(block, 'head', [(at, (at + by) % count) for at in range(coun...  36.5 us
    all_to_all x1, blocking collectives, over_frames(): return lax.all_to_all(blocks, 'seq', 0, 0, axis_index_groups=groups)  35.3 us
    ppermute x15, starting transfers between devices, shifted(): lax.ppermute(block, 'head', [(at, (at + by) % count) for at in range(coun...  25.2 us
    pallas_call x1, Pallas kernels, spatial(): pl.pallas_call(functools.partial(spatial_kernel, head_count), grid_spec=p...  14.3 us
    all_to_all x1, starting transfers between devices, over_frames(): return lax.all_to_all(blocks, 'seq', 0, 0, axis_index_groups=groups)  11.7 us
    all_to_all x1, waiting for transfers between devices, over_frames(): return lax.all_to_all(blocks, 'seq', 0, 0, axis_index_groups=groups)  7.48 us
    pallas_call x1, Pallas kernels, weight_blocks(): pl.pallas_call(weight_kernel, grid_spec=pltpu.PrefetchScalarGridSpec(num_...  6.46 us
    pallas_call x2, Pallas kernels, summing(): pl.pallas_call(kernel, in_specs=[whole] * len(operands), out_specs=whole,...  5.75 us
  transfers between devices with their start and end apart: 19, of which 8 were waited for; matrix products, arithmetic and copies ran while one was open for 6% of the time, Pallas kernels for 16%

profile of v9, /device:TPU:8, one launch (start us, length us, event | category | flops | bytes accessed | tf_op | source)
XLA Modules:
  0.0 164.6 jit_solution(15045402073606122426)
XLA Ops:
  0.0 5.2 %pack.1 = bf16[1024,1536]{1,0:T(8,128)(2,1)} custom-call(s32[6]{0:T(128)} %classes.7, bf16[1024,768]{1,0:T(8,128)(2,1)} %query.3, bf16[1024,768]{1,0:T(8,128)(2,1)} %key.3, bf16[1024,768]{1,0:T(8,128)(2,1)} %value.3, f32[1,128]{1,0:T(1,128)} %bitcast.13, f32[1,128]{1,0:T(1,128)} %bitcast.15), custom_call_target="tpu_custom_call" | custom-call | flops 4194304 | bytes 6291456 | tf_op jit(solution)/shard_map/pack/pallas_call | solution.py:105
  5.2 11.7 %all-to-all-start = ((bf16[32,32,1536]{2,1,0:T(8,128)(2,1)}), bf16[32,32,1536]{2,1,0:T(8,128)(2,1)S(1)}, u32[]{:S(2)}, u32[]{:S(2)}) async-start(bf16[32,32,1536]{2,1,0:T(8,128)(2,1)} %bitcast.12), calls=%async_computation | async-start | bytes 6291456 | tf_op jit(solution)/shard_map/all_to_all | solution.py:401
  18.1 6.5 %weight_blocks.1 = (bf16[768,768]{1,0:T(8,128)(2,1)}, bf16[384,768]{1,0:T(8,128)(2,1)}, bf16[384,768]{1,0:T(8,128)(2,1)}, bf16[384,768]{1,0:T(8,128)(2,1)}) custom-call(s32[6]{0:T(128)} %classes.7, s32[2]{0:T(128)} %pad_add_fusion.place, bf16[768,3072]{1,0:T(8,128)(2,1)} %weight.1), custom_call_target="tpu_custom_call" | custom-call | bytes 9437184 | tf_op jit(solution)/shard_map/weight_blocks/pallas_call | solution.py:290
  26.1 2.7 %collective-permute-start.9 = (bf16[384,768]{1,0:T(8,128)(2,1)}, bf16[384,768]{1,0:T(8,128)(2,1)}, u32[]{:S(2)}, u32[]{:S(2)}) collective-permute-start(bf16[384,768]{1,0:T(8,128)(2,1)} %get-tuple-element.16), channel_id=1, source_target_pairs={{0,2},{1,3},{2,0},{3,1},{4,6},{5,7},{6,4},{7,5},{8,10},{9,11},{10,... | collective-permute-start | bytes 1769480 | tf_op jit(solution)/shard_map/ppermute | solution.py:383
  30.3 14.3 %spatial.1 = (bf16[1024,512]{1,0:T(8,128)(2,1)}, bf16[1024,256]{1,0:T(8,128)(2,1)}) custom-call(s32[6]{0:T(128)} %classes.7, bf16[1024,768]{1,0:T(8,128)(2,1)} %query.3, bf16[1024,768]{1,0:T(8,128)(2,1)} %key.3, bf16[1024,768]{1,0:T(8,128)(2,1)} %collective-permute-done.other_key, bf16[1024,768]{1,0:T(8,128)(2,1)} %value.3, ...), custom_call_target="tpu_custom_call" | custom-call | flops 12884901888 | bytes 9437184 | tf_op jit(solution)/shard_map/spatial/pallas_call | solution.py:172
  44.5 10.3 %collective-permute-done.9.refs_1_ = bf16[384,768]{1,0:T(8,128)(2,1)} collective-permute-done((bf16[384,768]{1,0:T(8,128)(2,1)}, bf16[384,768]{1,0:T(8,128)(2,1)}, u32[]{:S(2)}, u32[]{:S(2)}) %collective-permute-start.9) | collective-permute-done | bytes 589856 | tf_op jit(solution)/shard_map/ppermute | solution.py:383
  54.9 2.9 %pad_maximum_fusion = bf16[3,384,768]{2,1,0:T(8,128)(2,1)} fusion(bf16[1,384,768]{2,1,0:T(8,128)(2,1)} %bitcast.7, bf16[1,384,768]{2,1,0:T(8,128)(2,1)} %bitcast.6, bf16[1,384,768]{2,1,0:T(8,128)(2,1)} %bitcast.5), kind=kLoop, calls=%fused_computation.1 | loop fusion | flops 1769472 | bytes 3538944 | tf_op jit(solution)/shard_map/stack | solution.py:419
  59.9 1.9 %collective-permute-start.5 = (bf16[512,256]{1,0:T(8,128)(2,1)}, bf16[512,256]{1,0:T(8,128)(2,1)}, u32[]{:S(2)}, u32[]{:S(2)}) collective-permute-start(bf16[512,256]{1,0:T(8,128)(2,1)} %get-tuple-element.27.own_bottom), channel_id=1, source_target_pairs={{0,3},{1,0},{2,1},{3,2},{4,7},{5,4},{6,5},{7,6},{8,11},{9,8},{10,9... | collective-permute-start | bytes 786440 | tf_op jit(solution)/shard_map/ppermute | solution.py:383
  62.0 3.1 %collective-permute-start.4 = (bf16[512,256]{1,0:T(8,128)(2,1)}, bf16[512,256]{1,0:T(8,128)(2,1)S(1)}, u32[]{:S(2)}, u32[]{:S(2)}) collective-permute-start(bf16[512,256]{1,0:T(8,128)(2,1)} %get-tuple-element.28.own_top), channel_id=1, source_target_pairs={{0,3},{1,0},{2,1},{3,2},{4,7},{5,4},{6,5},{7,6},{8,11},{9,8},{10,9... | collective-permute-start | bytes 786440 | tf_op jit(solution)/shard_map/ppermute | solution.py:383
  65.1 4.0 %collective-permute-done.2.rest_0_.right_top = bf16[512,256]{1,0:T(8,128)(2,1)S(1)} collective-permute-done((bf16[512,256]{1,0:T(8,128)(2,1)}, bf16[512,256]{1,0:T(8,128)(2,1)S(1)}, u32[]{:S(2)}, u32[]{:S(2)}) %collective-permute-start.2) | collective-permute-done | bytes 262176 | tf_op jit(solution)/shard_map/ppermute | solution.py:383
  69.4 3.1 %collective-permute-start.7 = (bf16[512,256]{1,0:T(8,128)(2,1)}, bf16[512,256]{1,0:T(8,128)(2,1)}, u32[]{:S(2)}, u32[]{:S(2)}) collective-permute-start(bf16[512,256]{1,0:T(8,128)(2,1)} %collective-permute-done.5.rest_3_.left_bottom), channel_id=1, source_target_pairs={{0,3},{1,0},{2,1},{3,2},{4,7},{5,4},{6,5},{7,6},{8,11},{9,8},{10,9... | collective-permute-start | bytes 786440 | tf_op jit(solution)/shard_map/ppermute | solution.py:383
  72.5 5.0 %maximum_select_fusion.rest_6_.w_others = bf16[3,768,768]{2,1,0:T(8,128)(2,1)} fusion(bf16[3,384,768]{2,1,0:T(8,128)(2,1)} %collective-permute-done.11, bf16[1,384,768]{2,1,0:T(8,128)(2,1)} %bitcast.7, bf16[1,384,768]{2,1,0:T(8,128)(2,1)} %bitcast.6, bf16[1,384,768]{2,1,0:T(8,128)(2,1)} %bitcast.5, pred[]{:T(512)S(6)} %eq.3), kind=kLoop, calls=%fused_computation | loop fusion | flops 30081024 | bytes 7077889 | tf_op jit(solution)/shard_map/jit(_where)/select_n | solution.py:421
  77.6 2.4 %collective-permute-done.6.rest_4_.far_top = bf16[512,256]{1,0:T(8,128)(2,1)S(1)} collective-permute-done((bf16[512,256]{1,0:T(8,128)(2,1)S(1)}, bf16[512,256]{1,0:T(8,128)(2,1)S(1)}, u32[]{:S(2)}, u32[]{:S(2)}) %collective-permute-start.6) | collective-permute-done | bytes 262176 | tf_op jit(solution)/shard_map/ppermute | solution.py:383
  80.7 7.5 %all-to-all-done.packed = bf16[32,32,1536]{2,1,0:T(8,128)(2,1)S(1)} async-done(((bf16[32,32,1536]{2,1,0:T(8,128)(2,1)}), bf16[32,32,1536]{2,1,0:T(8,128)(2,1)S(1)}, u32[]{:S(2)}, u32[]{:S(2)}) %all-to-all-start) | async-done | bytes 3145760 | tf_op jit(solution)/shard_map/all_to_all | solution.py:401
  88.2 3.6 %temporal.1 = bf16[32,32,512]{2,1,0:T(8,128)(2,1)} custom-call(s32[6]{0:T(128)S(1)} %copy-done.10, bf16[32,32,1536]{2,1,0:T(8,128)(2,1)S(1)} %all-to-all-done.packed, bf16[512,256]{1,0:T(8,128)(2,1)} %copy-done.2, bf16[512,256]{1,0:T(8,128)(2,1)} %copy-done.4, bf16[512,256]{1,0:T(8,128)(2,1)} %copy-done.6, ...), custom_call_target="tpu_custom_call" | custom-call | flops 536870912 | bytes 4194304 | tf_op jit(solution)/shard_map/temporal/pallas_call | solution.py:242
  91.8 35.3 %all_to_all.10 = bf16[32,32,512]{2,1,0:T(8,128)(2,1)S(1)} all-to-all(bf16[32,32,512]{2,1,0:T(8,128)(2,1)} %temporal.1), channel_id=1, replica_groups={{0,8,16,24,32,40,48,56,64,72,80,88,96,104,112,120,128,136,144,152,160,1..., dimensions={0} | all-to-all | bytes 2097152 | tf_op jit(solution)/shard_map/all_to_all | solution.py:401
  128.1 2.6 %collective-permute-start.14 = (bf16[512,512]{1,0:T(8,128)(2,1)S(1)}, bf16[512,512]{1,0:T(8,128)(2,1)S(1)}, u32[]{:S(2)}, u32[]{:S(2)}) collective-permute-start(bf16[512,512]{1,0:T(8,128)(2,1)S(1)} %get-tuple-element.23.own_bottom), channel_id=1, source_target_pairs={{0,3},{1,0},{2,1},{3,2},{4,7},{5,4},{6,5},{7,6},{8,11},{9,8},{10,9... | collective-permute-start | bytes 1572872 | tf_op jit(solution)/shard_map/ppermute | solution.py:383
  130.8 3.2 %collective-permute-start.17 = (bf16[512,512]{1,0:T(8,128)(2,1)S(1)}, bf16[512,512]{1,0:T(8,128)(2,1)S(1)}, u32[]{:S(2)}, u32[]{:S(2)}) collective-permute-start(bf16[512,512]{1,0:T(8,128)(2,1)S(1)} %get-tuple-element.24.own_top), channel_id=1, source_target_pairs={{0,3},{1,0},{2,1},{3,2},{4,7},{5,4},{6,5},{7,6},{8,11},{9,8},{10,9... | collective-permute-start | bytes 1572872 | tf_op jit(solution)/shard_map/ppermute | solution.py:383
  134.0 9.6 %collective-permute-done.12.right_top = bf16[512,512]{1,0:T(8,128)(2,1)S(1)} collective-permute-done((bf16[512,512]{1,0:T(8,128)(2,1)S(1)}, bf16[512,512]{1,0:T(8,128)(2,1)S(1)}, u32[]{:S(2)}, u32[]{:S(2)}) %collective-permute-start.12) | collective-permute-done | bytes 524320 | tf_op jit(solution)/shard_map/ppermute | solution.py:383
  143.6 3.2 %collective-permute-start.15 = (bf16[512,512]{1,0:T(8,128)(2,1)S(1)}, bf16[512,512]{1,0:T(8,128)(2,1)S(1)}, u32[]{:S(2)}, u32[]{:S(2)}) collective-permute-start(bf16[512,512]{1,0:T(8,128)(2,1)S(1)} %collective-permute-done.14.left_bottom), channel_id=1, source_target_pairs={{0,3},{1,0},{2,1},{3,2},{4,7},{5,4},{6,5},{7,6},{8,11},{9,8},{10,9... | collective-permute-start | bytes 1572872 | tf_op jit(solution)/shard_map/ppermute | solution.py:383
  146.9 3.0 %project_early.1.total = f32[1024,768]{1,0:T(8,128)S(1)} custom-call(bf16[512,256]{1,0:T(8,128)(2,1)} %get-tuple-element.28.own_top, bf16[512,256]{1,0:T(8,128)(2,1)} %get-tuple-element.27.own_bottom, bf16[512,256]{1,0:T(8,128)(2,1)S(1)} %copy-done.3, bf16[512,256]{1,0:T(8,128)(2,1)S(1)} %copy-done.5, bf16[512,256]{1,0:T(8,128)(2,1)S(1)} %copy-done.7, ...), custom_call_target="tpu_custom_call" | custom-call | flops 1610612736 | bytes 6291456 | tf_op jit(solution)/shard_map/project_early/pallas_call | solution.py:346
  149.9 4.9 %collective-permute-done.16.right_bottom = bf16[512,512]{1,0:T(8,128)(2,1)S(1)} collective-permute-done((bf16[512,512]{1,0:T(8,128)(2,1)S(1)}, bf16[512,512]{1,0:T(8,128)(2,1)S(1)}, u32[]{:S(2)}, u32[]{:S(2)}) %collective-permute-start.16) | collective-permute-done | bytes 524320 | tf_op jit(solution)/shard_map/ppermute | solution.py:383
  154.8 2.7 %near.1.total = f32[1024,768]{1,0:T(8,128)S(1)} custom-call(bf16[512,512]{1,0:T(8,128)(2,1)S(1)} %get-tuple-element.24.own_top, bf16[512,512]{1,0:T(8,128)(2,1)S(1)} %get-tuple-element.23.own_bottom, bf16[512,512]{1,0:T(8,128)(2,1)S(1)} %collective-permute-done.12.right_top, bf16[512,512]{1,0:T(8,128)(2,1)S(1)} %collective-permute-done.16.right_bottom, ...), custom_call_target="tpu_custom_call" | custom-call | flops 2415919104 | bytes 6291456 | tf_op jit(solution)/shard_map/near/pallas_call | solution.py:346
  157.6 5.1 %collective-permute-done.13.far_top = bf16[512,512]{1,0:T(8,128)(2,1)S(1)} collective-permute-done((bf16[512,512]{1,0:T(8,128)(2,1)S(1)}, bf16[512,512]{1,0:T(8,128)(2,1)S(1)}, u32[]{:S(2)}, u32[]{:S(2)}) %collective-permute-start.13) | collective-permute-done | bytes 524320 | tf_op jit(solution)/shard_map/ppermute | solution.py:383
  (55 shorter events, 10.3 us)
Async XLA Ops:
  5.2 83.0 %all-to-all-start = ((bf16[32,32,1536]{2,1,0:T(8,128)(2,1)}), bf16[32,32,1536]{2,1,0:T(8,128)(2,1)S(1)}, u32[]{:S(2)}, u32[]{:S(2)}) async-start(bf16[32,32,1536]{2,1,0:T(8,128)(2,1)} %bitcast.12), calls=%async_computation | async-start | bytes 6291456 | tf_op jit(solution)/shard_map/all_to_all | solution.py:401
  16.9 13.4 %collective-permute-start = (bf16[1024,768]{1,0:T(8,128)(2,1)}, bf16[1024,768]{1,0:T(8,128)(2,1)}, u32[]{:S(2)}, u32[]{:S(2)}) collective-permute-start(bf16[1024,768]{1,0:T(8,128)(2,1)} %key.3), channel_id=1, source_target_pairs={{0,4},{4,0},{8,12},{12,8},{16,20},{20,16},{24,28},{28,24},{32,36},... | collective-permute-start | bytes 4718600 | tf_op jit(solution)/shard_map/ppermute | solution.py:395
  17.0 13.3 %collective-permute-start.1 = (bf16[1024,768]{1,0:T(8,128)(2,1)}, bf16[1024,768]{1,0:T(8,128)(2,1)}, u32[]{:S(2)}, u32[]{:S(2)}) collective-permute-start(bf16[1024,768]{1,0:T(8,128)(2,1)} %value.3), channel_id=1, source_target_pairs={{0,4},{4,0},{8,12},{12,8},{16,20},{20,16},{24,28},{28,24},{32,36},... | collective-permute-start | bytes 4718600 | tf_op jit(solution)/shard_map/ppermute | solution.py:395
  24.6 19.9 %collective-permute-start.8 = (bf16[384,768]{1,0:T(8,128)(2,1)}, bf16[384,768]{1,0:T(8,128)(2,1)}, u32[]{:S(2)}, u32[]{:S(2)}) collective-permute-start(bf16[384,768]{1,0:T(8,128)(2,1)} %get-tuple-element.15), channel_id=1, source_target_pairs={{0,1},{1,2},{2,3},{3,0},{4,5},{5,6},{6,7},{7,4},{8,9},{9,10},{10,1... | collective-permute-start | bytes 1769480 | tf_op jit(solution)/shard_map/ppermute | solution.py:383
  26.1 28.7 %collective-permute-start.9 = (bf16[384,768]{1,0:T(8,128)(2,1)}, bf16[384,768]{1,0:T(8,128)(2,1)}, u32[]{:S(2)}, u32[]{:S(2)}) collective-permute-start(bf16[384,768]{1,0:T(8,128)(2,1)} %get-tuple-element.16), channel_id=1, source_target_pairs={{0,2},{1,3},{2,0},{3,1},{4,6},{5,7},{6,4},{7,5},{8,10},{9,11},{10,... | collective-permute-start | bytes 1769480 | tf_op jit(solution)/shard_map/ppermute | solution.py:383
  28.8 26.0 %collective-permute-start.10 = (bf16[384,768]{1,0:T(8,128)(2,1)}, bf16[384,768]{1,0:T(8,128)(2,1)}, u32[]{:S(2)}, u32[]{:S(2)}) collective-permute-start(bf16[384,768]{1,0:T(8,128)(2,1)} %get-tuple-element.17), channel_id=1, source_target_pairs={{0,3},{1,0},{2,1},{3,2},{4,7},{5,4},{6,5},{7,6},{8,11},{9,8},{10,9... | collective-permute-start | bytes 1769480 | tf_op jit(solution)/shard_map/ppermute | solution.py:383
  57.8 14.7 %collective-permute-start.11 = (bf16[3,384,768]{2,1,0:T(8,128)(2,1)}, bf16[3,384,768]{2,1,0:T(8,128)(2,1)}, u32[]{:S(2)}, u32[]{:S(2)}) collective-permute-start(bf16[3,384,768]{2,1,0:T(8,128)(2,1)} %pad_maximum_fusion), channel_id=1, source_target_pairs={{0,4},{4,0},{8,12},{12,8},{16,20},{20,16},{24,28},{28,24},{32,36},... | collective-permute-start | bytes 5308424 | tf_op jit(solution)/shard_map/ppermute | solution.py:395
  58.6 10.5 %collective-permute-start.2 = (bf16[512,256]{1,0:T(8,128)(2,1)}, bf16[512,256]{1,0:T(8,128)(2,1)S(1)}, u32[]{:S(2)}, u32[]{:S(2)}) collective-permute-start(bf16[512,256]{1,0:T(8,128)(2,1)} %get-tuple-element.28.own_top), channel_id=1, source_target_pairs={{0,1},{1,2},{2,3},{3,0},{4,5},{5,6},{6,7},{7,4},{8,9},{9,10},{10,1... | collective-permute-start | bytes 786440 | tf_op jit(solution)/shard_map/ppermute | solution.py:383
  59.9 9.5 %collective-permute-start.5 = (bf16[512,256]{1,0:T(8,128)(2,1)}, bf16[512,256]{1,0:T(8,128)(2,1)}, u32[]{:S(2)}, u32[]{:S(2)}) collective-permute-start(bf16[512,256]{1,0:T(8,128)(2,1)} %get-tuple-element.27.own_bottom), channel_id=1, source_target_pairs={{0,3},{1,0},{2,1},{3,2},{4,7},{5,4},{6,5},{7,6},{8,11},{9,8},{10,9... | collective-permute-start | bytes 786440 | tf_op jit(solution)/shard_map/ppermute | solution.py:383
  61.8 15.7 %collective-permute-start.3 = (bf16[512,256]{1,0:T(8,128)(2,1)}, bf16[512,256]{1,0:T(8,128)(2,1)S(1)}, u32[]{:S(2)}, u32[]{:S(2)}) collective-permute-start(bf16[512,256]{1,0:T(8,128)(2,1)} %get-tuple-element.27.own_bottom), channel_id=1, source_target_pairs={{0,1},{1,2},{2,3},{3,0},{4,5},{5,6},{6,7},{7,4},{8,9},{9,10},{10,1... | collective-permute-start | bytes 786440 | tf_op jit(solution)/shard_map/ppermute | solution.py:383
  62.0 15.6 %collective-permute-start.4 = (bf16[512,256]{1,0:T(8,128)(2,1)}, bf16[512,256]{1,0:T(8,128)(2,1)S(1)}, u32[]{:S(2)}, u32[]{:S(2)}) collective-permute-start(bf16[512,256]{1,0:T(8,128)(2,1)} %get-tuple-element.28.own_top), channel_id=1, source_target_pairs={{0,3},{1,0},{2,1},{3,2},{4,7},{5,4},{6,5},{7,6},{8,11},{9,8},{10,9... | collective-permute-start | bytes 786440 | tf_op jit(solution)/shard_map/ppermute | solution.py:383
  69.1 10.8 %collective-permute-start.6 = (bf16[512,256]{1,0:T(8,128)(2,1)S(1)}, bf16[512,256]{1,0:T(8,128)(2,1)S(1)}, u32[]{:S(2)}, u32[]{:S(2)}) collective-permute-start(bf16[512,256]{1,0:T(8,128)(2,1)S(1)} %collective-permute-done.2.rest_0_.right_top), channel_id=1, source_target_pairs={{0,1},{1,2},{2,3},{3,0},{4,5},{5,6},{6,7},{7,4},{8,9},{9,10},{10,1... | collective-permute-start | bytes 786440 | tf_op jit(solution)/shard_map/ppermute | solution.py:383
  69.4 11.3 %collective-permute-start.7 = (bf16[512,256]{1,0:T(8,128)(2,1)}, bf16[512,256]{1,0:T(8,128)(2,1)}, u32[]{:S(2)}, u32[]{:S(2)}) collective-permute-start(bf16[512,256]{1,0:T(8,128)(2,1)} %collective-permute-done.5.rest_3_.left_bottom), channel_id=1, source_target_pairs={{0,3},{1,0},{2,1},{3,2},{4,7},{5,4},{6,5},{7,6},{8,11},{9,8},{10,9... | collective-permute-start | bytes 786440 | tf_op jit(solution)/shard_map/ppermute | solution.py:383
  91.7 55.1 %copy-start = (bf16[3,768,768]{2,1,0:T(8,128)(2,1)S(1)}, bf16[3,768,768]{2,1,0:T(8,128)(2,1)}, u32[]{:S(2)}) copy-start(bf16[3,768,768]{2,1,0:T(8,128)(2,1)} %maximum_select_fusion.rest_6_.w_others) | copy-start | bytes 10616836
  91.8 55.1 %copy-start.1 = (bf16[768,768]{1,0:T(8,128)(2,1)S(1)}, bf16[768,768]{1,0:T(8,128)(2,1)}, u32[]{:S(2)}) copy-start(bf16[768,768]{1,0:T(8,128)(2,1)} %get-tuple-element.22.w_own) | copy-start | bytes 3538948
  91.8 55.1 %copy-start.3 = (bf16[512,256]{1,0:T(8,128)(2,1)S(1)}, bf16[512,256]{1,0:T(8,128)(2,1)}, u32[]{:S(2)}) copy-start(bf16[512,256]{1,0:T(8,128)(2,1)} %copy-done.2) | copy-start | bytes 786436
  91.8 55.1 %copy-start.5 = (bf16[512,256]{1,0:T(8,128)(2,1)S(1)}, bf16[512,256]{1,0:T(8,128)(2,1)}, u32[]{:S(2)}) copy-start(bf16[512,256]{1,0:T(8,128)(2,1)} %copy-done.4) | copy-start | bytes 786436
  91.8 55.1 %copy-start.7 = (bf16[512,256]{1,0:T(8,128)(2,1)S(1)}, bf16[512,256]{1,0:T(8,128)(2,1)}, u32[]{:S(2)}) copy-start(bf16[512,256]{1,0:T(8,128)(2,1)} %copy-done.6) | copy-start | bytes 786436
  127.4 16.1 %collective-permute-start.12 = (bf16[512,512]{1,0:T(8,128)(2,1)S(1)}, bf16[512,512]{1,0:T(8,128)(2,1)S(1)}, u32[]{:S(2)}, u32[]{:S(2)}) collective-permute-start(bf16[512,512]{1,0:T(8,128)(2,1)S(1)} %get-tuple-element.24.own_top), channel_id=1, source_target_pairs={{0,1},{1,2},{2,3},{3,0},{4,5},{5,6},{6,7},{7,4},{8,9},{9,10},{10,1... | collective-permute-start | bytes 1572872 | tf_op jit(solution)/shard_map/ppermute | solution.py:383
  128.1 15.5 %collective-permute-start.14 = (bf16[512,512]{1,0:T(8,128)(2,1)S(1)}, bf16[512,512]{1,0:T(8,128)(2,1)S(1)}, u32[]{:S(2)}, u32[]{:S(2)}) collective-permute-start(bf16[512,512]{1,0:T(8,128)(2,1)S(1)} %get-tuple-element.23.own_bottom), channel_id=1, source_target_pairs={{0,3},{1,0},{2,1},{3,2},{4,7},{5,4},{6,5},{7,6},{8,11},{9,8},{10,9... | collective-permute-start | bytes 1572872 | tf_op jit(solution)/shard_map/ppermute | solution.py:383
  130.8 24.1 %collective-permute-start.16 = (bf16[512,512]{1,0:T(8,128)(2,1)S(1)}, bf16[512,512]{1,0:T(8,128)(2,1)S(1)}, u32[]{:S(2)}, u32[]{:S(2)}) collective-permute-start(bf16[512,512]{1,0:T(8,128)(2,1)S(1)} %get-tuple-element.23.own_bottom), channel_id=1, source_target_pairs={{0,1},{1,2},{2,3},{3,0},{4,5},{5,6},{6,7},{7,4},{8,9},{9,10},{10,1... | collective-permute-start | bytes 1572872 | tf_op jit(solution)/shard_map/ppermute | solution.py:383
  130.8 24.1 %collective-permute-start.17 = (bf16[512,512]{1,0:T(8,128)(2,1)S(1)}, bf16[512,512]{1,0:T(8,128)(2,1)S(1)}, u32[]{:S(2)}, u32[]{:S(2)}) collective-permute-start(bf16[512,512]{1,0:T(8,128)(2,1)S(1)} %get-tuple-element.24.own_top), channel_id=1, source_target_pairs={{0,3},{1,0},{2,1},{3,2},{4,7},{5,4},{6,5},{7,6},{8,11},{9,8},{10,9... | collective-permute-start | bytes 1572872 | tf_op jit(solution)/shard_map/ppermute | solution.py:383
  143.6 19.1 %collective-permute-start.13 = (bf16[512,512]{1,0:T(8,128)(2,1)S(1)}, bf16[512,512]{1,0:T(8,128)(2,1)S(1)}, u32[]{:S(2)}, u32[]{:S(2)}) collective-permute-start(bf16[512,512]{1,0:T(8,128)(2,1)S(1)} %collective-permute-done.12.right_top), channel_id=1, source_target_pairs={{0,1},{1,2},{2,3},{3,0},{4,5},{5,6},{6,7},{7,4},{8,9},{9,10},{10,1... | collective-permute-start | bytes 1572872 | tf_op jit(solution)/shard_map/ppermute | solution.py:383
  143.6 19.1 %collective-permute-start.15 = (bf16[512,512]{1,0:T(8,128)(2,1)S(1)}, bf16[512,512]{1,0:T(8,128)(2,1)S(1)}, u32[]{:S(2)}, u32[]{:S(2)}) collective-permute-start(bf16[512,512]{1,0:T(8,128)(2,1)S(1)} %collective-permute-done.14.left_bottom), channel_id=1, source_target_pairs={{0,3},{1,0},{2,1},{3,2},{4,7},{5,4},{6,5},{7,6},{8,11},{9,8},{10,9... | collective-permute-start | bytes 1572872 | tf_op jit(solution)/shard_map/ppermute | solution.py:383
  (8 other events, 137.3 us)

commit v10 on v9

--- a/solution.py
+++ b/solution.py
@@ -10,8 +10,10 @@
 
 FRAMES = 32
 TMAX = 4
+ORDER_WEIGHT = 20
 SMALL_VMEM = 16 * 1024 * 1024
 CORES = 2
+FIRST = 2
 ROWS = 8
 HD = 128
 EPSILON = 1e-06
@@ -74,10 +76,10 @@
         input_output_aliases={at: at for at in range(len(arrays))},
         cost_estimate=pl.CostEstimate(flops=0, bytes_accessed=0, transcendentals=0),
         name="hold",
-    )(*[from_hbm(array) for array in (*arrays, *after)])
-
-
-def pack_kernel(head_count, classes, query, key, value, query_gain, key_gain, out, raw, ready, in_sems, out_sems):
+    )(*[from_hbm(array) for array in arrays], *after)
+
+
+def pack_kernel(head_count, classes, query, key, value, query_gain, key_gain, now, later, raw, ready, in_sems, out_sems):
     heads = [head_of(classes, slot, head_count) for slot in range(TMAX)]
     gains = (query_gain, key_gain, None)
     loads, stores = [], []
@@ -92,7 +94,12 @@
         loads[at].wait()
         if gain is not None:
             ready[at] = normed(raw[at], gain[...])
-        stores.append(pltpu.make_async_copy(ready.at[at], out.at[:, pl.ds(at * HD, HD)], out_sems.at[at]))
+        split = 3 * FIRST
+        if at < split:
+            target = now.at[:, pl.ds(at * HD, HD)]
+        else:
+            target = later.at[:, pl.ds((FIRST + at - split) * HD, HD)]
+        stores.append(pltpu.make_async_copy(ready.at[at], target, out_sems.at[at]))
         stores[-1].start()
     for store in stores:
         store.wait()
@@ -108,7 +115,7 @@
             num_scalar_prefetch=1,
             grid=(1,),
             in_specs=[anywhere] * 3 + [gain_spec] * 2,
-            out_specs=anywhere,
+            out_specs=[anywhere] * 2,
             scratch_shapes=[
                 pltpu.VMEM((3 * TMAX, tokens, HD), jnp.bfloat16),
                 pltpu.VMEM((3 * TMAX, tokens, HD), jnp.bfloat16),
@@ -116,7 +123,10 @@
                 pltpu.SemaphoreType.DMA((3 * TMAX,)),
             ],
         ),
-        out_shape=in_hbm((tokens, TMAX * 3 * HD), jnp.bfloat16),
+        out_shape=[
+            in_hbm((tokens, FIRST * 3 * HD), jnp.bfloat16),
+            in_hbm((tokens, (FIRST + (TMAX - FIRST) * 3) * HD), jnp.bfloat16),
+        ],
         cost_estimate=pl.CostEstimate(flops=8 * tokens * TMAX * HD, bytes_accessed=12 * tokens * TMAX * HD, transcendentals=0),
         name="pack",
     )(head_class, from_hbm(query_rows), from_hbm(key_rows), from_hbm(value_rows), query_gain, key_gain)
@@ -195,7 +205,7 @@
     )(head_class, query_rows, key_rows, from_hbm(other_keys), value_rows, from_hbm(other_values), query_gain, key_gain)
 
 
-def temporal_kernel(head_count, classes, packed, *rest):
+def temporal_kernel(head_count, begin, slots, base, classes, packed, *rest):
     out, held, sems = rest[-3:]
     frames, positions, _ = packed.shape
     count = frames * ROWS
@@ -214,13 +224,13 @@
     def store(slot):
         return pltpu.make_async_copy(held.at[slot], out.at[:, :, pl.ds(slot * HD, HD)], sems.at[slot])
 
-    for slot in range(TMAX):
-
-        @pl.when(slot < total)
+    for slot in range(slots):
+
+        @pl.when(begin + slot < total)
         def _(slot=slot):
-            for begin in range(0, positions, 2 * ROWS):
-                at = slice(begin, begin + 2 * ROWS)
-                columns = [slice((3 * slot + which) * HD, (3 * slot + which + 1) * HD) for which in range(3)]
+            for start in range(0, positions, 2 * ROWS):
+                at = slice(start, start + 2 * ROWS)
+                columns = [slice(base + (3 * slot + which) * HD, base + (3 * slot + which + 1) * HD) for which in range(3)]
                 wide = [packed[:, at, column].astype(jnp.float32) for column in columns]
                 results = []
                 for first in (0, ROWS):
@@ -228,38 +238,42 @@
                     results.append(attend(*parts))
                 held[slot, :, at] = jnp.concatenate(results, axis=1).astype(jnp.bfloat16)
 
-        @pl.when(slot >= total)
+        @pl.when(begin + slot >= total)
         def _(slot=slot):
             held[slot] = jnp.zeros(held.shape[1:], held.dtype)
 
         store(slot).start()
-    for slot in range(TMAX):
+    for slot in range(slots):
         store(slot).wait()
 
 
-def temporal(head_class, packed, after):
+def temporal(head_class, packed, begin, slots, base, after, into=None):
     frames, positions, _ = packed.shape
-    return pl.pallas_call(
-        functools.partial(temporal_kernel, head_class.shape[0]),
+    anywhere = pl.BlockSpec(memory_space=pl.ANY)
+    shape = (frames, positions, slots * HD) if into is None else into.shape
+    extra = [] if into is None else [into]
+    return pl.pallas_call(
+        functools.partial(temporal_kernel, head_class.shape[0], begin, slots, base),
         grid_spec=pltpu.PrefetchScalarGridSpec(
             num_scalar_prefetch=1,
             grid=(1,),
-            in_specs=[pl.BlockSpec(memory_space=pltpu.VMEM)] + [pl.BlockSpec(memory_space=pl.ANY)] * len(after),
-            out_specs=pl.BlockSpec(memory_space=pl.ANY),
+            in_specs=[pl.BlockSpec(memory_space=pltpu.VMEM)] + [anywhere] * (len(after) + len(extra)),
+            out_specs=anywhere,
             scratch_shapes=[
-                pltpu.VMEM((TMAX, frames, positions, HD), jnp.bfloat16),
-                pltpu.SemaphoreType.DMA((TMAX,)),
+                pltpu.VMEM((slots, frames, positions, HD), jnp.bfloat16),
+                pltpu.SemaphoreType.DMA((slots,)),
             ],
         ),
-        out_shape=in_hbm((frames, positions, TMAX * HD), jnp.bfloat16),
+        out_shape=in_hbm(shape, jnp.bfloat16),
+        input_output_aliases={} if into is None else {2 + len(after): 0},
         compiler_params=pltpu.CompilerParams(vmem_limit_bytes=SMALL_VMEM),
         cost_estimate=pl.CostEstimate(
-            flops=32 * frames * frames * positions * TMAX * HD,
-            bytes_accessed=8 * frames * positions * TMAX * HD,
-            transcendentals=8 * frames * frames * positions * TMAX,
+            flops=32 * frames * frames * positions * slots * HD,
+            bytes_accessed=8 * frames * positions * slots * HD,
+            transcendentals=8 * frames * frames * positions * slots,
         ),
         name="temporal",
-    )(head_class, from_vmem(packed), *[from_hbm(array) for array in after])
+    )(head_class, from_vmem(packed), *[from_hbm(array) for array in (*after, *extra)])
 
 
 def weight_kernel(classes, place, weight, own, *others):
@@ -306,32 +320,34 @@
     return jnp.dot(rows, weight[first : first + rows.shape[1]], preferred_element_type=jnp.float32)
 
 
-def near_sum(own, right, left, w_own, w_others, first):
-    return product(own[...], w_own, first) + product(right[...], w_others.at[0], first) + product(left[...], w_others.at[2], first)
-
-
-def early_kernel(first, own_top, own_bottom, right_top, right_bottom, left_top, left_bottom, far_top, far_bottom, w_own, w_others, out):
-    half = own_top.shape[0]
-    parts = ((own_top, right_top, left_top, far_top), (own_bottom, right_bottom, left_bottom, far_bottom))
-    for part, (own, right, left, far) in enumerate(parts):
-        total = near_sum(own, right, left, w_own, w_others, first) + product(far[...], w_others.at[1], first)
-        out[part * half : (part + 1) * half] = total
-
-
-def near_kernel(own_top, own_bottom, right_top, right_bottom, left_top, left_bottom, w_own, w_others, total, out):
-    half = own_top.shape[0]
-    for part, (own, right, left) in enumerate(((own_top, right_top, left_top), (own_bottom, right_bottom, left_bottom))):
-        rows = slice(part * half, (part + 1) * half)
-        out[rows] = total[rows] + near_sum(own, right, left, w_own, w_others, 0)
-
-
-def far_kernel(far_top, far_bottom, w_others, total, out, held, sems):
+def near_sum(own, right, left, w_own, w_others, first, rows):
+    total = product(own[rows], w_own, first)
+    return total + product(right[rows], w_others.at[0], first) + product(left[rows], w_others.at[2], first)
+
+
+def halves(tokens):
+    return slice(0, tokens // 2), slice(tokens // 2, tokens)
+
+
+def all_kernel(first, own, right, left, far_top, far_bottom, w_own, w_others, *rest):
+    out = rest[-1]
+    for rows, far in zip(halves(own.shape[0]), (far_top, far_bottom), strict=True):
+        total = near_sum(own, right, left, w_own, w_others, first, rows) + product(far[...], w_others.at[1], first)
+        out[rows] = total if len(rest) == 1 else total + rest[0][rows]
+
+
+def near_kernel(first, own, right, left, w_own, w_others, total, out):
+    for rows in halves(own.shape[0]):
+        out[rows] = total[rows] + near_sum(own, right, left, w_own, w_others, first, rows)
+
+
+def far_kernel(first, far_top, far_bottom, w_others, total, out, held, sems):
     steps, rows, _ = held.shape
     stores = []
     for step in range(steps):
         far = (far_top, far_bottom)[2 * step // steps]
         begin = step * rows % far.shape[0]
-        summed = product(far[begin : begin + rows], w_others.at[1], 0) + total[step * rows : (step + 1) * rows]
+        summed = product(far[begin : begin + rows], w_others.at[1], first) + total[step * rows : (step + 1) * rows]
         held[step] = summed.astype(held.dtype)
         stores.append(pltpu.make_async_copy(held.at[step], out.at[pl.ds(step * rows, rows)], sems.at[step]))
         stores[-1].start()
@@ -340,7 +356,7 @@
 
 
 def summing(kernel, name, operands, depth_terms):
-    tokens, width = 2 * operands[0].shape[0], operands[-1].shape[-1]
+    tokens, width = operands[0].shape[0], operands[-1].shape[-1]
     depth = operands[0].shape[1]
     whole = pl.BlockSpec(memory_space=pltpu.VMEM)
     return pl.pallas_call(
@@ -350,24 +366,23 @@
         out_shape=pltpu.VMEM((tokens, width), jnp.float32),
         compiler_params=pltpu.CompilerParams(vmem_limit_bytes=SMALL_VMEM),
         cost_estimate=pl.CostEstimate(
-            flops=2 * depth_terms * tokens * depth * width, bytes_accessed=8 * tokens * width, transcendentals=0
+            flops=ORDER_WEIGHT * depth_terms * tokens * depth * width, bytes_accessed=8 * tokens * width, transcendentals=0
         ),
         name=name,
     )(*[from_vmem(array) for array in operands])
 
 
-def project_early(pieces, w_own, w_others):
-    first = TMAX * HD
-    return summing(functools.partial(early_kernel, first), "project_early", (*pieces, w_own, w_others), 4)
-
-
-def project_late(pieces, w_own, w_others, total):
-    near = summing(near_kernel, "near", (*pieces[:6], w_own, w_others, total), 3)
+def project_all(name, first, pieces, w_own, w_others, *total):
+    return summing(functools.partial(all_kernel, first), name, (*pieces, w_own, w_others, *total), 4)
+
+
+def project_last(first, pieces, w_own, w_others, total):
+    near = summing(functools.partial(near_kernel, first), "near", (*pieces[:3], w_own, w_others, total), 3)
     tokens, width = near.shape
     depth = pieces[0].shape[1]
     steps = 4
     return pl.pallas_call(
-        far_kernel,
+        functools.partial(far_kernel, first),
         in_specs=[pl.BlockSpec(memory_space=pltpu.VMEM)] * 4,
         out_specs=pl.BlockSpec(memory_space=pl.ANY),
         out_shape=in_hbm((tokens, width), jnp.bfloat16),
@@ -375,7 +390,7 @@
         compiler_params=pltpu.CompilerParams(vmem_limit_bytes=SMALL_VMEM),
         cost_estimate=pl.CostEstimate(flops=2 * tokens * depth * width, bytes_accessed=8 * tokens * width, transcendentals=0),
         name="far",
-    )(*[from_vmem(array) for array in (*pieces[6:], w_others, near)])
+    )(*[from_vmem(array) for array in (*pieces[3:], w_others, near)])
 
 
 def shifted(block, by):
@@ -383,11 +398,10 @@
     return lax.ppermute(block, "head", [(at, (at + by) % count) for at in range(count)])
 
 
-def ring(top, bottom):
-    right_top, left_bottom = shifted(top, 1), shifted(bottom, -1)
-    right_bottom, left_top = shifted(bottom, 1), shifted(top, -1)
-    far_top, far_bottom = shifted(right_top, 1), shifted(left_bottom, -1)
-    return top, bottom, right_top, right_bottom, left_top, left_bottom, far_top, far_bottom
+def ring(block):
+    half = block.shape[0] // 2
+    right, left = shifted(block, 1), shifted(block, -1)
+    return block, right, left, shifted(right[:half], 1), shifted(left[half:], -1)
 
 
 def other_core(block):
@@ -406,26 +420,40 @@
     group_count = lax.axis_size("head")
     query_gain = query_gain.reshape(1, HD)
     key_gain = key_gain.reshape(1, HD)
-    packed = pack(head_class, query_rows, key_rows, value_rows, query_gain, key_gain)
-    arrived = over_frames(packed.reshape(FRAMES, tokens // FRAMES, TMAX * 3 * HD))
-
-    other_keys, other_values = other_core(key_rows), other_core(value_rows)
-    front, back = spatial(head_class, query_rows, key_rows, other_keys, value_rows, other_values, query_gain, key_gain)
+    now, later = pack(head_class, query_rows, key_rows, value_rows, query_gain, key_gain)
+    arrived = over_frames(now.reshape(FRAMES, tokens // FRAMES, -1))
+
     core = lax.rem(lax.axis_index("seq"), CORES)
     place = jnp.stack([lax.axis_index("head"), core]).astype(jnp.int32)
-    w_own, *halves = weight_blocks(head_class, place, out_weight, group_count)
-
-    fetched = [shifted(half, by + 1) for by, half in enumerate(halves)]
-    fetched = jnp.stack(hold(fetched, (back,)))
+    w_own, *halves_of_others = weight_blocks(head_class, place, out_weight, group_count)
+    (other_keys,) = hold((other_core(key_rows),), halves_of_others)
+    other_values = other_core(value_rows)
+    front, back = spatial(head_class, query_rows, key_rows, other_keys, value_rows, other_values, query_gain, key_gain)
+
+    fetched = [shifted(half, by + 1) for by, half in enumerate(halves_of_others)]
+    fetched = hold(fetched, (back,))
+    fetched_first = fetched
+    fetched = jnp.stack(fetched)
     rest = other_core(fetched)
     w_others = jnp.where(core == 0, jnp.concatenate([fetched, rest], axis=1), jnp.concatenate([rest, fetched], axis=1))
 
-    middle = tokens // 2
-    pieces = ring(back[:middle], back[middle:])
-    returned = over_frames(temporal(head_class, arrived, (*pieces[2:], w_others))).reshape(tokens, TMAX * HD)
-    early = project_early(pieces, w_own, w_others)
-    pieces = ring(returned[:middle] + front[:middle], returned[middle:] + front[middle:])
-    return project_late(pieces, w_own, w_others, early)
+    width = FIRST * HD
+    early = ring(back)
+    mixed = temporal(head_class, arrived, 0, FIRST, 0, (front, *fetched_first), into=later.reshape(FRAMES, tokens // FRAMES, -1))
+    arrived = over_frames(mixed)
+    (front,) = hold((front,), (*early[1:], w_others))
+    sent = temporal(head_class, arrived, FIRST, TMAX - FIRST, width, (front,))
+    (front,) = hold((front,), (sent,))
+    chosen = arrived[:, :, :width].reshape(tokens, width) + front[:, :width]
+    first = ring(chosen)
+    (sent,) = hold((sent,), (chosen,))
+    total = project_all("early", TMAX * HD, early, w_own, w_others)
+    returned = over_frames(sent).reshape(tokens, -1)
+    (rest,) = hold((front,), (*first[1:], total))
+    last = ring(returned + rest[:, width:])
+
+    total = project_all("first", 0, first, w_own, w_others, total)
+    return project_last(width, last, w_own, w_others, total)
 
 
 def solution(mesh):

time: 165 us -> 178 us (1.079); the launches traced: 165 us -> 176 us
  blocking collectives: 35.3 us -> 0 us
  starting transfers between devices: 37.5 us -> 56 us
  local copies, waits for them, and re-layouts: 1.69 us -> 13.9 us
  Pallas kernels: 37 us -> 48.5 us
  other arithmetic: 8.76 us -> 11.3 us
    all_to_all x1 -> x0, blocking collectives: 35.3 us -> none  [over_frames(): return lax.all_to_all(blocks, 'seq', 0, 0, axis_index_groups=groups)]
    all_to_all x1 -> x3, starting transfers between devices: 11.7 us -> 28.6 us  [over_frames(): return lax.all_to_all(blocks, 'seq', 0, 0, axis_index_groups=groups)]
    all_to_all x1 -> x3, waiting for transfers between devices: 7.48 us -> 20.3 us  [over_frames(): return lax.all_to_all(blocks, 'seq', 0, 0, axis_index_groups=groups)]
    ppermute x15, waiting for transfers between devices: 36.5 us -> 25.3 us  [shifted(): lax.ppermute(block, 'head', [(at, (at + by) % count) for at in range(coun...]
    pallas_call x1, Pallas kernels: 14.3 us -> 24.3 us  [spatial(): pl.pallas_call(functools.partial(spatial_kernel, head_count), grid_spec=p...]
    unnamed x26 -> x30, local copies, waits for them, and re-layouts: 0.75 us -> 10.6 us
    add x1 -> x2, other arithmetic: 0.2 us -> 3.19 us  [the longest x1 1.93 us: body(): chosen = arrived[:, :, :width].reshape(tokens, width) + front[:, :width]]
    slice x2 -> x7, local copies, waits for them, and re-layouts: 0.93 us -> 3.24 us  [the longest x1 1.23 us: body(): chosen = arrived[:, :, :width].reshape(tokens, width) + front[:, :width]]
  transfers between devices with their start and end apart: 19 -> 21, of which waited for: 8 -> 7; matrix products, arithmetic and copies ran while one was open for 6% -> 6% of each run, Pallas kernels for 16% -> 22%
where the time goes in v10:
time: 178 us; the launch traced here: 176 us
  starting transfers between devices  56 us (31%)
  Pallas kernels  48.5 us (27%)
  waiting for transfers between devices  45.6 us (26%)
  local copies, waits for them, and re-layouts  13.9 us (8%)
  other arithmetic  11.3 us (6%)
    all_to_all x3, starting transfers between devices, over_frames(): return lax.all_to_all(blocks, 'seq', 0, 0, axis_index_groups=groups)  28.6 us
    ppermute x15, starting transfers between devices, shifted(): lax.ppermute(block, 'head', [(at, (at + by) % count) for at in range(coun...  26.8 us
    ppermute x15, waiting for transfers between devices, shifted(): lax.ppermute(block, 'head', [(at, (at + by) % count) for at in range(coun...  25.3 us
    pallas_call x1, Pallas kernels, spatial(): pl.pallas_call(functools.partial(spatial_kernel, head_count), grid_spec=p...  24.3 us
    all_to_all x3, waiting for transfers between devices, over_frames(): return lax.all_to_all(blocks, 'seq', 0, 0, axis_index_groups=groups)  20.3 us
    unnamed x30, local copies, waits for them, and re-layouts  10.6 us
    pallas_call x3, Pallas kernels, summing(): pl.pallas_call(kernel, in_specs=[whole] * len(operands), out_specs=whole,...  7.6 us
    pallas_call x1, Pallas kernels, weight_blocks(): pl.pallas_call(weight_kernel, grid_spec=pltpu.PrefetchScalarGridSpec(num_...  6.52 us
  transfers between devices with their start and end apart: 21, of which 7 were waited for; matrix products, arithmetic and copies ran while one was open for 6% of the time, Pallas kernels for 22%

profile of v10, /device:TPU:8, one launch (start us, length us, event | category | flops | bytes accessed | tf_op | source)
XLA Modules:
  0.0 175.6 jit_solution(11228956897806755308)
XLA Ops:
  0.0 5.1 %pack.1 = (bf16[1024,768]{1,0:T(8,128)(2,1)}, bf16[1024,1024]{1,0:T(8,128)(2,1)}) custom-call(s32[6]{0:T(128)} %classes.9, bf16[1024,768]{1,0:T(8,128)(2,1)} %query.3, bf16[1024,768]{1,0:T(8,128)(2,1)} %key.3, bf16[1024,768]{1,0:T(8,128)(2,1)} %value.3, f32[1,128]{1,0:T(1,128)} %bitcast.17, f32[1,128]{1,0:T(1,128)} %bitcast.19), custom_call_target="tpu_custom_call" | custom-call | flops 4194304 | bytes 6291456 | tf_op jit(solution)/shard_map/pack/pallas_call | solution.py:112
  5.1 11.7 %all-to-all-start = ((bf16[32,32,768]{2,1,0:T(8,128)(2,1)}), bf16[32,32,768]{2,1,0:T(8,128)(2,1)S(1)}, u32[]{:S(2)}, u32[]{:S(2)}) async-start(bf16[32,32,768]{2,1,0:T(8,128)(2,1)} %bitcast.16), calls=%async_computation | async-start | bytes 3145728 | tf_op jit(solution)/shard_map/all_to_all | solution.py:415
  18.0 6.5 %weight_blocks.1 = (bf16[768,768]{1,0:T(8,128)(2,1)}, bf16[384,768]{1,0:T(8,128)(2,1)}, bf16[384,768]{1,0:T(8,128)(2,1)}, bf16[384,768]{1,0:T(8,128)(2,1)}) custom-call(s32[6]{0:T(128)} %classes.9, s32[2]{0:T(128)} %pad_add_fusion.place, bf16[768,3072]{1,0:T(8,128)(2,1)} %weight.1), custom_call_target="tpu_custom_call" | custom-call | bytes 9437184 | tf_op jit(solution)/shard_map/weight_blocks/pallas_call | solution.py:304
  26.1 2.7 %collective-permute-start.3 = (bf16[384,768]{1,0:T(8,128)(2,1)}, bf16[384,768]{1,0:T(8,128)(2,1)}, u32[]{:S(2)}, u32[]{:S(2)}) collective-permute-start(bf16[384,768]{1,0:T(8,128)(2,1)} %get-tuple-element.18.refs_2_), channel_id=1, source_target_pairs={{0,2},{1,3},{2,0},{3,1},{4,6},{5,7},{6,4},{7,5},{8,10},{9,11},{10,... | collective-permute-start | bytes 1769480 | tf_op jit(solution)/shard_map/ppermute | solution.py:398
  30.2 24.3 %spatial.1 = (bf16[1024,512]{1,0:T(8,128)(2,1)}, bf16[1024,256]{1,0:T(8,128)(2,1)}) custom-call(s32[6]{0:T(128)} %classes.9, bf16[1024,768]{1,0:T(8,128)(2,1)} %query.3, bf16[1024,768]{1,0:T(8,128)(2,1)} %key.3, bf16[1024,768]{1,0:T(8,128)(2,1)} %hold.6.other_key, bf16[1024,768]{1,0:T(8,128)(2,1)} %value.3, ...), custom_call_target="tpu_custom_call" | custom-call | flops 12884901888 | bytes 9437184 | tf_op jit(solution)/shard_map/spatial/pallas_call | solution.py:182
  55.6 2.0 %temporal.2 = bf16[32,32,1024]{2,1,0:T(8,128)(2,1)} custom-call(s32[6]{0:T(128)S(1)} %copy-done.10, bf16[32,32,768]{2,1,0:T(8,128)(2,1)S(1)} %all-to-all-done.packed, bf16[1024,512]{1,0:T(8,128)(2,1)} %get-tuple-element.20.rest_0_.refs_0_, bf16[384,768]{1,0:T(8,128)(2,1)} %get-tuple-element.22.rest_1_, ...), custom_call_target="tpu_custom_call", output_to_operand_aliasing={{}: (6, {})} | custom-call | flops 268435456 | bytes 2097152 | tf_op jit(solution)/shard_map/temporal/pallas_call | solution.py:255
  57.6 9.9 %all-to-all-start.1 = ((bf16[32,32,1024]{2,1,0:T(8,128)(2,1)}), bf16[32,32,1024]{2,1,0:T(8,128)(2,1)S(1)}, u32[]{:S(2)}, u32[]{:S(2)}) async-start(bf16[32,32,1024]{2,1,0:T(8,128)(2,1)} %temporal.2), calls=%async_computation.1 | async-start | bytes 4194304 | tf_op jit(solution)/shard_map/all_to_all | solution.py:415
  67.6 2.7 %pad_maximum_fusion = bf16[3,384,768]{2,1,0:T(8,128)(2,1)} fusion(bf16[1,384,768]{2,1,0:T(8,128)(2,1)S(1)} %bitcast.14, bf16[1,384,768]{2,1,0:T(8,128)(2,1)} %bitcast.7, bf16[1,384,768]{2,1,0:T(8,128)(2,1)} %bitcast.6), kind=kLoop, calls=%fused_computation.1 | loop fusion | flops 1769472 | bytes 3538944 | tf_op jit(solution)/shard_map/stack | solution.py:436
  73.5 12.5 %collective-permute-done.5.refs_1_.right = bf16[1024,256]{1,0:T(8,128)(2,1)S(1)} collective-permute-done((bf16[1024,256]{1,0:T(8,128)(2,1)}, bf16[1024,256]{1,0:T(8,128)(2,1)S(1)}, u32[]{:S(2)}, u32[]{:S(2)}) %collective-permute-start.5) | collective-permute-done | bytes 524320 | tf_op jit(solution)/shard_map/ppermute | solution.py:398
  86.6 3.0 %collective-permute-start.8 = (bf16[512,256]{1,0:T(8,128)(2,1)S(1)}, bf16[512,256]{1,0:T(8,128)(2,1)}, u32[]{:S(2)}, u32[]{:S(2)}) collective-permute-start(bf16[512,256]{1,0:T(8,128)(2,1)S(1)} %slice.37), channel_id=1, source_target_pairs={{0,3},{1,0},{2,1},{3,2},{4,7},{5,4},{6,5},{7,6},{8,11},{9,8},{10,9... | collective-permute-start | bytes 786440 | tf_op jit(solution)/shard_map/ppermute | solution.py:398
  89.6 4.8 %maximum_select_fusion.refs_5_.w_others = bf16[3,768,768]{2,1,0:T(8,128)(2,1)} fusion(bf16[3,384,768]{2,1,0:T(8,128)(2,1)} %collective-permute-done.9, bf16[1,384,768]{2,1,0:T(8,128)(2,1)} %bitcast.13, bf16[1,384,768]{2,1,0:T(8,128)(2,1)} %bitcast.7, bf16[1,384,768]{2,1,0:T(8,128)(2,1)} %bitcast.6, pred[]{:T(512)S(6)} %eq.3), kind=kLoop, calls=%fused_computation | loop fusion | flops 30081024 | bytes 7077889 | tf_op jit(solution)/shard_map/jit(_where)/select_n | solution.py:438
  95.9 20.2 %all-to-all-done.1.packed = bf16[32,32,1024]{2,1,0:T(8,128)(2,1)S(1)} async-done(((bf16[32,32,1024]{2,1,0:T(8,128)(2,1)}), bf16[32,32,1024]{2,1,0:T(8,128)(2,1)S(1)}, u32[]{:S(2)}, u32[]{:S(2)}) %all-to-all-start.1) | async-done | bytes 2097184 | tf_op jit(solution)/shard_map/all_to_all | solution.py:415
  119.0 1.9 %slice_add_fusion.1.refs_1_.own = bf16[1024,256]{1,0:T(8,128)(2,1)} fusion(bf16[1024,512]{1,0:T(8,128)(2,1)} %hold.9.refs_0_, bf16[32,32,256]{2,1,0:T(8,128)(2,1)S(1)} %slice.38), kind=kLoop, calls=%fused_computation.3 | loop fusion | flops 262144 | bytes 1572864 | tf_op jit(solution)/shard_map/add | solution.py:447
  120.9 2.7 %collective-permute-start.10 = (bf16[1024,256]{1,0:T(8,128)(2,1)}, bf16[1024,256]{1,0:T(8,128)(2,1)}, u32[]{:S(2)}, u32[]{:S(2)}) collective-permute-start(bf16[1024,256]{1,0:T(8,128)(2,1)} %slice_add_fusion.1.refs_1_.own), channel_id=1, source_target_pairs={{0,1},{1,2},{2,3},{3,0},{4,5},{5,6},{6,7},{7,4},{8,9},{9,10},{10,1... | collective-permute-start | bytes 1572872 | tf_op jit(solution)/shard_map/ppermute | solution.py:398
  125.2 6.9 %all-to-all-start.2 = ((bf16[32,32,256]{2,1,0:T(8,128)(2,1)}), bf16[32,32,256]{2,1,0:T(8,128)(2,1)}, u32[]{:S(2)}, u32[]{:S(2)}) async-start(bf16[32,32,256]{2,1,0:T(8,128)(2,1)} %hold.10), calls=%async_computation.2 | async-start | bytes 1048576 | tf_op jit(solution)/shard_map/all_to_all | solution.py:415
  132.2 5.1 %collective-permute-done.10.refs_1_.right = bf16[1024,256]{1,0:T(8,128)(2,1)} collective-permute-done((bf16[1024,256]{1,0:T(8,128)(2,1)}, bf16[1024,256]{1,0:T(8,128)(2,1)}, u32[]{:S(2)}, u32[]{:S(2)}) %collective-permute-start.10) | collective-permute-done | bytes 524320 | tf_op jit(solution)/shard_map/ppermute | solution.py:398
  139.3 3.3 %collective-permute-start.13 = (bf16[512,256]{1,0:T(8,128)(2,1)S(1)}, bf16[512,256]{1,0:T(8,128)(2,1)}, u32[]{:S(2)}, u32[]{:S(2)}) collective-permute-start(bf16[512,256]{1,0:T(8,128)(2,1)S(1)} %slice.41), channel_id=1, source_target_pairs={{0,3},{1,0},{2,1},{3,2},{4,7},{5,4},{6,5},{7,6},{8,11},{9,8},{10,9... | collective-permute-start | bytes 786440 | tf_op jit(solution)/shard_map/ppermute | solution.py:398
  146.9 2.9 %early.1.refs_5_.rest_0_ = f32[1024,768]{1,0:T(8,128)S(1)} custom-call(bf16[1024,256]{1,0:T(8,128)(2,1)} %get-tuple-element.21.refs_3_.own, bf16[1024,256]{1,0:T(8,128)(2,1)S(1)} %copy-done.5, bf16[1024,256]{1,0:T(8,128)(2,1)S(1)} %copy-done.7, bf16[512,256]{1,0:T(8,128)(2,1)S(1)} %copy-done.9, bf16[512,256]{1,0:T(8,128)(2,1)} %collective-permute-done.8.refs_4_.far_bottom, ...), custom_call_target="tpu_custom_call" | custom-call | flops 16106127360 | bytes 6291456 | tf_op jit(solution)/shard_map/early/pallas_call | solution.py:362
  152.8 3.2 %collective-permute-start.16 = (bf16[1024,256]{1,0:T(8,128)(2,1)S(1)}, bf16[1024,256]{1,0:T(8,128)(2,1)S(1)}, u32[]{:S(2)}, u32[]{:S(2)}) collective-permute-start(bf16[1024,256]{1,0:T(8,128)(2,1)S(1)} %slice_add_fusion.own), channel_id=1, source_target_pairs={{0,3},{1,0},{2,1},{3,2},{4,7},{5,4},{6,5},{7,6},{8,11},{9,8},{10,9... | collective-permute-start | bytes 1572872 | tf_op jit(solution)/shard_map/ppermute | solution.py:398
  156.0 1.9 %copy-done.3 = f32[1024,768]{1,0:T(8,128)S(1)} copy-done((f32[1024,768]{1,0:T(8,128)S(1)}, f32[1024,768]{1,0:T(8,128)}, u32[]{:S(2)}) %copy-start.3) | copy-done | bytes 3145752
  159.2 3.3 %first.1.total = f32[1024,768]{1,0:T(8,128)S(1)} custom-call(bf16[1024,256]{1,0:T(8,128)(2,1)} %slice_add_fusion.1.refs_1_.own, bf16[1024,256]{1,0:T(8,128)(2,1)} %collective-permute-done.10.refs_1_.right, bf16[1024,256]{1,0:T(8,128)(2,1)} %collective-permute-done.11.refs_2_.left, bf16[512,256]{1,0:T(8,128)(2,1)} %collective-permute-done.12.refs_3_.far_top, ...), custom_call_target="tpu_custom_call" | custom-call | flops 16106127360 | bytes 6291456 | tf_op jit(solution)/shard_map/first/pallas_call | solution.py:362
  162.5 3.8 %collective-permute-done.14.right = bf16[1024,256]{1,0:T(8,128)(2,1)S(1)} collective-permute-done((bf16[1024,256]{1,0:T(8,128)(2,1)S(1)}, bf16[1024,256]{1,0:T(8,128)(2,1)S(1)}, u32[]{:S(2)}, u32[]{:S(2)}) %collective-permute-start.14) | collective-permute-done | bytes 524320 | tf_op jit(solution)/shard_map/ppermute | solution.py:398
  166.5 3.3 %collective-permute-start.17 = (bf16[512,256]{1,0:T(8,128)(2,1)S(1)}, bf16[512,256]{1,0:T(8,128)(2,1)S(1)}, u32[]{:S(2)}, u32[]{:S(2)}) collective-permute-start(bf16[512,256]{1,0:T(8,128)(2,1)S(1)} %slice.44), channel_id=1, source_target_pairs={{0,3},{1,0},{2,1},{3,2},{4,7},{5,4},{6,5},{7,6},{8,11},{9,8},{10,9... | collective-permute-start | bytes 786440 | tf_op jit(solution)/shard_map/ppermute | solution.py:398
  171.1 2.8 %collective-permute-done.15.far_top = bf16[512,256]{1,0:T(8,128)(2,1)S(1)} collective-permute-done((bf16[512,256]{1,0:T(8,128)(2,1)S(1)}, bf16[512,256]{1,0:T(8,128)(2,1)S(1)}, u32[]{:S(2)}, u32[]{:S(2)}) %collective-permute-start.15) | collective-permute-done | bytes 262176 | tf_op jit(solution)/shard_map/ppermute | solution.py:398
  (75 shorter events, 28.5 us)
Async XLA Ops:
  5.1 50.5 %all-to-all-start = ((bf16[32,32,768]{2,1,0:T(8,128)(2,1)}), bf16[32,32,768]{2,1,0:T(8,128)(2,1)S(1)}, u32[]{:S(2)}, u32[]{:S(2)}) async-start(bf16[32,32,768]{2,1,0:T(8,128)(2,1)} %bitcast.16), calls=%async_computation | async-start | bytes 3145728 | tf_op jit(solution)/shard_map/all_to_all | solution.py:415
  16.8 13.4 %collective-permute-start = (bf16[1024,768]{1,0:T(8,128)(2,1)}, bf16[1024,768]{1,0:T(8,128)(2,1)}, u32[]{:S(2)}, u32[]{:S(2)}) collective-permute-start(bf16[1024,768]{1,0:T(8,128)(2,1)} %key.3), channel_id=1, source_target_pairs={{0,4},{4,0},{8,12},{12,8},{16,20},{20,16},{24,28},{28,24},{32,36},... | collective-permute-start | bytes 4718600 | tf_op jit(solution)/shard_map/ppermute | solution.py:409
  16.9 13.3 %collective-permute-start.1 = (bf16[1024,768]{1,0:T(8,128)(2,1)}, bf16[1024,768]{1,0:T(8,128)(2,1)}, u32[]{:S(2)}, u32[]{:S(2)}) collective-permute-start(bf16[1024,768]{1,0:T(8,128)(2,1)} %value.3), channel_id=1, source_target_pairs={{0,4},{4,0},{8,12},{12,8},{16,20},{20,16},{24,28},{28,24},{32,36},... | collective-permute-start | bytes 4718600 | tf_op jit(solution)/shard_map/ppermute | solution.py:409
  24.6 30.0 %collective-permute-start.2 = (bf16[384,768]{1,0:T(8,128)(2,1)}, bf16[384,768]{1,0:T(8,128)(2,1)}, u32[]{:S(2)}, u32[]{:S(2)}) collective-permute-start(bf16[384,768]{1,0:T(8,128)(2,1)} %get-tuple-element.17.refs_1_), channel_id=1, source_target_pairs={{0,1},{1,2},{2,3},{3,0},{4,5},{5,6},{6,7},{7,4},{8,9},{9,10},{10,1... | collective-permute-start | bytes 1769480 | tf_op jit(solution)/shard_map/ppermute | solution.py:398
  26.1 28.7 %collective-permute-start.3 = (bf16[384,768]{1,0:T(8,128)(2,1)}, bf16[384,768]{1,0:T(8,128)(2,1)}, u32[]{:S(2)}, u32[]{:S(2)}) collective-permute-start(bf16[384,768]{1,0:T(8,128)(2,1)} %get-tuple-element.18.refs_2_), channel_id=1, source_target_pairs={{0,2},{1,3},{2,0},{3,1},{4,6},{5,7},{6,4},{7,5},{8,10},{9,11},{10,... | collective-permute-start | bytes 1769480 | tf_op jit(solution)/shard_map/ppermute | solution.py:398
  28.8 26.0 %collective-permute-start.4 = (bf16[384,768]{1,0:T(8,128)(2,1)}, bf16[384,768]{1,0:T(8,128)(2,1)S(1)}, u32[]{:S(2)}, u32[]{:S(2)}) collective-permute-start(bf16[384,768]{1,0:T(8,128)(2,1)} %get-tuple-element.19.refs_3_), channel_id=1, source_target_pairs={{0,3},{1,0},{2,1},{3,2},{4,7},{5,4},{6,5},{7,6},{8,11},{9,8},{10,9... | collective-permute-start | bytes 1769480 | tf_op jit(solution)/shard_map/ppermute | solution.py:398
  30.2 25.4 %copy-start.10 = (s32[6]{0:T(128)S(1)}, s32[6]{0:T(128)}, u32[]{:S(2)}) copy-start(s32[6]{0:T(128)} %classes.9) | copy-start | bytes 76
  57.6 9.9 %copy-start.14 = (bf16[384,768]{1,0:T(8,128)(2,1)S(1)}, bf16[384,768]{1,0:T(8,128)(2,1)}, u32[]{:S(2)}) copy-start(bf16[384,768]{1,0:T(8,128)(2,1)} %get-tuple-element.24.rest_3_) | copy-start | bytes 1769476
  57.6 58.6 %all-to-all-start.1 = ((bf16[32,32,1024]{2,1,0:T(8,128)(2,1)}), bf16[32,32,1024]{2,1,0:T(8,128)(2,1)S(1)}, u32[]{:S(2)}, u32[]{:S(2)}) async-start(bf16[32,32,1024]{2,1,0:T(8,128)(2,1)} %temporal.2), calls=%async_computation.1 | async-start | bytes 4194304 | tf_op jit(solution)/shard_map/all_to_all | solution.py:415
  70.2 19.4 %collective-permute-start.9 = (bf16[3,384,768]{2,1,0:T(8,128)(2,1)}, bf16[3,384,768]{2,1,0:T(8,128)(2,1)}, u32[]{:S(2)}, u32[]{:S(2)}) collective-permute-start(bf16[3,384,768]{2,1,0:T(8,128)(2,1)} %pad_maximum_fusion), channel_id=1, source_target_pairs={{0,4},{4,0},{8,12},{12,8},{16,20},{20,16},{24,28},{28,24},{32,36},... | collective-permute-start | bytes 5308424 | tf_op jit(solution)/shard_map/ppermute | solution.py:409
  70.2 15.8 %collective-permute-start.5 = (bf16[1024,256]{1,0:T(8,128)(2,1)}, bf16[1024,256]{1,0:T(8,128)(2,1)S(1)}, u32[]{:S(2)}, u32[]{:S(2)}) collective-permute-start(bf16[1024,256]{1,0:T(8,128)(2,1)} %get-tuple-element.21.refs_3_.own), channel_id=1, source_target_pairs={{0,1},{1,2},{2,3},{3,0},{4,5},{5,6},{6,7},{7,4},{8,9},{9,10},{10,1... | collective-permute-start | bytes 1572872 | tf_op jit(solution)/shard_map/ppermute | solution.py:398
  71.9 14.7 %collective-permute-start.6 = (bf16[1024,256]{1,0:T(8,128)(2,1)}, bf16[1024,256]{1,0:T(8,128)(2,1)S(1)}, u32[]{:S(2)}, u32[]{:S(2)}) collective-permute-start(bf16[1024,256]{1,0:T(8,128)(2,1)} %get-tuple-element.21.refs_3_.own), channel_id=1, source_target_pairs={{0,3},{1,0},{2,1},{3,2},{4,7},{5,4},{6,5},{7,6},{8,11},{9,8},{10,9... | collective-permute-start | bytes 1572872 | tf_op jit(solution)/shard_map/ppermute | solution.py:398
  86.0 9.2 %collective-permute-start.7 = (bf16[512,256]{1,0:T(8,128)(2,1)S(1)}, bf16[512,256]{1,0:T(8,128)(2,1)S(1)}, u32[]{:S(2)}, u32[]{:S(2)}) collective-permute-start(bf16[512,256]{1,0:T(8,128)(2,1)S(1)} %slice.36), channel_id=1, source_target_pairs={{0,1},{1,2},{2,3},{3,0},{4,5},{5,6},{6,7},{7,4},{8,9},{9,10},{10,1... | collective-permute-start | bytes 786440 | tf_op jit(solution)/shard_map/ppermute | solution.py:398
  86.6 8.6 %collective-permute-start.8 = (bf16[512,256]{1,0:T(8,128)(2,1)S(1)}, bf16[512,256]{1,0:T(8,128)(2,1)}, u32[]{:S(2)}, u32[]{:S(2)}) collective-permute-start(bf16[512,256]{1,0:T(8,128)(2,1)S(1)} %slice.37), channel_id=1, source_target_pairs={{0,3},{1,0},{2,1},{3,2},{4,7},{5,4},{6,5},{7,6},{8,11},{9,8},{10,9... | collective-permute-start | bytes 786440 | tf_op jit(solution)/shard_map/ppermute | solution.py:398
  117.8 24.8 %copy-start = (bf16[3,768,768]{2,1,0:T(8,128)(2,1)S(1)}, bf16[3,768,768]{2,1,0:T(8,128)(2,1)}, u32[]{:S(2)}) copy-start(bf16[3,768,768]{2,1,0:T(8,128)(2,1)} %maximum_select_fusion.refs_5_.w_others) | copy-start | bytes 10616836
  120.9 16.3 %collective-permute-start.10 = (bf16[1024,256]{1,0:T(8,128)(2,1)}, bf16[1024,256]{1,0:T(8,128)(2,1)}, u32[]{:S(2)}, u32[]{:S(2)}) collective-permute-start(bf16[1024,256]{1,0:T(8,128)(2,1)} %slice_add_fusion.1.refs_1_.own), channel_id=1, source_target_pairs={{0,1},{1,2},{2,3},{3,0},{4,5},{5,6},{6,7},{7,4},{8,9},{9,10},{10,1... | collective-permute-start | bytes 1572872 | tf_op jit(solution)/shard_map/ppermute | solution.py:398
  123.7 14.6 %collective-permute-start.11 = (bf16[1024,256]{1,0:T(8,128)(2,1)}, bf16[1024,256]{1,0:T(8,128)(2,1)}, u32[]{:S(2)}, u32[]{:S(2)}) collective-permute-start(bf16[1024,256]{1,0:T(8,128)(2,1)} %slice_add_fusion.1.refs_1_.own), channel_id=1, source_target_pairs={{0,3},{1,0},{2,1},{3,2},{4,7},{5,4},{6,5},{7,6},{8,11},{9,8},{10,9... | collective-permute-start | bytes 1572872 | tf_op jit(solution)/shard_map/ppermute | solution.py:398
  125.2 26.2 %all-to-all-start.2 = ((bf16[32,32,256]{2,1,0:T(8,128)(2,1)}), bf16[32,32,256]{2,1,0:T(8,128)(2,1)}, u32[]{:S(2)}, u32[]{:S(2)}) async-start(bf16[32,32,256]{2,1,0:T(8,128)(2,1)} %hold.10), calls=%async_computation.2 | async-start | bytes 1048576 | tf_op jit(solution)/shard_map/all_to_all | solution.py:415
  138.2 13.2 %collective-permute-start.12 = (bf16[512,256]{1,0:T(8,128)(2,1)S(1)}, bf16[512,256]{1,0:T(8,128)(2,1)}, u32[]{:S(2)}, u32[]{:S(2)}) collective-permute-start(bf16[512,256]{1,0:T(8,128)(2,1)S(1)} %slice.40), channel_id=1, source_target_pairs={{0,1},{1,2},{2,3},{3,0},{4,5},{5,6},{6,7},{7,4},{8,9},{9,10},{10,1... | collective-permute-start | bytes 786440 | tf_op jit(solution)/shard_map/ppermute | solution.py:398
  139.3 12.2 %collective-permute-start.13 = (bf16[512,256]{1,0:T(8,128)(2,1)S(1)}, bf16[512,256]{1,0:T(8,128)(2,1)}, u32[]{:S(2)}, u32[]{:S(2)}) collective-permute-start(bf16[512,256]{1,0:T(8,128)(2,1)S(1)} %slice.41), channel_id=1, source_target_pairs={{0,3},{1,0},{2,1},{3,2},{4,7},{5,4},{6,5},{7,6},{8,11},{9,8},{10,9... | collective-permute-start | bytes 786440 | tf_op jit(solution)/shard_map/ppermute | solution.py:398
  152.7 13.6 %collective-permute-start.14 = (bf16[1024,256]{1,0:T(8,128)(2,1)S(1)}, bf16[1024,256]{1,0:T(8,128)(2,1)S(1)}, u32[]{:S(2)}, u32[]{:S(2)}) collective-permute-start(bf16[1024,256]{1,0:T(8,128)(2,1)S(1)} %slice_add_fusion.own), channel_id=1, source_target_pairs={{0,1},{1,2},{2,3},{3,0},{4,5},{5,6},{6,7},{7,4},{8,9},{9,10},{10,1... | collective-permute-start | bytes 1572872 | tf_op jit(solution)/shard_map/ppermute | solution.py:398
  152.8 13.6 %collective-permute-start.16 = (bf16[1024,256]{1,0:T(8,128)(2,1)S(1)}, bf16[1024,256]{1,0:T(8,128)(2,1)S(1)}, u32[]{:S(2)}, u32[]{:S(2)}) collective-permute-start(bf16[1024,256]{1,0:T(8,128)(2,1)S(1)} %slice_add_fusion.own), channel_id=1, source_target_pairs={{0,3},{1,0},{2,1},{3,2},{4,7},{5,4},{6,5},{7,6},{8,11},{9,8},{10,9... | collective-permute-start | bytes 1572872 | tf_op jit(solution)/shard_map/ppermute | solution.py:398
  166.3 7.7 %collective-permute-start.15 = (bf16[512,256]{1,0:T(8,128)(2,1)S(1)}, bf16[512,256]{1,0:T(8,128)(2,1)S(1)}, u32[]{:S(2)}, u32[]{:S(2)}) collective-permute-start(bf16[512,256]{1,0:T(8,128)(2,1)S(1)} %slice.43), channel_id=1, source_target_pairs={{0,1},{1,2},{2,3},{3,0},{4,5},{5,6},{6,7},{7,4},{8,9},{9,10},{10,1... | collective-permute-start | bytes 786440 | tf_op jit(solution)/shard_map/ppermute | solution.py:398
  166.5 7.5 %collective-permute-start.17 = (bf16[512,256]{1,0:T(8,128)(2,1)S(1)}, bf16[512,256]{1,0:T(8,128)(2,1)S(1)}, u32[]{:S(2)}, u32[]{:S(2)}) collective-permute-start(bf16[512,256]{1,0:T(8,128)(2,1)S(1)} %slice.44), channel_id=1, source_target_pairs={{0,3},{1,0},{2,1},{3,2},{4,7},{5,4},{6,5},{7,6},{8,11},{9,8},{10,9... | collective-permute-start | bytes 786440 | tf_op jit(solution)/shard_map/ppermute | solution.py:398
  (12 other events, 28.5 us)

commit v11 on v9

--- a/solution.py
+++ b/solution.py
@@ -204,34 +204,28 @@
     same = (row & (ROWS - 1)) == (column & (ROWS - 1))
     total = temporal_count(classes, head_count)
 
-    def attend(queries, keys, values):
-        exponents = jnp.where(same, scores_of(queries, keys) * LOG2_SCALE, -1e30)
-        weights = jnp.exp2(exponents).astype(jnp.bfloat16)
-        both = jnp.concatenate([values, jnp.ones_like(values)], axis=1)
-        summed = jnp.dot(weights, both, preferred_element_type=jnp.float32)
-        return (summed[:, :HD] / summed[:, HD:]).reshape(frames, ROWS, HD)
+    ones = jnp.ones((count, HD), jnp.bfloat16)
 
     def store(slot):
         return pltpu.make_async_copy(held.at[slot], out.at[:, :, pl.ds(slot * HD, HD)], sems.at[slot])
 
     for slot in range(TMAX):
-
-        @pl.when(slot < total)
-        def _(slot=slot):
-            for begin in range(0, positions, 2 * ROWS):
-                at = slice(begin, begin + 2 * ROWS)
-                columns = [slice((3 * slot + which) * HD, (3 * slot + which + 1) * HD) for which in range(3)]
-                wide = [packed[:, at, column].astype(jnp.float32) for column in columns]
-                results = []
-                for first in (0, ROWS):
-                    parts = [array[:, first : first + ROWS].reshape(count, HD).astype(jnp.bfloat16) for array in wide]
-                    results.append(attend(*parts))
-                held[slot, :, at] = jnp.concatenate(results, axis=1).astype(jnp.bfloat16)
-
-        @pl.when(slot >= total)
-        def _(slot=slot):
-            held[slot] = jnp.zeros(held.shape[1:], held.dtype)
-
+        parts = []
+        for begin in range(0, positions, 2 * ROWS):
+            columns = [slice((3 * slot + which) * HD, (3 * slot + which + 1) * HD) for which in range(3)]
+            wide = [packed[:, begin : begin + 2 * ROWS, column].astype(jnp.float32) for column in columns]
+            for first in (0, ROWS):
+                parts.append([array[:, first : first + ROWS].reshape(count, HD).astype(jnp.bfloat16) for array in wide])
+        scores = [scores_of(queries, keys) for queries, keys, _ in parts]
+        weights = [jnp.exp2(jnp.where(same, score * LOG2_SCALE, -1e30)).astype(jnp.bfloat16) for score in scores]
+        results = []
+        for weight, (_, _, values) in zip(weights, parts, strict=True):
+            summed = jnp.dot(weight, jnp.concatenate([values, ones], axis=1), preferred_element_type=jnp.float32)
+            result = jnp.where(slot < total, summed[:, :HD] / summed[:, HD:], 0.0)
+            results.append(result.reshape(frames, ROWS, HD))
+        for pair in range(len(results) // 2):
+            both = jnp.concatenate(results[2 * pair : 2 * pair + 2], axis=1)
+            held[slot, :, 2 * ROWS * pair : 2 * ROWS * (pair + 1)] = both.astype(jnp.bfloat16)
         store(slot).start()
     for slot in range(TMAX):
         store(slot).wait()

time: 165 us -> 165 us (level)
  waiting for transfers between devices: 44 us -> 40.8 us
  Pallas kernels: 37 us -> 39.3 us
    pallas_call x1, Pallas kernels: 14.3 us -> 17.5 us  [spatial(): pl.pallas_call(functools.partial(spatial_kernel, head_count), grid_spec=p...]
    ppermute x15, waiting for transfers between devices: 36.5 us -> 33.3 us  [shifted(): lax.ppermute(block, 'head', [(at, (at + by) % count) for at in range(coun...]
  transfers between devices with their start and end apart: 19 -> 19, of which waited for: 8 -> 9; matrix products, arithmetic and copies ran while one was open for 6% -> 6% of each run, Pallas kernels for 16% -> 18%
where the time goes in v11:
time: 165 us; the launch traced here: 164 us
  waiting for transfers between devices  40.8 us (25%)
  Pallas kernels  39.3 us (24%)
  starting transfers between devices  37.5 us (23%)
  blocking collectives  35.3 us (21%)
  other arithmetic  8.76 us (5%)
  local copies, waits for them, and re-layouts  1.69 us (1%)
    all_to_all x1, blocking collectives, over_frames(): return lax.all_to_all(blocks, 'seq', 0, 0, axis_index_groups=groups)  35.3 us
    ppermute x15, waiting for transfers between devices, shifted(): lax.ppermute(block, 'head', [(at, (at + by) % count) for at in range(coun...  33.3 us
    ppermute x15, starting transfers between devices, shifted(): lax.ppermute(block, 'head', [(at, (at + by) % count) for at in range(coun...  25.2 us
    pallas_call x1, Pallas kernels, spatial(): pl.pallas_call(functools.partial(spatial_kernel, head_count), grid_spec=p...  17.5 us
    all_to_all x1, starting transfers between devices, over_frames(): return lax.all_to_all(blocks, 'seq', 0, 0, axis_index_groups=groups)  11.7 us
    all_to_all x1, waiting for transfers between devices, over_frames(): return lax.all_to_all(blocks, 'seq', 0, 0, axis_index_groups=groups)  7.48 us
    pallas_call x1, Pallas kernels, weight_blocks(): pl.pallas_call(weight_kernel, grid_spec=pltpu.PrefetchScalarGridSpec(num_...  6.46 us
    pallas_call x2, Pallas kernels, summing(): pl.pallas_call(kernel, in_specs=[whole] * len(operands), out_specs=whole,...  5.74 us
  transfers between devices with their start and end apart: 19, of which 9 were waited for; matrix products, arithmetic and copies ran while one was open for 6% of the time, Pallas kernels for 18%

profile of v11, /device:TPU:8, one launch (start us, length us, event | category | flops | bytes accessed | tf_op | source)
XLA Modules:
  0.0 163.7 jit_solution(17139787377914745738)
XLA Ops:
  0.0 5.2 %pack.1 = bf16[1024,1536]{1,0:T(8,128)(2,1)} custom-call(s32[6]{0:T(128)} %classes.7, bf16[1024,768]{1,0:T(8,128)(2,1)} %query.3, bf16[1024,768]{1,0:T(8,128)(2,1)} %key.3, bf16[1024,768]{1,0:T(8,128)(2,1)} %value.3, f32[1,128]{1,0:T(1,128)} %bitcast.13, f32[1,128]{1,0:T(1,128)} %bitcast.15), custom_call_target="tpu_custom_call" | custom-call | flops 4194304 | bytes 6291456 | tf_op jit(solution)/shard_map/pack/pallas_call | solution.py:105
  5.2 11.7 %all-to-all-start = ((bf16[32,32,1536]{2,1,0:T(8,128)(2,1)}), bf16[32,32,1536]{2,1,0:T(8,128)(2,1)S(1)}, u32[]{:S(2)}, u32[]{:S(2)}) async-start(bf16[32,32,1536]{2,1,0:T(8,128)(2,1)} %bitcast.12), calls=%async_computation | async-start | bytes 6291456 | tf_op jit(solution)/shard_map/all_to_all | solution.py:395
  18.1 6.5 %weight_blocks.1 = (bf16[768,768]{1,0:T(8,128)(2,1)}, bf16[384,768]{1,0:T(8,128)(2,1)}, bf16[384,768]{1,0:T(8,128)(2,1)}, bf16[384,768]{1,0:T(8,128)(2,1)}) custom-call(s32[6]{0:T(128)} %classes.7, s32[2]{0:T(128)} %pad_add_fusion.place, bf16[768,3072]{1,0:T(8,128)(2,1)} %weight.1), custom_call_target="tpu_custom_call" | custom-call | bytes 9437184 | tf_op jit(solution)/shard_map/weight_blocks/pallas_call | solution.py:284
  26.1 2.7 %collective-permute-start.9 = (bf16[384,768]{1,0:T(8,128)(2,1)}, bf16[384,768]{1,0:T(8,128)(2,1)}, u32[]{:S(2)}, u32[]{:S(2)}) collective-permute-start(bf16[384,768]{1,0:T(8,128)(2,1)} %get-tuple-element.16), channel_id=1, source_target_pairs={{0,2},{1,3},{2,0},{3,1},{4,6},{5,7},{6,4},{7,5},{8,10},{9,11},{10,... | collective-permute-start | bytes 1769480 | tf_op jit(solution)/shard_map/ppermute | solution.py:377
  30.3 17.5 %spatial.1 = (bf16[1024,512]{1,0:T(8,128)(2,1)}, bf16[1024,256]{1,0:T(8,128)(2,1)}) custom-call(s32[6]{0:T(128)} %classes.7, bf16[1024,768]{1,0:T(8,128)(2,1)} %query.3, bf16[1024,768]{1,0:T(8,128)(2,1)} %key.3, bf16[1024,768]{1,0:T(8,128)(2,1)} %collective-permute-done.other_key, bf16[1024,768]{1,0:T(8,128)(2,1)} %value.3, ...), custom_call_target="tpu_custom_call" | custom-call | flops 12884901888 | bytes 9437184 | tf_op jit(solution)/shard_map/spatial/pallas_call | solution.py:172
  47.7 7.1 %collective-permute-done.9.refs_1_ = bf16[384,768]{1,0:T(8,128)(2,1)} collective-permute-done((bf16[384,768]{1,0:T(8,128)(2,1)}, bf16[384,768]{1,0:T(8,128)(2,1)}, u32[]{:S(2)}, u32[]{:S(2)}) %collective-permute-start.9) | collective-permute-done | bytes 589856 | tf_op jit(solution)/shard_map/ppermute | solution.py:377
  54.9 2.9 %pad_maximum_fusion = bf16[3,384,768]{2,1,0:T(8,128)(2,1)} fusion(bf16[1,384,768]{2,1,0:T(8,128)(2,1)} %bitcast.7, bf16[1,384,768]{2,1,0:T(8,128)(2,1)} %bitcast.6, bf16[1,384,768]{2,1,0:T(8,128)(2,1)} %bitcast.5), kind=kLoop, calls=%fused_computation.1 | loop fusion | flops 1769472 | bytes 3538944 | tf_op jit(solution)/shard_map/stack | solution.py:413
  59.9 1.9 %collective-permute-start.5 = (bf16[512,256]{1,0:T(8,128)(2,1)}, bf16[512,256]{1,0:T(8,128)(2,1)}, u32[]{:S(2)}, u32[]{:S(2)}) collective-permute-start(bf16[512,256]{1,0:T(8,128)(2,1)} %get-tuple-element.27.own_bottom), channel_id=1, source_target_pairs={{0,3},{1,0},{2,1},{3,2},{4,7},{5,4},{6,5},{7,6},{8,11},{9,8},{10,9... | collective-permute-start | bytes 786440 | tf_op jit(solution)/shard_map/ppermute | solution.py:377
  62.0 3.1 %collective-permute-start.4 = (bf16[512,256]{1,0:T(8,128)(2,1)}, bf16[512,256]{1,0:T(8,128)(2,1)S(1)}, u32[]{:S(2)}, u32[]{:S(2)}) collective-permute-start(bf16[512,256]{1,0:T(8,128)(2,1)} %get-tuple-element.28.own_top), channel_id=1, source_target_pairs={{0,3},{1,0},{2,1},{3,2},{4,7},{5,4},{6,5},{7,6},{8,11},{9,8},{10,9... | collective-permute-start | bytes 786440 | tf_op jit(solution)/shard_map/ppermute | solution.py:377
  65.1 4.0 %collective-permute-done.2.rest_0_.right_top = bf16[512,256]{1,0:T(8,128)(2,1)S(1)} collective-permute-done((bf16[512,256]{1,0:T(8,128)(2,1)}, bf16[512,256]{1,0:T(8,128)(2,1)S(1)}, u32[]{:S(2)}, u32[]{:S(2)}) %collective-permute-start.2) | collective-permute-done | bytes 262176 | tf_op jit(solution)/shard_map/ppermute | solution.py:377
  69.4 3.1 %collective-permute-start.7 = (bf16[512,256]{1,0:T(8,128)(2,1)}, bf16[512,256]{1,0:T(8,128)(2,1)}, u32[]{:S(2)}, u32[]{:S(2)}) collective-permute-start(bf16[512,256]{1,0:T(8,128)(2,1)} %collective-permute-done.5.rest_3_.left_bottom), channel_id=1, source_target_pairs={{0,3},{1,0},{2,1},{3,2},{4,7},{5,4},{6,5},{7,6},{8,11},{9,8},{10,9... | collective-permute-start | bytes 786440 | tf_op jit(solution)/shard_map/ppermute | solution.py:377
  72.5 5.0 %maximum_select_fusion.rest_6_.w_others = bf16[3,768,768]{2,1,0:T(8,128)(2,1)} fusion(bf16[3,384,768]{2,1,0:T(8,128)(2,1)} %collective-permute-done.11, bf16[1,384,768]{2,1,0:T(8,128)(2,1)} %bitcast.7, bf16[1,384,768]{2,1,0:T(8,128)(2,1)} %bitcast.6, bf16[1,384,768]{2,1,0:T(8,128)(2,1)} %bitcast.5, pred[]{:T(512)S(6)} %eq.3), kind=kLoop, calls=%fused_computation | loop fusion | flops 30081024 | bytes 7077889 | tf_op jit(solution)/shard_map/jit(_where)/select_n | solution.py:415
  77.6 2.4 %collective-permute-done.6.rest_4_.far_top = bf16[512,256]{1,0:T(8,128)(2,1)S(1)} collective-permute-done((bf16[512,256]{1,0:T(8,128)(2,1)S(1)}, bf16[512,256]{1,0:T(8,128)(2,1)S(1)}, u32[]{:S(2)}, u32[]{:S(2)}) %collective-permute-start.6) | collective-permute-done | bytes 262176 | tf_op jit(solution)/shard_map/ppermute | solution.py:377
  80.7 7.5 %all-to-all-done.packed = bf16[32,32,1536]{2,1,0:T(8,128)(2,1)S(1)} async-done(((bf16[32,32,1536]{2,1,0:T(8,128)(2,1)}), bf16[32,32,1536]{2,1,0:T(8,128)(2,1)S(1)}, u32[]{:S(2)}, u32[]{:S(2)}) %all-to-all-start) | async-done | bytes 3145760 | tf_op jit(solution)/shard_map/all_to_all | solution.py:395
  88.2 2.7 %temporal.1 = bf16[32,32,512]{2,1,0:T(8,128)(2,1)} custom-call(s32[6]{0:T(128)S(1)} %copy-done.10, bf16[32,32,1536]{2,1,0:T(8,128)(2,1)S(1)} %all-to-all-done.packed, bf16[512,256]{1,0:T(8,128)(2,1)} %copy-done.2, bf16[512,256]{1,0:T(8,128)(2,1)} %copy-done.4, bf16[512,256]{1,0:T(8,128)(2,1)} %copy-done.6, ...), custom_call_target="tpu_custom_call" | custom-call | flops 536870912 | bytes 4194304 | tf_op jit(solution)/shard_map/temporal/pallas_call | solution.py:236
  90.9 35.3 %all_to_all.10 = bf16[32,32,512]{2,1,0:T(8,128)(2,1)S(1)} all-to-all(bf16[32,32,512]{2,1,0:T(8,128)(2,1)} %temporal.1), channel_id=1, replica_groups={{0,8,16,24,32,40,48,56,64,72,80,88,96,104,112,120,128,136,144,152,160,1..., dimensions={0} | all-to-all | bytes 2097152 | tf_op jit(solution)/shard_map/all_to_all | solution.py:395
  130.1 3.0 %collective-permute-start.17 = (bf16[512,512]{1,0:T(8,128)(2,1)S(1)}, bf16[512,512]{1,0:T(8,128)(2,1)S(1)}, u32[]{:S(2)}, u32[]{:S(2)}) collective-permute-start(bf16[512,512]{1,0:T(8,128)(2,1)S(1)} %get-tuple-element.24.own_top), channel_id=1, source_target_pairs={{0,3},{1,0},{2,1},{3,2},{4,7},{5,4},{6,5},{7,6},{8,11},{9,8},{10,9... | collective-permute-start | bytes 1572872 | tf_op jit(solution)/shard_map/ppermute | solution.py:377
  133.1 9.6 %collective-permute-done.12.right_top = bf16[512,512]{1,0:T(8,128)(2,1)S(1)} collective-permute-done((bf16[512,512]{1,0:T(8,128)(2,1)S(1)}, bf16[512,512]{1,0:T(8,128)(2,1)S(1)}, u32[]{:S(2)}, u32[]{:S(2)}) %collective-permute-start.12) | collective-permute-done | bytes 524320 | tf_op jit(solution)/shard_map/ppermute | solution.py:377
  143.0 3.0 %collective-permute-start.15 = (bf16[512,512]{1,0:T(8,128)(2,1)S(1)}, bf16[512,512]{1,0:T(8,128)(2,1)S(1)}, u32[]{:S(2)}, u32[]{:S(2)}) collective-permute-start(bf16[512,512]{1,0:T(8,128)(2,1)S(1)} %collective-permute-done.14.left_bottom), channel_id=1, source_target_pairs={{0,3},{1,0},{2,1},{3,2},{4,7},{5,4},{6,5},{7,6},{8,11},{9,8},{10,9... | collective-permute-start | bytes 1572872 | tf_op jit(solution)/shard_map/ppermute | solution.py:377
  146.0 3.0 %project_early.1.total = f32[1024,768]{1,0:T(8,128)S(1)} custom-call(bf16[512,256]{1,0:T(8,128)(2,1)} %get-tuple-element.28.own_top, bf16[512,256]{1,0:T(8,128)(2,1)} %get-tuple-element.27.own_bottom, bf16[512,256]{1,0:T(8,128)(2,1)S(1)} %copy-done.3, bf16[512,256]{1,0:T(8,128)(2,1)S(1)} %copy-done.5, bf16[512,256]{1,0:T(8,128)(2,1)S(1)} %copy-done.7, ...), custom_call_target="tpu_custom_call" | custom-call | flops 1610612736 | bytes 6291456 | tf_op jit(solution)/shard_map/project_early/pallas_call | solution.py:340
  149.0 4.9 %collective-permute-done.16.right_bottom = bf16[512,512]{1,0:T(8,128)(2,1)S(1)} collective-permute-done((bf16[512,512]{1,0:T(8,128)(2,1)S(1)}, bf16[512,512]{1,0:T(8,128)(2,1)S(1)}, u32[]{:S(2)}, u32[]{:S(2)}) %collective-permute-start.16) | collective-permute-done | bytes 524320 | tf_op jit(solution)/shard_map/ppermute | solution.py:377
  154.2 2.7 %near.1.total = f32[1024,768]{1,0:T(8,128)S(1)} custom-call(bf16[512,512]{1,0:T(8,128)(2,1)S(1)} %get-tuple-element.24.own_top, bf16[512,512]{1,0:T(8,128)(2,1)S(1)} %get-tuple-element.23.own_bottom, bf16[512,512]{1,0:T(8,128)(2,1)S(1)} %collective-permute-done.12.right_top, bf16[512,512]{1,0:T(8,128)(2,1)S(1)} %collective-permute-done.16.right_bottom, ...), custom_call_target="tpu_custom_call" | custom-call | flops 2415919104 | bytes 6291456 | tf_op jit(solution)/shard_map/near/pallas_call | solution.py:340
  156.9 4.8 %collective-permute-done.13.far_top = bf16[512,512]{1,0:T(8,128)(2,1)S(1)} collective-permute-done((bf16[512,512]{1,0:T(8,128)(2,1)S(1)}, bf16[512,512]{1,0:T(8,128)(2,1)S(1)}, u32[]{:S(2)}, u32[]{:S(2)}) %collective-permute-start.13) | collective-permute-done | bytes 524320 | tf_op jit(solution)/shard_map/ppermute | solution.py:377
  161.8 1.8 %far.1 = bf16[1024,768]{1,0:T(8,128)(2,1)} custom-call(bf16[512,512]{1,0:T(8,128)(2,1)S(1)} %collective-permute-done.13.far_top, bf16[512,512]{1,0:T(8,128)(2,1)S(1)} %collective-permute-done.15.far_bottom, bf16[3,768,768]{2,1,0:T(8,128)(2,1)S(1)} %copy-done, f32[1024,768]{1,0:T(8,128)S(1)} %near.1.total), custom_call_target="tpu_custom_call" | custom-call | flops 805306368 | bytes 6291456 | tf_op jit(solution)/shard_map/far/pallas_call | solution.py:363
  (55 shorter events, 11.9 us)
Async XLA Ops:
  5.2 83.0 %all-to-all-start = ((bf16[32,32,1536]{2,1,0:T(8,128)(2,1)}), bf16[32,32,1536]{2,1,0:T(8,128)(2,1)S(1)}, u32[]{:S(2)}, u32[]{:S(2)}) async-start(bf16[32,32,1536]{2,1,0:T(8,128)(2,1)} %bitcast.12), calls=%async_computation | async-start | bytes 6291456 | tf_op jit(solution)/shard_map/all_to_all | solution.py:395
  16.9 13.4 %collective-permute-start = (bf16[1024,768]{1,0:T(8,128)(2,1)}, bf16[1024,768]{1,0:T(8,128)(2,1)}, u32[]{:S(2)}, u32[]{:S(2)}) collective-permute-start(bf16[1024,768]{1,0:T(8,128)(2,1)} %key.3), channel_id=1, source_target_pairs={{0,4},{4,0},{8,12},{12,8},{16,20},{20,16},{24,28},{28,24},{32,36},... | collective-permute-start | bytes 4718600 | tf_op jit(solution)/shard_map/ppermute | solution.py:389
  17.0 13.3 %collective-permute-start.1 = (bf16[1024,768]{1,0:T(8,128)(2,1)}, bf16[1024,768]{1,0:T(8,128)(2,1)}, u32[]{:S(2)}, u32[]{:S(2)}) collective-permute-start(bf16[1024,768]{1,0:T(8,128)(2,1)} %value.3), channel_id=1, source_target_pairs={{0,4},{4,0},{8,12},{12,8},{16,20},{20,16},{24,28},{28,24},{32,36},... | collective-permute-start | bytes 4718600 | tf_op jit(solution)/shard_map/ppermute | solution.py:389
  24.6 23.1 %collective-permute-start.8 = (bf16[384,768]{1,0:T(8,128)(2,1)}, bf16[384,768]{1,0:T(8,128)(2,1)}, u32[]{:S(2)}, u32[]{:S(2)}) collective-permute-start(bf16[384,768]{1,0:T(8,128)(2,1)} %get-tuple-element.15), channel_id=1, source_target_pairs={{0,1},{1,2},{2,3},{3,0},{4,5},{5,6},{6,7},{7,4},{8,9},{9,10},{10,1... | collective-permute-start | bytes 1769480 | tf_op jit(solution)/shard_map/ppermute | solution.py:377
  26.1 28.7 %collective-permute-start.9 = (bf16[384,768]{1,0:T(8,128)(2,1)}, bf16[384,768]{1,0:T(8,128)(2,1)}, u32[]{:S(2)}, u32[]{:S(2)}) collective-permute-start(bf16[384,768]{1,0:T(8,128)(2,1)} %get-tuple-element.16), channel_id=1, source_target_pairs={{0,2},{1,3},{2,0},{3,1},{4,6},{5,7},{6,4},{7,5},{8,10},{9,11},{10,... | collective-permute-start | bytes 1769480 | tf_op jit(solution)/shard_map/ppermute | solution.py:377
  28.8 26.0 %collective-permute-start.10 = (bf16[384,768]{1,0:T(8,128)(2,1)}, bf16[384,768]{1,0:T(8,128)(2,1)}, u32[]{:S(2)}, u32[]{:S(2)}) collective-permute-start(bf16[384,768]{1,0:T(8,128)(2,1)} %get-tuple-element.17), channel_id=1, source_target_pairs={{0,3},{1,0},{2,1},{3,2},{4,7},{5,4},{6,5},{7,6},{8,11},{9,8},{10,9... | collective-permute-start | bytes 1769480 | tf_op jit(solution)/shard_map/ppermute | solution.py:377
  57.8 14.7 %collective-permute-start.11 = (bf16[3,384,768]{2,1,0:T(8,128)(2,1)}, bf16[3,384,768]{2,1,0:T(8,128)(2,1)}, u32[]{:S(2)}, u32[]{:S(2)}) collective-permute-start(bf16[3,384,768]{2,1,0:T(8,128)(2,1)} %pad_maximum_fusion), channel_id=1, source_target_pairs={{0,4},{4,0},{8,12},{12,8},{16,20},{20,16},{24,28},{28,24},{32,36},... | collective-permute-start | bytes 5308424 | tf_op jit(solution)/shard_map/ppermute | solution.py:389
  58.6 10.5 %collective-permute-start.2 = (bf16[512,256]{1,0:T(8,128)(2,1)}, bf16[512,256]{1,0:T(8,128)(2,1)S(1)}, u32[]{:S(2)}, u32[]{:S(2)}) collective-permute-start(bf16[512,256]{1,0:T(8,128)(2,1)} %get-tuple-element.28.own_top), channel_id=1, source_target_pairs={{0,1},{1,2},{2,3},{3,0},{4,5},{5,6},{6,7},{7,4},{8,9},{9,10},{10,1... | collective-permute-start | bytes 786440 | tf_op jit(solution)/shard_map/ppermute | solution.py:377
  59.9 9.5 %collective-permute-start.5 = (bf16[512,256]{1,0:T(8,128)(2,1)}, bf16[512,256]{1,0:T(8,128)(2,1)}, u32[]{:S(2)}, u32[]{:S(2)}) collective-permute-start(bf16[512,256]{1,0:T(8,128)(2,1)} %get-tuple-element.27.own_bottom), channel_id=1, source_target_pairs={{0,3},{1,0},{2,1},{3,2},{4,7},{5,4},{6,5},{7,6},{8,11},{9,8},{10,9... | collective-permute-start | bytes 786440 | tf_op jit(solution)/shard_map/ppermute | solution.py:377
  61.8 15.7 %collective-permute-start.3 = (bf16[512,256]{1,0:T(8,128)(2,1)}, bf16[512,256]{1,0:T(8,128)(2,1)S(1)}, u32[]{:S(2)}, u32[]{:S(2)}) collective-permute-start(bf16[512,256]{1,0:T(8,128)(2,1)} %get-tuple-element.27.own_bottom), channel_id=1, source_target_pairs={{0,1},{1,2},{2,3},{3,0},{4,5},{5,6},{6,7},{7,4},{8,9},{9,10},{10,1... | collective-permute-start | bytes 786440 | tf_op jit(solution)/shard_map/ppermute | solution.py:377
  62.0 15.6 %collective-permute-start.4 = (bf16[512,256]{1,0:T(8,128)(2,1)}, bf16[512,256]{1,0:T(8,128)(2,1)S(1)}, u32[]{:S(2)}, u32[]{:S(2)}) collective-permute-start(bf16[512,256]{1,0:T(8,128)(2,1)} %get-tuple-element.28.own_top), channel_id=1, source_target_pairs={{0,3},{1,0},{2,1},{3,2},{4,7},{5,4},{6,5},{7,6},{8,11},{9,8},{10,9... | collective-permute-start | bytes 786440 | tf_op jit(solution)/shard_map/ppermute | solution.py:377
  69.1 10.8 %collective-permute-start.6 = (bf16[512,256]{1,0:T(8,128)(2,1)S(1)}, bf16[512,256]{1,0:T(8,128)(2,1)S(1)}, u32[]{:S(2)}, u32[]{:S(2)}) collective-permute-start(bf16[512,256]{1,0:T(8,128)(2,1)S(1)} %collective-permute-done.2.rest_0_.right_top), channel_id=1, source_target_pairs={{0,1},{1,2},{2,3},{3,0},{4,5},{5,6},{6,7},{7,4},{8,9},{9,10},{10,1... | collective-permute-start | bytes 786440 | tf_op jit(solution)/shard_map/ppermute | solution.py:377
  69.4 11.3 %collective-permute-start.7 = (bf16[512,256]{1,0:T(8,128)(2,1)}, bf16[512,256]{1,0:T(8,128)(2,1)}, u32[]{:S(2)}, u32[]{:S(2)}) collective-permute-start(bf16[512,256]{1,0:T(8,128)(2,1)} %collective-permute-done.5.rest_3_.left_bottom), channel_id=1, source_target_pairs={{0,3},{1,0},{2,1},{3,2},{4,7},{5,4},{6,5},{7,6},{8,11},{9,8},{10,9... | collective-permute-start | bytes 786440 | tf_op jit(solution)/shard_map/ppermute | solution.py:377
  90.8 55.1 %copy-start = (bf16[3,768,768]{2,1,0:T(8,128)(2,1)S(1)}, bf16[3,768,768]{2,1,0:T(8,128)(2,1)}, u32[]{:S(2)}) copy-start(bf16[3,768,768]{2,1,0:T(8,128)(2,1)} %maximum_select_fusion.rest_6_.w_others) | copy-start | bytes 10616836
  90.8 55.1 %copy-start.1 = (bf16[768,768]{1,0:T(8,128)(2,1)S(1)}, bf16[768,768]{1,0:T(8,128)(2,1)}, u32[]{:S(2)}) copy-start(bf16[768,768]{1,0:T(8,128)(2,1)} %get-tuple-element.22.w_own) | copy-start | bytes 3538948
  90.9 55.1 %copy-start.3 = (bf16[512,256]{1,0:T(8,128)(2,1)S(1)}, bf16[512,256]{1,0:T(8,128)(2,1)}, u32[]{:S(2)}) copy-start(bf16[512,256]{1,0:T(8,128)(2,1)} %copy-done.2) | copy-start | bytes 786436
  90.9 55.1 %copy-start.5 = (bf16[512,256]{1,0:T(8,128)(2,1)S(1)}, bf16[512,256]{1,0:T(8,128)(2,1)}, u32[]{:S(2)}) copy-start(bf16[512,256]{1,0:T(8,128)(2,1)} %copy-done.4) | copy-start | bytes 786436
  90.9 55.1 %copy-start.7 = (bf16[512,256]{1,0:T(8,128)(2,1)S(1)}, bf16[512,256]{1,0:T(8,128)(2,1)}, u32[]{:S(2)}) copy-start(bf16[512,256]{1,0:T(8,128)(2,1)} %copy-done.6) | copy-start | bytes 786436
  126.5 16.1 %collective-permute-start.12 = (bf16[512,512]{1,0:T(8,128)(2,1)S(1)}, bf16[512,512]{1,0:T(8,128)(2,1)S(1)}, u32[]{:S(2)}, u32[]{:S(2)}) collective-permute-start(bf16[512,512]{1,0:T(8,128)(2,1)S(1)} %get-tuple-element.24.own_top), channel_id=1, source_target_pairs={{0,1},{1,2},{2,3},{3,0},{4,5},{5,6},{6,7},{7,4},{8,9},{9,10},{10,1... | collective-permute-start | bytes 1572872 | tf_op jit(solution)/shard_map/ppermute | solution.py:377
  128.1 14.9 %collective-permute-start.14 = (bf16[512,512]{1,0:T(8,128)(2,1)S(1)}, bf16[512,512]{1,0:T(8,128)(2,1)S(1)}, u32[]{:S(2)}, u32[]{:S(2)}) collective-permute-start(bf16[512,512]{1,0:T(8,128)(2,1)S(1)} %get-tuple-element.23.own_bottom), channel_id=1, source_target_pairs={{0,3},{1,0},{2,1},{3,2},{4,7},{5,4},{6,5},{7,6},{8,11},{9,8},{10,9... | collective-permute-start | bytes 1572872 | tf_op jit(solution)/shard_map/ppermute | solution.py:377
  129.8 24.1 %collective-permute-start.16 = (bf16[512,512]{1,0:T(8,128)(2,1)S(1)}, bf16[512,512]{1,0:T(8,128)(2,1)S(1)}, u32[]{:S(2)}, u32[]{:S(2)}) collective-permute-start(bf16[512,512]{1,0:T(8,128)(2,1)S(1)} %get-tuple-element.23.own_bottom), channel_id=1, source_target_pairs={{0,1},{1,2},{2,3},{3,0},{4,5},{5,6},{6,7},{7,4},{8,9},{9,10},{10,1... | collective-permute-start | bytes 1572872 | tf_op jit(solution)/shard_map/ppermute | solution.py:377
  130.1 24.1 %collective-permute-start.17 = (bf16[512,512]{1,0:T(8,128)(2,1)S(1)}, bf16[512,512]{1,0:T(8,128)(2,1)S(1)}, u32[]{:S(2)}, u32[]{:S(2)}) collective-permute-start(bf16[512,512]{1,0:T(8,128)(2,1)S(1)} %get-tuple-element.24.own_top), channel_id=1, source_target_pairs={{0,3},{1,0},{2,1},{3,2},{4,7},{5,4},{6,5},{7,6},{8,11},{9,8},{10,9... | collective-permute-start | bytes 1572872 | tf_op jit(solution)/shard_map/ppermute | solution.py:377
  142.7 19.1 %collective-permute-start.13 = (bf16[512,512]{1,0:T(8,128)(2,1)S(1)}, bf16[512,512]{1,0:T(8,128)(2,1)S(1)}, u32[]{:S(2)}, u32[]{:S(2)}) collective-permute-start(bf16[512,512]{1,0:T(8,128)(2,1)S(1)} %collective-permute-done.12.right_top), channel_id=1, source_target_pairs={{0,1},{1,2},{2,3},{3,0},{4,5},{5,6},{6,7},{7,4},{8,9},{9,10},{10,1... | collective-permute-start | bytes 1572872 | tf_op jit(solution)/shard_map/ppermute | solution.py:377
  143.0 18.8 %collective-permute-start.15 = (bf16[512,512]{1,0:T(8,128)(2,1)S(1)}, bf16[512,512]{1,0:T(8,128)(2,1)S(1)}, u32[]{:S(2)}, u32[]{:S(2)}) collective-permute-start(bf16[512,512]{1,0:T(8,128)(2,1)S(1)} %collective-permute-done.14.left_bottom), channel_id=1, source_target_pairs={{0,3},{1,0},{2,1},{3,2},{4,7},{5,4},{6,5},{7,6},{8,11},{9,8},{10,9... | collective-permute-start | bytes 1572872 | tf_op jit(solution)/shard_map/ppermute | solution.py:377
  (8 other events, 136.4 us)

commit v12 on v11

--- a/solution.py
+++ b/solution.py
@@ -319,18 +319,36 @@
         out[rows] = total[rows] + near_sum(own, right, left, w_own, w_others, 0)
 
 
-def far_kernel(far_top, far_bottom, w_others, total, out, held, sems):
-    steps, rows, _ = held.shape
+def far_kernel(begin, far, w_others, total, *rest):
+    out, held, sems = rest[-3:]
     stores = []
-    for step in range(steps):
-        far = (far_top, far_bottom)[2 * step // steps]
-        begin = step * rows % far.shape[0]
-        summed = product(far[begin : begin + rows], w_others.at[1], 0) + total[step * rows : (step + 1) * rows]
+    for step in range(held.shape[0]):
+        rows = held.shape[1]
+        at = step * rows
+        summed = product(far[at : at + rows], w_others.at[1], 0) + total[begin + at : begin + at + rows]
         held[step] = summed.astype(held.dtype)
-        stores.append(pltpu.make_async_copy(held.at[step], out.at[pl.ds(step * rows, rows)], sems.at[step]))
+        stores.append(pltpu.make_async_copy(held.at[step], out.at[pl.ds(begin + at, rows)], sems.at[step]))
         stores[-1].start()
     for store in stores:
         store.wait()
+
+
+def project_far(begin, far, w_others, total, into):
+    tokens, width = total.shape
+    rows, depth = far.shape
+    steps = 2
+    extra = [] if into is None else [from_hbm(into)]
+    return pl.pallas_call(
+        functools.partial(far_kernel, begin),
+        in_specs=[pl.BlockSpec(memory_space=pltpu.VMEM)] * 3 + [pl.BlockSpec(memory_space=pl.ANY)] * len(extra),
+        out_specs=pl.BlockSpec(memory_space=pl.ANY),
+        out_shape=in_hbm((tokens, width), jnp.bfloat16),
+        scratch_shapes=[pltpu.VMEM((steps, rows // steps, width), jnp.bfloat16), pltpu.SemaphoreType.DMA((steps,))],
+        input_output_aliases={3: 0} if extra else {},
+        compiler_params=pltpu.CompilerParams(vmem_limit_bytes=SMALL_VMEM),
+        cost_estimate=pl.CostEstimate(flops=2 * rows * depth * width, bytes_accessed=6 * rows * width, transcendentals=0),
+        name="far",
+    )(*[from_vmem(array) for array in (far, w_others, total)], *extra)
 
 
 def summing(kernel, name, operands, depth_terms):
@@ -357,19 +375,9 @@
 
 def project_late(pieces, w_own, w_others, total):
     near = summing(near_kernel, "near", (*pieces[:6], w_own, w_others, total), 3)
-    tokens, width = near.shape
-    depth = pieces[0].shape[1]
-    steps = 4
-    return pl.pallas_call(
-        far_kernel,
-        in_specs=[pl.BlockSpec(memory_space=pltpu.VMEM)] * 4,
-        out_specs=pl.BlockSpec(memory_space=pl.ANY),
-        out_shape=in_hbm((tokens, width), jnp.bfloat16),
-        scratch_shapes=[pltpu.VMEM((steps, tokens // steps, width), jnp.bfloat16), pltpu.SemaphoreType.DMA((steps,))],
-        compiler_params=pltpu.CompilerParams(vmem_limit_bytes=SMALL_VMEM),
-        cost_estimate=pl.CostEstimate(flops=2 * tokens * depth * width, bytes_accessed=8 * tokens * width, transcendentals=0),
-        name="far",
-    )(*[from_vmem(array) for array in (*pieces[6:], w_others, near)])
+    far_top, far_bottom = pieces[6:]
+    out = project_far(0, far_top, w_others, near, None)
+    return project_far(far_top.shape[0], far_bottom, w_others, near, out)
 
 
 def shifted(block, by):

time: 165 us -> 165 us (level)
  waiting for transfers between devices: 40.8 us -> 44 us
  Pallas kernels: 39.3 us -> 37 us
    pallas_call x1, Pallas kernels: 17.5 us -> 14.3 us  [spatial(): pl.pallas_call(functools.partial(spatial_kernel, head_count), grid_spec=p...]
    ppermute x15, waiting for transfers between devices: 33.3 us -> 36.5 us  [shifted(): lax.ppermute(block, 'head', [(at, (at + by) % count) for at in range(coun...]
  transfers between devices with their start and end apart: 19 -> 19, of which waited for: 9 -> 9; matrix products, arithmetic and copies ran while one was open for 6% -> 6% of each run, Pallas kernels for 18% -> 17%
where the time goes in v12:
time: 165 us
  waiting for transfers between devices  44 us (27%)
  starting transfers between devices  37.5 us (23%)
  Pallas kernels  37 us (22%)
  blocking collectives  35.3 us (21%)
  other arithmetic  8.76 us (5%)
  local copies, waits for them, and re-layouts  1.69 us (1%)
    ppermute x15, waiting for transfers between devices, shifted(): lax.ppermute(block, 'head', [(at, (at + by) % count) for at in range(coun...  36.5 us
    all_to_all x1, blocking collectives, over_frames(): return lax.all_to_all(blocks, 'seq', 0, 0, axis_index_groups=groups)  35.3 us
    ppermute x15, starting transfers between devices, shifted(): lax.ppermute(block, 'head', [(at, (at + by) % count) for at in range(coun...  25.2 us
    pallas_call x1, Pallas kernels, spatial(): pl.pallas_call(functools.partial(spatial_kernel, head_count), grid_spec=p...  14.3 us
    all_to_all x1, starting transfers between devices, over_frames(): return lax.all_to_all(blocks, 'seq', 0, 0, axis_index_groups=groups)  11.7 us
    all_to_all x1, waiting for transfers between devices, over_frames(): return lax.all_to_all(blocks, 'seq', 0, 0, axis_index_groups=groups)  7.48 us
    pallas_call x1, Pallas kernels, weight_blocks(): pl.pallas_call(weight_kernel, grid_spec=pltpu.PrefetchScalarGridSpec(num_...  6.46 us
    pallas_call x2, Pallas kernels, summing(): pl.pallas_call(kernel, in_specs=[whole] * len(operands), out_specs=whole,...  5.75 us
  transfers between devices with their start and end apart: 19, of which 9 were waited for; matrix products, arithmetic and copies ran while one was open for 6% of the time, Pallas kernels for 17%

profile of v12, /device:TPU:8, one launch (start us, length us, event | category | flops | bytes accessed | tf_op | source)
XLA Modules:
  0.0 164.6 jit_solution(14309680596563680543)
XLA Ops:
  0.0 5.2 %pack.1 = bf16[1024,1536]{1,0:T(8,128)(2,1)} custom-call(s32[6]{0:T(128)} %classes.7, bf16[1024,768]{1,0:T(8,128)(2,1)} %query.3, bf16[1024,768]{1,0:T(8,128)(2,1)} %key.3, bf16[1024,768]{1,0:T(8,128)(2,1)} %value.3, f32[1,128]{1,0:T(1,128)} %bitcast.13, f32[1,128]{1,0:T(1,128)} %bitcast.15), custom_call_target="tpu_custom_call" | custom-call | flops 4194304 | bytes 6291456 | tf_op jit(solution)/shard_map/pack/pallas_call | solution.py:105
  5.2 11.7 %all-to-all-start = ((bf16[32,32,1536]{2,1,0:T(8,128)(2,1)}), bf16[32,32,1536]{2,1,0:T(8,128)(2,1)S(1)}, u32[]{:S(2)}, u32[]{:S(2)}) async-start(bf16[32,32,1536]{2,1,0:T(8,128)(2,1)} %bitcast.12), calls=%async_computation | async-start | bytes 6291456 | tf_op jit(solution)/shard_map/all_to_all | solution.py:403
  18.1 6.5 %weight_blocks.1 = (bf16[768,768]{1,0:T(8,128)(2,1)}, bf16[384,768]{1,0:T(8,128)(2,1)}, bf16[384,768]{1,0:T(8,128)(2,1)}, bf16[384,768]{1,0:T(8,128)(2,1)}) custom-call(s32[6]{0:T(128)} %classes.7, s32[2]{0:T(128)} %pad_add_fusion.place, bf16[768,3072]{1,0:T(8,128)(2,1)} %weight.1), custom_call_target="tpu_custom_call" | custom-call | bytes 9437184 | tf_op jit(solution)/shard_map/weight_blocks/pallas_call | solution.py:284
  26.1 2.7 %collective-permute-start.9 = (bf16[384,768]{1,0:T(8,128)(2,1)}, bf16[384,768]{1,0:T(8,128)(2,1)}, u32[]{:S(2)}, u32[]{:S(2)}) collective-permute-start(bf16[384,768]{1,0:T(8,128)(2,1)} %get-tuple-element.16), channel_id=1, source_target_pairs={{0,2},{1,3},{2,0},{3,1},{4,6},{5,7},{6,4},{7,5},{8,10},{9,11},{10,... | collective-permute-start | bytes 1769480 | tf_op jit(solution)/shard_map/ppermute | solution.py:385
  30.3 14.3 %spatial.1 = (bf16[1024,512]{1,0:T(8,128)(2,1)}, bf16[1024,256]{1,0:T(8,128)(2,1)}) custom-call(s32[6]{0:T(128)} %classes.7, bf16[1024,768]{1,0:T(8,128)(2,1)} %query.3, bf16[1024,768]{1,0:T(8,128)(2,1)} %key.3, bf16[1024,768]{1,0:T(8,128)(2,1)} %collective-permute-done.other_key, bf16[1024,768]{1,0:T(8,128)(2,1)} %value.3, ...), custom_call_target="tpu_custom_call" | custom-call | flops 12884901888 | bytes 9437184 | tf_op jit(solution)/shard_map/spatial/pallas_call | solution.py:172
  44.5 10.3 %collective-permute-done.9.refs_1_ = bf16[384,768]{1,0:T(8,128)(2,1)} collective-permute-done((bf16[384,768]{1,0:T(8,128)(2,1)}, bf16[384,768]{1,0:T(8,128)(2,1)}, u32[]{:S(2)}, u32[]{:S(2)}) %collective-permute-start.9) | collective-permute-done | bytes 589856 | tf_op jit(solution)/shard_map/ppermute | solution.py:385
  54.9 2.9 %pad_maximum_fusion = bf16[3,384,768]{2,1,0:T(8,128)(2,1)} fusion(bf16[1,384,768]{2,1,0:T(8,128)(2,1)} %bitcast.7, bf16[1,384,768]{2,1,0:T(8,128)(2,1)} %bitcast.6, bf16[1,384,768]{2,1,0:T(8,128)(2,1)} %bitcast.5), kind=kLoop, calls=%fused_computation.1 | loop fusion | flops 1769472 | bytes 3538944 | tf_op jit(solution)/shard_map/stack | solution.py:421
  59.9 1.9 %collective-permute-start.5 = (bf16[512,256]{1,0:T(8,128)(2,1)}, bf16[512,256]{1,0:T(8,128)(2,1)}, u32[]{:S(2)}, u32[]{:S(2)}) collective-permute-start(bf16[512,256]{1,0:T(8,128)(2,1)} %get-tuple-element.27.own_bottom), channel_id=1, source_target_pairs={{0,3},{1,0},{2,1},{3,2},{4,7},{5,4},{6,5},{7,6},{8,11},{9,8},{10,9... | collective-permute-start | bytes 786440 | tf_op jit(solution)/shard_map/ppermute | solution.py:385
  62.0 3.1 %collective-permute-start.4 = (bf16[512,256]{1,0:T(8,128)(2,1)}, bf16[512,256]{1,0:T(8,128)(2,1)S(1)}, u32[]{:S(2)}, u32[]{:S(2)}) collective-permute-start(bf16[512,256]{1,0:T(8,128)(2,1)} %get-tuple-element.28.own_top), channel_id=1, source_target_pairs={{0,3},{1,0},{2,1},{3,2},{4,7},{5,4},{6,5},{7,6},{8,11},{9,8},{10,9... | collective-permute-start | bytes 786440 | tf_op jit(solution)/shard_map/ppermute | solution.py:385
  65.1 4.0 %collective-permute-done.2.rest_0_.right_top = bf16[512,256]{1,0:T(8,128)(2,1)S(1)} collective-permute-done((bf16[512,256]{1,0:T(8,128)(2,1)}, bf16[512,256]{1,0:T(8,128)(2,1)S(1)}, u32[]{:S(2)}, u32[]{:S(2)}) %collective-permute-start.2) | collective-permute-done | bytes 262176 | tf_op jit(solution)/shard_map/ppermute | solution.py:385
  69.4 3.1 %collective-permute-start.7 = (bf16[512,256]{1,0:T(8,128)(2,1)}, bf16[512,256]{1,0:T(8,128)(2,1)}, u32[]{:S(2)}, u32[]{:S(2)}) collective-permute-start(bf16[512,256]{1,0:T(8,128)(2,1)} %collective-permute-done.5.rest_3_.left_bottom), channel_id=1, source_target_pairs={{0,3},{1,0},{2,1},{3,2},{4,7},{5,4},{6,5},{7,6},{8,11},{9,8},{10,9... | collective-permute-start | bytes 786440 | tf_op jit(solution)/shard_map/ppermute | solution.py:385
  72.5 5.0 %maximum_select_fusion.rest_6_.w_others = bf16[3,768,768]{2,1,0:T(8,128)(2,1)} fusion(bf16[3,384,768]{2,1,0:T(8,128)(2,1)} %collective-permute-done.11, bf16[1,384,768]{2,1,0:T(8,128)(2,1)} %bitcast.7, bf16[1,384,768]{2,1,0:T(8,128)(2,1)} %bitcast.6, bf16[1,384,768]{2,1,0:T(8,128)(2,1)} %bitcast.5, pred[]{:T(512)S(6)} %eq.3), kind=kLoop, calls=%fused_computation | loop fusion | flops 30081024 | bytes 7077889 | tf_op jit(solution)/shard_map/jit(_where)/select_n | solution.py:423
  77.6 2.4 %collective-permute-done.6.rest_4_.far_top = bf16[512,256]{1,0:T(8,128)(2,1)S(1)} collective-permute-done((bf16[512,256]{1,0:T(8,128)(2,1)S(1)}, bf16[512,256]{1,0:T(8,128)(2,1)S(1)}, u32[]{:S(2)}, u32[]{:S(2)}) %collective-permute-start.6) | collective-permute-done | bytes 262176 | tf_op jit(solution)/shard_map/ppermute | solution.py:385
  80.7 7.5 %all-to-all-done.packed = bf16[32,32,1536]{2,1,0:T(8,128)(2,1)S(1)} async-done(((bf16[32,32,1536]{2,1,0:T(8,128)(2,1)}), bf16[32,32,1536]{2,1,0:T(8,128)(2,1)S(1)}, u32[]{:S(2)}, u32[]{:S(2)}) %all-to-all-start) | async-done | bytes 3145760 | tf_op jit(solution)/shard_map/all_to_all | solution.py:403
  88.2 2.7 %temporal.1 = bf16[32,32,512]{2,1,0:T(8,128)(2,1)} custom-call(s32[6]{0:T(128)S(1)} %copy-done.10, bf16[32,32,1536]{2,1,0:T(8,128)(2,1)S(1)} %all-to-all-done.packed, bf16[512,256]{1,0:T(8,128)(2,1)} %copy-done.2, bf16[512,256]{1,0:T(8,128)(2,1)} %copy-done.4, bf16[512,256]{1,0:T(8,128)(2,1)} %copy-done.6, ...), custom_call_target="tpu_custom_call" | custom-call | flops 536870912 | bytes 4194304 | tf_op jit(solution)/shard_map/temporal/pallas_call | solution.py:236
  90.9 35.3 %all_to_all.10 = bf16[32,32,512]{2,1,0:T(8,128)(2,1)S(1)} all-to-all(bf16[32,32,512]{2,1,0:T(8,128)(2,1)} %temporal.1), channel_id=1, replica_groups={{0,8,16,24,32,40,48,56,64,72,80,88,96,104,112,120,128,136,144,152,160,1..., dimensions={0} | all-to-all | bytes 2097152 | tf_op jit(solution)/shard_map/all_to_all | solution.py:403
  128.1 1.7 %collective-permute-start.12 = (bf16[512,512]{1,0:T(8,128)(2,1)S(1)}, bf16[512,512]{1,0:T(8,128)(2,1)S(1)}, u32[]{:S(2)}, u32[]{:S(2)}) collective-permute-start(bf16[512,512]{1,0:T(8,128)(2,1)S(1)} %get-tuple-element.24.own_bottom), channel_id=1, source_target_pairs={{0,3},{1,0},{2,1},{3,2},{4,7},{5,4},{6,5},{7,6},{8,11},{9,8},{10,9... | collective-permute-start | bytes 1572872 | tf_op jit(solution)/shard_map/ppermute | solution.py:385
  130.1 3.0 %collective-permute-start.16 = (bf16[512,512]{1,0:T(8,128)(2,1)S(1)}, bf16[512,512]{1,0:T(8,128)(2,1)S(1)}, u32[]{:S(2)}, u32[]{:S(2)}) collective-permute-start(bf16[512,512]{1,0:T(8,128)(2,1)S(1)} %get-tuple-element.23.own_top), channel_id=1, source_target_pairs={{0,3},{1,0},{2,1},{3,2},{4,7},{5,4},{6,5},{7,6},{8,11},{9,8},{10,9... | collective-permute-start | bytes 1572872 | tf_op jit(solution)/shard_map/ppermute | solution.py:385
  133.1 9.6 %collective-permute-done.14.right_top = bf16[512,512]{1,0:T(8,128)(2,1)S(1)} collective-permute-done((bf16[512,512]{1,0:T(8,128)(2,1)S(1)}, bf16[512,512]{1,0:T(8,128)(2,1)S(1)}, u32[]{:S(2)}, u32[]{:S(2)}) %collective-permute-start.14) | collective-permute-done | bytes 524320 | tf_op jit(solution)/shard_map/ppermute | solution.py:385
  143.0 3.0 %collective-permute-start.13 = (bf16[512,512]{1,0:T(8,128)(2,1)S(1)}, bf16[512,512]{1,0:T(8,128)(2,1)S(1)}, u32[]{:S(2)}, u32[]{:S(2)}) collective-permute-start(bf16[512,512]{1,0:T(8,128)(2,1)S(1)} %collective-permute-done.12.left_bottom), channel_id=1, source_target_pairs={{0,3},{1,0},{2,1},{3,2},{4,7},{5,4},{6,5},{7,6},{8,11},{9,8},{10,9... | collective-permute-start | bytes 1572872 | tf_op jit(solution)/shard_map/ppermute | solution.py:385
  146.0 3.0 %project_early.1.total = f32[1024,768]{1,0:T(8,128)S(1)} custom-call(bf16[512,256]{1,0:T(8,128)(2,1)} %get-tuple-element.28.own_top, bf16[512,256]{1,0:T(8,128)(2,1)} %get-tuple-element.27.own_bottom, bf16[512,256]{1,0:T(8,128)(2,1)S(1)} %copy-done.3, bf16[512,256]{1,0:T(8,128)(2,1)S(1)} %copy-done.5, bf16[512,256]{1,0:T(8,128)(2,1)S(1)} %copy-done.7, ...), custom_call_target="tpu_custom_call" | custom-call | flops 1610612736 | bytes 6291456 | tf_op jit(solution)/shard_map/project_early/pallas_call | solution.py:358
  149.0 4.9 %collective-permute-done.15.right_bottom = bf16[512,512]{1,0:T(8,128)(2,1)S(1)} collective-permute-done((bf16[512,512]{1,0:T(8,128)(2,1)S(1)}, bf16[512,512]{1,0:T(8,128)(2,1)S(1)}, u32[]{:S(2)}, u32[]{:S(2)}) %collective-permute-start.15) | collective-permute-done | bytes 524320 | tf_op jit(solution)/shard_map/ppermute | solution.py:385
  154.2 2.7 %near.1.total = f32[1024,768]{1,0:T(8,128)S(1)} custom-call(bf16[512,512]{1,0:T(8,128)(2,1)S(1)} %get-tuple-element.23.own_top, bf16[512,512]{1,0:T(8,128)(2,1)S(1)} %get-tuple-element.24.own_bottom, bf16[512,512]{1,0:T(8,128)(2,1)S(1)} %collective-permute-done.14.right_top, bf16[512,512]{1,0:T(8,128)(2,1)S(1)} %collective-permute-done.15.right_bottom, ...), custom_call_target="tpu_custom_call" | custom-call | flops 2415919104 | bytes 6291456 | tf_op jit(solution)/shard_map/near/pallas_call | solution.py:358
  156.9 4.8 %collective-permute-done.17.far = bf16[512,512]{1,0:T(8,128)(2,1)S(1)} collective-permute-done((bf16[512,512]{1,0:T(8,128)(2,1)S(1)}, bf16[512,512]{1,0:T(8,128)(2,1)S(1)}, u32[]{:S(2)}, u32[]{:S(2)}) %collective-permute-start.17) | collective-permute-done | bytes 524320 | tf_op jit(solution)/shard_map/ppermute | solution.py:385
  (56 shorter events, 12.9 us)
Async XLA Ops:
  5.2 83.0 %all-to-all-start = ((bf16[32,32,1536]{2,1,0:T(8,128)(2,1)}), bf16[32,32,1536]{2,1,0:T(8,128)(2,1)S(1)}, u32[]{:S(2)}, u32[]{:S(2)}) async-start(bf16[32,32,1536]{2,1,0:T(8,128)(2,1)} %bitcast.12), calls=%async_computation | async-start | bytes 6291456 | tf_op jit(solution)/shard_map/all_to_all | solution.py:403
  16.9 13.4 %collective-permute-start = (bf16[1024,768]{1,0:T(8,128)(2,1)}, bf16[1024,768]{1,0:T(8,128)(2,1)}, u32[]{:S(2)}, u32[]{:S(2)}) collective-permute-start(bf16[1024,768]{1,0:T(8,128)(2,1)} %key.3), channel_id=1, source_target_pairs={{0,4},{4,0},{8,12},{12,8},{16,20},{20,16},{24,28},{28,24},{32,36},... | collective-permute-start | bytes 4718600 | tf_op jit(solution)/shard_map/ppermute | solution.py:397
  17.0 13.3 %collective-permute-start.1 = (bf16[1024,768]{1,0:T(8,128)(2,1)}, bf16[1024,768]{1,0:T(8,128)(2,1)}, u32[]{:S(2)}, u32[]{:S(2)}) collective-permute-start(bf16[1024,768]{1,0:T(8,128)(2,1)} %value.3), channel_id=1, source_target_pairs={{0,4},{4,0},{8,12},{12,8},{16,20},{20,16},{24,28},{28,24},{32,36},... | collective-permute-start | bytes 4718600 | tf_op jit(solution)/shard_map/ppermute | solution.py:397
  24.6 19.9 %collective-permute-start.8 = (bf16[384,768]{1,0:T(8,128)(2,1)}, bf16[384,768]{1,0:T(8,128)(2,1)}, u32[]{:S(2)}, u32[]{:S(2)}) collective-permute-start(bf16[384,768]{1,0:T(8,128)(2,1)} %get-tuple-element.15), channel_id=1, source_target_pairs={{0,1},{1,2},{2,3},{3,0},{4,5},{5,6},{6,7},{7,4},{8,9},{9,10},{10,1... | collective-permute-start | bytes 1769480 | tf_op jit(solution)/shard_map/ppermute | solution.py:385
  26.1 28.7 %collective-permute-start.9 = (bf16[384,768]{1,0:T(8,128)(2,1)}, bf16[384,768]{1,0:T(8,128)(2,1)}, u32[]{:S(2)}, u32[]{:S(2)}) collective-permute-start(bf16[384,768]{1,0:T(8,128)(2,1)} %get-tuple-element.16), channel_id=1, source_target_pairs={{0,2},{1,3},{2,0},{3,1},{4,6},{5,7},{6,4},{7,5},{8,10},{9,11},{10,... | collective-permute-start | bytes 1769480 | tf_op jit(solution)/shard_map/ppermute | solution.py:385
  28.8 26.0 %collective-permute-start.10 = (bf16[384,768]{1,0:T(8,128)(2,1)}, bf16[384,768]{1,0:T(8,128)(2,1)}, u32[]{:S(2)}, u32[]{:S(2)}) collective-permute-start(bf16[384,768]{1,0:T(8,128)(2,1)} %get-tuple-element.17), channel_id=1, source_target_pairs={{0,3},{1,0},{2,1},{3,2},{4,7},{5,4},{6,5},{7,6},{8,11},{9,8},{10,9... | collective-permute-start | bytes 1769480 | tf_op jit(solution)/shard_map/ppermute | solution.py:385
  57.8 14.7 %collective-permute-start.11 = (bf16[3,384,768]{2,1,0:T(8,128)(2,1)}, bf16[3,384,768]{2,1,0:T(8,128)(2,1)}, u32[]{:S(2)}, u32[]{:S(2)}) collective-permute-start(bf16[3,384,768]{2,1,0:T(8,128)(2,1)} %pad_maximum_fusion), channel_id=1, source_target_pairs={{0,4},{4,0},{8,12},{12,8},{16,20},{20,16},{24,28},{28,24},{32,36},... | collective-permute-start | bytes 5308424 | tf_op jit(solution)/shard_map/ppermute | solution.py:397
  58.6 10.5 %collective-permute-start.2 = (bf16[512,256]{1,0:T(8,128)(2,1)}, bf16[512,256]{1,0:T(8,128)(2,1)S(1)}, u32[]{:S(2)}, u32[]{:S(2)}) collective-permute-start(bf16[512,256]{1,0:T(8,128)(2,1)} %get-tuple-element.28.own_top), channel_id=1, source_target_pairs={{0,1},{1,2},{2,3},{3,0},{4,5},{5,6},{6,7},{7,4},{8,9},{9,10},{10,1... | collective-permute-start | bytes 786440 | tf_op jit(solution)/shard_map/ppermute | solution.py:385
  59.9 9.5 %collective-permute-start.5 = (bf16[512,256]{1,0:T(8,128)(2,1)}, bf16[512,256]{1,0:T(8,128)(2,1)}, u32[]{:S(2)}, u32[]{:S(2)}) collective-permute-start(bf16[512,256]{1,0:T(8,128)(2,1)} %get-tuple-element.27.own_bottom), channel_id=1, source_target_pairs={{0,3},{1,0},{2,1},{3,2},{4,7},{5,4},{6,5},{7,6},{8,11},{9,8},{10,9... | collective-permute-start | bytes 786440 | tf_op jit(solution)/shard_map/ppermute | solution.py:385
  61.8 15.7 %collective-permute-start.3 = (bf16[512,256]{1,0:T(8,128)(2,1)}, bf16[512,256]{1,0:T(8,128)(2,1)S(1)}, u32[]{:S(2)}, u32[]{:S(2)}) collective-permute-start(bf16[512,256]{1,0:T(8,128)(2,1)} %get-tuple-element.27.own_bottom), channel_id=1, source_target_pairs={{0,1},{1,2},{2,3},{3,0},{4,5},{5,6},{6,7},{7,4},{8,9},{9,10},{10,1... | collective-permute-start | bytes 786440 | tf_op jit(solution)/shard_map/ppermute | solution.py:385
  62.0 15.6 %collective-permute-start.4 = (bf16[512,256]{1,0:T(8,128)(2,1)}, bf16[512,256]{1,0:T(8,128)(2,1)S(1)}, u32[]{:S(2)}, u32[]{:S(2)}) collective-permute-start(bf16[512,256]{1,0:T(8,128)(2,1)} %get-tuple-element.28.own_top), channel_id=1, source_target_pairs={{0,3},{1,0},{2,1},{3,2},{4,7},{5,4},{6,5},{7,6},{8,11},{9,8},{10,9... | collective-permute-start | bytes 786440 | tf_op jit(solution)/shard_map/ppermute | solution.py:385
  69.1 10.8 %collective-permute-start.6 = (bf16[512,256]{1,0:T(8,128)(2,1)S(1)}, bf16[512,256]{1,0:T(8,128)(2,1)S(1)}, u32[]{:S(2)}, u32[]{:S(2)}) collective-permute-start(bf16[512,256]{1,0:T(8,128)(2,1)S(1)} %collective-permute-done.2.rest_0_.right_top), channel_id=1, source_target_pairs={{0,1},{1,2},{2,3},{3,0},{4,5},{5,6},{6,7},{7,4},{8,9},{9,10},{10,1... | collective-permute-start | bytes 786440 | tf_op jit(solution)/shard_map/ppermute | solution.py:385
  69.4 11.3 %collective-permute-start.7 = (bf16[512,256]{1,0:T(8,128)(2,1)}, bf16[512,256]{1,0:T(8,128)(2,1)}, u32[]{:S(2)}, u32[]{:S(2)}) collective-permute-start(bf16[512,256]{1,0:T(8,128)(2,1)} %collective-permute-done.5.rest_3_.left_bottom), channel_id=1, source_target_pairs={{0,3},{1,0},{2,1},{3,2},{4,7},{5,4},{6,5},{7,6},{8,11},{9,8},{10,9... | collective-permute-start | bytes 786440 | tf_op jit(solution)/shard_map/ppermute | solution.py:385
  90.8 55.1 %copy-start = (bf16[3,768,768]{2,1,0:T(8,128)(2,1)S(1)}, bf16[3,768,768]{2,1,0:T(8,128)(2,1)}, u32[]{:S(2)}) copy-start(bf16[3,768,768]{2,1,0:T(8,128)(2,1)} %maximum_select_fusion.rest_6_.w_others) | copy-start | bytes 10616836
  90.8 55.1 %copy-start.1 = (bf16[768,768]{1,0:T(8,128)(2,1)S(1)}, bf16[768,768]{1,0:T(8,128)(2,1)}, u32[]{:S(2)}) copy-start(bf16[768,768]{1,0:T(8,128)(2,1)} %get-tuple-element.22.w_own) | copy-start | bytes 3538948
  90.9 55.1 %copy-start.3 = (bf16[512,256]{1,0:T(8,128)(2,1)S(1)}, bf16[512,256]{1,0:T(8,128)(2,1)}, u32[]{:S(2)}) copy-start(bf16[512,256]{1,0:T(8,128)(2,1)} %copy-done.2) | copy-start | bytes 786436
  90.9 55.1 %copy-start.5 = (bf16[512,256]{1,0:T(8,128)(2,1)S(1)}, bf16[512,256]{1,0:T(8,128)(2,1)}, u32[]{:S(2)}) copy-start(bf16[512,256]{1,0:T(8,128)(2,1)} %copy-done.4) | copy-start | bytes 786436
  90.9 55.1 %copy-start.7 = (bf16[512,256]{1,0:T(8,128)(2,1)S(1)}, bf16[512,256]{1,0:T(8,128)(2,1)}, u32[]{:S(2)}) copy-start(bf16[512,256]{1,0:T(8,128)(2,1)} %copy-done.6) | copy-start | bytes 786436
  126.5 16.1 %collective-permute-start.14 = (bf16[512,512]{1,0:T(8,128)(2,1)S(1)}, bf16[512,512]{1,0:T(8,128)(2,1)S(1)}, u32[]{:S(2)}, u32[]{:S(2)}) collective-permute-start(bf16[512,512]{1,0:T(8,128)(2,1)S(1)} %get-tuple-element.23.own_top), channel_id=1, source_target_pairs={{0,1},{1,2},{2,3},{3,0},{4,5},{5,6},{6,7},{7,4},{8,9},{9,10},{10,1... | collective-permute-start | bytes 1572872 | tf_op jit(solution)/shard_map/ppermute | solution.py:385
  128.1 14.9 %collective-permute-start.12 = (bf16[512,512]{1,0:T(8,128)(2,1)S(1)}, bf16[512,512]{1,0:T(8,128)(2,1)S(1)}, u32[]{:S(2)}, u32[]{:S(2)}) collective-permute-start(bf16[512,512]{1,0:T(8,128)(2,1)S(1)} %get-tuple-element.24.own_bottom), channel_id=1, source_target_pairs={{0,3},{1,0},{2,1},{3,2},{4,7},{5,4},{6,5},{7,6},{8,11},{9,8},{10,9... | collective-permute-start | bytes 1572872 | tf_op jit(solution)/shard_map/ppermute | solution.py:385
  129.8 24.1 %collective-permute-start.15 = (bf16[512,512]{1,0:T(8,128)(2,1)S(1)}, bf16[512,512]{1,0:T(8,128)(2,1)S(1)}, u32[]{:S(2)}, u32[]{:S(2)}) collective-permute-start(bf16[512,512]{1,0:T(8,128)(2,1)S(1)} %get-tuple-element.24.own_bottom), channel_id=1, source_target_pairs={{0,1},{1,2},{2,3},{3,0},{4,5},{5,6},{6,7},{7,4},{8,9},{9,10},{10,1... | collective-permute-start | bytes 1572872 | tf_op jit(solution)/shard_map/ppermute | solution.py:385
  130.1 24.1 %collective-permute-start.16 = (bf16[512,512]{1,0:T(8,128)(2,1)S(1)}, bf16[512,512]{1,0:T(8,128)(2,1)S(1)}, u32[]{:S(2)}, u32[]{:S(2)}) collective-permute-start(bf16[512,512]{1,0:T(8,128)(2,1)S(1)} %get-tuple-element.23.own_top), channel_id=1, source_target_pairs={{0,3},{1,0},{2,1},{3,2},{4,7},{5,4},{6,5},{7,6},{8,11},{9,8},{10,9... | collective-permute-start | bytes 1572872 | tf_op jit(solution)/shard_map/ppermute | solution.py:385
  142.7 19.1 %collective-permute-start.17 = (bf16[512,512]{1,0:T(8,128)(2,1)S(1)}, bf16[512,512]{1,0:T(8,128)(2,1)S(1)}, u32[]{:S(2)}, u32[]{:S(2)}) collective-permute-start(bf16[512,512]{1,0:T(8,128)(2,1)S(1)} %collective-permute-done.14.right_top), channel_id=1, source_target_pairs={{0,1},{1,2},{2,3},{3,0},{4,5},{5,6},{6,7},{7,4},{8,9},{9,10},{10,1... | collective-permute-start | bytes 1572872 | tf_op jit(solution)/shard_map/ppermute | solution.py:385
  143.0 20.1 %collective-permute-start.13 = (bf16[512,512]{1,0:T(8,128)(2,1)S(1)}, bf16[512,512]{1,0:T(8,128)(2,1)S(1)}, u32[]{:S(2)}, u32[]{:S(2)}) collective-permute-start(bf16[512,512]{1,0:T(8,128)(2,1)S(1)} %collective-permute-done.12.left_bottom), channel_id=1, source_target_pairs={{0,3},{1,0},{2,1},{3,2},{4,7},{5,4},{6,5},{7,6},{8,11},{9,8},{10,9... | collective-permute-start | bytes 1572872 | tf_op jit(solution)/shard_map/ppermute | solution.py:385
  (8 other events, 136.4 us)

commit v13 on v11

--- a/solution.py
+++ b/solution.py
@@ -84,16 +84,18 @@
     for at in range(3 * TMAX):
         slot, which = divmod(at, 3)
         source = (query, key, value)[which].at[:, pl.ds(pl.multiple_of(heads[slot] * HD, HD), HD)]
-        landing = raw if gains[which] is not None else ready
-        loads.append(pltpu.make_async_copy(source, landing.at[at], in_sems.at[at]))
+        landing = raw.at[at] if gains[which] is not None else ready.at[slot, :, pl.ds(which * HD, HD)]
+        loads.append(pltpu.make_async_copy(source, landing, in_sems.at[at]))
         loads[-1].start()
     for at in range(3 * TMAX):
-        gain = gains[at % 3]
+        slot, which = divmod(at, 3)
         loads[at].wait()
-        if gain is not None:
-            ready[at] = normed(raw[at], gain[...])
-        stores.append(pltpu.make_async_copy(ready.at[at], out.at[:, pl.ds(at * HD, HD)], out_sems.at[at]))
-        stores[-1].start()
+        if gains[which] is not None:
+            ready[slot, :, which * HD : (which + 1) * HD] = normed(raw[at], gains[which][...])
+        if which == 2:
+            target = out.at[:, pl.ds(3 * slot * HD, 3 * HD)]
+            stores.append(pltpu.make_async_copy(ready.at[slot], target, out_sems.at[slot]))
+            stores[-1].start()
     for store in stores:
         store.wait()
 
@@ -111,9 +113,9 @@
             out_specs=anywhere,
             scratch_shapes=[
                 pltpu.VMEM((3 * TMAX, tokens, HD), jnp.bfloat16),
-                pltpu.VMEM((3 * TMAX, tokens, HD), jnp.bfloat16),
+                pltpu.VMEM((TMAX, tokens, 3 * HD), jnp.bfloat16),
                 pltpu.SemaphoreType.DMA((3 * TMAX,)),
-                pltpu.SemaphoreType.DMA((3 * TMAX,)),
+                pltpu.SemaphoreType.DMA((TMAX,)),
             ],
         ),
         out_shape=in_hbm((tokens, TMAX * 3 * HD), jnp.bfloat16),

time: 165 us -> 165 us (level)
  Pallas kernels: 39.3 us -> 46 us
  waiting for transfers between devices: 40.8 us -> 34.1 us
    pallas_call x1, Pallas kernels: 17.5 us -> 24.2 us  [spatial(): pl.pallas_call(functools.partial(spatial_kernel, head_count), grid_spec=p...]
    ppermute x15, waiting for transfers between devices: 33.3 us -> 26.6 us  [shifted(): lax.ppermute(block, 'head', [(at, (at + by) % count) for at in range(coun...]
  transfers between devices with their start and end apart: 19 -> 19, of which waited for: 9 -> 9; matrix products, arithmetic and copies ran while one was open for 6% -> 6% of each run, Pallas kernels for 18% -> 22%
where the time goes in v13:
time: 165 us; the launch traced here: 164 us
  Pallas kernels  46 us (28%)
  starting transfers between devices  37.5 us (23%)
  blocking collectives  35.3 us (21%)
  waiting for transfers between devices  34.1 us (21%)
  other arithmetic  8.76 us (5%)
  local copies, waits for them, and re-layouts  1.69 us (1%)
    all_to_all x1, blocking collectives, over_frames(): return lax.all_to_all(blocks, 'seq', 0, 0, axis_index_groups=groups)  35.3 us
    ppermute x15, waiting for transfers between devices, shifted(): lax.ppermute(block, 'head', [(at, (at + by) % count) for at in range(coun...  26.6 us
    ppermute x15, starting transfers between devices, shifted(): lax.ppermute(block, 'head', [(at, (at + by) % count) for at in range(coun...  25.2 us
    pallas_call x1, Pallas kernels, spatial(): pl.pallas_call(functools.partial(spatial_kernel, head_count), grid_spec=p...  24.2 us
    all_to_all x1, starting transfers between devices, over_frames(): return lax.all_to_all(blocks, 'seq', 0, 0, axis_index_groups=groups)  11.7 us
    all_to_all x1, waiting for transfers between devices, over_frames(): return lax.all_to_all(blocks, 'seq', 0, 0, axis_index_groups=groups)  7.48 us
    pallas_call x1, Pallas kernels, weight_blocks(): pl.pallas_call(weight_kernel, grid_spec=pltpu.PrefetchScalarGridSpec(num_...  6.46 us
    pallas_call x2, Pallas kernels, summing(): pl.pallas_call(kernel, in_specs=[whole] * len(operands), out_specs=whole,...  5.74 us
  transfers between devices with their start and end apart: 19, of which 9 were waited for; matrix products, arithmetic and copies ran while one was open for 6% of the time, Pallas kernels for 22%

profile of v13, /device:TPU:8, one launch (start us, length us, event | category | flops | bytes accessed | tf_op | source)
XLA Modules:
  0.0 163.6 jit_solution(15284981848177693168)
XLA Ops:
  0.0 5.1 %pack.1 = bf16[1024,1536]{1,0:T(8,128)(2,1)} custom-call(s32[6]{0:T(128)} %classes.7, bf16[1024,768]{1,0:T(8,128)(2,1)} %query.3, bf16[1024,768]{1,0:T(8,128)(2,1)} %key.3, bf16[1024,768]{1,0:T(8,128)(2,1)} %value.3, f32[1,128]{1,0:T(1,128)} %bitcast.13, f32[1,128]{1,0:T(1,128)} %bitcast.15), custom_call_target="tpu_custom_call" | custom-call | flops 4194304 | bytes 6291456 | tf_op jit(solution)/shard_map/pack/pallas_call | solution.py:107
  5.1 11.7 %all-to-all-start = ((bf16[32,32,1536]{2,1,0:T(8,128)(2,1)}), bf16[32,32,1536]{2,1,0:T(8,128)(2,1)S(1)}, u32[]{:S(2)}, u32[]{:S(2)}) async-start(bf16[32,32,1536]{2,1,0:T(8,128)(2,1)} %bitcast.12), calls=%async_computation | async-start | bytes 6291456 | tf_op jit(solution)/shard_map/all_to_all | solution.py:397
  18.1 6.5 %weight_blocks.1 = (bf16[768,768]{1,0:T(8,128)(2,1)}, bf16[384,768]{1,0:T(8,128)(2,1)}, bf16[384,768]{1,0:T(8,128)(2,1)}, bf16[384,768]{1,0:T(8,128)(2,1)}) custom-call(s32[6]{0:T(128)} %classes.7, s32[2]{0:T(128)} %pad_add_fusion.place, bf16[768,3072]{1,0:T(8,128)(2,1)} %weight.1), custom_call_target="tpu_custom_call" | custom-call | bytes 9437184 | tf_op jit(solution)/shard_map/weight_blocks/pallas_call | solution.py:286
  26.1 2.7 %collective-permute-start.9 = (bf16[384,768]{1,0:T(8,128)(2,1)}, bf16[384,768]{1,0:T(8,128)(2,1)}, u32[]{:S(2)}, u32[]{:S(2)}) collective-permute-start(bf16[384,768]{1,0:T(8,128)(2,1)} %get-tuple-element.16), channel_id=1, source_target_pairs={{0,2},{1,3},{2,0},{3,1},{4,6},{5,7},{6,4},{7,5},{8,10},{9,11},{10,... | collective-permute-start | bytes 1769480 | tf_op jit(solution)/shard_map/ppermute | solution.py:379
  30.2 24.2 %spatial.1 = (bf16[1024,512]{1,0:T(8,128)(2,1)}, bf16[1024,256]{1,0:T(8,128)(2,1)}) custom-call(s32[6]{0:T(128)} %classes.7, bf16[1024,768]{1,0:T(8,128)(2,1)} %query.3, bf16[1024,768]{1,0:T(8,128)(2,1)} %key.3, bf16[1024,768]{1,0:T(8,128)(2,1)} %collective-permute-done.other_key, bf16[1024,768]{1,0:T(8,128)(2,1)} %value.3, ...), custom_call_target="tpu_custom_call" | custom-call | flops 12884901888 | bytes 9437184 | tf_op jit(solution)/shard_map/spatial/pallas_call | solution.py:174
  54.8 2.9 %pad_maximum_fusion = bf16[3,384,768]{2,1,0:T(8,128)(2,1)} fusion(bf16[1,384,768]{2,1,0:T(8,128)(2,1)} %bitcast.7, bf16[1,384,768]{2,1,0:T(8,128)(2,1)} %bitcast.6, bf16[1,384,768]{2,1,0:T(8,128)(2,1)} %bitcast.5), kind=kLoop, calls=%fused_computation.1 | loop fusion | flops 1769472 | bytes 3538944 | tf_op jit(solution)/shard_map/stack | solution.py:415
  59.9 1.9 %collective-permute-start.5 = (bf16[512,256]{1,0:T(8,128)(2,1)}, bf16[512,256]{1,0:T(8,128)(2,1)}, u32[]{:S(2)}, u32[]{:S(2)}) collective-permute-start(bf16[512,256]{1,0:T(8,128)(2,1)} %get-tuple-element.27.own_bottom), channel_id=1, source_target_pairs={{0,3},{1,0},{2,1},{3,2},{4,7},{5,4},{6,5},{7,6},{8,11},{9,8},{10,9... | collective-permute-start | bytes 786440 | tf_op jit(solution)/shard_map/ppermute | solution.py:379
  61.9 3.1 %collective-permute-start.4 = (bf16[512,256]{1,0:T(8,128)(2,1)}, bf16[512,256]{1,0:T(8,128)(2,1)S(1)}, u32[]{:S(2)}, u32[]{:S(2)}) collective-permute-start(bf16[512,256]{1,0:T(8,128)(2,1)} %get-tuple-element.28.own_top), channel_id=1, source_target_pairs={{0,3},{1,0},{2,1},{3,2},{4,7},{5,4},{6,5},{7,6},{8,11},{9,8},{10,9... | collective-permute-start | bytes 786440 | tf_op jit(solution)/shard_map/ppermute | solution.py:379
  65.0 4.0 %collective-permute-done.2.rest_0_.right_top = bf16[512,256]{1,0:T(8,128)(2,1)S(1)} collective-permute-done((bf16[512,256]{1,0:T(8,128)(2,1)}, bf16[512,256]{1,0:T(8,128)(2,1)S(1)}, u32[]{:S(2)}, u32[]{:S(2)}) %collective-permute-start.2) | collective-permute-done | bytes 262176 | tf_op jit(solution)/shard_map/ppermute | solution.py:379
  69.3 3.1 %collective-permute-start.7 = (bf16[512,256]{1,0:T(8,128)(2,1)}, bf16[512,256]{1,0:T(8,128)(2,1)}, u32[]{:S(2)}, u32[]{:S(2)}) collective-permute-start(bf16[512,256]{1,0:T(8,128)(2,1)} %collective-permute-done.5.rest_3_.left_bottom), channel_id=1, source_target_pairs={{0,3},{1,0},{2,1},{3,2},{4,7},{5,4},{6,5},{7,6},{8,11},{9,8},{10,9... | collective-permute-start | bytes 786440 | tf_op jit(solution)/shard_map/ppermute | solution.py:379
  72.5 5.0 %maximum_select_fusion.rest_6_.w_others = bf16[3,768,768]{2,1,0:T(8,128)(2,1)} fusion(bf16[3,384,768]{2,1,0:T(8,128)(2,1)} %collective-permute-done.11, bf16[1,384,768]{2,1,0:T(8,128)(2,1)} %bitcast.7, bf16[1,384,768]{2,1,0:T(8,128)(2,1)} %bitcast.6, bf16[1,384,768]{2,1,0:T(8,128)(2,1)} %bitcast.5, pred[]{:T(512)S(6)} %eq.3), kind=kLoop, calls=%fused_computation | loop fusion | flops 30081024 | bytes 7077889 | tf_op jit(solution)/shard_map/jit(_where)/select_n | solution.py:417
  77.5 2.4 %collective-permute-done.6.rest_4_.far_top = bf16[512,256]{1,0:T(8,128)(2,1)S(1)} collective-permute-done((bf16[512,256]{1,0:T(8,128)(2,1)S(1)}, bf16[512,256]{1,0:T(8,128)(2,1)S(1)}, u32[]{:S(2)}, u32[]{:S(2)}) %collective-permute-start.6) | collective-permute-done | bytes 262176 | tf_op jit(solution)/shard_map/ppermute | solution.py:379
  80.6 7.5 %all-to-all-done.packed = bf16[32,32,1536]{2,1,0:T(8,128)(2,1)S(1)} async-done(((bf16[32,32,1536]{2,1,0:T(8,128)(2,1)}), bf16[32,32,1536]{2,1,0:T(8,128)(2,1)S(1)}, u32[]{:S(2)}, u32[]{:S(2)}) %all-to-all-start) | async-done | bytes 3145760 | tf_op jit(solution)/shard_map/all_to_all | solution.py:397
  88.1 2.7 %temporal.1 = bf16[32,32,512]{2,1,0:T(8,128)(2,1)} custom-call(s32[6]{0:T(128)S(1)} %copy-done.10, bf16[32,32,1536]{2,1,0:T(8,128)(2,1)S(1)} %all-to-all-done.packed, bf16[512,256]{1,0:T(8,128)(2,1)} %copy-done.2, bf16[512,256]{1,0:T(8,128)(2,1)} %copy-done.4, bf16[512,256]{1,0:T(8,128)(2,1)} %copy-done.6, ...), custom_call_target="tpu_custom_call" | custom-call | flops 536870912 | bytes 4194304 | tf_op jit(solution)/shard_map/temporal/pallas_call | solution.py:238
  90.9 35.3 %all_to_all.10 = bf16[32,32,512]{2,1,0:T(8,128)(2,1)S(1)} all-to-all(bf16[32,32,512]{2,1,0:T(8,128)(2,1)} %temporal.1), channel_id=1, replica_groups={{0,8,16,24,32,40,48,56,64,72,80,88,96,104,112,120,128,136,144,152,160,1..., dimensions={0} | all-to-all | bytes 2097152 | tf_op jit(solution)/shard_map/all_to_all | solution.py:397
  128.1 1.7 %collective-permute-start.14 = (bf16[512,512]{1,0:T(8,128)(2,1)S(1)}, bf16[512,512]{1,0:T(8,128)(2,1)S(1)}, u32[]{:S(2)}, u32[]{:S(2)}) collective-permute-start(bf16[512,512]{1,0:T(8,128)(2,1)S(1)} %get-tuple-element.23.own_bottom), channel_id=1, source_target_pairs={{0,3},{1,0},{2,1},{3,2},{4,7},{5,4},{6,5},{7,6},{8,11},{9,8},{10,9... | collective-permute-start | bytes 1572872 | tf_op jit(solution)/shard_map/ppermute | solution.py:379
  130.1 3.0 %collective-permute-start.17 = (bf16[512,512]{1,0:T(8,128)(2,1)S(1)}, bf16[512,512]{1,0:T(8,128)(2,1)S(1)}, u32[]{:S(2)}, u32[]{:S(2)}) collective-permute-start(bf16[512,512]{1,0:T(8,128)(2,1)S(1)} %get-tuple-element.24.own_top), channel_id=1, source_target_pairs={{0,3},{1,0},{2,1},{3,2},{4,7},{5,4},{6,5},{7,6},{8,11},{9,8},{10,9... | collective-permute-start | bytes 1572872 | tf_op jit(solution)/shard_map/ppermute | solution.py:379
  133.0 9.6 %collective-permute-done.12.right_top = bf16[512,512]{1,0:T(8,128)(2,1)S(1)} collective-permute-done((bf16[512,512]{1,0:T(8,128)(2,1)S(1)}, bf16[512,512]{1,0:T(8,128)(2,1)S(1)}, u32[]{:S(2)}, u32[]{:S(2)}) %collective-permute-start.12) | collective-permute-done | bytes 524320 | tf_op jit(solution)/shard_map/ppermute | solution.py:379
  142.9 3.0 %collective-permute-start.15 = (bf16[512,512]{1,0:T(8,128)(2,1)S(1)}, bf16[512,512]{1,0:T(8,128)(2,1)S(1)}, u32[]{:S(2)}, u32[]{:S(2)}) collective-permute-start(bf16[512,512]{1,0:T(8,128)(2,1)S(1)} %collective-permute-done.14.left_bottom), channel_id=1, source_target_pairs={{0,3},{1,0},{2,1},{3,2},{4,7},{5,4},{6,5},{7,6},{8,11},{9,8},{10,9... | collective-permute-start | bytes 1572872 | tf_op jit(solution)/shard_map/ppermute | solution.py:379
  145.9 3.0 %project_early.1.total = f32[1024,768]{1,0:T(8,128)S(1)} custom-call(bf16[512,256]{1,0:T(8,128)(2,1)} %get-tuple-element.28.own_top, bf16[512,256]{1,0:T(8,128)(2,1)} %get-tuple-element.27.own_bottom, bf16[512,256]{1,0:T(8,128)(2,1)S(1)} %copy-done.3, bf16[512,256]{1,0:T(8,128)(2,1)S(1)} %copy-done.5, bf16[512,256]{1,0:T(8,128)(2,1)S(1)} %copy-done.7, ...), custom_call_target="tpu_custom_call" | custom-call | flops 1610612736 | bytes 6291456 | tf_op jit(solution)/shard_map/project_early/pallas_call | solution.py:342
  148.9 4.9 %collective-permute-done.16.right_bottom = bf16[512,512]{1,0:T(8,128)(2,1)S(1)} collective-permute-done((bf16[512,512]{1,0:T(8,128)(2,1)S(1)}, bf16[512,512]{1,0:T(8,128)(2,1)S(1)}, u32[]{:S(2)}, u32[]{:S(2)}) %collective-permute-start.16) | collective-permute-done | bytes 524320 | tf_op jit(solution)/shard_map/ppermute | solution.py:379
  154.2 2.7 %near.1.total = f32[1024,768]{1,0:T(8,128)S(1)} custom-call(bf16[512,512]{1,0:T(8,128)(2,1)S(1)} %get-tuple-element.24.own_top, bf16[512,512]{1,0:T(8,128)(2,1)S(1)} %get-tuple-element.23.own_bottom, bf16[512,512]{1,0:T(8,128)(2,1)S(1)} %collective-permute-done.12.right_top, bf16[512,512]{1,0:T(8,128)(2,1)S(1)} %collective-permute-done.16.right_bottom, ...), custom_call_target="tpu_custom_call" | custom-call | flops 2415919104 | bytes 6291456 | tf_op jit(solution)/shard_map/near/pallas_call | solution.py:342
  156.9 4.8 %collective-permute-done.13.far_top = bf16[512,512]{1,0:T(8,128)(2,1)S(1)} collective-permute-done((bf16[512,512]{1,0:T(8,128)(2,1)S(1)}, bf16[512,512]{1,0:T(8,128)(2,1)S(1)}, u32[]{:S(2)}, u32[]{:S(2)}) %collective-permute-start.13) | collective-permute-done | bytes 524320 | tf_op jit(solution)/shard_map/ppermute | solution.py:379
  161.7 1.8 %far.1 = bf16[1024,768]{1,0:T(8,128)(2,1)} custom-call(bf16[512,512]{1,0:T(8,128)(2,1)S(1)} %collective-permute-done.13.far_top, bf16[512,512]{1,0:T(8,128)(2,1)S(1)} %collective-permute-done.15.far_bottom, bf16[3,768,768]{2,1,0:T(8,128)(2,1)S(1)} %copy-done, f32[1024,768]{1,0:T(8,128)S(1)} %near.1.total), custom_call_target="tpu_custom_call" | custom-call | flops 805306368 | bytes 6291456 | tf_op jit(solution)/shard_map/far/pallas_call | solution.py:365
  (55 shorter events, 10.5 us)
Async XLA Ops:
  5.1 83.0 %all-to-all-start = ((bf16[32,32,1536]{2,1,0:T(8,128)(2,1)}), bf16[32,32,1536]{2,1,0:T(8,128)(2,1)S(1)}, u32[]{:S(2)}, u32[]{:S(2)}) async-start(bf16[32,32,1536]{2,1,0:T(8,128)(2,1)} %bitcast.12), calls=%async_computation | async-start | bytes 6291456 | tf_op jit(solution)/shard_map/all_to_all | solution.py:397
  16.9 13.4 %collective-permute-start = (bf16[1024,768]{1,0:T(8,128)(2,1)}, bf16[1024,768]{1,0:T(8,128)(2,1)}, u32[]{:S(2)}, u32[]{:S(2)}) collective-permute-start(bf16[1024,768]{1,0:T(8,128)(2,1)} %key.3), channel_id=1, source_target_pairs={{0,4},{4,0},{8,12},{12,8},{16,20},{20,16},{24,28},{28,24},{32,36},... | collective-permute-start | bytes 4718600 | tf_op jit(solution)/shard_map/ppermute | solution.py:391
  17.0 13.3 %collective-permute-start.1 = (bf16[1024,768]{1,0:T(8,128)(2,1)}, bf16[1024,768]{1,0:T(8,128)(2,1)}, u32[]{:S(2)}, u32[]{:S(2)}) collective-permute-start(bf16[1024,768]{1,0:T(8,128)(2,1)} %value.3), channel_id=1, source_target_pairs={{0,4},{4,0},{8,12},{12,8},{16,20},{20,16},{24,28},{28,24},{32,36},... | collective-permute-start | bytes 4718600 | tf_op jit(solution)/shard_map/ppermute | solution.py:391
  24.6 29.9 %collective-permute-start.8 = (bf16[384,768]{1,0:T(8,128)(2,1)}, bf16[384,768]{1,0:T(8,128)(2,1)}, u32[]{:S(2)}, u32[]{:S(2)}) collective-permute-start(bf16[384,768]{1,0:T(8,128)(2,1)} %get-tuple-element.15), channel_id=1, source_target_pairs={{0,1},{1,2},{2,3},{3,0},{4,5},{5,6},{6,7},{7,4},{8,9},{9,10},{10,1... | collective-permute-start | bytes 1769480 | tf_op jit(solution)/shard_map/ppermute | solution.py:379
  26.1 28.7 %collective-permute-start.9 = (bf16[384,768]{1,0:T(8,128)(2,1)}, bf16[384,768]{1,0:T(8,128)(2,1)}, u32[]{:S(2)}, u32[]{:S(2)}) collective-permute-start(bf16[384,768]{1,0:T(8,128)(2,1)} %get-tuple-element.16), channel_id=1, source_target_pairs={{0,2},{1,3},{2,0},{3,1},{4,6},{5,7},{6,4},{7,5},{8,10},{9,11},{10,... | collective-permute-start | bytes 1769480 | tf_op jit(solution)/shard_map/ppermute | solution.py:379
  28.8 26.0 %collective-permute-start.10 = (bf16[384,768]{1,0:T(8,128)(2,1)}, bf16[384,768]{1,0:T(8,128)(2,1)}, u32[]{:S(2)}, u32[]{:S(2)}) collective-permute-start(bf16[384,768]{1,0:T(8,128)(2,1)} %get-tuple-element.17), channel_id=1, source_target_pairs={{0,3},{1,0},{2,1},{3,2},{4,7},{5,4},{6,5},{7,6},{8,11},{9,8},{10,9... | collective-permute-start | bytes 1769480 | tf_op jit(solution)/shard_map/ppermute | solution.py:379
  57.7 14.7 %collective-permute-start.11 = (bf16[3,384,768]{2,1,0:T(8,128)(2,1)}, bf16[3,384,768]{2,1,0:T(8,128)(2,1)}, u32[]{:S(2)}, u32[]{:S(2)}) collective-permute-start(bf16[3,384,768]{2,1,0:T(8,128)(2,1)} %pad_maximum_fusion), channel_id=1, source_target_pairs={{0,4},{4,0},{8,12},{12,8},{16,20},{20,16},{24,28},{28,24},{32,36},... | collective-permute-start | bytes 5308424 | tf_op jit(solution)/shard_map/ppermute | solution.py:391
  58.6 10.5 %collective-permute-start.2 = (bf16[512,256]{1,0:T(8,128)(2,1)}, bf16[512,256]{1,0:T(8,128)(2,1)S(1)}, u32[]{:S(2)}, u32[]{:S(2)}) collective-permute-start(bf16[512,256]{1,0:T(8,128)(2,1)} %get-tuple-element.28.own_top), channel_id=1, source_target_pairs={{0,1},{1,2},{2,3},{3,0},{4,5},{5,6},{6,7},{7,4},{8,9},{9,10},{10,1... | collective-permute-start | bytes 786440 | tf_op jit(solution)/shard_map/ppermute | solution.py:379
  59.9 9.5 %collective-permute-start.5 = (bf16[512,256]{1,0:T(8,128)(2,1)}, bf16[512,256]{1,0:T(8,128)(2,1)}, u32[]{:S(2)}, u32[]{:S(2)}) collective-permute-start(bf16[512,256]{1,0:T(8,128)(2,1)} %get-tuple-element.27.own_bottom), channel_id=1, source_target_pairs={{0,3},{1,0},{2,1},{3,2},{4,7},{5,4},{6,5},{7,6},{8,11},{9,8},{10,9... | collective-permute-start | bytes 786440 | tf_op jit(solution)/shard_map/ppermute | solution.py:379
  61.8 15.7 %collective-permute-start.3 = (bf16[512,256]{1,0:T(8,128)(2,1)}, bf16[512,256]{1,0:T(8,128)(2,1)S(1)}, u32[]{:S(2)}, u32[]{:S(2)}) collective-permute-start(bf16[512,256]{1,0:T(8,128)(2,1)} %get-tuple-element.27.own_bottom), channel_id=1, source_target_pairs={{0,1},{1,2},{2,3},{3,0},{4,5},{5,6},{6,7},{7,4},{8,9},{9,10},{10,1... | collective-permute-start | bytes 786440 | tf_op jit(solution)/shard_map/ppermute | solution.py:379
  61.9 15.6 %collective-permute-start.4 = (bf16[512,256]{1,0:T(8,128)(2,1)}, bf16[512,256]{1,0:T(8,128)(2,1)S(1)}, u32[]{:S(2)}, u32[]{:S(2)}) collective-permute-start(bf16[512,256]{1,0:T(8,128)(2,1)} %get-tuple-element.28.own_top), channel_id=1, source_target_pairs={{0,3},{1,0},{2,1},{3,2},{4,7},{5,4},{6,5},{7,6},{8,11},{9,8},{10,9... | collective-permute-start | bytes 786440 | tf_op jit(solution)/shard_map/ppermute | solution.py:379
  69.1 10.8 %collective-permute-start.6 = (bf16[512,256]{1,0:T(8,128)(2,1)S(1)}, bf16[512,256]{1,0:T(8,128)(2,1)S(1)}, u32[]{:S(2)}, u32[]{:S(2)}) collective-permute-start(bf16[512,256]{1,0:T(8,128)(2,1)S(1)} %collective-permute-done.2.rest_0_.right_top), channel_id=1, source_target_pairs={{0,1},{1,2},{2,3},{3,0},{4,5},{5,6},{6,7},{7,4},{8,9},{9,10},{10,1... | collective-permute-start | bytes 786440 | tf_op jit(solution)/shard_map/ppermute | solution.py:379
  69.3 11.3 %collective-permute-start.7 = (bf16[512,256]{1,0:T(8,128)(2,1)}, bf16[512,256]{1,0:T(8,128)(2,1)}, u32[]{:S(2)}, u32[]{:S(2)}) collective-permute-start(bf16[512,256]{1,0:T(8,128)(2,1)} %collective-permute-done.5.rest_3_.left_bottom), channel_id=1, source_target_pairs={{0,3},{1,0},{2,1},{3,2},{4,7},{5,4},{6,5},{7,6},{8,11},{9,8},{10,9... | collective-permute-start | bytes 786440 | tf_op jit(solution)/shard_map/ppermute | solution.py:379
  90.8 55.1 %copy-start = (bf16[3,768,768]{2,1,0:T(8,128)(2,1)S(1)}, bf16[3,768,768]{2,1,0:T(8,128)(2,1)}, u32[]{:S(2)}) copy-start(bf16[3,768,768]{2,1,0:T(8,128)(2,1)} %maximum_select_fusion.rest_6_.w_others) | copy-start | bytes 10616836
  90.8 55.1 %copy-start.1 = (bf16[768,768]{1,0:T(8,128)(2,1)S(1)}, bf16[768,768]{1,0:T(8,128)(2,1)}, u32[]{:S(2)}) copy-start(bf16[768,768]{1,0:T(8,128)(2,1)} %get-tuple-element.22.w_own) | copy-start | bytes 3538948
  90.8 55.1 %copy-start.3 = (bf16[512,256]{1,0:T(8,128)(2,1)S(1)}, bf16[512,256]{1,0:T(8,128)(2,1)}, u32[]{:S(2)}) copy-start(bf16[512,256]{1,0:T(8,128)(2,1)} %copy-done.2) | copy-start | bytes 786436
  90.8 55.1 %copy-start.5 = (bf16[512,256]{1,0:T(8,128)(2,1)S(1)}, bf16[512,256]{1,0:T(8,128)(2,1)}, u32[]{:S(2)}) copy-start(bf16[512,256]{1,0:T(8,128)(2,1)} %copy-done.4) | copy-start | bytes 786436
  90.8 55.1 %copy-start.7 = (bf16[512,256]{1,0:T(8,128)(2,1)S(1)}, bf16[512,256]{1,0:T(8,128)(2,1)}, u32[]{:S(2)}) copy-start(bf16[512,256]{1,0:T(8,128)(2,1)} %copy-done.6) | copy-start | bytes 786436
  126.5 16.1 %collective-permute-start.12 = (bf16[512,512]{1,0:T(8,128)(2,1)S(1)}, bf16[512,512]{1,0:T(8,128)(2,1)S(1)}, u32[]{:S(2)}, u32[]{:S(2)}) collective-permute-start(bf16[512,512]{1,0:T(8,128)(2,1)S(1)} %get-tuple-element.24.own_top), channel_id=1, source_target_pairs={{0,1},{1,2},{2,3},{3,0},{4,5},{5,6},{6,7},{7,4},{8,9},{9,10},{10,1... | collective-permute-start | bytes 1572872 | tf_op jit(solution)/shard_map/ppermute | solution.py:379
  128.1 14.9 %collective-permute-start.14 = (bf16[512,512]{1,0:T(8,128)(2,1)S(1)}, bf16[512,512]{1,0:T(8,128)(2,1)S(1)}, u32[]{:S(2)}, u32[]{:S(2)}) collective-permute-start(bf16[512,512]{1,0:T(8,128)(2,1)S(1)} %get-tuple-element.23.own_bottom), channel_id=1, source_target_pairs={{0,3},{1,0},{2,1},{3,2},{4,7},{5,4},{6,5},{7,6},{8,11},{9,8},{10,9... | collective-permute-start | bytes 1572872 | tf_op jit(solution)/shard_map/ppermute | solution.py:379
  129.8 24.1 %collective-permute-start.16 = (bf16[512,512]{1,0:T(8,128)(2,1)S(1)}, bf16[512,512]{1,0:T(8,128)(2,1)S(1)}, u32[]{:S(2)}, u32[]{:S(2)}) collective-permute-start(bf16[512,512]{1,0:T(8,128)(2,1)S(1)} %get-tuple-element.23.own_bottom), channel_id=1, source_target_pairs={{0,1},{1,2},{2,3},{3,0},{4,5},{5,6},{6,7},{7,4},{8,9},{9,10},{10,1... | collective-permute-start | bytes 1572872 | tf_op jit(solution)/shard_map/ppermute | solution.py:379
  130.1 24.1 %collective-permute-start.17 = (bf16[512,512]{1,0:T(8,128)(2,1)S(1)}, bf16[512,512]{1,0:T(8,128)(2,1)S(1)}, u32[]{:S(2)}, u32[]{:S(2)}) collective-permute-start(bf16[512,512]{1,0:T(8,128)(2,1)S(1)} %get-tuple-element.24.own_top), channel_id=1, source_target_pairs={{0,3},{1,0},{2,1},{3,2},{4,7},{5,4},{6,5},{7,6},{8,11},{9,8},{10,9... | collective-permute-start | bytes 1572872 | tf_op jit(solution)/shard_map/ppermute | solution.py:379
  142.6 19.1 %collective-permute-start.13 = (bf16[512,512]{1,0:T(8,128)(2,1)S(1)}, bf16[512,512]{1,0:T(8,128)(2,1)S(1)}, u32[]{:S(2)}, u32[]{:S(2)}) collective-permute-start(bf16[512,512]{1,0:T(8,128)(2,1)S(1)} %collective-permute-done.12.right_top), channel_id=1, source_target_pairs={{0,1},{1,2},{2,3},{3,0},{4,5},{5,6},{6,7},{7,4},{8,9},{9,10},{10,1... | collective-permute-start | bytes 1572872 | tf_op jit(solution)/shard_map/ppermute | solution.py:379
  142.9 18.8 %collective-permute-start.15 = (bf16[512,512]{1,0:T(8,128)(2,1)S(1)}, bf16[512,512]{1,0:T(8,128)(2,1)S(1)}, u32[]{:S(2)}, u32[]{:S(2)}) collective-permute-start(bf16[512,512]{1,0:T(8,128)(2,1)S(1)} %collective-permute-done.14.left_bottom), channel_id=1, source_target_pairs={{0,3},{1,0},{2,1},{3,2},{4,7},{5,4},{6,5},{7,6},{8,11},{9,8},{10,9... | collective-permute-start | bytes 1572872 | tf_op jit(solution)/shard_map/ppermute | solution.py:379
  (8 other events, 136.4 us)
